TPU v7x, 32 devices: a whole 2x2x4 slice. The times are simulated.
32 devices in a mesh: head: 2 (over x), seq: 16 (over z, y, core).
Axes of the slice: x: 2, y: 2, z: 4, core: 2. Of those that a mesh axis runs over, the one named last changes fastest.
Arguments:
- tokens: bfloat16 [16384, 4096], P('seq')
- qkv_weight: bfloat16 [4096, 1536], P('seq', 'head'), may hold values from -0.09375 to 0.09375
- out_weight: bfloat16 [512, 4096], P('head', 'seq'), may hold values from -0.25 to 0.25
- centroids: float32 [4, 64, 128], P('head', 'seq'), may hold values from -6 to 6
- clusters: int32 [4, 128], P('head', 'seq'), may hold values from 0 to 63, as said below
- slots: int32 [4, 128], P('head', 'seq'), may hold values from 0 to 1, as said below
Outputs:
- output: bfloat16 [4096, 16384], P('head', 'seq')
- new_centroids: float32 [4, 64, 128], P('head', 'seq')
Inputs may be any that keep to these rules, and one draw needn't show every extreme that they name: `clusters`: for each head at most 2 tiles name one cluster, and in each head every cluster of some owner holds 2 tiles; the owner of cluster c is the index c // 4 of seq. A tile of head h from the index s of seq names an owner o with s + o - h divisible by 2. The tiles of one index of seq, over the 2 heads of one index of head, name pairwise different owners. Tiles of one head naming the same cluster have different slots.
All inputs are finite; a program needn't handle non-finite values.
Results may differ from a plain program's by a relative error of at most 0.017.
Values may be sent and summed in bfloat16 or wider, within the bound.
No kernel may reach another device: no remote copies, remote signals or barrier semaphores. Data moves between devices by JAX's collectives and lax.ppermute only.
A program may use at most 128 MiB of HBM per device.

v0:
```python
import jax
import jax.numpy as jnp
from jax import lax
from jax.sharding import PartitionSpec as P

CAP = 2


LOGIT_SCALE = 8.0
KEEP_RATE = 0.75


def unit_rows(values, epsilon):
    return values * lax.rsqrt(jnp.mean(values * values, axis=-1, keepdims=True) + epsilon)


def update_centroids(centroid_rows, key_float, token_live, tiles_held, tile_rows):
    key_sums = jnp.sum(key_float * token_live[:, :, None], axis=1)
    counts = tiles_held * tile_rows
    means = key_sums / jnp.maximum(counts, 1.0)[:, None]
    return centroid_rows + (1.0 - KEEP_RATE) * jnp.where(
        counts[:, None] > 0, means - centroid_rows, 0.0
    )


def on_device(tokens, qkv_weight, out_weight, centroids, clusters, slots):
    tok_rows, model_width = tokens.shape
    heads_here, tiles_here = clusters.shape
    clus_here = centroids.shape[1]
    head_dim = centroids.shape[2]
    tile_rows = tok_rows // tiles_here
    seq_count = lax.axis_size("seq")
    normed = unit_rows(tokens.astype(jnp.float32), 1e-05).astype(jnp.bfloat16)
    columns = normed
    projected = jnp.dot(
        columns,
        lax.all_gather(qkv_weight, "seq", axis=0, tiled=True),
        preferred_element_type=jnp.float32,
    ).astype(jnp.bfloat16)
    item_width = tile_rows * 3 * head_dim
    tile_items = (
        projected.reshape(tiles_here, tile_rows, heads_here, 3 * head_dim)
        .transpose(2, 0, 1, 3)
        .reshape(heads_here * tiles_here, item_width)
    )
    owners = (clusters // clus_here).reshape(-1)
    targets = (owners[None, :] == jnp.arange(seq_count, dtype=jnp.int32)[:, None]).astype(jnp.int32)
    outgoing = jnp.dot(
        targets.astype(jnp.bfloat16), tile_items, preferred_element_type=jnp.float32
    ).astype(jnp.bfloat16)
    slot_labels = (
        jnp.arange(heads_here, dtype=jnp.int32)[:, None] * clus_here * CAP
        + clusters % clus_here * CAP
        + slots
    ).reshape(-1) + 1
    tile_labels = jnp.broadcast_to(
        lax.axis_index("seq") * tiles_here + jnp.arange(tiles_here, dtype=jnp.int32),
        (heads_here, tiles_here),
    ).reshape(-1)
    labels = jnp.stack(
        [
            jnp.sum(targets * slot_labels[None, :], axis=1),
            jnp.sum(targets * tile_labels[None, :], axis=1),
        ],
        axis=1,
    )
    incoming, arrived = (
        lax.all_to_all(outgoing, "seq", split_axis=0, concat_axis=0, tiled=True),
        lax.all_to_all(labels, "seq", split_axis=0, concat_axis=0, tiled=True),
    )
    total_slots = heads_here * clus_here * CAP
    placing = (arrived[None, :, 0] - 1 == jnp.arange(total_slots, dtype=jnp.int32)[:, None]).astype(
        jnp.int32
    )
    slotted = jnp.dot(
        placing.astype(jnp.bfloat16), incoming, preferred_element_type=jnp.float32
    ).astype(jnp.bfloat16)
    occupied = jnp.sum(placing, axis=1).astype(jnp.float32)
    tile_of = jnp.sum(placing * arrived[None, :, 1], axis=1)
    batches = heads_here * clus_here
    span_rows = CAP * tile_rows
    cluster_grouped_rows = slotted.reshape(batches, span_rows, 3, head_dim)
    token_live = jnp.repeat(occupied.reshape(batches, CAP), tile_rows, axis=1)
    position = (
        tile_of.reshape(batches, CAP, 1) * tile_rows
        + jnp.arange(tile_rows, dtype=jnp.int32)[None, None, :]
    ).reshape(batches, span_rows)
    normalized_query = unit_rows(cluster_grouped_rows[:, :, 0].astype(jnp.float32), 1e-06).astype(
        jnp.bfloat16
    )
    key_float = unit_rows(cluster_grouped_rows[:, :, 1].astype(jnp.float32), 1e-06)
    normalized_key = key_float.astype(jnp.bfloat16)
    attention_logits = (
        LOGIT_SCALE
        / head_dim
        * jnp.einsum(
            "tra,tla->trl", normalized_query, normalized_key, preferred_element_type=jnp.float32
        )
    )
    diagonal = jnp.arange(span_rows)[:, None] == jnp.arange(span_rows)[None, :]
    allowed = (token_live[:, None, :] > 0) & (
        position[:, None, :] <= position[:, :, None]
    ) | diagonal[None]
    exp_scores = jnp.where(allowed, jnp.exp(attention_logits), 0.0)
    attention_probs = (exp_scores / jnp.sum(exp_scores, axis=-1, keepdims=True)).astype(
        jnp.bfloat16
    )
    attended = jnp.einsum(
        "xjs,xsv->xjv",
        attention_probs,
        cluster_grouped_rows[:, :, 2],
        preferred_element_type=jnp.float32,
    ).astype(jnp.bfloat16)
    tiles_held = jnp.sum(occupied.reshape(batches, CAP), axis=1)
    new_centroids = update_centroids(
        centroids.reshape(batches, head_dim), key_float, token_live, tiles_held, tile_rows
    ).reshape(centroids.shape)
    returning = jnp.dot(
        placing.T.astype(jnp.bfloat16),
        attended.reshape(total_slots, tile_rows * head_dim),
        preferred_element_type=jnp.float32,
    ).astype(jnp.bfloat16)
    answered = lax.all_to_all(returning, "seq", split_axis=0, concat_axis=0, tiled=True)
    returned_rows = jnp.dot(
        targets.T.astype(jnp.bfloat16), answered, preferred_element_type=jnp.float32
    ).astype(jnp.bfloat16)
    attention = (
        returned_rows.reshape(heads_here, tiles_here, tile_rows, head_dim)
        .transpose(1, 2, 0, 3)
        .reshape(tok_rows, heads_here * head_dim)
    )
    full_weight = lax.all_gather(out_weight, "seq", axis=1, tiled=True)
    columns = full_weight
    summed = lax.psum_scatter(
        lax.dot_general(
            columns, attention, (((0,), (1,)), ((), ())), preferred_element_type=jnp.float32
        ).astype(jnp.bfloat16),
        "head",
        scatter_dimension=0,
        tiled=True,
    )
    return (summed, new_centroids)


def solution(mesh):
    placed = (
        P("seq", None),
        P("seq", "head"),
        P("head", "seq"),
        P("head", "seq", None),
        P("head", "seq"),
        P("head", "seq"),
    )
    return jax.shard_map(
        on_device,
        mesh=mesh,
        in_specs=placed,
        out_specs=(P("head", "seq"), P("head", "seq", None)),
        check_vma=False,
    )
```

profile of v0, /device:TPU:0, one launch (start us, length us, event | category | flops | bytes accessed | tf_op | source)
XLA Modules:
  0.0 303.2 jit_solution(2208695305127846466)
XLA Ops:
  7.2 0.7 all-gather.3.cloned.1.call-update
  7.9 0.1 mul.127
  8.0 0.8 and_select_fusion.1
  8.8 0.1 eq.61
  8.9 0.1 select_reduce_fusion.2
  9.1 0.7 copy.44
  9.8 7.4 %all-to-all-start = ((s32[16,1,2]{2,1,0:T(1,128)}), s32[16,1,2]{2,1,0:T(1,128)S(1)}, u32[]{:S(2)}, u32[]{:S(2)}) async-start(s32[16,1,2]{2,1,0:T(1,128)} %copy.44), calls=%async_computation | async-start | bytes 16384 | tf_op jit(solution)/shard_map/all_to_all | solution.py:69
  17.1 5.2 %fusion.2 = f32[1024]{0:T(1024)S(1)} fusion(bf16[1024,4096]{1,0:T(8,128)(2,1)} %param.6), kind=kLoop, calls=%fused_computation.8 | loop fusion | flops 12581888 | bytes 8392704 | tf_op jit(solution)/shard_map/reduce_sum | solution.py:14
  22.3 52.5 %all-gather.3.cloned.1.call-done = bf16[4096,768]{1,0:T(8,128)(2,1)} async-done(((bf16[256,768]{1,0:T(8,128)(2,1)}), bf16[4096,768]{1,0:T(8,128)(2,1)}) %all-gather.3.cloned.1.call-update) | async-done | bytes 6291472 | tf_op jit(solution)/shard_map/all_gather | solution.py:37
  74.9 11.1 %fusion.7 = bf16[1024,768]{1,0:T(8,128)(2,1)S(1)} fusion(bf16[4096,768]{1,0:T(8,128)(2,1)} %all-gather.3.cloned.1.call-done, bf16[1024,4096]{1,0:T(8,128)(2,1)} %param.6, f32[1024]{0:T(1024)S(1)} %add_rsqrt_fusion.2), kind=kOutput, calls=%fused_computation.15 | convolution fusion | flops 6455820288 | bytes 16257024 | tf_op jit(solution)/shard_map/dot_general | solution.py:35
  86.0 0.4 reshape.173
  86.4 0.3 copy.76
  86.7 0.9 copy.59
  87.6 0.6 fusion
  88.2 0.5 broadcast.209
  88.7 1.9 reduce
  90.6 2.2 reshape.181
  92.8 4.4 %all-to-all-start.1 = ((bf16[16,2,24576]{2,1,0:T(2,128)(2,1)}), bf16[16,2,24576]{2,1,0:T(2,128)(2,1)}, u32[]{:S(2)}, u32[]{:S(2)}) async-start(bf16[16,2,24576]{2,1,0:T(2,128)(2,1)} %reshape.181), calls=%async_computation.1 | async-start | bytes 3145728 | tf_op jit(solution)/shard_map/all_to_all | solution.py:68
  97.2 0.7 all-gather.5.cloned.1.call-update
  97.9 0.2 reduce-scatter.2.cloned.1.call-start
  98.3 0.1 convert_reduce_fusion
  98.5 0.1 copy.46
  98.6 0.1 copy.47
  98.9 34.5 %all-to-all-done.1 = bf16[16,2,24576]{2,1,0:T(2,128)(2,1)} async-done(((bf16[16,2,24576]{2,1,0:T(2,128)(2,1)}), bf16[16,2,24576]{2,1,0:T(2,128)(2,1)}, u32[]{:S(2)}, u32[]{:S(2)}) %all-to-all-start.1) | async-done | bytes 1572896 | tf_op jit(solution)/shard_map/all_to_all | solution.py:68
  133.3 8.1 %reshape.182 = bf16[16,1,49152]{2,1,0:T(2,128)(2,1)S(1)} reshape(bf16[16,2,24576]{2,1,0:T(2,128)(2,1)} %all-to-all-done.1) | data formatting | bytes 3145728
  141.4 3.0 convolution_convert_fusion
  144.4 3.4 %reshape.175 = bf16[8,256,3,128]{3,2,1,0:T(4,128)(2,1)S(1)} reshape(bf16[16,49152]{1,0:T(8,128)(2,1)} %convolution_convert_fusion) | data formatting | bytes 3145728 | tf_op jit(solution)/shard_map/reshape | solution.py:82
  147.8 3.0 fusion.26
  150.8 0.3 multiply_reduce_fusion.1
  151.2 0.3 multiply_reduce_fusion.2
  151.5 2.9 exponential_select_fusion
  154.4 2.8 convolution_convert_fusion.4
  157.3 0.2 reshape.176
  157.5 0.3 fusion.1
  157.9 1.0 reduce.1
  158.9 0.4 reshape.183
  159.3 23.4 %all_to_all.36 = bf16[16,2,8192]{2,1,0:T(2,128)(2,1)S(1)} all-to-all(bf16[16,2,8192]{2,1,0:T(2,128)(2,1)S(1)} %reshape.183), channel_id=1, replica_groups=mesh['head'=2,'seq'=16] {'seq'}, dimensions={0} | all-to-all | bytes 1048576 | tf_op jit(solution)/shard_map/all_to_all | solution.py:123
  182.6 0.5 reshape.184
  183.2 0.7 fusion.12
  183.8 0.5 copy.53
  184.3 7.2 %convert_bitcast_fusion = bf16[4096,1024]{0,1:T(8,128)(2,1)} fusion(bf16[256,4096]{1,0:T(8,128)(2,1)} %all-gather.5.cloned.1.call-done, bf16[32,8,8,128]{3,2,1,0:T(8,128)(2,1)S(1)} %bitcast.62), kind=kOutput, calls=%fused_computation.11 | convolution fusion | flops 2151677952 | bytes 11010048 | tf_op jit(solution)/shard_map/dot_general | solution.py:135
  191.6 0.1 reduce_sum.100
  191.7 0.1 gt.25
  191.8 0.1 max.11
  191.9 0.6 multiply_reduce_fusion
  192.6 0.7 multiply_add_fusion
  193.2 97.0 %reduce-scatter.2.cloned.1.call-done = bf16[2048,1024]{0,1:T(8,128)(2,1)} async-done(((bf16[4096,1024]{0,1:T(8,128)(2,1)}), bf16[2048,1024]{0,1:T(8,128)(2,1)}) %reduce-scatter.2.cloned.1.call-update) | async-done | bytes 4194320 | tf_op jit(solution)/shard_map/reduce_scatter | solution.py:134
  290.3 6.4 %copy.54 = bf16[2048,1024]{1,0:T(8,128)(2,1)} copy(bf16[2048,1024]{0,1:T(8,128)(2,1)} %reduce-scatter.2.cloned.1.call-done) | data formatting | bytes 8388608
  (29 shorter events, 0.8 us)
Async XLA Ops:
  7.2 67.7 %all-gather.3.cloned.1.call-start = ((), (), s32[]{:S(2)}) async-start(), calls=%async_computation.4 | async-start | bytes 6684672 | tf_op jit(solution)/shard_map/all_gather | solution.py:37
  9.8 83.0 %all-to-all-start = ((s32[16,1,2]{2,1,0:T(1,128)}), s32[16,1,2]{2,1,0:T(1,128)S(1)}, u32[]{:S(2)}, u32[]{:S(2)}) async-start(s32[16,1,2]{2,1,0:T(1,128)} %copy.44), calls=%async_computation | async-start | bytes 16384 | tf_op jit(solution)/shard_map/all_to_all | solution.py:69
  92.8 40.6 %all-to-all-start.1 = ((bf16[16,2,24576]{2,1,0:T(2,128)(2,1)}), bf16[16,2,24576]{2,1,0:T(2,128)(2,1)}, u32[]{:S(2)}, u32[]{:S(2)}) async-start(bf16[16,2,24576]{2,1,0:T(2,128)(2,1)} %reshape.181), calls=%async_computation.1 | async-start | bytes 3145728 | tf_op jit(solution)/shard_map/all_to_all | solution.py:68
  97.2 87.2 %all-gather.5.cloned.1.call-start = ((), (), s32[]{:S(2)}) async-start(), calls=%async_computation.5 | async-start | bytes 2228224 | tf_op jit(solution)/shard_map/all_gather | solution.py:132
  97.9 192.4 %reduce-scatter.2.cloned.1.call-start = ((), (), s32[]{:S(2)}) async-start(), calls=%async_computation.6 | async-start | bytes 12582912 | tf_op jit(solution)/shard_map/reduce_scatter | solution.py:134
  151.5 2.9 copy-start
  191.5 1.0 copy-start.1
Sparse Core Ops, SparseCore 0:
  10.3 64.5 all-gather.2
  100.2 52.7 all-gather.4
  191.7 98.5 reduce-scatter.1
where the time goes:
time: 304 us; the launch traced here: 303 us
  waiting for transfers between devices  185 us (61%)
  matrix products  28.7 us (9%)
  local copies, waits for them, and re-layouts  25.3 us (8%)
  blocking collectives  23.4 us (8%)
  other arithmetic  14.4 us (5%)
  between operations  14 us (5%)
  starting transfers between devices  12.1 us (4%)
    reduce_scatter x1, waiting for transfers between devices, on_device(): lax.psum_scatter(lax.dot_general(columns, attention, (((0,), (1,)), ((),...  97 us
    all_gather x1, waiting for transfers between devices, on_device(): lax.all_gather(qkv_weight, 'seq', axis=0, tiled=True)  52.5 us
    all_to_all x1, waiting for transfers between devices, on_device(): lax.all_to_all(outgoing, 'seq', split_axis=0, concat_axis=0, tiled=True)  34.5 us
    all_to_all x1, blocking collectives, on_device(): lax.all_to_all(returning, 'seq', split_axis=0, concat_axis=0, tiled=True)  23.4 us
    unnamed x10, local copies, waits for them, and re-layouts  18.5 us
    dot_general x1, matrix products, on_device(): jnp.dot(columns, lax.all_gather(qkv_weight, 'seq', axis=0, tiled=True), p...  11.1 us
    all_to_all x1, starting transfers between devices, on_device(): lax.all_to_all(labels, 'seq', split_axis=0, concat_axis=0, tiled=True)  7.39 us
    dot_general x1, matrix products, on_device(): lax.dot_general(columns, attention, (((0,), (1,)), ((), ())), preferred_e...  7.2 us
  transfers between devices with their start and end apart: 5, of which 3 were waited for; matrix products, arithmetic and copies ran while one was open for 18% of the time, Pallas kernels for 0%

commit v1 on v0

v1 whole, which is shorter than its diff:
```python
import functools

import jax
import jax.numpy as jnp
from jax import lax
from jax.experimental import pallas as pl
from jax.experimental.pallas import tpu as pltpu
from jax.sharding import PartitionSpec as P

LOGIT_SCALE = 8.0
KEEP_RATE = 0.75
VMEM_BYTES = 40 * 1024 * 1024
LABEL_ROWS = 16
NT_DIMS = (((1,), (1,)), ((), ()))
TN_DIMS = (((0,), (0,)), ((), ()))
tie = lax.optimization_barrier


def params(axes=1):
    return pltpu.CompilerParams(
        vmem_limit_bytes=VMEM_BYTES, dimension_semantics=("arbitrary",) * axes
    )


def cost(flops, moved, exps=0):
    return pl.CostEstimate(flops=flops, bytes_accessed=moved, transcendentals=exps)


def whole_block(shape):
    zeros = (0,) * len(shape)
    return pl.BlockSpec(shape, lambda *_: zeros)


def norm_kernel(x_ref, out_ref):
    x = x_ref[...].astype(jnp.float32)
    scale = lax.rsqrt(jnp.mean(x * x, axis=-1, keepdims=True) + 1e-05)
    out_ref[...] = (x * scale).astype(out_ref.dtype)


def norm_rows(tokens):
    rows, width = tokens.shape
    step = min(128, rows)
    return pl.pallas_call(
        norm_kernel,
        out_shape=jax.ShapeDtypeStruct(tokens.shape, jnp.bfloat16),
        grid=(rows // step,),
        in_specs=[pl.BlockSpec((step, width), lambda i: (i, 0))],
        out_specs=pl.BlockSpec((step, width), lambda i: (i, 0)),
        compiler_params=params(),
        cost_estimate=cost(4 * rows * width, 4 * rows * width),
        name="norm_rows",
    )(tokens)


def early_kernel(n_early, n_late, place_ref, x_ref, *refs):
    weights, (acc_ref, rest_ref) = refs[: 2 * n_early], refs[2 * n_early :]
    depth, half = weights[0].shape

    def columns(i):
        return x_ref[:, pl.ds(pl.multiple_of(place_ref[i] * depth, depth), depth)]

    for part in range(2):
        total = None
        for i in range(n_early):
            term = jnp.dot(
                columns(i), weights[2 * i + part][...], preferred_element_type=jnp.float32
            )
            total = term if total is None else total + term
        acc_ref[:, part * half : (part + 1) * half] = total
    for i in range(n_late):
        rest_ref[:, i * depth : (i + 1) * depth] = columns(n_early + i)


def early_projection(normed, places, early, n_late):
    rows, width = normed.shape
    depth, half = early[0][0].shape
    n_early = len(early)
    step = 256
    flat = [part for pair in early for part in pair]
    return pl.pallas_call(
        functools.partial(early_kernel, n_early, n_late),
        out_shape=(
            jax.ShapeDtypeStruct((rows, 2 * half), jnp.float32),
            jax.ShapeDtypeStruct((rows, n_late * depth), jnp.bfloat16),
        ),
        grid_spec=pltpu.PrefetchScalarGridSpec(
            num_scalar_prefetch=1,
            grid=(rows // step,),
            in_specs=[pl.BlockSpec((step, width), lambda i, _: (i, 0))]
            + [whole_block((depth, half))] * (2 * n_early),
            out_specs=(
                pl.BlockSpec((step, 2 * half), lambda i, _: (i, 0)),
                pl.BlockSpec((step, n_late * depth), lambda i, _: (i, 0)),
            ),
        ),
        compiler_params=params(),
        cost_estimate=cost(
            4 * rows * n_early * depth * half, 2 * rows * width + 8 * rows * half
        ),
        name="early_projection",
    )(places, normed, *flat)


def unit_rows(values):
    values = values.astype(jnp.float32)
    scale = lax.rsqrt(jnp.mean(values * values, axis=-1, keepdims=True) + 1e-06)
    return (values * scale).astype(jnp.bfloat16)


def late_kernel(n_late, heads, tiles, tile_rows, owner_ref, later_ref, acc_ref, rest_ref, *refs):
    weights, (qkv_ref, out_ref) = refs[: 2 * n_late], refs[2 * n_late :]
    depth, half = weights[0].shape
    head_dim = out_ref.shape[2] // 2
    step = pl.program_id(0)
    tiles_step = acc_ref.shape[0] // tile_rows

    if out_ref.shape[0] > heads * tiles:

        @pl.when(step == 0)
        def _():
            out_ref[...] = jnp.zeros_like(out_ref)

    for part in range(2):
        total = acc_ref[:, part * half : (part + 1) * half]
        for i in range(n_late):
            total += jnp.dot(
                rest_ref[:, i * depth : (i + 1) * depth],
                weights[2 * i + part][...],
                preferred_element_type=jnp.float32,
            )
        projected = total.astype(jnp.bfloat16)
        for local in range(heads // 2):
            head = part * (heads // 2) + local
            base = local * 3 * head_dim
            query = unit_rows(projected[:, base : base + head_dim])
            key = unit_rows(projected[:, base + head_dim : base + 2 * head_dim])
            value = projected[:, base + 2 * head_dim : base + 3 * head_dim]
            at = head * 3 * head_dim
            qkv_ref[:, at : at + head_dim] = query
            qkv_ref[:, at + head_dim : at + 2 * head_dim] = key
            qkv_ref[:, at + 2 * head_dim : at + 3 * head_dim] = value
            for t in range(tiles_step):
                index = head * tiles + step * tiles_step + t
                owner = owner_ref[index]
                span = slice(t * tile_rows, (t + 1) * tile_rows)
                out_ref[owner, :, :head_dim] = key[span]
                out_ref[owner, :, head_dim:] = jnp.where(
                    later_ref[index] > 0, query[span], value[span]
                )


def late_projection(acc, rest, late, owners, later, n_owners, heads, tiles):
    rows, cols = acc.shape
    depth, half = late[0][0].shape
    n_late = len(late)
    tile_rows = rows // tiles
    head_dim = cols // (3 * heads)
    step = 2 * tile_rows
    flat = [part for pair in late for part in pair]
    return pl.pallas_call(
        functools.partial(late_kernel, n_late, heads, tiles, tile_rows),
        out_shape=(
            jax.ShapeDtypeStruct((rows, cols), jnp.bfloat16),
            jax.ShapeDtypeStruct((n_owners, tile_rows, 2 * head_dim), jnp.bfloat16),
        ),
        grid_spec=pltpu.PrefetchScalarGridSpec(
            num_scalar_prefetch=2,
            grid=(rows // step,),
            in_specs=[
                pl.BlockSpec((step, cols), lambda i, *_: (i, 0)),
                pl.BlockSpec((step, n_late * depth), lambda i, *_: (i, 0)),
            ]
            + [whole_block((depth, half))] * (2 * n_late),
            out_specs=(
                pl.BlockSpec((step, cols), lambda i, *_: (i, 0)),
                whole_block((n_owners, tile_rows, 2 * head_dim)),
            ),
        ),
        compiler_params=params(),
        cost_estimate=cost(4 * rows * n_late * depth * half, 9 * rows * cols),
        name="late_projection",
    )(owners, later, acc, rest, *flat)


def inner_kernel(heads, qkv_ref, sums_ref, mass_ref):
    rows = qkv_ref.shape[0]
    head_dim = qkv_ref.shape[1] // (3 * heads)
    allowed = lax.broadcasted_iota(jnp.int32, (rows, rows), 1) <= lax.broadcasted_iota(
        jnp.int32, (rows, rows), 0
    )
    ones = jnp.ones((rows, head_dim), jnp.bfloat16)
    for head in range(heads):
        at = head * 3 * head_dim
        query = qkv_ref[:, at : at + head_dim]
        key = qkv_ref[:, at + head_dim : at + 2 * head_dim]
        value = qkv_ref[:, at + 2 * head_dim : at + 3 * head_dim]
        scores = lax.dot_general(query, key, NT_DIMS, preferred_element_type=jnp.float32)
        weights = jnp.where(allowed, jnp.exp(scores * (LOGIT_SCALE / head_dim)), 0.0)
        weights = weights.astype(jnp.bfloat16)
        span = slice(head * head_dim, (head + 1) * head_dim)
        sums_ref[:, span] = jnp.dot(weights, value, preferred_element_type=jnp.float32)
        mass_ref[:, span] = jnp.dot(weights, ones, preferred_element_type=jnp.float32)


def inner_attention(qkv, heads, tiles):
    rows, cols = qkv.shape
    tile_rows = rows // tiles
    out = jax.ShapeDtypeStruct((rows, cols // 3), jnp.float32)
    return pl.pallas_call(
        functools.partial(inner_kernel, heads),
        out_shape=(out, out),
        grid=(tiles,),
        in_specs=[pl.BlockSpec((tile_rows, cols), lambda i: (i, 0))],
        out_specs=(pl.BlockSpec((tile_rows, cols // 3), lambda i: (i, 0)),) * 2,
        compiler_params=params(),
        cost_estimate=cost(
            2 * rows * tile_rows * cols, 5 * rows * cols, rows * tile_rows * heads
        ),
        name="inner_attention",
    )(qkv)


def owner_kernel(first_ref, second_ref, held_ref, in_ref, cent_ref, out_ref, new_ref):
    tile_rows = in_ref.shape[1]
    head_dim = in_ref.shape[2] // 2
    out_ref[...] = jnp.zeros_like(out_ref)
    ones = jnp.ones((LABEL_ROWS, tile_rows), jnp.bfloat16)
    line = lax.broadcasted_iota(jnp.int32, (LABEL_ROWS, tile_rows), 0)
    for c in range(cent_ref.shape[0]):
        first, second, held = first_ref[c], second_ref[c], held_ref[c]
        key = in_ref[first, :, :head_dim]

        @pl.when(held > 1)
        def _():
            value = in_ref[first, :, head_dim:]
            query = in_ref[second, :, head_dim:]
            scores = lax.dot_general(query, key, NT_DIMS, preferred_element_type=jnp.float32)
            weights = jnp.exp(scores * (LOGIT_SCALE / head_dim)).astype(jnp.bfloat16)
            out_ref[second, :tile_rows, :] = jnp.dot(
                weights, value, preferred_element_type=jnp.float32
            ).astype(jnp.bfloat16)
            mass = lax.dot_general(ones, weights, NT_DIMS, preferred_element_type=jnp.float32)
            high = mass.astype(jnp.bfloat16).astype(jnp.float32)
            out_ref[second, tile_rows:, :] = jnp.where(
                line == 0, high, jnp.where(line == 1, mass - high, 0.0)
            ).astype(jnp.bfloat16)

        other = in_ref[second, :, :head_dim]
        first_sum = jnp.sum(key.astype(jnp.float32), axis=0, keepdims=True)
        other_sum = jnp.sum(other.astype(jnp.float32), axis=0, keepdims=True)
        key_sum = jnp.where(held > 1, first_sum + other_sum, first_sum)
        count = jnp.maximum(held, 1).astype(jnp.float32) * tile_rows
        old = cent_ref[c : c + 1, :]
        moved = old + (1.0 - KEEP_RATE) * (key_sum / count - old)
        new_ref[c : c + 1, :] = jnp.where(held > 0, moved, old)


def owner_attention(incoming, centroid_rows, first, second, held):
    n, tile_rows, width = incoming.shape
    head_dim = width // 2
    returning = (n, tile_rows + LABEL_ROWS, head_dim)
    return pl.pallas_call(
        owner_kernel,
        out_shape=(
            jax.ShapeDtypeStruct(returning, jnp.bfloat16),
            jax.ShapeDtypeStruct(centroid_rows.shape, jnp.float32),
        ),
        grid_spec=pltpu.PrefetchScalarGridSpec(
            num_scalar_prefetch=3,
            grid=(1,),
            in_specs=[whole_block(incoming.shape), whole_block(centroid_rows.shape)],
            out_specs=(whole_block(returning), whole_block(centroid_rows.shape)),
        ),
        compiler_params=params(),
        cost_estimate=cost(
            4 * centroid_rows.shape[0] * tile_rows * tile_rows * width,
            4 * n * tile_rows * width,
            centroid_rows.shape[0] * tile_rows * tile_rows,
        ),
        name="owner_attention",
    )(first, second, held, incoming, centroid_rows)


def merge_kernel(heads, tiles, owner_ref, later_ref, sums_ref, mass_ref, back_ref, out_ref):
    tile_rows = sums_ref.shape[0]
    head_dim = sums_ref.shape[1] // heads
    step = pl.program_id(0)
    pick = (lax.broadcasted_iota(jnp.int32, (LABEL_ROWS, head_dim), 0) < 2).astype(jnp.bfloat16)
    for head in range(heads):
        index = head * tiles + step
        owner, later = owner_ref[index], later_ref[index] > 0
        span = slice(head * head_dim, (head + 1) * head_dim)
        sums = sums_ref[:, span]
        mass = mass_ref[:, span]
        far_mass = lax.dot_general(
            back_ref[owner, tile_rows:, :], pick, TN_DIMS, preferred_element_type=jnp.float32
        )
        far_sums = back_ref[owner, :tile_rows, :].astype(jnp.float32)
        sums = jnp.where(later, sums + far_sums, sums)
        mass = jnp.where(later, mass + far_mass, mass)
        out_ref[:, span] = (sums / mass).astype(out_ref.dtype)


def merge_attention(sums, mass, back, owners, later, heads, tiles):
    rows, cols = sums.shape
    tile_rows = rows // tiles
    block = pl.BlockSpec((tile_rows, cols), lambda i, *_: (i, 0))
    return pl.pallas_call(
        functools.partial(merge_kernel, heads, tiles),
        out_shape=jax.ShapeDtypeStruct((rows, cols), jnp.bfloat16),
        grid_spec=pltpu.PrefetchScalarGridSpec(
            num_scalar_prefetch=2,
            grid=(tiles,),
            in_specs=[block, block, whole_block(back.shape)],
            out_specs=block,
        ),
        compiler_params=params(),
        cost_estimate=cost(8 * rows * cols, 12 * rows * cols),
        name="merge_attention",
    )(owners, later, sums, mass, back)


def output_kernel(place_ref, weight_ref, *refs):
    parts, out_ref = refs[:-1], refs[-1]
    total, at = None, 0
    for part in parts:
        width = part.shape[1]
        term = lax.dot_general(
            weight_ref[0, :, at : at + width],
            part[...],
            NT_DIMS,
            preferred_element_type=jnp.float32,
        )
        total = term if total is None else total + term
        at += width
    out_ref[...] = total.astype(out_ref.dtype)


def output_projection(weight_blocks, places, parts):
    n, features, depth = weight_blocks.shape
    rows = parts[0].shape[0]
    return pl.pallas_call(
        output_kernel,
        out_shape=jax.ShapeDtypeStruct((n * features, rows), jnp.bfloat16),
        grid_spec=pltpu.PrefetchScalarGridSpec(
            num_scalar_prefetch=1,
            grid=(n,),
            in_specs=[pl.BlockSpec((1, features, depth), lambda i, _: (i, 0, 0))]
            + [whole_block(part.shape) for part in parts],
            out_specs=pl.BlockSpec((features, rows), lambda i, place: (place[i], 0)),
        ),
        compiler_params=params(),
        cost_estimate=cost(
            2 * n * features * depth * rows, 2 * n * features * (rows + depth)
        ),
        name="output_projection",
    )(places, weight_blocks, *parts)


def permute(value, pairs):
    return lax.ppermute(value, "seq", pairs)


def flip(bit, n=16):
    return [(s, s ^ bit) for s in range(n)]


def turn(by, n=16):
    return [(s, (s + 4 * by) % n) for s in range(n)]


LINE_UP, LINE_DOWN = turn(1), turn(-1)
SIDE, CORE = flip(2), flip(1)


def gather_weights(weight):
    half = weight.shape[1] // 2
    own = tie((weight[:, :half], weight[:, half:]))
    lines, sides, far = [[o] for o in own], [[], []], [[], []]

    def hop(p, last=False):
        moves = []
        if not last:
            moves.append((lines[p], lines[p][-1], LINE_UP))
        if not last or p == 0:
            moves.append((sides[p], lines[p][-1], SIDE))
        else:
            moves.append((sides[p], sides[p][0], LINE_DOWN))
        moves.append((far[p], lines[p][-1], CORE))
        if sides[p]:
            moves.append((far[p], sides[p][-1], CORE))
        results = tie(tuple(permute(value, pairs) for _, value, pairs in moves))
        for (group, _, _), value in zip(moves, results):
            group.append(value)

    for k in range(4):
        for p in range(2):
            hop(p, last=k == 3)
    for p in range(2):
        far[p].append(permute(sides[p][3], CORE))

    early = [
        tuple(lines[p][k] for p in range(2)) for k in range(4)
    ] + [
        tuple(sides[p][k] for p in range(2)) for k in range(3)
    ] + [tuple(far[p][k] for p in range(2)) for k in range(5)]
    late = [tuple(sides[p][3] for p in range(2))] + [
        tuple(far[p][k] for p in range(2)) for k in range(5, 8)
    ]
    return early, late


def weight_places(me):
    line, side, core = me // 4, me // 2 % 2, me % 2

    def at(back, other_side, other_core):
        where = jnp.mod(line - back, 4) * 4
        where += (1 - side if other_side else side) * 2
        return where + (1 - core if other_core else core)

    early = [at(k, 0, 0) for k in range(4)] + [at(k, 1, 0) for k in range(3)]
    early += [at(0, 0, 1), at(1, 0, 1), at(0, 1, 1), at(2, 0, 1), at(1, 1, 1)]
    late = [at(3, 1, 0), at(3, 0, 1), at(2, 1, 1), at(3, 1, 1)]
    return jnp.stack(early + late).astype(jnp.int32)


def gather_labels(labels):
    gathered = labels[None]
    for bit in (1, 2, 4, 8):
        gathered = jnp.concatenate([gathered, permute(gathered, flip(bit))], axis=0)
    return gathered


def gather_out_weight(weight, me, group):
    mine = weight.T
    across = permute(mine, flip(8))
    inside = me // 8 == group
    keep = jnp.where(inside, mine, across)
    give = jnp.where(inside, across, mine)
    got = lax.ppermute(give, "head", [(0, 1), (1, 0)])
    blocks = jnp.concatenate([keep, got], axis=1)[None]
    for bit in (4, 2, 1):
        blocks = jnp.concatenate([blocks, permute(blocks, flip(bit))], axis=0)
    order = jnp.arange(8, dtype=jnp.int32)
    places = (me % 8) ^ (order % 2 * 4) ^ (order // 2 % 2 * 2) ^ (order // 4)
    return blocks, places.astype(jnp.int32)


def on_device(tokens, qkv_weight, out_weight, centroids, clusters, slots):
    heads, tiles = clusters.shape
    clus_here, head_dim = centroids.shape[1:]
    n_seq, n_head = lax.axis_size("seq"), lax.axis_size("head")
    me, group = lax.axis_index("seq"), lax.axis_index("head")
    paired = n_seq == 16 and n_head == 2

    if paired:
        early, late = gather_weights(qkv_weight)
        places = weight_places(me)
        labels = gather_labels(clusters)
        sources = me ^ jnp.arange(n_seq, dtype=jnp.int32)
    else:
        full = lax.all_gather(qkv_weight, "seq", axis=0, tiled=True)
        depth, half = full.shape[0] // 16, full.shape[1] // 2
        blocks = [
            (full[i * depth : (i + 1) * depth, :half], full[i * depth : (i + 1) * depth, half:])
            for i in range(16)
        ]
        early, late = blocks[:12], blocks[12:]
        places = jnp.arange(16, dtype=jnp.int32)
        labels = lax.all_gather(clusters, "seq", axis=0)
        sources = jnp.arange(n_seq, dtype=jnp.int32)

    numbers = (sources[:, None] * tiles + jnp.arange(tiles, dtype=jnp.int32)).reshape(-1)
    labels = labels.transpose(1, 0, 2).reshape(heads, -1)
    own_numbers = me * tiles + jnp.arange(tiles, dtype=jnp.int32)
    earlier = (labels[:, None, :] == clusters[:, :, None]) & (
        numbers[None, None, :] < own_numbers[None, :, None]
    )
    later = jnp.any(earlier, axis=2).astype(jnp.int32).reshape(-1)
    owners = (clusters // clus_here).reshape(-1)
    owned = me * clus_here + jnp.arange(clus_here, dtype=jnp.int32)
    member = labels[:, None, :] == owned[None, :, None]
    held = jnp.sum(member.astype(jnp.int32), axis=2).reshape(-1)
    total = n_seq * tiles
    first = jnp.min(jnp.where(member, numbers[None, None, :], total - 1), axis=2).reshape(-1)
    second = jnp.max(jnp.where(member, numbers[None, None, :], 0), axis=2).reshape(-1)
    first, second = first // tiles, second // tiles

    normed = norm_rows(tokens)
    acc, rest = early_projection(normed, places, early, len(late))
    qkv, outgoing = late_projection(acc, rest, late, owners, later, n_seq, heads, tiles)
    incoming = lax.all_to_all(outgoing, "seq", split_axis=0, concat_axis=0, tiled=True)
    sums, mass = inner_attention(qkv, heads, tiles)
    returning, new_rows = owner_attention(
        incoming, centroids.reshape(heads * clus_here, head_dim), first, second, held
    )
    back = lax.all_to_all(returning, "seq", split_axis=0, concat_axis=0, tiled=True)
    attention = merge_attention(sums, mass, back, owners, later, heads, tiles)

    if paired:
        weight_blocks, feature_places = gather_out_weight(out_weight, me, group)
        parts = [attention, lax.ppermute(attention, "head", [(0, 1), (1, 0)])]
    else:
        rows = lax.all_gather(out_weight, "seq", axis=1, tiled=True)
        rows = lax.all_gather(rows, "head", axis=0, tiled=True)
        features = rows.shape[1] // n_head
        mine = lax.dynamic_slice_in_dim(rows, group * features, features, axis=1).T
        weight_blocks = mine.reshape(-1, min(256, features), mine.shape[1])
        feature_places = jnp.arange(weight_blocks.shape[0], dtype=jnp.int32)
        parts = [lax.all_gather(attention, "head", axis=1, tiled=True)]
    summed = output_projection(weight_blocks, feature_places, parts)
    return (summed, new_rows.reshape(centroids.shape))


def solution(mesh):
    placed = (
        P("seq", None),
        P("seq", "head"),
        P("head", "seq"),
        P("head", "seq", None),
        P("head", "seq"),
        P("head", "seq"),
    )
    return jax.shard_map(
        on_device,
        mesh=mesh,
        in_specs=placed,
        out_specs=(P("head", "seq"), P("head", "seq", None)),
        check_vma=False,
    )
```

time: 304 us -> 187 us (0.62)
  waiting for transfers between devices: 185 us -> 78.9 us
  Pallas kernels: 0 us -> 36.2 us
  matrix products: 28.7 us -> 0 us
  starting transfers between devices: 12.1 us -> 40.7 us
  blocking collectives: 23.4 us -> 0 us
  between operations: 14 us -> 1.01 us
  other arithmetic: 14.4 us -> 6 us
    reduce_scatter x1 -> x0, waiting for transfers between devices: 97 us -> none  [on_device(): lax.psum_scatter(lax.dot_general(columns, attention, (((0,), (1,)), ((),...]
    ppermute x0 -> x40, waiting for transfers between devices: none -> 71.6 us  [the longest x38 57.3 us: permute(): return lax.ppermute(value, 'seq', pairs)]
    all_gather x2 -> x0, waiting for transfers between devices: 52.6 us -> none  [the longest x1 52.5 us: on_device(): lax.all_gather(qkv_weight, 'seq', axis=0, tiled=True)]
    pallas_call x0 -> x7, Pallas kernels: none -> 36.2 us  [the longest x1 9.97 us: early_projection(): pl.pallas_call(functools.partial(early_kernel, n_early, n_late), out_shap...]
    all_to_all x1, waiting for transfers between devices: 34.5 us -> 0.01 us  [on_device(): lax.all_to_all(outgoing, 'seq', split_axis=0, concat_axis=0, tiled=True)]
    ppermute x0 -> x40, starting transfers between devices: none -> 32.7 us  [the longest x38 29.5 us: permute(): return lax.ppermute(value, 'seq', pairs)]
    dot_general x8 -> x0, matrix products: 28.7 us -> none  [the longest x1 11.1 us: on_device(): jnp.dot(columns, lax.all_gather(qkv_weight, 'seq', axis=0, tiled=True), p...]
    all_to_all x1 -> x0, blocking collectives: 23.4 us -> none  [on_device(): lax.all_to_all(returning, 'seq', split_axis=0, concat_axis=0, tiled=True)]
  transfers between devices with their start and end apart: 5 -> 42, of which waited for: 3 -> 15; matrix products, arithmetic and copies ran while one was open for 18% -> 4% of each run, Pallas kernels for 0% -> 14%
where the time goes in v1:
time: 187 us; the launch traced here: 186 us
  waiting for transfers between devices  78.9 us (42%)
  starting transfers between devices  40.7 us (22%)
  Pallas kernels  36.2 us (19%)
  local copies, waits for them, and re-layouts  23.5 us (13%)
  other arithmetic  6 us (3%)
    ppermute x38, waiting for transfers between devices, permute(): return lax.ppermute(value, 'seq', pairs)  57.3 us
    ppermute x38, starting transfers between devices, permute(): return lax.ppermute(value, 'seq', pairs)  29.5 us
    unnamed x59, local copies, waits for them, and re-layouts  21.7 us
    ppermute x1, waiting for transfers between devices, on_device(): parts = [attention, lax.ppermute(attention, 'head', [(0, 1), (1, 0)])]  10.8 us
    pallas_call x1, Pallas kernels, early_projection(): pl.pallas_call(functools.partial(early_kernel, n_early, n_late), out_shap...  9.97 us
    pallas_call x1, Pallas kernels, norm_rows(): pl.pallas_call(norm_kernel, out_shape=jax.ShapeDtypeStruct(tokens.shape,...  7.37 us
    all_to_all x1, waiting for transfers between devices, on_device(): lax.all_to_all(returning, 'seq', split_axis=0, concat_axis=0, tiled=True)  7.26 us
    pallas_call x1, Pallas kernels, output_projection(): pl.pallas_call(output_kernel, out_shape=jax.ShapeDtypeStruct((n * feature...  6.09 us
  transfers between devices with their start and end apart: 42, of which 15 were waited for; matrix products, arithmetic and copies ran while one was open for 4% of the time, Pallas kernels for 14%

profile of v1, /device:TPU:0, one launch (start us, length us, event | category | flops | bytes accessed | tf_op | source)
XLA Modules:
  0.0 186.2 jit_solution(12816645998346005886)
XLA Ops:
  0.6 1.1 fusion.9
  1.7 3.1 %collective-permute-start.12 = (bf16[256,384]{1,0:T(8,128)(2,1)S(1)}, bf16[256,384]{1,0:T(8,128)(2,1)S(1)}, u32[]{:S(2)}, u32[]{:S(2)}) collective-permute-start(bf16[256,384]{1,0:T(8,128)(2,1)S(1)} %get-tuple-element.41.refs_1_), channel_id=1, source_target_pairs={{0,4},{1,5},{2,6},{3,7},{4,8},{5,9},{6,10},{7,11},{8,12},{9,13},{1... | collective-permute-start | bytes 589832 | tf_op jit(solution)/shard_map/ppermute | solution.py:361
  4.8 1.5 collective-permute-start.13
  6.8 1.6 collective-permute-start.9
  9.9 5.4 %collective-permute-done.10.refs_8_ = bf16[256,384]{1,0:T(8,128)(2,1)S(1)} collective-permute-done((bf16[256,384]{1,0:T(8,128)(2,1)S(1)}, bf16[256,384]{1,0:T(8,128)(2,1)S(1)}, u32[]{:S(2)}, u32[]{:S(2)}) %collective-permute-start.10) | collective-permute-done | bytes 196640 | tf_op jit(solution)/shard_map/ppermute | solution.py:361
  15.9 1.1 collective-permute-start.15
  17.0 1.5 collective-permute-start.16
  18.8 7.4 %norm_rows.1.x_ref = bf16[1024,4096]{1,0:T(8,128)(2,1)S(1)} custom-call(bf16[1024,4096]{1,0:T(8,128)(2,1)} %x_ref.1), custom_call_target="tpu_custom_call" | custom-call | flops 16777216 | bytes 16777216 | tf_op jit(solution)/shard_map/norm_rows/pallas_call | solution.py:43
  26.2 3.3 %copy-done = bf16[1024,4096]{1,0:T(8,128)(2,1)} copy-done((bf16[1024,4096]{1,0:T(8,128)(2,1)}, bf16[1024,4096]{1,0:T(8,128)(2,1)S(1)}, u32[]{:S(2)}) %copy-start) | copy-done | bytes 8388632
  30.0 1.6 collective-permute-start.19
  32.7 1.1 collective-permute-done.18.refs_18_
  34.5 1.5 collective-permute-start.6
  36.0 2.2 %collective-permute-done.6 = s32[2,2,8]{2,1,0:T(2,128)S(1)} collective-permute-done((s32[2,2,8]{2,1,0:T(2,128)S(1)}, s32[2,2,8]{2,1,0:T(2,128)S(1)}, u32[]{:S(2)}, u32[]{:S(2)}) %collective-permute-start.6) | collective-permute-done | bytes 160 | tf_op jit(solution)/shard_map/ppermute | solution.py:361
  38.2 1.3 collective-permute-start.23
  42.3 1.5 collective-permute-start.7
  43.8 2.4 %collective-permute-done.7 = s32[4,2,8]{2,1,0:T(2,128)S(1)} collective-permute-done((s32[4,2,8]{2,1,0:T(2,128)S(1)}, s32[4,2,8]{2,1,0:T(2,128)S(1)}, u32[]{:S(2)}, u32[]{:S(2)}) %collective-permute-start.7) | collective-permute-done | bytes 288 | tf_op jit(solution)/shard_map/ppermute | solution.py:361
  46.2 2.7 %collective-permute-start.34 = (bf16[256,384]{1,0:T(8,128)(2,1)S(1)}, bf16[256,384]{1,0:T(8,128)(2,1)S(1)}, u32[]{:S(2)}, u32[]{:S(2)}) collective-permute-start(bf16[256,384]{1,0:T(8,128)(2,1)S(1)} %collective-permute-done.13.refs_9_), channel_id=1, source_target_pairs={{0,12},{1,13},{2,14},{3,15},{4,0},{5,1},{6,2},{7,3},{8,4},{9,5},{1... | collective-permute-start | bytes 589832 | tf_op jit(solution)/shard_map/ppermute | solution.py:361
  52.9 4.9 %collective-permute-done.27.refs_7_ = bf16[256,384]{1,0:T(8,128)(2,1)} collective-permute-done((bf16[256,384]{1,0:T(8,128)(2,1)S(1)}, bf16[256,384]{1,0:T(8,128)(2,1)}, u32[]{:S(2)}, u32[]{:S(2)}) %collective-permute-start.27) | collective-permute-done | bytes 196640 | tf_op jit(solution)/shard_map/ppermute | solution.py:361
  57.7 1.2 collective-permute-start.8
  65.7 0.9 copy-done.8
  66.7 0.9 copy-done.10
  67.6 0.9 copy-done.12
  69.4 0.9 copy-done.16
  70.4 0.9 copy-done.18
  71.3 0.9 copy-done.20
  73.1 10.0 %early_projection.1 = (f32[1024,768]{1,0:T(8,128)S(1)}, bf16[1024,1024]{1,0:T(8,128)(2,1)S(1)}) custom-call(s32[16]{0:T(128)S(1)} %stack.67.place_ref, bf16[1024,4096]{1,0:T(8,128)(2,1)} %copy-done, bf16[256,384]{1,0:T(8,128)(2,1)S(1)} %get-tuple-element.40.refs_0_, bf16[256,384]{1,0:T(8,128)(2,1)S(1)} %get-tuple-element.41.refs_1_, ...), custom_call_target="tpu_custom_call" | custom-call | flops 4831838208 | bytes 11534336 | tf_op jit(solution)/shard_map/early_projection/pallas_call | solution.py:80
  83.1 3.7 %late_projection.1 = (bf16[1024,768]{1,0:T(8,128)(2,1)S(1)}, bf16[16,128,256]{2,1,0:T(8,128)(2,1)S(1)}) custom-call(s32[16]{0:T(128)S(1)} %reshape.80.owner_ref, s32[16]{0:T(128)S(1)} %reshape.86.later_ref, f32[1024,768]{1,0:T(8,128)S(1)} %get-tuple-element.64.acc_ref, bf16[1024,1024]{1,0:T(8,128)(2,1)S(1)} %get-tuple-element.65.rest_ref, ...), custom_call_target="tpu_custom_call" | custom-call | flops 1610612736 | bytes 7077888 | tf_op jit(solution)/shard_map/late_projection/pallas_call | solution.py:160
  86.9 1.0 copy-done.1
  87.9 4.4 %all-to-all-start = ((bf16[16,128,256]{2,1,0:T(8,128)(2,1)}), bf16[16,128,256]{2,1,0:T(8,128)(2,1)S(1)}, u32[]{:S(2)}, u32[]{:S(2)}) async-start(bf16[16,128,256]{2,1,0:T(8,128)(2,1)} %copy-done.1), calls=%async_computation | async-start | bytes 2097152 | tf_op jit(solution)/shard_map/all_to_all | solution.py:492
  92.4 2.9 %collective-permute-start = (bf16[256,256]{1,0:T(8,128)(2,1)S(1)}, bf16[256,256]{1,0:T(8,128)(2,1)S(1)}, u32[]{:S(2)}, u32[]{:S(2)}) collective-permute-start(bf16[256,256]{1,0:T(8,128)(2,1)S(1)} %bitcast.27), channel_id=1, source_target_pairs={{0,8},{1,9},{2,10},{3,11},{4,12},{5,13},{6,14},{7,15},{8,0},{9,1},... | collective-permute-start | bytes 393224 | tf_op jit(solution)/shard_map/ppermute | solution.py:361
  95.3 29.2 %collective-permute-done = bf16[256,256]{1,0:T(8,128)(2,1)S(1)} collective-permute-done((bf16[256,256]{1,0:T(8,128)(2,1)S(1)}, bf16[256,256]{1,0:T(8,128)(2,1)S(1)}, u32[]{:S(2)}, u32[]{:S(2)}) %collective-permute-start) | collective-permute-done | bytes 131104 | tf_op jit(solution)/shard_map/ppermute | solution.py:361
  124.5 1.6 collective-permute-start.1
  126.1 3.5 %collective-permute-done.1 = bf16[256,256]{1,0:T(8,128)(2,1)S(1)} collective-permute-done((bf16[256,256]{1,0:T(8,128)(2,1)S(1)}, bf16[256,256]{1,0:T(8,128)(2,1)S(1)}, u32[]{:S(2)}, u32[]{:S(2)}) %collective-permute-start.1) | collective-permute-done | bytes 131104 | tf_op jit(solution)/shard_map/ppermute | solution.py:440
  129.7 6.9 %collective-permute-done.2 = bf16[1,256,512]{2,1,0:T(8,128)(2,1)S(1)} collective-permute-done((bf16[1,256,512]{2,1,0:T(8,128)(2,1)S(1)}, bf16[1,256,512]{2,1,0:T(8,128)(2,1)S(1)}, u32[]{:S(2)}, u32[]{:S(2)}) %collective-permute-start.2) | collective-permute-done | bytes 262176 | tf_op jit(solution)/shard_map/ppermute | solution.py:361
  137.5 1.5 collective-permute-start.3
  139.6 4.0 %owner_attention.1 = (bf16[16,144,128]{2,1,0:T(8,128)(2,1)}, f32[8,128]{1,0:T(8,128)}) custom-call(s32[8]{0:T(128)S(1)} %get-tuple-element.86.first_ref, s32[8]{0:T(128)S(1)} %get-tuple-element.85.second_ref, s32[8]{0:T(128)S(1)} %reshape.83.held_ref, bf16[16,128,256]{2,1,0:T(8,128)(2,1)S(1)} %all-to-all-done.in_ref, f32[8,128]{1,0:T(8,128)S(1)} %bitcast.26), custom_call_target="tpu_custom_call" | custom-call | flops 134217728 | bytes 2097152 | tf_op jit(solution)/shard_map/owner_attention/pallas_call | solution.py:262
  143.5 3.6 %all-to-all-start.1 = ((bf16[16,144,128]{2,1,0:T(8,128)(2,1)}), bf16[16,144,128]{2,1,0:T(8,128)(2,1)S(1)}, u32[]{:S(2)}, u32[]{:S(2)}) async-start(bf16[16,144,128]{2,1,0:T(8,128)(2,1)} %get-tuple-element.76), calls=%async_computation.1 | async-start | bytes 1179648 | tf_op jit(solution)/shard_map/all_to_all | solution.py:497
  147.1 2.4 %collective-permute-done.3 = bf16[2,256,512]{2,1,0:T(8,128)(2,1)} collective-permute-done((bf16[2,256,512]{2,1,0:T(8,128)(2,1)}, bf16[2,256,512]{2,1,0:T(8,128)(2,1)}, u32[]{:S(2)}, u32[]{:S(2)}) %collective-permute-start.3) | collective-permute-done | bytes 524320 | tf_op jit(solution)/shard_map/ppermute | solution.py:361
  149.5 2.1 %pad_maximum_fusion.1 = bf16[4,256,512]{2,1,0:T(8,128)(2,1)} fusion(bf16[2,256,512]{2,1,0:T(8,128)(2,1)} %collective-permute-done.3, bf16[1,256,512]{2,1,0:T(8,128)(2,1)S(1)} %collective-permute-done.2, bf16[1,256,512]{2,1,0:T(8,128)(2,1)S(1)} %maximum_bitcast_fusion), kind=kLoop, calls=%fused_computation.1 | loop fusion | flops 1048576 | bytes 2097152 | tf_op jit(solution)/shard_map/concatenate | solution.py:443
  151.6 2.8 %inner_attention.1 = (f32[1024,256]{1,0:T(8,128)S(1)}, f32[1024,256]{1,0:T(8,128)S(1)}) custom-call(bf16[1024,768]{1,0:T(8,128)(2,1)S(1)} %get-tuple-element.72.qkv_ref), custom_call_target="tpu_custom_call" | custom-call | flops 201326592 | bytes 3932160 | tf_op jit(solution)/shard_map/inner_attention/pallas_call | solution.py:209
  154.4 1.0 copy-done.2
  155.4 7.3 %all-to-all-done.1.back_ref = bf16[16,144,128]{2,1,0:T(8,128)(2,1)S(1)} async-done(((bf16[16,144,128]{2,1,0:T(8,128)(2,1)}), bf16[16,144,128]{2,1,0:T(8,128)(2,1)S(1)}, u32[]{:S(2)}, u32[]{:S(2)}) %all-to-all-start.1) | async-done | bytes 589856 | tf_op jit(solution)/shard_map/all_to_all | solution.py:497
  162.6 1.2 copy-done.3
  163.9 2.3 %merge_attention.1.refs_0_ = bf16[1024,256]{1,0:T(8,128)(2,1)S(1)} custom-call(s32[16]{0:T(128)S(1)} %reshape.80.owner_ref, s32[16]{0:T(128)S(1)} %reshape.86.later_ref, f32[1024,256]{1,0:T(8,128)S(1)} %get-tuple-element.73.sums_ref, f32[1024,256]{1,0:T(8,128)S(1)} %copy-done.3, bf16[16,144,128]{2,1,0:T(8,128)(2,1)S(1)} %all-to-all-done.1.back_ref), custom_call_target="tpu_custom_call" | custom-call | flops 2097152 | bytes 3145728 | tf_op jit(solution)/shard_map/merge_attention/pallas_call | solution.py:308
  166.2 1.6 collective-permute-start.39
  167.8 1.6 pad_maximum_fusion.weight_ref
  169.4 10.8 %collective-permute-done.39.refs_1_ = bf16[1024,256]{1,0:T(8,128)(2,1)S(1)} collective-permute-done((bf16[1024,256]{1,0:T(8,128)(2,1)S(1)}, bf16[1024,256]{1,0:T(8,128)(2,1)S(1)}, u32[]{:S(2)}, u32[]{:S(2)}) %collective-permute-start.39) | collective-permute-done | bytes 524320 | tf_op jit(solution)/shard_map/ppermute | solution.py:502
  180.1 6.1 %output_projection.1 = bf16[2048,1024]{1,0:T(8,128)(2,1)} custom-call(s32[8]{0:T(128)S(1)} %fusion.3.place_ref, bf16[8,256,512]{2,1,0:T(8,128)(2,1)S(1)} %pad_maximum_fusion.weight_ref, bf16[1024,256]{1,0:T(8,128)(2,1)S(1)} %merge_attention.1.refs_0_, bf16[1024,256]{1,0:T(8,128)(2,1)S(1)} %collective-permute-done.39.refs_1_), custom_call_target="tpu_custom_call" | custom-call | flops 2147483648 | bytes 6291456 | tf_op jit(solution)/shard_map/output_projection/pallas_call | solution.py:342
  (132 shorter events, 22.2 us)
Async XLA Ops:
  1.7 16.8 %collective-permute-start.12 = (bf16[256,384]{1,0:T(8,128)(2,1)S(1)}, bf16[256,384]{1,0:T(8,128)(2,1)S(1)}, u32[]{:S(2)}, u32[]{:S(2)}) collective-permute-start(bf16[256,384]{1,0:T(8,128)(2,1)S(1)} %get-tuple-element.41.refs_1_), channel_id=1, source_target_pairs={{0,4},{1,5},{2,6},{3,7},{4,8},{5,9},{6,10},{7,11},{8,12},{9,13},{1... | collective-permute-start | bytes 589832 | tf_op jit(solution)/shard_map/ppermute | solution.py:361
  4.8 24.7 %collective-permute-start.13 = (bf16[256,384]{1,0:T(8,128)(2,1)S(1)}, bf16[256,384]{1,0:T(8,128)(2,1)S(1)}, u32[]{:S(2)}, u32[]{:S(2)}) collective-permute-start(bf16[256,384]{1,0:T(8,128)(2,1)S(1)} %get-tuple-element.41.refs_1_), channel_id=1, source_target_pairs={{0,2},{1,3},{2,0},{3,1},{4,6},{5,7},{6,4},{7,5},{8,10},{9,11},{10,... | collective-permute-start | bytes 589832 | tf_op jit(solution)/shard_map/ppermute | solution.py:361
  6.3 9.1 %collective-permute-start.10 = (bf16[256,384]{1,0:T(8,128)(2,1)S(1)}, bf16[256,384]{1,0:T(8,128)(2,1)S(1)}, u32[]{:S(2)}, u32[]{:S(2)}) collective-permute-start(bf16[256,384]{1,0:T(8,128)(2,1)S(1)} %get-tuple-element.40.refs_0_), channel_id=1, source_target_pairs={{0,2},{1,3},{2,0},{3,1},{4,6},{5,7},{6,4},{7,5},{8,10},{9,11},{10,... | collective-permute-start | bytes 589832 | tf_op jit(solution)/shard_map/ppermute | solution.py:361
  6.8 8.6 %collective-permute-start.11 = (bf16[256,384]{1,0:T(8,128)(2,1)S(1)}, bf16[256,384]{1,0:T(8,128)(2,1)S(1)}, u32[]{:S(2)}, u32[]{:S(2)}) collective-permute-start(bf16[256,384]{1,0:T(8,128)(2,1)S(1)} %get-tuple-element.40.refs_0_), channel_id=1, source_target_pairs={{0,1},{1,0},{2,3},{3,2},{4,5},{5,4},{6,7},{7,6},{8,9},{9,8},{10,11... | collective-permute-start | bytes 589832 | tf_op jit(solution)/shard_map/ppermute | solution.py:361
  6.8 9.1 %collective-permute-start.9 = (bf16[256,384]{1,0:T(8,128)(2,1)S(1)}, bf16[256,384]{1,0:T(8,128)(2,1)S(1)}, u32[]{:S(2)}, u32[]{:S(2)}) collective-permute-start(bf16[256,384]{1,0:T(8,128)(2,1)S(1)} %get-tuple-element.40.refs_0_), channel_id=1, source_target_pairs={{0,4},{1,5},{2,6},{3,7},{4,8},{5,9},{6,10},{7,11},{8,12},{9,13},{1... | collective-permute-start | bytes 589832 | tf_op jit(solution)/shard_map/ppermute | solution.py:361
  15.3 14.6 %collective-permute-start.14 = (bf16[256,384]{1,0:T(8,128)(2,1)S(1)}, bf16[256,384]{1,0:T(8,128)(2,1)S(1)}, u32[]{:S(2)}, u32[]{:S(2)}) collective-permute-start(bf16[256,384]{1,0:T(8,128)(2,1)S(1)} %get-tuple-element.41.refs_1_), channel_id=1, source_target_pairs={{0,1},{1,0},{2,3},{3,2},{4,5},{5,4},{6,7},{7,6},{8,9},{9,8},{10,11... | collective-permute-start | bytes 589832 | tf_op jit(solution)/shard_map/ppermute | solution.py:361
  15.9 16.2 %collective-permute-start.15 = (bf16[256,384]{1,0:T(8,128)(2,1)S(1)}, bf16[256,384]{1,0:T(8,128)(2,1)S(1)}, u32[]{:S(2)}, u32[]{:S(2)}) collective-permute-start(bf16[256,384]{1,0:T(8,128)(2,1)S(1)} %collective-permute-done.9.refs_2_), channel_id=1, source_target_pairs={{0,4},{1,5},{2,6},{3,7},{4,8},{5,9},{6,10},{7,11},{8,12},{9,13},{1... | collective-permute-start | bytes 589832 | tf_op jit(solution)/shard_map/ppermute | solution.py:361
  17.0 15.1 %collective-permute-start.16 = (bf16[256,384]{1,0:T(8,128)(2,1)S(1)}, bf16[256,384]{1,0:T(8,128)(2,1)S(1)}, u32[]{:S(2)}, u32[]{:S(2)}) collective-permute-start(bf16[256,384]{1,0:T(8,128)(2,1)S(1)} %collective-permute-done.9.refs_2_), channel_id=1, source_target_pairs={{0,2},{1,3},{2,0},{3,1},{4,6},{5,7},{6,4},{7,5},{8,10},{9,11},{10,... | collective-permute-start | bytes 589832 | tf_op jit(solution)/shard_map/ppermute | solution.py:361
  18.5 14.1 %collective-permute-start.17 = (bf16[256,384]{1,0:T(8,128)(2,1)S(1)}, bf16[256,384]{1,0:T(8,128)(2,1)S(1)}, u32[]{:S(2)}, u32[]{:S(2)}) collective-permute-start(bf16[256,384]{1,0:T(8,128)(2,1)S(1)} %collective-permute-done.9.refs_2_), channel_id=1, source_target_pairs={{0,1},{1,0},{2,3},{3,2},{4,5},{5,4},{6,7},{7,6},{8,9},{9,8},{10,11... | collective-permute-start | bytes 589832 | tf_op jit(solution)/shard_map/ppermute | solution.py:361
  18.8 10.7 %copy-start.26 = (s32[2,8]{1,0:T(2,128)S(1)}, s32[2,8]{1,0:T(2,128)}, u32[]{:S(2)}) copy-start(s32[2,8]{1,0:T(2,128)} %param.10) | copy-start | bytes 196
  26.2 3.3 %copy-start = (bf16[1024,4096]{1,0:T(8,128)(2,1)}, bf16[1024,4096]{1,0:T(8,128)(2,1)S(1)}, u32[]{:S(2)}) copy-start(bf16[1024,4096]{1,0:T(8,128)(2,1)S(1)} %norm_rows.1.x_ref) | copy-start | bytes 25165828
  29.5 2.0 %collective-permute-start.5 = (s32[1,2,8]{2,1,0:T(2,128)S(1)}, s32[1,2,8]{2,1,0:T(2,128)S(1)}, u32[]{:S(2)}, u32[]{:S(2)}) collective-permute-start(s32[1,2,8]{2,1,0:T(2,128)S(1)} %bitcast.28), channel_id=1, source_target_pairs={{0,1},{1,0},{2,3},{3,2},{4,5},{5,4},{6,7},{7,6},{8,9},{9,8},{10,11... | collective-permute-start | bytes 200 | tf_op jit(solution)/shard_map/ppermute | solution.py:361
  30.0 9.6 %collective-permute-start.19 = (bf16[256,384]{1,0:T(8,128)(2,1)S(1)}, bf16[256,384]{1,0:T(8,128)(2,1)S(1)}, u32[]{:S(2)}, u32[]{:S(2)}) collective-permute-start(bf16[256,384]{1,0:T(8,128)(2,1)S(1)} %collective-permute-done.12.refs_3_), channel_id=1, source_target_pairs={{0,4},{1,5},{2,6},{3,7},{4,8},{5,9},{6,10},{7,11},{8,12},{9,13},{1... | collective-permute-start | bytes 589832 | tf_op jit(solution)/shard_map/ppermute | solution.py:361
  31.6 8.8 %collective-permute-start.20 = (bf16[256,384]{1,0:T(8,128)(2,1)S(1)}, bf16[256,384]{1,0:T(8,128)(2,1)S(1)}, u32[]{:S(2)}, u32[]{:S(2)}) collective-permute-start(bf16[256,384]{1,0:T(8,128)(2,1)S(1)} %collective-permute-done.12.refs_3_), channel_id=1, source_target_pairs={{0,2},{1,3},{2,0},{3,1},{4,6},{5,7},{6,4},{7,5},{8,10},{9,11},{10,... | collective-permute-start | bytes 589832 | tf_op jit(solution)/shard_map/ppermute | solution.py:361
  32.1 8.3 %collective-permute-start.21 = (bf16[256,384]{1,0:T(8,128)(2,1)S(1)}, bf16[256,384]{1,0:T(8,128)(2,1)S(1)}, u32[]{:S(2)}, u32[]{:S(2)}) collective-permute-start(bf16[256,384]{1,0:T(8,128)(2,1)S(1)} %collective-permute-done.12.refs_3_), channel_id=1, source_target_pairs={{0,1},{1,0},{2,3},{3,2},{4,5},{5,4},{6,7},{7,6},{8,9},{9,8},{10,11... | collective-permute-start | bytes 589832 | tf_op jit(solution)/shard_map/ppermute | solution.py:361
  32.1 1.7 collective-permute-start.18
  32.6 9.0 %collective-permute-start.22 = (bf16[256,384]{1,0:T(8,128)(2,1)S(1)}, bf16[256,384]{1,0:T(8,128)(2,1)S(1)}, u32[]{:S(2)}, u32[]{:S(2)}) collective-permute-start(bf16[256,384]{1,0:T(8,128)(2,1)S(1)} %collective-permute-done.13.refs_9_), channel_id=1, source_target_pairs={{0,1},{1,0},{2,3},{3,2},{4,5},{5,4},{6,7},{7,6},{8,9},{9,8},{10,11... | collective-permute-start | bytes 589832 | tf_op jit(solution)/shard_map/ppermute | solution.py:361
  34.5 3.7 %collective-permute-start.6 = (s32[2,2,8]{2,1,0:T(2,128)S(1)}, s32[2,2,8]{2,1,0:T(2,128)S(1)}, u32[]{:S(2)}, u32[]{:S(2)}) collective-permute-start(s32[2,2,8]{2,1,0:T(2,128)S(1)} %pad_add_fusion.2), channel_id=1, source_target_pairs={{0,2},{1,3},{2,0},{3,1},{4,6},{5,7},{6,4},{7,5},{8,10},{9,11},{10,... | collective-permute-start | bytes 392 | tf_op jit(solution)/shard_map/ppermute | solution.py:361
  38.2 10.7 %collective-permute-start.23 = (bf16[256,384]{1,0:T(8,128)(2,1)S(1)}, bf16[256,384]{1,0:T(8,128)(2,1)}, u32[]{:S(2)}, u32[]{:S(2)}) collective-permute-start(bf16[256,384]{1,0:T(8,128)(2,1)S(1)} %collective-permute-done.15.refs_4_), channel_id=1, source_target_pairs={{0,4},{1,5},{2,6},{3,7},{4,8},{5,9},{6,10},{7,11},{8,12},{9,13},{1... | collective-permute-start | bytes 589832 | tf_op jit(solution)/shard_map/ppermute | solution.py:361
  39.5 9.4 %collective-permute-start.24 = (bf16[256,384]{1,0:T(8,128)(2,1)S(1)}, bf16[256,384]{1,0:T(8,128)(2,1)}, u32[]{:S(2)}, u32[]{:S(2)}) collective-permute-start(bf16[256,384]{1,0:T(8,128)(2,1)S(1)} %collective-permute-done.15.refs_4_), channel_id=1, source_target_pairs={{0,2},{1,3},{2,0},{3,1},{4,6},{5,7},{6,4},{7,5},{8,10},{9,11},{10,... | collective-permute-start | bytes 589832 | tf_op jit(solution)/shard_map/ppermute | solution.py:361
  40.4 9.2 %collective-permute-start.25 = (bf16[256,384]{1,0:T(8,128)(2,1)S(1)}, bf16[256,384]{1,0:T(8,128)(2,1)S(1)}, u32[]{:S(2)}, u32[]{:S(2)}) collective-permute-start(bf16[256,384]{1,0:T(8,128)(2,1)S(1)} %collective-permute-done.15.refs_4_), channel_id=1, source_target_pairs={{0,1},{1,0},{2,3},{3,2},{4,5},{5,4},{6,7},{7,6},{8,9},{9,8},{10,11... | collective-permute-start | bytes 589832 | tf_op jit(solution)/shard_map/ppermute | solution.py:361
  41.1 9.9 %collective-permute-start.26 = (bf16[256,384]{1,0:T(8,128)(2,1)S(1)}, bf16[256,384]{1,0:T(8,128)(2,1)S(1)}, u32[]{:S(2)}, u32[]{:S(2)}) collective-permute-start(bf16[256,384]{1,0:T(8,128)(2,1)S(1)} %collective-permute-done.16.refs_10_), channel_id=1, source_target_pairs={{0,1},{1,0},{2,3},{3,2},{4,5},{5,4},{6,7},{7,6},{8,9},{9,8},{10,11... | collective-permute-start | bytes 589832 | tf_op jit(solution)/shard_map/ppermute | solution.py:361
  42.3 3.9 %collective-permute-start.7 = (s32[4,2,8]{2,1,0:T(2,128)S(1)}, s32[4,2,8]{2,1,0:T(2,128)S(1)}, u32[]{:S(2)}, u32[]{:S(2)}) collective-permute-start(s32[4,2,8]{2,1,0:T(2,128)S(1)} %pad_add_fusion.1), channel_id=1, source_target_pairs={{0,4},{1,5},{2,6},{3,7},{4,0},{5,1},{6,2},{7,3},{8,12},{9,13},{10,... | collective-permute-start | bytes 776 | tf_op jit(solution)/shard_map/ppermute | solution.py:361
  46.2 16.1 %collective-permute-start.34 = (bf16[256,384]{1,0:T(8,128)(2,1)S(1)}, bf16[256,384]{1,0:T(8,128)(2,1)S(1)}, u32[]{:S(2)}, u32[]{:S(2)}) collective-permute-start(bf16[256,384]{1,0:T(8,128)(2,1)S(1)} %collective-permute-done.13.refs_9_), channel_id=1, source_target_pairs={{0,12},{1,13},{2,14},{3,15},{4,0},{5,1},{6,2},{7,3},{8,4},{9,5},{1... | collective-permute-start | bytes 589832 | tf_op jit(solution)/shard_map/ppermute | solution.py:361
  48.9 8.8 %collective-permute-start.27 = (bf16[256,384]{1,0:T(8,128)(2,1)S(1)}, bf16[256,384]{1,0:T(8,128)(2,1)}, u32[]{:S(2)}, u32[]{:S(2)}) collective-permute-start(bf16[256,384]{1,0:T(8,128)(2,1)S(1)} %collective-permute-done.19.refs_5_), channel_id=1, source_target_pairs={{0,4},{1,5},{2,6},{3,7},{4,8},{5,9},{6,10},{7,11},{8,12},{9,13},{1... | collective-permute-start | bytes 589832 | tf_op jit(solution)/shard_map/ppermute | solution.py:361
  48.9 10.0 %collective-permute-start.28 = (bf16[256,384]{1,0:T(8,128)(2,1)S(1)}, bf16[256,384]{1,0:T(8,128)(2,1)}, u32[]{:S(2)}, u32[]{:S(2)}) collective-permute-start(bf16[256,384]{1,0:T(8,128)(2,1)S(1)} %collective-permute-done.19.refs_5_), channel_id=1, source_target_pairs={{0,2},{1,3},{2,0},{3,1},{4,6},{5,7},{6,4},{7,5},{8,10},{9,11},{10,... | collective-permute-start | bytes 589832 | tf_op jit(solution)/shard_map/ppermute | solution.py:361
  50.3 9.3 %collective-permute-start.29 = (bf16[256,384]{1,0:T(8,128)(2,1)S(1)}, bf16[256,384]{1,0:T(8,128)(2,1)S(1)}, u32[]{:S(2)}, u32[]{:S(2)}) collective-permute-start(bf16[256,384]{1,0:T(8,128)(2,1)S(1)} %collective-permute-done.19.refs_5_), channel_id=1, source_target_pairs={{0,1},{1,0},{2,3},{3,2},{4,5},{5,4},{6,7},{7,6},{8,9},{9,8},{10,11... | collective-permute-start | bytes 589832 | tf_op jit(solution)/shard_map/ppermute | solution.py:361
  51.7 8.6 %collective-permute-start.30 = (bf16[256,384]{1,0:T(8,128)(2,1)S(1)}, bf16[256,384]{1,0:T(8,128)(2,1)S(1)}, u32[]{:S(2)}, u32[]{:S(2)}) collective-permute-start(bf16[256,384]{1,0:T(8,128)(2,1)S(1)} %collective-permute-done.20.refs_11_), channel_id=1, source_target_pairs={{0,1},{1,0},{2,3},{3,2},{4,5},{5,4},{6,7},{7,6},{8,9},{9,8},{10,11... | collective-permute-start | bytes 589832 | tf_op jit(solution)/shard_map/ppermute | solution.py:361
  57.7 4.5 %collective-permute-start.8 = (s32[8,2,8]{2,1,0:T(2,128)S(1)}, s32[8,2,8]{2,1,0:T(2,128)S(1)}, u32[]{:S(2)}, u32[]{:S(2)}) collective-permute-start(s32[8,2,8]{2,1,0:T(2,128)S(1)} %pad_add_fusion), channel_id=1, source_target_pairs={{0,8},{1,9},{2,10},{3,11},{4,12},{5,13},{6,14},{7,15},{8,0},{9,1},... | collective-permute-start | bytes 1544 | tf_op jit(solution)/shard_map/ppermute | solution.py:361
  58.9 5.9 %collective-permute-start.31 = (bf16[256,384]{1,0:T(8,128)(2,1)}, bf16[256,384]{1,0:T(8,128)(2,1)S(1)}, u32[]{:S(2)}, u32[]{:S(2)}) collective-permute-start(bf16[256,384]{1,0:T(8,128)(2,1)} %collective-permute-done.23.refs_6_), channel_id=1, source_target_pairs={{0,2},{1,3},{2,0},{3,1},{4,6},{5,7},{6,4},{7,5},{8,10},{9,11},{10,... | collective-permute-start | bytes 589832 | tf_op jit(solution)/shard_map/ppermute | solution.py:361
  60.3 4.5 %collective-permute-start.32 = (bf16[256,384]{1,0:T(8,128)(2,1)}, bf16[256,384]{1,0:T(8,128)(2,1)S(1)}, u32[]{:S(2)}, u32[]{:S(2)}) collective-permute-start(bf16[256,384]{1,0:T(8,128)(2,1)} %collective-permute-done.23.refs_6_), channel_id=1, source_target_pairs={{0,1},{1,0},{2,3},{3,2},{4,5},{5,4},{6,7},{7,6},{8,9},{9,8},{10,11... | collective-permute-start | bytes 589832 | tf_op jit(solution)/shard_map/ppermute | solution.py:361
  61.0 2.2 %collective-permute-start.35 = (bf16[256,384]{1,0:T(8,128)(2,1)}, bf16[256,384]{1,0:T(8,128)(2,1)S(1)}, u32[]{:S(2)}, u32[]{:S(2)}) collective-permute-start(bf16[256,384]{1,0:T(8,128)(2,1)} %collective-permute-done.27.refs_7_), channel_id=1, source_target_pairs={{0,1},{1,0},{2,3},{3,2},{4,5},{5,4},{6,7},{7,6},{8,9},{9,8},{10,11... | collective-permute-start | bytes 589832 | tf_op jit(solution)/shard_map/ppermute | solution.py:361
  62.3 1.7 collective-permute-start.36
  62.3 2.5 %collective-permute-start.33 = (bf16[256,384]{1,0:T(8,128)(2,1)}, bf16[256,384]{1,0:T(8,128)(2,1)S(1)}, u32[]{:S(2)}, u32[]{:S(2)}) collective-permute-start(bf16[256,384]{1,0:T(8,128)(2,1)} %collective-permute-done.24.refs_12_), channel_id=1, source_target_pairs={{0,1},{1,0},{2,3},{3,2},{4,5},{5,4},{6,7},{7,6},{8,9},{9,8},{10,11... | collective-permute-start | bytes 589832 | tf_op jit(solution)/shard_map/ppermute | solution.py:361
  63.9 19.2 %collective-permute-start.38 = (bf16[256,384]{1,0:T(8,128)(2,1)S(1)}, bf16[256,384]{1,0:T(8,128)(2,1)S(1)}, u32[]{:S(2)}, u32[]{:S(2)}) collective-permute-start(bf16[256,384]{1,0:T(8,128)(2,1)S(1)} %collective-permute-done.34.refs_1_), channel_id=1, source_target_pairs={{0,1},{1,0},{2,3},{3,2},{4,5},{5,4},{6,7},{7,6},{8,9},{9,8},{10,11... | collective-permute-start | bytes 589832 | tf_op jit(solution)/shard_map/ppermute | solution.py:361
  64.8 18.3 %collective-permute-start.37 = (bf16[256,384]{1,0:T(8,128)(2,1)S(1)}, bf16[256,384]{1,0:T(8,128)(2,1)S(1)}, u32[]{:S(2)}, u32[]{:S(2)}) collective-permute-start(bf16[256,384]{1,0:T(8,128)(2,1)S(1)} %collective-permute-done.31.refs_0_), channel_id=1, source_target_pairs={{0,1},{1,0},{2,3},{3,2},{4,5},{5,4},{6,7},{7,6},{8,9},{9,8},{10,11... | collective-permute-start | bytes 589832 | tf_op jit(solution)/shard_map/ppermute | solution.py:361
  87.9 4.4 %copy-start.25 = (bf16[256,256]{1,0:T(8,128)(2,1)S(1)}, bf16[256,256]{1,0:T(8,128)(2,1)}, u32[]{:S(2)}) copy-start(bf16[256,256]{1,0:T(8,128)(2,1)} %param.8) | copy-start | bytes 393220
  87.9 51.7 %copy-start.4 = (f32[2,4,128]{2,1,0:T(4,128)S(1)}, f32[2,4,128]{2,1,0:T(4,128)}, u32[]{:S(2)}) copy-start(f32[2,4,128]{2,1,0:T(4,128)} %param.9) | copy-start | bytes 12292
  87.9 51.7 %all-to-all-start = ((bf16[16,128,256]{2,1,0:T(8,128)(2,1)}), bf16[16,128,256]{2,1,0:T(8,128)(2,1)S(1)}, u32[]{:S(2)}, u32[]{:S(2)}) async-start(bf16[16,128,256]{2,1,0:T(8,128)(2,1)} %copy-done.1), calls=%async_computation | async-start | bytes 2097152 | tf_op jit(solution)/shard_map/all_to_all | solution.py:492
  92.4 32.0 %collective-permute-start = (bf16[256,256]{1,0:T(8,128)(2,1)S(1)}, bf16[256,256]{1,0:T(8,128)(2,1)S(1)}, u32[]{:S(2)}, u32[]{:S(2)}) collective-permute-start(bf16[256,256]{1,0:T(8,128)(2,1)S(1)} %bitcast.27), channel_id=1, source_target_pairs={{0,8},{1,9},{2,10},{3,11},{4,12},{5,13},{6,14},{7,15},{8,0},{9,1},... | collective-permute-start | bytes 393224 | tf_op jit(solution)/shard_map/ppermute | solution.py:361
  124.5 5.1 %collective-permute-start.1 = (bf16[256,256]{1,0:T(8,128)(2,1)S(1)}, bf16[256,256]{1,0:T(8,128)(2,1)S(1)}, u32[]{:S(2)}, u32[]{:S(2)}) collective-permute-start(bf16[256,256]{1,0:T(8,128)(2,1)S(1)} %get-tuple-element.84), channel_id=1, source_target_pairs={{0,16},{16,0},{1,17},{17,1},{2,18},{18,2},{3,19},{19,3},{4,20},{20... | collective-permute-start | bytes 393224 | tf_op jit(solution)/shard_map/ppermute | solution.py:440
  129.6 7.0 %collective-permute-start.2 = (bf16[1,256,512]{2,1,0:T(8,128)(2,1)S(1)}, bf16[1,256,512]{2,1,0:T(8,128)(2,1)S(1)}, u32[]{:S(2)}, u32[]{:S(2)}) collective-permute-start(bf16[1,256,512]{2,1,0:T(8,128)(2,1)S(1)} %maximum_bitcast_fusion), channel_id=1, source_target_pairs={{0,4},{1,5},{2,6},{3,7},{4,0},{5,1},{6,2},{7,3},{8,12},{9,13},{10,... | collective-permute-start | bytes 786440 | tf_op jit(solution)/shard_map/ppermute | solution.py:361
  136.6 15.0 %copy-start.23 = (bf16[1,256,512]{2,1,0:T(8,128)(2,1)}, bf16[1,256,512]{2,1,0:T(8,128)(2,1)S(1)}, u32[]{:S(2)}) copy-start(bf16[1,256,512]{2,1,0:T(8,128)(2,1)S(1)} %collective-permute-done.2) | copy-start | bytes 786436
  137.5 12.0 %collective-permute-start.3 = (bf16[2,256,512]{2,1,0:T(8,128)(2,1)}, bf16[2,256,512]{2,1,0:T(8,128)(2,1)}, u32[]{:S(2)}, u32[]{:S(2)}) collective-permute-start(bf16[2,256,512]{2,1,0:T(8,128)(2,1)} %pad_maximum_fusion.2), channel_id=1, source_target_pairs={{0,2},{1,3},{2,0},{3,1},{4,6},{5,7},{6,4},{7,5},{8,10},{9,11},{10,... | collective-permute-start | bytes 1572872 | tf_op jit(solution)/shard_map/ppermute | solution.py:361
  143.5 19.1 %all-to-all-start.1 = ((bf16[16,144,128]{2,1,0:T(8,128)(2,1)}), bf16[16,144,128]{2,1,0:T(8,128)(2,1)S(1)}, u32[]{:S(2)}, u32[]{:S(2)}) async-start(bf16[16,144,128]{2,1,0:T(8,128)(2,1)} %get-tuple-element.76), calls=%async_computation.1 | async-start | bytes 1179648 | tf_op jit(solution)/shard_map/all_to_all | solution.py:497
  151.6 16.2 %collective-permute-start.4 = (bf16[4,256,512]{2,1,0:T(8,128)(2,1)}, bf16[4,256,512]{2,1,0:T(8,128)(2,1)}, u32[]{:S(2)}, u32[]{:S(2)}) collective-permute-start(bf16[4,256,512]{2,1,0:T(8,128)(2,1)} %pad_maximum_fusion.1), channel_id=1, source_target_pairs={{0,1},{1,0},{2,3},{3,2},{4,5},{5,4},{6,7},{7,6},{8,9},{9,8},{10,11... | collective-permute-start | bytes 3145736 | tf_op jit(solution)/shard_map/ppermute | solution.py:361
  163.9 3.9 %copy-start.24 = (bf16[1,256,512]{2,1,0:T(8,128)(2,1)S(1)}, bf16[1,256,512]{2,1,0:T(8,128)(2,1)}, u32[]{:S(2)}) copy-start(bf16[1,256,512]{2,1,0:T(8,128)(2,1)} %copy-done.23) | copy-start | bytes 786436
  166.2 13.9 %collective-permute-start.39 = (bf16[1024,256]{1,0:T(8,128)(2,1)S(1)}, bf16[1024,256]{1,0:T(8,128)(2,1)S(1)}, u32[]{:S(2)}, u32[]{:S(2)}) collective-permute-start(bf16[1024,256]{1,0:T(8,128)(2,1)S(1)} %merge_attention.1.refs_0_), channel_id=1, source_target_pairs={{0,16},{16,0},{1,17},{17,1},{2,18},{18,2},{3,19},{19,3},{4,20},{20... | collective-permute-start | bytes 1572872 | tf_op jit(solution)/shard_map/ppermute | solution.py:502
  (21 other events, 17.6 us)

commit v2 on v1

v2 whole, which is shorter than its diff:
```python
import functools

import jax
import jax.numpy as jnp
from jax import lax
from jax.experimental import pallas as pl
from jax.experimental.pallas import tpu as pltpu
from jax.sharding import PartitionSpec as P

LOGIT_SCALE = 8.0
KEEP_RATE = 0.75
VMEM_BYTES = 16 * 1024 * 1024
LABEL_ROWS = 16
NT_DIMS = (((1,), (1,)), ((), ()))
TN_DIMS = (((0,), (0,)), ((), ()))
tie = lax.optimization_barrier


def params(axes=1):
    return pltpu.CompilerParams(
        vmem_limit_bytes=VMEM_BYTES, dimension_semantics=("arbitrary",) * axes
    )


def cost(flops, moved, exps=0):
    return pl.CostEstimate(flops=flops, bytes_accessed=moved, transcendentals=exps)


def whole_block(shape):
    zeros = (0,) * len(shape)
    return pl.BlockSpec(shape, lambda *_: zeros)


def in_hbm(value):
    return pltpu.with_memory_space_constraint(value, pltpu.HBM)


def in_vmem(value):
    return pltpu.with_memory_space_constraint(value, pltpu.VMEM)


W_PLACE = in_vmem
VMEM_SPEC = pl.BlockSpec(memory_space=pltpu.VMEM)
SMEM_SPEC = pl.BlockSpec(memory_space=pltpu.SMEM)
W_SPEC = VMEM_SPEC


ORDER = [(0, 0, 0), (1, 0, 0), (0, 1, 0), (0, 0, 1)]
ORDER += [(2, 0, 0), (1, 1, 0), (1, 0, 1), (0, 1, 1)]
ORDER += [(3, 0, 0), (2, 1, 0), (2, 0, 1), (1, 1, 1)]
ORDER += [(3, 1, 0), (3, 0, 1), (2, 1, 1), (3, 1, 1)]


def place_of(i, me, paired):
    if not paired:
        return i
    back, side, core = ORDER[i]
    return ((me // 4 + 4 - back) % 4 * 4 + me % 4) ^ (side * 2 + core)


def split_kernel(weight_ref, clusters_ref, first_ref, second_ref):
    rows, half = second_ref.shape
    first_ref[:rows, :] = weight_ref[:, :half]
    second_ref[...] = weight_ref[:, half:]
    marks = jnp.zeros((LABEL_ROWS, 128), jnp.float32)
    line = lax.broadcasted_iota(jnp.int32, marks.shape, 0)
    lane = lax.broadcasted_iota(jnp.int32, marks.shape, 1)
    heads, tiles = clusters_ref.shape
    for head in range(heads):
        for t in range(tiles):
            number = clusters_ref[head, t].astype(jnp.float32)
            marks = jnp.where((line == head) & (lane == t), number, marks)
    first_ref[rows:, :] = jnp.zeros((LABEL_ROWS, half), first_ref.dtype)
    first_ref[rows:, :128] = marks.astype(first_ref.dtype)


def split_weight(weight, clusters):
    rows, half = weight.shape[0], weight.shape[1] // 2
    return pl.pallas_call(
        split_kernel,
        out_shape=(
            pltpu.VMEM((rows + LABEL_ROWS, half), weight.dtype),
            pltpu.VMEM((rows, half), weight.dtype),
        ),
        in_specs=[VMEM_SPEC, SMEM_SPEC],
        out_specs=(VMEM_SPEC,) * 2,
        compiler_params=pltpu.CompilerParams(vmem_limit_bytes=VMEM_BYTES),
        cost_estimate=cost(0, 8 * rows * half),
        name="split_weight",
    )(weight, clusters)


def spread_marks(blocks, depth, start, total):
    for i, ref in enumerate(blocks):
        marks = ref[depth : depth + LABEL_ROWS, :128].astype(jnp.float32)
        shift = (start + i) * 8
        moved = pltpu.roll(marks, shift, 1) if shift else marks
        total = moved if total is None else total + moved
    return total


def early_kernel(n_early, n_late, paired, me_ref, x_ref, *refs):
    weights, (acc_ref, rest_ref, marks_ref) = refs[: 2 * n_early], refs[2 * n_early :]
    depth, half = weights[1].shape
    me = me_ref[0]

    @pl.when(pl.program_id(0) == 0)
    def _():
        marks_ref[...] = jnp.zeros_like(marks_ref)
        if paired:
            marks_ref[...] = spread_marks(weights[::2], depth, 0, None)

    def columns(i):
        at = place_of(i, me, paired) * depth
        return x_ref[:, pl.ds(pl.multiple_of(at, depth), depth)]

    square = None
    for at in range(0, x_ref.shape[1], 128):
        x = x_ref[:, at : at + 128].astype(jnp.float32)
        square = x * x if square is None else square + x * x
    mean = jnp.sum(square, axis=-1, keepdims=True) / x_ref.shape[1]
    scale = lax.rsqrt(mean + 1e-05)
    for part in range(2):
        total = None
        for i in range(n_early):
            term = jnp.dot(
                columns(i), weights[2 * i + part][:depth, :], preferred_element_type=jnp.float32
            )
            total = term if total is None else total + term
        acc_ref[:, part * half : (part + 1) * half] = jnp.where(scale > 0, total * scale, 0.0)
    for i in range(n_late):
        x = columns(n_early + i).astype(jnp.float32)
        rest_ref[:, i * depth : (i + 1) * depth] = (x * scale).astype(rest_ref.dtype)


def project_early(tokens, me, early, n_late, paired):
    rows, width = tokens.shape
    depth, half = early[0][1].shape
    n_early = len(early)
    step = min(256, rows)
    flat = [part for pair in early for part in pair]
    return pl.pallas_call(
        functools.partial(early_kernel, n_early, n_late, paired),
        out_shape=(
            pltpu.HBM((rows, 2 * half), jnp.float32),
            pltpu.HBM((rows, n_late * depth), jnp.bfloat16),
            pltpu.HBM((LABEL_ROWS, 128), jnp.float32),
        ),
        grid_spec=pltpu.PrefetchScalarGridSpec(
            num_scalar_prefetch=1,
            grid=(rows // step,),
            in_specs=[pl.BlockSpec((step, width), lambda i, _: (i, 0))] + [W_SPEC] * len(flat),
            out_specs=(
                pl.BlockSpec((step, 2 * half), lambda i, _: (i, 0)),
                pl.BlockSpec((step, n_late * depth), lambda i, _: (i, 0)),
                whole_block((LABEL_ROWS, 128)),
            ),
        ),
        compiler_params=pltpu.CompilerParams(vmem_limit_bytes=26 * 1024 * 1024),
        cost_estimate=cost(
            4 * rows * n_early * depth * half, 2 * rows * width + 8 * rows * half
        ),
        name="project_early",
    )(me, in_hbm(tokens), *map(W_PLACE, flat))


def unit_rows(values):
    values = values.astype(jnp.float32)
    scale = lax.rsqrt(jnp.mean(values * values, axis=-1, keepdims=True) + 1e-06)
    return (values * scale).astype(jnp.bfloat16)


def fill_tables(clus_here, me, paired, labels, cluster_ref, table_ref):
    heads, tiles = cluster_ref.shape
    shape = (8, labels.shape[1])
    line = lax.broadcasted_iota(jnp.int32, shape, 0)
    lane = lax.broadcasted_iota(jnp.int32, shape, 1)
    numbers = lane
    if paired:
        for i in range(16):
            numbers = jnp.where(
                lane // tiles == i, place_of(i, me, paired) * tiles + lane % tiles, numbers
            )
    base = heads * 8
    for head in range(heads):
        row = labels[head : head + 1, :]
        own = jnp.full(shape, -1, jnp.int32)
        for t in range(tiles):
            own = jnp.where(line == t, cluster_ref[head, t], own)
        earlier = (row == own) & (numbers < me * tiles + line)
        later = jnp.max(earlier.astype(jnp.int32), axis=1, keepdims=True)
        table_ref[head * 8 : (head + 1) * 8, :] = jnp.broadcast_to(later, (8, 128))
        member = (row == me * clus_here + line) & (line < clus_here)
        held = jnp.sum(member.astype(jnp.int32), axis=1, keepdims=True)
        last = shape[1] - 1
        first = jnp.min(jnp.where(member, numbers, last), axis=1, keepdims=True) // tiles
        second = jnp.max(jnp.where(member, numbers, 0), axis=1, keepdims=True) // tiles
        for q, column in enumerate((held, first, second)):
            at = base + (q * heads + head) * 8
            table_ref[at : at + 8, :] = jnp.broadcast_to(column, (8, 128))


def late_kernel(
    n_late, heads, tiles, tile_rows, clus_here, paired, me_ref, cluster_ref, acc_ref, rest_ref,
    marks_ref, *refs
):
    weights, (qkv_ref, out_ref, table_ref) = refs[: 2 * n_late], refs[2 * n_late :]
    depth, half = weights[1].shape
    head_dim = out_ref.shape[2] // 2
    step = pl.program_id(0)
    tiles_step = acc_ref.shape[0] // tile_rows

    @pl.when(step == 0)
    def _():
        labels = marks_ref[...]
        if paired:
            labels = spread_marks(weights[::2], depth, 16 - n_late, labels)
        labels = labels.astype(jnp.int32)
        fill_tables(clus_here, me_ref[0], paired, labels, cluster_ref, table_ref)
        if out_ref.shape[0] > heads * tiles:
            out_ref[...] = jnp.zeros_like(out_ref)

    for part in range(2):
        total = acc_ref[:, part * half : (part + 1) * half]
        for i in range(n_late):
            total += jnp.dot(
                rest_ref[:, i * depth : (i + 1) * depth],
                weights[2 * i + part][:depth, :],
                preferred_element_type=jnp.float32,
            )
        projected = total.astype(jnp.bfloat16)
        for local in range(heads // 2):
            head = part * (heads // 2) + local
            base = local * 3 * head_dim
            query = unit_rows(projected[:, base : base + head_dim])
            key = unit_rows(projected[:, base + head_dim : base + 2 * head_dim])
            value = projected[:, base + 2 * head_dim : base + 3 * head_dim]
            at = head * 3 * head_dim
            qkv_ref[:, at : at + head_dim] = query
            qkv_ref[:, at + head_dim : at + 2 * head_dim] = key
            qkv_ref[:, at + 2 * head_dim : at + 3 * head_dim] = value
            for t in range(tiles_step):
                tile = step * tiles_step + t
                owner = cluster_ref[head, tile] // clus_here
                later = table_ref[pl.ds(head * 8 + tile, 1), :]
                span = slice(t * tile_rows, (t + 1) * tile_rows)
                out_ref[owner, :, :head_dim] = key[span]
                out_ref[owner, :, head_dim:] = jnp.where(later > 0, query[span], value[span])


def project_late(me, clusters, clus_here, acc, rest, marks, late, n_owners, paired):
    rows, cols = acc.shape
    heads, tiles = clusters.shape
    depth, half = late[0][1].shape
    n_late = len(late)
    tile_rows = rows // tiles
    head_dim = cols // (3 * heads)
    step = 2 * tile_rows
    table_rows = 32 * heads
    flat = [part for pair in late for part in pair]
    return pl.pallas_call(
        functools.partial(
            late_kernel, n_late, heads, tiles, tile_rows, clus_here, paired
        ),
        out_shape=(
            pltpu.HBM((rows, cols), jnp.bfloat16),
            pltpu.HBM((n_owners, tile_rows, 2 * head_dim), jnp.bfloat16),
            pltpu.HBM((table_rows, 128), jnp.int32),
        ),
        grid_spec=pltpu.PrefetchScalarGridSpec(
            num_scalar_prefetch=2,
            grid=(rows // step,),
            in_specs=[
                pl.BlockSpec((step, cols), lambda i, *_: (i, 0)),
                pl.BlockSpec((step, n_late * depth), lambda i, *_: (i, 0)),
                whole_block(marks.shape),
            ]
            + [W_SPEC] * len(flat),
            out_specs=(
                pl.BlockSpec((step, cols), lambda i, *_: (i, 0)),
                whole_block((n_owners, tile_rows, 2 * head_dim)),
                whole_block((table_rows, 128)),
            ),
        ),
        compiler_params=params(),
        cost_estimate=cost(4 * rows * n_late * depth * half, 9 * rows * cols),
        name="project_late",
    )(me, clusters, in_hbm(acc), in_hbm(rest), in_hbm(marks), *map(W_PLACE, flat))


def inner_kernel(heads, qkv_ref, sums_ref, mass_ref):
    rows = qkv_ref.shape[0]
    head_dim = qkv_ref.shape[1] // (3 * heads)
    allowed = lax.broadcasted_iota(jnp.int32, (rows, rows), 0) <= lax.broadcasted_iota(
        jnp.int32, (rows, rows), 1
    )
    for head in range(heads):
        at = head * 3 * head_dim
        query = qkv_ref[:, at : at + head_dim]
        key = qkv_ref[:, at + head_dim : at + 2 * head_dim]
        value = qkv_ref[:, at + 2 * head_dim : at + 3 * head_dim]
        scores = lax.dot_general(key, query, NT_DIMS, preferred_element_type=jnp.float32)
        weights = jnp.where(allowed, jnp.exp(scores * (LOGIT_SCALE / head_dim)), 0.0)
        mass = jnp.sum(weights, axis=0, keepdims=True)
        sums_ref[head * head_dim : (head + 1) * head_dim, :] = lax.dot_general(
            value, weights.astype(jnp.bfloat16), TN_DIMS, preferred_element_type=jnp.float32
        )
        mass_ref[head * 8 : (head + 1) * 8, :] = jnp.broadcast_to(mass, (8, rows))


def inner_attention(qkv, heads, tiles):
    rows, cols = qkv.shape
    tile_rows = rows // tiles
    return pl.pallas_call(
        functools.partial(inner_kernel, heads),
        out_shape=(
            pltpu.HBM((cols // 3, rows), jnp.float32),
            pltpu.HBM((heads * 8, rows), jnp.float32),
        ),
        grid=(tiles,),
        in_specs=[pl.BlockSpec((tile_rows, cols), lambda i: (i, 0))],
        out_specs=(
            pl.BlockSpec((cols // 3, tile_rows), lambda i: (0, i)),
            pl.BlockSpec((heads * 8, tile_rows), lambda i: (0, i)),
        ),
        compiler_params=params(),
        cost_estimate=cost(
            2 * rows * tile_rows * cols, 5 * rows * cols, rows * tile_rows * heads
        ),
        name="inner_attention",
    )(in_hbm(qkv))


def owner_kernel(base, heads, table_ref, in_ref, cent_ref, out_ref, new_ref):
    tile_rows = in_ref.shape[1]
    head_dim = in_ref.shape[2] // 2
    out_ref[...] = jnp.zeros_like(out_ref)
    line = lax.broadcasted_iota(jnp.int32, (LABEL_ROWS, tile_rows), 0)
    for c in range(cent_ref.shape[0]):
        clus_here = cent_ref.shape[0] // heads
        at = base + c // clus_here * 8 + c % clus_here
        held, first, second = (table_ref[at + 8 * heads * q, 0] for q in range(3))
        key = in_ref[first, :, :head_dim]

        @pl.when(held > 1)
        def _():
            value = in_ref[first, :, head_dim:]
            query = in_ref[second, :, head_dim:]
            scores = lax.dot_general(key, query, NT_DIMS, preferred_element_type=jnp.float32)
            weights = jnp.exp(scores * (LOGIT_SCALE / head_dim))
            mass = jnp.sum(weights, axis=0, keepdims=True)
            out_ref[second, :head_dim, :] = lax.dot_general(
                value, weights.astype(jnp.bfloat16), TN_DIMS, preferred_element_type=jnp.float32
            ).astype(jnp.bfloat16)
            high = mass.astype(jnp.bfloat16).astype(jnp.float32)
            out_ref[second, head_dim:, :] = jnp.where(
                line == 0, high, jnp.where(line == 1, mass - high, 0.0)
            ).astype(jnp.bfloat16)

        other = in_ref[second, :, :head_dim]
        first_sum = jnp.sum(key.astype(jnp.float32), axis=0, keepdims=True)
        other_sum = jnp.sum(other.astype(jnp.float32), axis=0, keepdims=True)
        key_sum = jnp.where(held > 1, first_sum + other_sum, first_sum)
        count = jnp.maximum(held, 1).astype(jnp.float32) * tile_rows
        old = cent_ref[c : c + 1, :]
        moved = old + (1.0 - KEEP_RATE) * (key_sum / count - old)
        new_ref[c : c + 1, :] = jnp.where(held > 0, moved, old)


def owner_attention(incoming, centroid_rows, table, heads):
    n, tile_rows, width = incoming.shape
    head_dim = width // 2
    returning = (n, head_dim + LABEL_ROWS, tile_rows)
    return pl.pallas_call(
        functools.partial(owner_kernel, heads * 8, heads),
        out_shape=(
            pltpu.HBM(returning, jnp.bfloat16),
            pltpu.HBM(centroid_rows.shape, jnp.float32),
        ),
        grid=(1,),
        in_specs=[
            pl.BlockSpec(memory_space=pltpu.SMEM),
            whole_block(incoming.shape),
            whole_block(centroid_rows.shape),
        ],
        out_specs=(whole_block(returning), whole_block(centroid_rows.shape)),
        compiler_params=params(),
        cost_estimate=cost(
            4 * centroid_rows.shape[0] * tile_rows * tile_rows * width,
            4 * n * tile_rows * width,
            centroid_rows.shape[0] * tile_rows * tile_rows,
        ),
        name="owner_attention",
    )(table, incoming, in_hbm(centroid_rows))


def merge_kernel(clus_here, cluster_ref, table_ref, sums_ref, mass_ref, back_ref, out_ref):
    heads, tiles = cluster_ref.shape
    head_dim = sums_ref.shape[0] // heads
    step = pl.program_id(0)
    for head in range(heads):
        index = head * 8 + step
        owner = cluster_ref[head, step] // clus_here
        later = table_ref[index, 0] > 0
        span = slice(head * head_dim, (head + 1) * head_dim)
        sums = sums_ref[span, :]
        mass = mass_ref[head * 8 : head * 8 + 1, :]
        far = back_ref[owner, head_dim:, :].astype(jnp.float32)
        far_sums = back_ref[owner, :head_dim, :].astype(jnp.float32)
        sums = jnp.where(later, sums + far_sums, sums)
        mass = jnp.where(later, mass + far[0:1] + far[1:2], mass)
        out_ref[span, :] = (sums / mass).astype(out_ref.dtype)


def merge_attention(sums, mass, back, clusters, clus_here, table):
    cols, rows = sums.shape
    tiles = clusters.shape[1]
    tile_rows = rows // tiles
    block = pl.BlockSpec((cols, tile_rows), lambda i: (0, i))
    return pl.pallas_call(
        functools.partial(merge_kernel, clus_here),
        out_shape=jax.ShapeDtypeStruct((cols, rows), jnp.bfloat16),
        grid=(tiles,),
        in_specs=[
            pl.BlockSpec(memory_space=pltpu.SMEM),
            pl.BlockSpec(memory_space=pltpu.SMEM),
            block,
            pl.BlockSpec((mass.shape[0], tile_rows), lambda i: (0, i)),
            whole_block(back.shape),
        ],
        out_specs=block,
        compiler_params=params(),
        cost_estimate=cost(8 * rows * cols, 12 * rows * cols),
        name="merge_attention",
    )(clusters, table, in_hbm(sums), in_hbm(mass), back)


def output_kernel(me_ref, weight_ref, *refs):
    parts, out_ref = refs[:-1], refs[-1]
    total, at = None, 0
    for part in parts:
        depth = part.shape[0]
        term = jnp.dot(
            weight_ref[0, :, at : at + depth], part[...], preferred_element_type=jnp.float32
        )
        total = term if total is None else total + term
        at += depth
    out_ref[...] = total.astype(out_ref.dtype)


def output_projection(weight_blocks, me, parts, paired):
    n, features, depth = weight_blocks.shape
    rows = parts[0].shape[1]

    def place(i, me_ref):
        return ((me_ref[0] % 8) ^ (i % 2 * 4 + i // 2 % 2 * 2 + i // 4) if paired else i, 0)

    return pl.pallas_call(
        output_kernel,
        out_shape=jax.ShapeDtypeStruct((n * features, rows), jnp.bfloat16),
        grid_spec=pltpu.PrefetchScalarGridSpec(
            num_scalar_prefetch=1,
            grid=(n,),
            in_specs=[pl.BlockSpec((1, features, depth), lambda i, _: (i, 0, 0))]
            + [whole_block(part.shape) for part in parts],
            out_specs=pl.BlockSpec((features, rows), place),
        ),
        compiler_params=params(),
        cost_estimate=cost(
            2 * n * features * depth * rows, 2 * n * features * (rows + depth)
        ),
        name="output_projection",
    )(me, in_hbm(weight_blocks), *parts)


def permute(value, pairs):
    return lax.ppermute(value, "seq", pairs)


def flip(bit, n=16):
    return [(s, s ^ bit) for s in range(n)]


def turn(by, n=16):
    return [(s, (s + 4 * by) % n) for s in range(n)]


LINE_UP, LINE_DOWN = turn(1), turn(-1)
SIDE, CORE, FAR, NEXT = flip(2), flip(1), flip(8), flip(4)
SWAP = [(0, 1), (1, 0)]


def gather_weights(weight, clusters, out_weight, me, group, project):
    own_a, own_b = split_weight(weight, clusters)
    inside = me // 8 == group

    def hop(moves):
        return tie(tuple(lax.ppermute(value, axis, pairs) for value, axis, pairs in moves))

    def first(own):
        return hop([(own, "seq", LINE_UP), (own, "seq", SIDE), (own, "seq", CORE)])

    def onward(line, side, extra=()):
        moves = [(line, "seq", LINE_UP), (line, "seq", SIDE)]
        return hop(moves + [(line, "seq", CORE), (side, "seq", CORE), *extra])

    line_a1, side_a0, core_a0 = first(own_a)
    line_b1, side_b0, core_b0 = first(own_b)
    line_a1, out_weight = tie((line_a1, out_weight))
    mine = out_weight.T
    line_a2, side_a1, core_a1, cross_a0, across = onward(
        line_a1, side_a0, [(mine, "seq", FAR)]
    )
    line_b2, side_b1, core_b1, cross_b0 = onward(line_b1, side_b0)
    keep, give = jnp.where(inside, mine, across), jnp.where(inside, across, mine)
    line_a3, side_a2, core_a2, cross_a1, got = onward(
        line_a2, side_a1, [(give, "head", SWAP)]
    )
    line_b3, side_b2, core_b2, cross_b1 = onward(line_b2, side_b1)
    blocks = jnp.concatenate([keep, got], axis=1)[None]
    side_a3, core_a3, cross_a2, beside = hop(
        [
            (line_a3, "seq", SIDE),
            (line_a3, "seq", CORE),
            (side_a2, "seq", CORE),
            (blocks, "seq", NEXT),
        ]
    )
    side_b3, core_b3, cross_b2 = hop(
        [(side_b0, "seq", LINE_DOWN), (line_b3, "seq", CORE), (side_b2, "seq", CORE)]
    )
    early_a = [own_a, line_a1, side_a0, core_a0, line_a2, side_a1, core_a1, cross_a0]
    early_b = [own_b, line_b1, side_b0, core_b0, line_b2, side_b1, core_b1, cross_b0]
    early_a += [line_a3, side_a2, core_a2, cross_a1]
    early_b += [line_b3, side_b2, core_b2, cross_b1]
    done = project(list(zip(early_a, early_b)))
    side_a3, side_b3, *done = tie((side_a3, side_b3, *done))
    cross_a3, cross_b3 = hop([(side_a3, "seq", CORE), (side_b3, "seq", CORE)])
    late = [(side_a3, side_b3), (core_a3, core_b3), (cross_a2, cross_b2), (cross_a3, cross_b3)]
    blocks = jnp.concatenate([blocks, beside], axis=0)
    return done, late, blocks


def on_device(tokens, qkv_weight, out_weight, centroids, clusters, slots):
    heads, tiles = clusters.shape
    clus_here, head_dim = centroids.shape[1:]
    n_seq, n_head = lax.axis_size("seq"), lax.axis_size("head")
    me, group = lax.axis_index("seq"), lax.axis_index("head")
    paired = n_seq == 16 and n_head == 2

    me_here = me[None].astype(jnp.int32)

    if paired:
        (acc, rest, marks), late, weight_blocks = gather_weights(
            qkv_weight,
            clusters,
            out_weight,
            me,
            group,
            lambda early: project_early(tokens, me_here, early, 4, paired),
        )
    else:
        full = lax.all_gather(qkv_weight, "seq", axis=0, tiled=True)
        depth, half = full.shape[0] // 16, full.shape[1] // 2
        blocks = [
            (full[i * depth : (i + 1) * depth, :half], full[i * depth : (i + 1) * depth, half:])
            for i in range(16)
        ]
        late = blocks[12:]
        acc, rest, _ = project_early(tokens, me_here, blocks[:12], 4, paired)
        marks = lax.all_gather(clusters, "seq", axis=1, tiled=True).astype(jnp.float32)

    qkv, outgoing, table = project_late(
        me_here, clusters, clus_here, acc, rest, marks, late, n_seq, paired
    )
    incoming = lax.all_to_all(outgoing, "seq", split_axis=0, concat_axis=0, tiled=True)
    sums, mass = inner_attention(qkv, heads, tiles)
    if paired:
        weight_blocks = jnp.concatenate(
            [weight_blocks, lax.ppermute(weight_blocks, "seq", SIDE)], axis=0
        )
    incoming, sums, mass = tie((incoming, sums, mass))
    returning, new_rows = owner_attention(
        incoming, centroids.reshape(heads * clus_here, head_dim), table, heads
    )
    if paired:
        returning, weight_blocks = tie((returning, weight_blocks))
    back = lax.all_to_all(returning, "seq", split_axis=0, concat_axis=0, tiled=True)
    attention = merge_attention(sums, mass, back, clusters, clus_here, table)

    if paired:
        weight_blocks = jnp.concatenate(
            [weight_blocks, lax.ppermute(weight_blocks, "seq", CORE)], axis=0
        )
        parts = [attention, lax.ppermute(attention, "head", SWAP)]
    else:
        rows = lax.all_gather(out_weight, "seq", axis=1, tiled=True)
        rows = lax.all_gather(rows, "head", axis=0, tiled=True)
        features = rows.shape[1] // n_head
        mine = lax.dynamic_slice_in_dim(rows, group * features, features, axis=1).T
        weight_blocks = mine.reshape(-1, min(256, features), mine.shape[1])
        parts = [lax.all_gather(attention, "head", axis=0, tiled=True)]
    summed = output_projection(weight_blocks, me_here, parts, paired)
    return (summed, new_rows.reshape(centroids.shape))


def solution(mesh):
    placed = (
        P("seq", None),
        P("seq", "head"),
        P("head", "seq"),
        P("head", "seq", None),
        P("head", "seq"),
        P("head", "seq"),
    )
    return jax.shard_map(
        on_device,
        mesh=mesh,
        in_specs=placed,
        out_specs=(P("head", "seq"), P("head", "seq", None)),
        check_vma=False,
    )
```

time: 187 us -> 163 us (0.87)
  local copies, waits for them, and re-layouts: 23.5 us -> 2.7 us
  waiting for transfers between devices: 78.9 us -> 69.5 us
  Pallas kernels: 36.2 us -> 42.7 us
  other arithmetic: 6 us -> 3.91 us
    unnamed x59 -> x20, local copies, waits for them, and re-layouts: 21.7 us -> 1.7 us
    ppermute x40 -> x36, waiting for transfers between devices: 71.6 us -> 54.3 us  [the longest x33 28.4 us: hop(): lax.ppermute(value, axis, pairs)]
    all_to_all x1, waiting for transfers between devices: 7.26 us -> 15.1 us  [on_device(): lax.all_to_all(returning, 'seq', split_axis=0, concat_axis=0, tiled=True)]
    pallas_call x6, Pallas kernels: 30.1 us -> 35.1 us  [the longest x1 11.5 us: project_early(): pl.pallas_call(functools.partial(early_kernel, n_early, n_late, paired),...]
    all_to_all x1, starting transfers between devices: 4.42 us -> 6.36 us  [on_device(): lax.all_to_all(outgoing, 'seq', split_axis=0, concat_axis=0, tiled=True)]
    concatenate x6 -> x3, other arithmetic: 4.59 us -> 2.9 us  [the longest x1 2.75 us: on_device(): jnp.concatenate([weight_blocks, lax.ppermute(weight_blocks, 'seq', CORE)]...]
    ppermute x40 -> x36, starting transfers between devices: 32.7 us -> 31.4 us  [the longest x33 27.5 us: hop(): lax.ppermute(value, axis, pairs)]
  transfers between devices with their start and end apart: 42 -> 38, of which waited for: 15 -> 11; matrix products, arithmetic and copies ran while one was open for 4% -> 3% of each run, Pallas kernels for 14% -> 14%
where the time goes in v2:
time: 163 us; the launch traced here: 162 us
  waiting for transfers between devices  69.5 us (43%)
  Pallas kernels  42.7 us (26%)
  starting transfers between devices  42.4 us (26%)
  other arithmetic  3.91 us (2%)
  local copies, waits for them, and re-layouts  2.7 us (2%)
    ppermute x33, waiting for transfers between devices, hop(): lax.ppermute(value, axis, pairs)  28.4 us
    ppermute x33, starting transfers between devices, hop(): lax.ppermute(value, axis, pairs)  27.5 us
    ppermute x1, waiting for transfers between devices, on_device(): lax.ppermute(weight_blocks, 'seq', SIDE)  16.4 us
    all_to_all x1, waiting for transfers between devices, on_device(): lax.all_to_all(returning, 'seq', split_axis=0, concat_axis=0, tiled=True)  15.1 us
    pallas_call x1, Pallas kernels, project_early(): pl.pallas_call(functools.partial(early_kernel, n_early, n_late, paired),...  11.5 us
    ppermute x1, waiting for transfers between devices, on_device(): parts = [attention, lax.ppermute(attention, 'head', SWAP)]  9.6 us
    pallas_call x1, Pallas kernels, output_projection(): pl.pallas_call(output_kernel, out_shape=jax.ShapeDtypeStruct((n * feature...  7.6 us
    pallas_call x1, Pallas kernels, project_late(): pl.pallas_call(functools.partial(late_kernel, n_late, heads, tiles, tile_...  7.18 us
  transfers between devices with their start and end apart: 38, of which 11 were waited for; matrix products, arithmetic and copies ran while one was open for 3% of the time, Pallas kernels for 14%

profile of v2, /device:TPU:0, one launch (start us, length us, event | category | flops | bytes accessed | tf_op | source)
XLA Modules:
  0.0 162.1 jit_solution(8072126163859834918)
XLA Ops:
  0.6 1.0 copy-done
  1.6 0.7 copy-done.2
  2.3 0.6 split_weight.1
  2.9 3.1 %collective-permute-start.17 = (bf16[256,384]{1,0:T(8,128)(2,1)S(1)}, bf16[256,384]{1,0:T(8,128)(2,1)S(1)}, u32[]{:S(2)}, u32[]{:S(2)}) collective-permute-start(bf16[256,384]{1,0:T(8,128)(2,1)S(1)} %get-tuple-element.71.refs_1_), channel_id=1, source_target_pairs={{0,4},{1,5},{2,6},{3,7},{4,8},{5,9},{6,10},{7,11},{8,12},{9,13},{1... | collective-permute-start | bytes 589832 | tf_op jit(solution)/shard_map/ppermute | solution.py:498
  6.0 1.5 collective-permute-start.18
  7.5 1.6 collective-permute-start
  9.1 0.5 collective-permute-start.1
  9.6 3.8 %collective-permute-done.17.refs_3_ = bf16[256,384]{1,0:T(8,128)(2,1)S(1)} collective-permute-done((bf16[256,384]{1,0:T(8,128)(2,1)S(1)}, bf16[256,384]{1,0:T(8,128)(2,1)S(1)}, u32[]{:S(2)}, u32[]{:S(2)}) %collective-permute-start.17) | collective-permute-done | bytes 196640 | tf_op jit(solution)/shard_map/ppermute | solution.py:498
  13.4 1.0 collective-permute-start.21
  14.4 2.5 %collective-permute-start.22 = (bf16[256,384]{1,0:T(8,128)(2,1)S(1)}, bf16[256,384]{1,0:T(8,128)(2,1)S(1)}, u32[]{:S(2)}, u32[]{:S(2)}) collective-permute-start(bf16[256,384]{1,0:T(8,128)(2,1)S(1)} %collective-permute-done.17.refs_3_), channel_id=1, source_target_pairs={{0,2},{1,3},{2,0},{3,1},{4,6},{5,7},{6,4},{7,5},{8,10},{9,11},{10,... | collective-permute-start | bytes 589832 | tf_op jit(solution)/shard_map/ppermute | solution.py:498
  16.8 0.5 collective-permute-done.refs_2_
  17.4 0.5 collective-permute-start.24
  17.9 1.1 collective-permute-start.3
  19.0 3.5 %collective-permute-done.21.refs_9_ = bf16[256,384]{1,0:T(8,128)(2,1)S(1)} collective-permute-done((bf16[256,384]{1,0:T(8,128)(2,1)S(1)}, bf16[256,384]{1,0:T(8,128)(2,1)S(1)}, u32[]{:S(2)}, u32[]{:S(2)}) %collective-permute-start.21) | collective-permute-done | bytes 196640 | tf_op jit(solution)/shard_map/ppermute | solution.py:498
  22.5 2.6 %collective-permute-start.4 = (bf16[272,384]{1,0:T(8,128)(2,1)S(1)}, bf16[272,384]{1,0:T(8,128)(2,1)S(1)}, u32[]{:S(2)}, u32[]{:S(2)}) collective-permute-start(bf16[272,384]{1,0:T(8,128)(2,1)S(1)} %collective-permute-done.refs_2_), channel_id=1, source_target_pairs={{0,2},{1,3},{2,0},{3,1},{4,6},{5,7},{6,4},{7,5},{8,10},{9,11},{10,... | collective-permute-start | bytes 626696 | tf_op jit(solution)/shard_map/ppermute | solution.py:498
  25.1 1.0 copy.7
  26.3 0.5 collective-permute-start.6
  26.8 5.8 %collective-permute-done.7 = bf16[256,256]{1,0:T(8,128)(2,1)S(1)} collective-permute-done((bf16[256,256]{1,0:T(8,128)(2,1)S(1)}, bf16[256,256]{1,0:T(8,128)(2,1)S(1)}, u32[]{:S(2)}, u32[]{:S(2)}) %collective-permute-start.7) | collective-permute-done | bytes 131104 | tf_op jit(solution)/shard_map/ppermute | solution.py:498
  32.6 2.2 %collective-permute-start.26 = (bf16[256,384]{1,0:T(8,128)(2,1)S(1)}, bf16[256,384]{1,0:T(8,128)(2,1)}, u32[]{:S(2)}, u32[]{:S(2)}) collective-permute-start(bf16[256,384]{1,0:T(8,128)(2,1)S(1)} %collective-permute-done.21.refs_9_), channel_id=1, source_target_pairs={{0,2},{1,3},{2,0},{3,1},{4,6},{5,7},{6,4},{7,5},{8,10},{9,11},{10,... | collective-permute-start | bytes 589832 | tf_op jit(solution)/shard_map/ppermute | solution.py:498
  34.8 0.5 collective-permute-start.28
  35.3 0.1 collective-permute-start.10
  35.4 4.9 %collective-permute-done.25.refs_17_ = bf16[256,384]{1,0:T(8,128)(2,1)S(1)} collective-permute-done((bf16[256,384]{1,0:T(8,128)(2,1)S(1)}, bf16[256,384]{1,0:T(8,128)(2,1)S(1)}, u32[]{:S(2)}, u32[]{:S(2)}) %collective-permute-start.25) | collective-permute-done | bytes 196640 | tf_op jit(solution)/shard_map/ppermute | solution.py:498
  40.3 3.0 %collective-permute-start.9 = (bf16[272,384]{1,0:T(8,128)(2,1)S(1)}, bf16[272,384]{1,0:T(8,128)(2,1)S(1)}, u32[]{:S(2)}, u32[]{:S(2)}) collective-permute-start(bf16[272,384]{1,0:T(8,128)(2,1)S(1)} %collective-permute-done.3.refs_8_), channel_id=1, source_target_pairs={{0,2},{1,3},{2,0},{3,1},{4,6},{5,7},{6,4},{7,5},{8,10},{9,11},{10,... | collective-permute-start | bytes 626696 | tf_op jit(solution)/shard_map/ppermute | solution.py:498
  43.4 1.0 broadcast_select_fusion
  44.4 1.6 collective-permute-start.12
  45.9 4.4 %collective-permute-done.12 = bf16[256,256]{1,0:T(8,128)(2,1)S(1)} collective-permute-done((bf16[256,256]{1,0:T(8,128)(2,1)S(1)}, bf16[256,256]{1,0:T(8,128)(2,1)S(1)}, u32[]{:S(2)}, u32[]{:S(2)}) %collective-permute-start.12) | collective-permute-done | bytes 131104 | tf_op jit(solution)/shard_map/ppermute | solution.py:498
  50.3 3.8 %collective-permute-start.20 = (bf16[256,384]{1,0:T(8,128)(2,1)S(1)}, bf16[256,384]{1,0:T(8,128)(2,1)S(1)}, u32[]{:S(2)}, u32[]{:S(2)}) collective-permute-start(bf16[256,384]{1,0:T(8,128)(2,1)S(1)} %collective-permute-done.18.refs_5_), channel_id=1, source_target_pairs={{0,12},{1,13},{2,14},{3,15},{4,0},{5,1},{6,2},{7,3},{8,4},{9,5},{1... | collective-permute-start | bytes 589832 | tf_op jit(solution)/shard_map/ppermute | solution.py:498
  54.2 0.5 collective-permute-start.30
  54.8 0.1 collective-permute-start.14
  54.9 4.0 %collective-permute-done.20.refs_1_ = bf16[256,384]{1,0:T(8,128)(2,1)S(1)} collective-permute-done((bf16[256,384]{1,0:T(8,128)(2,1)S(1)}, bf16[256,384]{1,0:T(8,128)(2,1)S(1)}, u32[]{:S(2)}, u32[]{:S(2)}) %collective-permute-start.20) | collective-permute-done | bytes 196640 | tf_op jit(solution)/shard_map/ppermute | solution.py:498
  58.9 11.5 %project_early.1 = (f32[1024,768]{1,0:T(8,128)}, bf16[1024,1024]{1,0:T(8,128)(2,1)}, f32[16,128]{1,0:T(8,128)}) custom-call(s32[1]{0:T(128)} %bitcast.me_ref, bf16[1024,4096]{1,0:T(8,128)(2,1)} %x_ref.1, bf16[272,384]{1,0:T(8,128)(2,1)S(1)} %get-tuple-element.59.refs_0_, bf16[256,384]{1,0:T(8,128)(2,1)S(1)} %get-tuple-element.71.refs_1_, ...), custom_call_target="tpu_custom_call" | custom-call | flops 4831838208 | bytes 11534336 | tf_op jit(solution)/shard_map/project_early/pallas_call | solution.py:142
  70.5 0.5 collective-permute-start.31
  71.1 1.4 collective-permute-done.32.refs_7_
  72.5 7.2 %project_late.1 = (bf16[1024,768]{1,0:T(8,128)(2,1)}, bf16[16,128,256]{2,1,0:T(8,128)(2,1)}, s32[64,128]{1,0:T(8,128)}) custom-call(s32[1]{0:T(128)} %bitcast.me_ref, s32[2,8]{1,0:T(2,128)S(1)} %copy-done.3, f32[1024,768]{1,0:T(8,128)} %get-tuple-element.92.acc_ref, bf16[1024,1024]{1,0:T(8,128)(2,1)} %get-tuple-element.93.rest_ref, ...), custom_call_target="tpu_custom_call" | custom-call | flops 1610612736 | bytes 7077888 | tf_op jit(solution)/shard_map/project_late/pallas_call | solution.py:261
  79.7 6.4 %all-to-all-start = ((bf16[16,128,256]{2,1,0:T(8,128)(2,1)}), bf16[16,128,256]{2,1,0:T(8,128)(2,1)S(1)}, u32[]{:S(2)}, u32[]{:S(2)}) async-start(bf16[16,128,256]{2,1,0:T(8,128)(2,1)} %get-tuple-element.104), calls=%async_computation | async-start | bytes 2097152 | tf_op jit(solution)/shard_map/all_to_all | solution.py:576
  86.1 2.0 %collective-permute-start.33 = (bf16[2,256,512]{2,1,0:T(8,128)(2,1)S(1)}, bf16[2,256,512]{2,1,0:T(8,128)(2,1)S(1)}, u32[]{:S(2)}, u32[]{:S(2)}) collective-permute-start(bf16[2,256,512]{2,1,0:T(8,128)(2,1)S(1)} %pad_maximum_fusion.2), channel_id=1, source_target_pairs={{0,2},{1,3},{2,0},{3,1},{4,6},{5,7},{6,4},{7,5},{8,10},{9,11},{10,... | collective-permute-start | bytes 1572872 | tf_op jit(solution)/shard_map/ppermute | solution.py:580
  88.1 7.1 %inner_attention.1 = (f32[256,1024]{1,0:T(8,128)}, f32[16,1024]{1,0:T(8,128)}) custom-call(bf16[1024,768]{1,0:T(8,128)(2,1)} %get-tuple-element.105.qkv_ref), custom_call_target="tpu_custom_call" | custom-call | flops 201326592 | bytes 3932160 | tf_op jit(solution)/shard_map/inner_attention/pallas_call | solution.py:314
  95.3 16.4 %collective-permute-done.33 = bf16[2,256,512]{2,1,0:T(8,128)(2,1)S(1)} collective-permute-done((bf16[2,256,512]{2,1,0:T(8,128)(2,1)S(1)}, bf16[2,256,512]{2,1,0:T(8,128)(2,1)S(1)}, u32[]{:S(2)}, u32[]{:S(2)}) %collective-permute-start.33) | collective-permute-done | bytes 524320 | tf_op jit(solution)/shard_map/ppermute | solution.py:580
  111.7 0.1 pad_maximum_fusion.1
  111.8 4.4 %owner_attention.1 = (bf16[16,144,128]{2,1,0:T(8,128)(2,1)}, f32[8,128]{1,0:T(8,128)}) custom-call(s32[64,128]{1,0:T(8,128)S(1)} %copy-done.1, bf16[16,128,256]{2,1,0:T(8,128)(2,1)S(1)} %all-to-all-done.in_ref, f32[8,128]{1,0:T(8,128)} %bitcast.9), custom_call_target="tpu_custom_call" | custom-call | flops 134217728 | bytes 2097152 | tf_op jit(solution)/shard_map/owner_attention/pallas_call | solution.py:374
  116.2 4.6 %all-to-all-start.1 = ((bf16[16,144,128]{2,1,0:T(8,128)(2,1)}), bf16[16,144,128]{2,1,0:T(8,128)(2,1)S(1)}, u32[]{:S(2)}, u32[]{:S(2)}) async-start(bf16[16,144,128]{2,1,0:T(8,128)(2,1)} %get-tuple-element.114), calls=%async_computation.1 | async-start | bytes 1179648 | tf_op jit(solution)/shard_map/all_to_all | solution.py:588
  120.9 0.4 collective-permute-start.34
  121.3 15.1 %all-to-all-done.1.back_ref = bf16[16,144,128]{2,1,0:T(8,128)(2,1)S(1)} async-done(((bf16[16,144,128]{2,1,0:T(8,128)(2,1)}), bf16[16,144,128]{2,1,0:T(8,128)(2,1)S(1)}, u32[]{:S(2)}, u32[]{:S(2)}) %all-to-all-start.1) | async-done | bytes 589856 | tf_op jit(solution)/shard_map/all_to_all | solution.py:588
  136.4 4.2 %merge_attention.1.refs_0_ = bf16[256,1024]{1,0:T(8,128)(2,1)S(1)} custom-call(s32[2,8]{1,0:T(2,128)S(1)} %copy-done.3, s32[64,128]{1,0:T(8,128)S(1)} %copy-done.1, f32[256,1024]{1,0:T(8,128)} %get-tuple-element.112.sums_ref, f32[16,1024]{1,0:T(8,128)} %get-tuple-element.113.mass_ref, bf16[16,144,128]{2,1,0:T(8,128)(2,1)S(1)} %all-to-all-done.1.back_ref), custom_call_target="tpu_custom_call" | custom-call | flops 2097152 | bytes 3145728 | tf_op jit(solution)/shard_map/merge_attention/pallas_call | solution.py:420
  140.6 1.6 collective-permute-start.35
  142.2 2.7 %pad_maximum_fusion.weight_ref = bf16[8,256,512]{2,1,0:T(8,128)(2,1)} fusion(bf16[4,256,512]{2,1,0:T(8,128)(2,1)} %collective-permute-done.34, bf16[4,256,512]{2,1,0:T(8,128)(2,1)S(1)} %pad_maximum_fusion.1), kind=kLoop, calls=%fused_computation | loop fusion | flops 1048576 | bytes 4194304 | tf_op jit(solution)/shard_map/concatenate | solution.py:592
  144.9 9.6 %collective-permute-done.35.refs_1_ = bf16[256,1024]{1,0:T(8,128)(2,1)S(1)} collective-permute-done((bf16[256,1024]{1,0:T(8,128)(2,1)S(1)}, bf16[256,1024]{1,0:T(8,128)(2,1)S(1)}, u32[]{:S(2)}, u32[]{:S(2)}) %collective-permute-start.35) | collective-permute-done | bytes 524320 | tf_op jit(solution)/shard_map/ppermute | solution.py:595
  154.5 7.6 %output_projection.1 = bf16[2048,1024]{1,0:T(8,128)(2,1)} custom-call(s32[1]{0:T(128)} %bitcast.me_ref, bf16[8,256,512]{2,1,0:T(8,128)(2,1)} %pad_maximum_fusion.weight_ref, bf16[256,1024]{1,0:T(8,128)(2,1)S(1)} %merge_attention.1.refs_0_, bf16[256,1024]{1,0:T(8,128)(2,1)S(1)} %collective-permute-done.35.refs_1_), custom_call_target="tpu_custom_call" | custom-call | flops 2147483648 | bytes 6291456 | tf_op jit(solution)/shard_map/output_projection/pallas_call | solution.py:458
  (61 shorter events, 0.5 us)
Async XLA Ops:
  0.6 1.0 copy-start
  1.6 0.7 copy-start.2
  2.9 10.4 %collective-permute-start.17 = (bf16[256,384]{1,0:T(8,128)(2,1)S(1)}, bf16[256,384]{1,0:T(8,128)(2,1)S(1)}, u32[]{:S(2)}, u32[]{:S(2)}) collective-permute-start(bf16[256,384]{1,0:T(8,128)(2,1)S(1)} %get-tuple-element.71.refs_1_), channel_id=1, source_target_pairs={{0,4},{1,5},{2,6},{3,7},{4,8},{5,9},{6,10},{7,11},{8,12},{9,13},{1... | collective-permute-start | bytes 589832 | tf_op jit(solution)/shard_map/ppermute | solution.py:498
  6.0 7.4 %collective-permute-start.18 = (bf16[256,384]{1,0:T(8,128)(2,1)S(1)}, bf16[256,384]{1,0:T(8,128)(2,1)S(1)}, u32[]{:S(2)}, u32[]{:S(2)}) collective-permute-start(bf16[256,384]{1,0:T(8,128)(2,1)S(1)} %get-tuple-element.71.refs_1_), channel_id=1, source_target_pairs={{0,2},{1,3},{2,0},{3,1},{4,6},{5,7},{6,4},{7,5},{8,10},{9,11},{10,... | collective-permute-start | bytes 589832 | tf_op jit(solution)/shard_map/ppermute | solution.py:498
  7.5 5.8 %collective-permute-start.19 = (bf16[256,384]{1,0:T(8,128)(2,1)S(1)}, bf16[256,384]{1,0:T(8,128)(2,1)S(1)}, u32[]{:S(2)}, u32[]{:S(2)}) collective-permute-start(bf16[256,384]{1,0:T(8,128)(2,1)S(1)} %get-tuple-element.71.refs_1_), channel_id=1, source_target_pairs={{0,1},{1,0},{2,3},{3,2},{4,5},{5,4},{6,7},{7,6},{8,9},{9,8},{10,11... | collective-permute-start | bytes 589832 | tf_op jit(solution)/shard_map/ppermute | solution.py:498
  7.5 9.9 %collective-permute-start = (bf16[272,384]{1,0:T(8,128)(2,1)S(1)}, bf16[272,384]{1,0:T(8,128)(2,1)S(1)}, u32[]{:S(2)}, u32[]{:S(2)}) collective-permute-start(bf16[272,384]{1,0:T(8,128)(2,1)S(1)} %get-tuple-element.59.refs_0_), channel_id=1, source_target_pairs={{0,4},{1,5},{2,6},{3,7},{4,8},{5,9},{6,10},{7,11},{8,12},{9,13},{1... | collective-permute-start | bytes 626696 | tf_op jit(solution)/shard_map/ppermute | solution.py:498
  9.1 8.3 %collective-permute-start.1 = (bf16[272,384]{1,0:T(8,128)(2,1)S(1)}, bf16[272,384]{1,0:T(8,128)(2,1)S(1)}, u32[]{:S(2)}, u32[]{:S(2)}) collective-permute-start(bf16[272,384]{1,0:T(8,128)(2,1)S(1)} %get-tuple-element.59.refs_0_), channel_id=1, source_target_pairs={{0,2},{1,3},{2,0},{3,1},{4,6},{5,7},{6,4},{7,5},{8,10},{9,11},{10,... | collective-permute-start | bytes 626696 | tf_op jit(solution)/shard_map/ppermute | solution.py:498
  13.3 4.6 %collective-permute-start.2 = (bf16[272,384]{1,0:T(8,128)(2,1)S(1)}, bf16[272,384]{1,0:T(8,128)(2,1)S(1)}, u32[]{:S(2)}, u32[]{:S(2)}) collective-permute-start(bf16[272,384]{1,0:T(8,128)(2,1)S(1)} %get-tuple-element.59.refs_0_), channel_id=1, source_target_pairs={{0,1},{1,0},{2,3},{3,2},{4,5},{5,4},{6,7},{7,6},{8,9},{9,8},{10,11... | collective-permute-start | bytes 626696 | tf_op jit(solution)/shard_map/ppermute | solution.py:498
  13.4 9.2 %collective-permute-start.21 = (bf16[256,384]{1,0:T(8,128)(2,1)S(1)}, bf16[256,384]{1,0:T(8,128)(2,1)S(1)}, u32[]{:S(2)}, u32[]{:S(2)}) collective-permute-start(bf16[256,384]{1,0:T(8,128)(2,1)S(1)} %collective-permute-done.17.refs_3_), channel_id=1, source_target_pairs={{0,4},{1,5},{2,6},{3,7},{4,8},{5,9},{6,10},{7,11},{8,12},{9,13},{1... | collective-permute-start | bytes 589832 | tf_op jit(solution)/shard_map/ppermute | solution.py:498
  14.4 11.7 %collective-permute-start.22 = (bf16[256,384]{1,0:T(8,128)(2,1)S(1)}, bf16[256,384]{1,0:T(8,128)(2,1)S(1)}, u32[]{:S(2)}, u32[]{:S(2)}) collective-permute-start(bf16[256,384]{1,0:T(8,128)(2,1)S(1)} %collective-permute-done.17.refs_3_), channel_id=1, source_target_pairs={{0,2},{1,3},{2,0},{3,1},{4,6},{5,7},{6,4},{7,5},{8,10},{9,11},{10,... | collective-permute-start | bytes 589832 | tf_op jit(solution)/shard_map/ppermute | solution.py:498
  17.4 8.8 %collective-permute-start.23 = (bf16[256,384]{1,0:T(8,128)(2,1)S(1)}, bf16[256,384]{1,0:T(8,128)(2,1)S(1)}, u32[]{:S(2)}, u32[]{:S(2)}) collective-permute-start(bf16[256,384]{1,0:T(8,128)(2,1)S(1)} %collective-permute-done.17.refs_3_), channel_id=1, source_target_pairs={{0,1},{1,0},{2,3},{3,2},{4,5},{5,4},{6,7},{7,6},{8,9},{9,8},{10,11... | collective-permute-start | bytes 589832 | tf_op jit(solution)/shard_map/ppermute | solution.py:498
  17.4 8.9 %collective-permute-start.24 = (bf16[256,384]{1,0:T(8,128)(2,1)S(1)}, bf16[256,384]{1,0:T(8,128)(2,1)S(1)}, u32[]{:S(2)}, u32[]{:S(2)}) collective-permute-start(bf16[256,384]{1,0:T(8,128)(2,1)S(1)} %collective-permute-done.18.refs_5_), channel_id=1, source_target_pairs={{0,1},{1,0},{2,3},{3,2},{4,5},{5,4},{6,7},{7,6},{8,9},{9,8},{10,11... | collective-permute-start | bytes 589832 | tf_op jit(solution)/shard_map/ppermute | solution.py:498
  17.9 14.7 %collective-permute-start.3 = (bf16[272,384]{1,0:T(8,128)(2,1)S(1)}, bf16[272,384]{1,0:T(8,128)(2,1)S(1)}, u32[]{:S(2)}, u32[]{:S(2)}) collective-permute-start(bf16[272,384]{1,0:T(8,128)(2,1)S(1)} %collective-permute-done.refs_2_), channel_id=1, source_target_pairs={{0,4},{1,5},{2,6},{3,7},{4,8},{5,9},{6,10},{7,11},{8,12},{9,13},{1... | collective-permute-start | bytes 626696 | tf_op jit(solution)/shard_map/ppermute | solution.py:498
  22.5 12.3 %collective-permute-start.4 = (bf16[272,384]{1,0:T(8,128)(2,1)S(1)}, bf16[272,384]{1,0:T(8,128)(2,1)S(1)}, u32[]{:S(2)}, u32[]{:S(2)}) collective-permute-start(bf16[272,384]{1,0:T(8,128)(2,1)S(1)} %collective-permute-done.refs_2_), channel_id=1, source_target_pairs={{0,2},{1,3},{2,0},{3,1},{4,6},{5,7},{6,4},{7,5},{8,10},{9,11},{10,... | collective-permute-start | bytes 626696 | tf_op jit(solution)/shard_map/ppermute | solution.py:498
  26.1 0.7 copy-start.8
  26.1 6.5 %collective-permute-start.7 = (bf16[256,256]{1,0:T(8,128)(2,1)S(1)}, bf16[256,256]{1,0:T(8,128)(2,1)S(1)}, u32[]{:S(2)}, u32[]{:S(2)}) collective-permute-start(bf16[256,256]{1,0:T(8,128)(2,1)S(1)} %bitcast.8), channel_id=1, source_target_pairs={{0,8},{1,9},{2,10},{3,11},{4,12},{5,13},{6,14},{7,15},{8,0},{9,1},... | collective-permute-start | bytes 393224 | tf_op jit(solution)/shard_map/ppermute | solution.py:498
  26.2 8.6 %collective-permute-start.5 = (bf16[272,384]{1,0:T(8,128)(2,1)S(1)}, bf16[272,384]{1,0:T(8,128)(2,1)S(1)}, u32[]{:S(2)}, u32[]{:S(2)}) collective-permute-start(bf16[272,384]{1,0:T(8,128)(2,1)S(1)} %collective-permute-done.refs_2_), channel_id=1, source_target_pairs={{0,1},{1,0},{2,3},{3,2},{4,5},{5,4},{6,7},{7,6},{8,9},{9,8},{10,11... | collective-permute-start | bytes 626696 | tf_op jit(solution)/shard_map/ppermute | solution.py:498
  26.3 9.0 %collective-permute-start.6 = (bf16[272,384]{1,0:T(8,128)(2,1)S(1)}, bf16[272,384]{1,0:T(8,128)(2,1)S(1)}, u32[]{:S(2)}, u32[]{:S(2)}) collective-permute-start(bf16[272,384]{1,0:T(8,128)(2,1)S(1)} %collective-permute-done.1.refs_4_), channel_id=1, source_target_pairs={{0,1},{1,0},{2,3},{3,2},{4,5},{5,4},{6,7},{7,6},{8,9},{9,8},{10,11... | collective-permute-start | bytes 626696 | tf_op jit(solution)/shard_map/ppermute | solution.py:498
  32.6 2.2 %copy-start.9 = (bf16[256,256]{1,0:T(8,128)(2,1)}, bf16[256,256]{1,0:T(8,128)(2,1)S(1)}, u32[]{:S(2)}) copy-start(bf16[256,256]{1,0:T(8,128)(2,1)S(1)} %collective-permute-done.7) | copy-start | bytes 393220
  32.6 7.8 %collective-permute-start.25 = (bf16[256,384]{1,0:T(8,128)(2,1)S(1)}, bf16[256,384]{1,0:T(8,128)(2,1)S(1)}, u32[]{:S(2)}, u32[]{:S(2)}) collective-permute-start(bf16[256,384]{1,0:T(8,128)(2,1)S(1)} %collective-permute-done.21.refs_9_), channel_id=1, source_target_pairs={{0,4},{1,5},{2,6},{3,7},{4,8},{5,9},{6,10},{7,11},{8,12},{9,13},{1... | collective-permute-start | bytes 589832 | tf_op jit(solution)/shard_map/ppermute | solution.py:498
  32.6 7.8 %collective-permute-start.26 = (bf16[256,384]{1,0:T(8,128)(2,1)S(1)}, bf16[256,384]{1,0:T(8,128)(2,1)}, u32[]{:S(2)}, u32[]{:S(2)}) collective-permute-start(bf16[256,384]{1,0:T(8,128)(2,1)S(1)} %collective-permute-done.21.refs_9_), channel_id=1, source_target_pairs={{0,2},{1,3},{2,0},{3,1},{4,6},{5,7},{6,4},{7,5},{8,10},{9,11},{10,... | collective-permute-start | bytes 589832 | tf_op jit(solution)/shard_map/ppermute | solution.py:498
  34.8 8.6 %collective-permute-start.27 = (bf16[256,384]{1,0:T(8,128)(2,1)S(1)}, bf16[256,384]{1,0:T(8,128)(2,1)}, u32[]{:S(2)}, u32[]{:S(2)}) collective-permute-start(bf16[256,384]{1,0:T(8,128)(2,1)S(1)} %collective-permute-done.21.refs_9_), channel_id=1, source_target_pairs={{0,1},{1,0},{2,3},{3,2},{4,5},{5,4},{6,7},{7,6},{8,9},{9,8},{10,11... | collective-permute-start | bytes 589832 | tf_op jit(solution)/shard_map/ppermute | solution.py:498
  34.8 9.5 %collective-permute-start.28 = (bf16[256,384]{1,0:T(8,128)(2,1)S(1)}, bf16[256,384]{1,0:T(8,128)(2,1)S(1)}, u32[]{:S(2)}, u32[]{:S(2)}) collective-permute-start(bf16[256,384]{1,0:T(8,128)(2,1)S(1)} %collective-permute-done.22.refs_11_), channel_id=1, source_target_pairs={{0,1},{1,0},{2,3},{3,2},{4,5},{5,4},{6,7},{7,6},{8,9},{9,8},{10,11... | collective-permute-start | bytes 589832 | tf_op jit(solution)/shard_map/ppermute | solution.py:498
  35.3 18.8 %collective-permute-start.10 = (bf16[272,384]{1,0:T(8,128)(2,1)S(1)}, bf16[272,384]{1,0:T(8,128)(2,1)S(1)}, u32[]{:S(2)}, u32[]{:S(2)}) collective-permute-start(bf16[272,384]{1,0:T(8,128)(2,1)S(1)} %collective-permute-done.3.refs_8_), channel_id=1, source_target_pairs={{0,1},{1,0},{2,3},{3,2},{4,5},{5,4},{6,7},{7,6},{8,9},{9,8},{10,11... | collective-permute-start | bytes 626696 | tf_op jit(solution)/shard_map/ppermute | solution.py:498
  40.3 13.8 %collective-permute-start.8 = (bf16[272,384]{1,0:T(8,128)(2,1)S(1)}, bf16[272,384]{1,0:T(8,128)(2,1)S(1)}, u32[]{:S(2)}, u32[]{:S(2)}) collective-permute-start(bf16[272,384]{1,0:T(8,128)(2,1)S(1)} %collective-permute-done.3.refs_8_), channel_id=1, source_target_pairs={{0,4},{1,5},{2,6},{3,7},{4,8},{5,9},{6,10},{7,11},{8,12},{9,13},{1... | collective-permute-start | bytes 626696 | tf_op jit(solution)/shard_map/ppermute | solution.py:498
  40.3 14.3 %collective-permute-start.9 = (bf16[272,384]{1,0:T(8,128)(2,1)S(1)}, bf16[272,384]{1,0:T(8,128)(2,1)S(1)}, u32[]{:S(2)}, u32[]{:S(2)}) collective-permute-start(bf16[272,384]{1,0:T(8,128)(2,1)S(1)} %collective-permute-done.3.refs_8_), channel_id=1, source_target_pairs={{0,2},{1,3},{2,0},{3,1},{4,6},{5,7},{6,4},{7,5},{8,10},{9,11},{10,... | collective-permute-start | bytes 626696 | tf_op jit(solution)/shard_map/ppermute | solution.py:498
  43.4 11.3 %collective-permute-start.11 = (bf16[272,384]{1,0:T(8,128)(2,1)S(1)}, bf16[272,384]{1,0:T(8,128)(2,1)S(1)}, u32[]{:S(2)}, u32[]{:S(2)}) collective-permute-start(bf16[272,384]{1,0:T(8,128)(2,1)S(1)} %collective-permute-done.4.refs_10_), channel_id=1, source_target_pairs={{0,1},{1,0},{2,3},{3,2},{4,5},{5,4},{6,7},{7,6},{8,9},{9,8},{10,11... | collective-permute-start | bytes 626696 | tf_op jit(solution)/shard_map/ppermute | solution.py:498
  44.4 6.0 %collective-permute-start.12 = (bf16[256,256]{1,0:T(8,128)(2,1)S(1)}, bf16[256,256]{1,0:T(8,128)(2,1)S(1)}, u32[]{:S(2)}, u32[]{:S(2)}) collective-permute-start(bf16[256,256]{1,0:T(8,128)(2,1)S(1)} %get-tuple-element.117), channel_id=1, source_target_pairs={{0,16},{16,0},{1,17},{17,1},{2,18},{18,2},{3,19},{19,3},{4,20},{20... | collective-permute-start | bytes 393224 | tf_op jit(solution)/shard_map/ppermute | solution.py:498
  50.3 8.6 %collective-permute-start.20 = (bf16[256,384]{1,0:T(8,128)(2,1)S(1)}, bf16[256,384]{1,0:T(8,128)(2,1)S(1)}, u32[]{:S(2)}, u32[]{:S(2)}) collective-permute-start(bf16[256,384]{1,0:T(8,128)(2,1)S(1)} %collective-permute-done.18.refs_5_), channel_id=1, source_target_pairs={{0,12},{1,13},{2,14},{3,15},{4,0},{5,1},{6,2},{7,3},{8,4},{9,5},{1... | collective-permute-start | bytes 589832 | tf_op jit(solution)/shard_map/ppermute | solution.py:498
  54.2 4.8 %collective-permute-start.29 = (bf16[256,384]{1,0:T(8,128)(2,1)S(1)}, bf16[256,384]{1,0:T(8,128)(2,1)S(1)}, u32[]{:S(2)}, u32[]{:S(2)}) collective-permute-start(bf16[256,384]{1,0:T(8,128)(2,1)S(1)} %collective-permute-done.25.refs_17_), channel_id=1, source_target_pairs={{0,1},{1,0},{2,3},{3,2},{4,5},{5,4},{6,7},{7,6},{8,9},{9,8},{10,11... | collective-permute-start | bytes 589832 | tf_op jit(solution)/shard_map/ppermute | solution.py:498
  54.2 16.3 %collective-permute-start.30 = (bf16[256,384]{1,0:T(8,128)(2,1)}, bf16[256,384]{1,0:T(8,128)(2,1)S(1)}, u32[]{:S(2)}, u32[]{:S(2)}) collective-permute-start(bf16[256,384]{1,0:T(8,128)(2,1)} %collective-permute-done.26.refs_19_), channel_id=1, source_target_pairs={{0,1},{1,0},{2,3},{3,2},{4,5},{5,4},{6,7},{7,6},{8,9},{9,8},{10,11... | collective-permute-start | bytes 589832 | tf_op jit(solution)/shard_map/ppermute | solution.py:498
  54.7 15.8 %collective-permute-start.13 = (bf16[272,384]{1,0:T(8,128)(2,1)S(1)}, bf16[272,384]{1,0:T(8,128)(2,1)S(1)}, u32[]{:S(2)}, u32[]{:S(2)}) collective-permute-start(bf16[272,384]{1,0:T(8,128)(2,1)S(1)} %collective-permute-done.8.refs_16_), channel_id=1, source_target_pairs={{0,2},{1,3},{2,0},{3,1},{4,6},{5,7},{6,4},{7,5},{8,10},{9,11},{10,... | collective-permute-start | bytes 626696 | tf_op jit(solution)/shard_map/ppermute | solution.py:498
  54.8 15.7 %collective-permute-start.14 = (bf16[272,384]{1,0:T(8,128)(2,1)S(1)}, bf16[272,384]{1,0:T(8,128)(2,1)S(1)}, u32[]{:S(2)}, u32[]{:S(2)}) collective-permute-start(bf16[272,384]{1,0:T(8,128)(2,1)S(1)} %collective-permute-done.8.refs_16_), channel_id=1, source_target_pairs={{0,1},{1,0},{2,3},{3,2},{4,5},{5,4},{6,7},{7,6},{8,9},{9,8},{10,11... | collective-permute-start | bytes 626696 | tf_op jit(solution)/shard_map/ppermute | solution.py:498
  54.9 15.6 %copy-start.4 = (bf16[1,256,512]{2,1,0:T(8,128)(2,1)}, bf16[1,256,512]{2,1,0:T(8,128)(2,1)S(1)}, u32[]{:S(2)}) copy-start(bf16[1,256,512]{2,1,0:T(8,128)(2,1)S(1)} %maximum_bitcast_fusion) | copy-start | bytes 786436
  58.9 11.6 %collective-permute-start.16 = (bf16[1,256,512]{2,1,0:T(8,128)(2,1)S(1)}, bf16[1,256,512]{2,1,0:T(8,128)(2,1)S(1)}, u32[]{:S(2)}, u32[]{:S(2)}) collective-permute-start(bf16[1,256,512]{2,1,0:T(8,128)(2,1)S(1)} %maximum_bitcast_fusion), channel_id=1, source_target_pairs={{0,4},{1,5},{2,6},{3,7},{4,0},{5,1},{6,2},{7,3},{8,12},{9,13},{10,... | collective-permute-start | bytes 786440 | tf_op jit(solution)/shard_map/ppermute | solution.py:498
  58.9 11.6 %collective-permute-start.15 = (bf16[272,384]{1,0:T(8,128)(2,1)S(1)}, bf16[272,384]{1,0:T(8,128)(2,1)S(1)}, u32[]{:S(2)}, u32[]{:S(2)}) collective-permute-start(bf16[272,384]{1,0:T(8,128)(2,1)S(1)} %collective-permute-done.9.refs_18_), channel_id=1, source_target_pairs={{0,1},{1,0},{2,3},{3,2},{4,5},{5,4},{6,7},{7,6},{8,9},{9,8},{10,11... | collective-permute-start | bytes 626696 | tf_op jit(solution)/shard_map/ppermute | solution.py:498
  58.9 13.6 %copy-start.3 = (s32[2,8]{1,0:T(2,128)S(1)}, s32[2,8]{1,0:T(2,128)}, u32[]{:S(2)}) copy-start(s32[2,8]{1,0:T(2,128)} %cluster_ref.3) | copy-start | bytes 196
  70.5 9.2 %copy-start.6 = (bf16[1,256,512]{2,1,0:T(8,128)(2,1)}, bf16[1,256,512]{2,1,0:T(8,128)(2,1)S(1)}, u32[]{:S(2)}) copy-start(bf16[1,256,512]{2,1,0:T(8,128)(2,1)S(1)} %collective-permute-done.16) | copy-start | bytes 786436
  70.5 2.0 %collective-permute-start.31 = (bf16[272,384]{1,0:T(8,128)(2,1)S(1)}, bf16[272,384]{1,0:T(8,128)(2,1)S(1)}, u32[]{:S(2)}, u32[]{:S(2)}) collective-permute-start(bf16[272,384]{1,0:T(8,128)(2,1)S(1)} %collective-permute-done.13.refs_0_), channel_id=1, source_target_pairs={{0,1},{1,0},{2,3},{3,2},{4,5},{5,4},{6,7},{7,6},{8,9},{9,8},{10,11... | collective-permute-start | bytes 626696 | tf_op jit(solution)/shard_map/ppermute | solution.py:498
  71.0 1.4 collective-permute-start.32
  79.7 6.4 %copy-start.5 = (bf16[1,256,512]{2,1,0:T(8,128)(2,1)S(1)}, bf16[1,256,512]{2,1,0:T(8,128)(2,1)}, u32[]{:S(2)}) copy-start(bf16[1,256,512]{2,1,0:T(8,128)(2,1)} %copy-done.4) | copy-start | bytes 786436
  79.7 6.4 %copy-start.7 = (bf16[1,256,512]{2,1,0:T(8,128)(2,1)S(1)}, bf16[1,256,512]{2,1,0:T(8,128)(2,1)}, u32[]{:S(2)}) copy-start(bf16[1,256,512]{2,1,0:T(8,128)(2,1)} %copy-done.6) | copy-start | bytes 786436
  79.7 32.1 %all-to-all-start = ((bf16[16,128,256]{2,1,0:T(8,128)(2,1)}), bf16[16,128,256]{2,1,0:T(8,128)(2,1)S(1)}, u32[]{:S(2)}, u32[]{:S(2)}) async-start(bf16[16,128,256]{2,1,0:T(8,128)(2,1)} %get-tuple-element.104), calls=%async_computation | async-start | bytes 2097152 | tf_op jit(solution)/shard_map/all_to_all | solution.py:576
  86.1 25.6 %copy-start.1 = (s32[64,128]{1,0:T(8,128)S(1)}, s32[64,128]{1,0:T(8,128)}, u32[]{:S(2)}) copy-start(s32[64,128]{1,0:T(8,128)} %get-tuple-element.103.table_ref) | copy-start | bytes 98308
  86.1 25.5 %collective-permute-start.33 = (bf16[2,256,512]{2,1,0:T(8,128)(2,1)S(1)}, bf16[2,256,512]{2,1,0:T(8,128)(2,1)S(1)}, u32[]{:S(2)}, u32[]{:S(2)}) collective-permute-start(bf16[2,256,512]{2,1,0:T(8,128)(2,1)S(1)} %pad_maximum_fusion.2), channel_id=1, source_target_pairs={{0,2},{1,3},{2,0},{3,1},{4,6},{5,7},{6,4},{7,5},{8,10},{9,11},{10,... | collective-permute-start | bytes 1572872 | tf_op jit(solution)/shard_map/ppermute | solution.py:580
  116.2 20.2 %all-to-all-start.1 = ((bf16[16,144,128]{2,1,0:T(8,128)(2,1)}), bf16[16,144,128]{2,1,0:T(8,128)(2,1)S(1)}, u32[]{:S(2)}, u32[]{:S(2)}) async-start(bf16[16,144,128]{2,1,0:T(8,128)(2,1)} %get-tuple-element.114), calls=%async_computation.1 | async-start | bytes 1179648 | tf_op jit(solution)/shard_map/all_to_all | solution.py:588
  120.9 21.3 %collective-permute-start.34 = (bf16[4,256,512]{2,1,0:T(8,128)(2,1)S(1)}, bf16[4,256,512]{2,1,0:T(8,128)(2,1)}, u32[]{:S(2)}, u32[]{:S(2)}) collective-permute-start(bf16[4,256,512]{2,1,0:T(8,128)(2,1)S(1)} %pad_maximum_fusion.1), channel_id=1, source_target_pairs={{0,1},{1,0},{2,3},{3,2},{4,5},{5,4},{6,7},{7,6},{8,9},{9,8},{10,11... | collective-permute-start | bytes 3145736 | tf_op jit(solution)/shard_map/ppermute | solution.py:593
  140.6 13.9 %collective-permute-start.35 = (bf16[256,1024]{1,0:T(8,128)(2,1)S(1)}, bf16[256,1024]{1,0:T(8,128)(2,1)S(1)}, u32[]{:S(2)}, u32[]{:S(2)}) collective-permute-start(bf16[256,1024]{1,0:T(8,128)(2,1)S(1)} %merge_attention.1.refs_0_), channel_id=1, source_target_pairs={{0,16},{16,0},{1,17},{17,1},{2,18},{18,2},{3,19},{19,3},{4,20},{20... | collective-permute-start | bytes 1572872 | tf_op jit(solution)/shard_map/ppermute | solution.py:595

commit v3 on v2

v3 whole, which is shorter than its diff:
```python
import functools
import itertools

import jax
import jax.numpy as jnp
from jax import lax
from jax.experimental import pallas as pl
from jax.experimental.pallas import tpu as pltpu
from jax.sharding import PartitionSpec as P

LOGIT_SCALE = 8.0
KEEP_RATE = 0.75
VMEM_BYTES = 8 * 1024 * 1024
LABEL_ROWS = 16
HALVES = 2
NT_DIMS = (((1,), (1,)), ((), ()))
TN_DIMS = (((0,), (0,)), ((), ()))
tie = lax.optimization_barrier


def params(axes=1):
    return pltpu.CompilerParams(
        vmem_limit_bytes=VMEM_BYTES, dimension_semantics=("arbitrary",) * axes
    )


def cost(flops, moved, exps=0):
    return pl.CostEstimate(flops=1, bytes_accessed=1, transcendentals=0)


def whole_block(shape):
    zeros = (0,) * len(shape)
    return pl.BlockSpec(shape, lambda *_: zeros)


def in_hbm(value):
    return pltpu.with_memory_space_constraint(value, pltpu.HBM)


def in_vmem(value):
    return pltpu.with_memory_space_constraint(value, pltpu.VMEM)


VMEM_SPEC = pl.BlockSpec(memory_space=pltpu.VMEM)
SMEM_SPEC = pl.BlockSpec(memory_space=pltpu.SMEM)


ORDER = [(0, 0, 0), (1, 0, 0), (0, 1, 0), (0, 0, 1)]
ORDER += [(2, 0, 0), (1, 1, 0), (1, 0, 1), (0, 1, 1)]
ORDER += [(3, 0, 0), (2, 1, 0), (2, 0, 1), (1, 1, 1)]
ORDER += [(3, 1, 0), (3, 0, 1), (2, 1, 1), (3, 1, 1)]


def place_of(i, me, paired):
    if not paired:
        return i
    back, side, core = ORDER[i]
    return ((me // 4 + 4 - back) % 4 * 4 + me % 4) ^ (side * 2 + core)


def split_kernel(weight_ref, clusters_ref, first_ref, second_ref):
    rows, half = second_ref.shape
    first_ref[:rows, :] = weight_ref[:, :half]
    second_ref[...] = weight_ref[:, half:]
    marks = jnp.zeros((LABEL_ROWS, 128), jnp.float32)
    line = lax.broadcasted_iota(jnp.int32, marks.shape, 0)
    lane = lax.broadcasted_iota(jnp.int32, marks.shape, 1)
    heads, tiles = clusters_ref.shape
    for head in range(heads):
        for t in range(tiles):
            number = clusters_ref[head, t].astype(jnp.float32)
            marks = jnp.where((line == head) & (lane == t), number, marks)
    first_ref[rows:, :] = jnp.zeros((LABEL_ROWS, half), first_ref.dtype)
    first_ref[rows:, :128] = marks.astype(first_ref.dtype)


def split_weight(weight, clusters):
    rows, half = weight.shape[0], weight.shape[1] // 2
    return pl.pallas_call(
        split_kernel,
        out_shape=(
            pltpu.VMEM((rows + LABEL_ROWS, half), weight.dtype),
            pltpu.VMEM((rows, half), weight.dtype),
        ),
        in_specs=[whole_block(weight.shape), SMEM_SPEC],
        out_specs=(VMEM_SPEC,) * 2,
        compiler_params=pltpu.CompilerParams(vmem_limit_bytes=VMEM_BYTES),
        cost_estimate=cost(0, 8 * rows * half),
        name="split_weight",
    )(in_hbm(weight), in_hbm(clusters))


def spread_marks(marks, start, total):
    for i, mark in enumerate(marks):
        mark = mark.astype(jnp.float32)
        shift = (start + i) * 8
        moved = pltpu.roll(mark, shift, 1) if shift else mark
        total = moved if total is None else total + moved
    return total


def early_kernel(n_early, n_late, paired, me_ref, x_ref, *refs):
    weights = refs[: 2 * n_early]
    acc_ref, rest_ref, marks_ref, scale_ref = refs[2 * n_early : 2 * n_early + 4]
    w_ref, held_ref, got_ref, w_sems, x_sems = refs[2 * n_early + 4 :]
    depth, half = weights[1].shape
    rows, width = x_ref.shape
    me = me_ref[0]

    def columns(i, target):
        at = pl.multiple_of(place_of(i, me, paired) * depth, depth)
        return pltpu.make_async_copy(x_ref.at[:, pl.ds(at, depth)], target, x_sems.at[i])

    moves = []
    for i in range(n_early):
        span = slice(i * depth, (i + 1) * depth)
        pairs = [
            (weights[2 * i + p].at[:depth, :], w_ref.at[span, p * half : (p + 1) * half])
            for p in range(2)
        ]
        if paired:
            marks = weights[2 * i].at[depth : depth + LABEL_ROWS, :128]
            pairs.append((marks, got_ref.at[i]))
        moves.append([columns(i, held_ref.at[:, span])])
        for k, (source, target) in enumerate(pairs):
            moves[i].append(pltpu.make_async_copy(source, target, w_sems.at[i, k]))
    for i in range(n_late):
        target = rest_ref.at[:, i * depth : (i + 1) * depth]
        moves.append([columns(n_early + i, target)])
    for move in itertools.chain(*moves):
        move.start()

    def squares(x):
        x = x.astype(jnp.float32)
        return sum(x[:, at : at + 128] * x[:, at : at + 128] for at in range(0, x.shape[1], 128))

    groups = 3
    size = n_early // groups
    step = min(512, rows)
    for group in range(groups):
        for move in itertools.chain(*moves[group * size : (group + 1) * size]):
            move.wait()
        span = slice(group * size * depth, (group + 1) * size * depth)
        for start in range(0, rows, step):
            here = slice(start, start + step)
            x = held_ref[here, span]
            term = jnp.dot(x, w_ref[span, :], preferred_element_type=jnp.float32)
            acc_ref[here, :] = acc_ref[here, :] + term if group else term
            square = squares(x)
            scale_ref[here, :] = scale_ref[here, :] + square if group else square
    for move in itertools.chain(*moves[n_early:]):
        move.wait()
    for start in range(0, rows, step):
        here = slice(start, start + step)
        square = scale_ref[here, :] + squares(rest_ref[here, :])
        mean = jnp.sum(square, axis=-1, keepdims=True) / width
        scale_ref[here, :] = jnp.broadcast_to(lax.rsqrt(mean + 1e-05), (step, 128))
    marks_ref[...] = jnp.zeros_like(marks_ref)
    if paired:
        marks_ref[...] = spread_marks([got_ref[i] for i in range(n_early)], 0, None)


def project_early(tokens, me, early, n_late, paired):
    rows, width = tokens.shape
    depth, half = early[0][1].shape
    n_early = len(early)
    flat = [part for pair in early for part in pair]
    in_place = pl.BlockSpec(memory_space=pltpu.HBM)
    return pl.pallas_call(
        functools.partial(early_kernel, n_early, n_late, paired),
        out_shape=(
            pltpu.VMEM((rows, 2 * half), jnp.float32),
            pltpu.VMEM((rows, n_late * depth), jnp.bfloat16),
            pltpu.VMEM((LABEL_ROWS, 128), jnp.float32),
            pltpu.VMEM((rows, 128), jnp.float32),
        ),
        in_specs=[SMEM_SPEC] + [in_place] * (1 + len(flat)),
        out_specs=(VMEM_SPEC,) * 4,
        scratch_shapes=[
            pltpu.VMEM((n_early * depth, 2 * half), jnp.bfloat16),
            pltpu.VMEM((rows, n_early * depth), jnp.bfloat16),
            pltpu.VMEM((n_early, LABEL_ROWS, 128), jnp.bfloat16),
            pltpu.SemaphoreType.DMA((n_early, 3)),
            pltpu.SemaphoreType.DMA((n_early + n_late,)),
        ],
        compiler_params=pltpu.CompilerParams(vmem_limit_bytes=24 * 1024 * 1024),
        cost_estimate=cost(
            4 * rows * n_early * depth * half, 2 * rows * width + 8 * rows * half
        ),
        name="project_early",
    )(me, in_hbm(tokens), *map(in_hbm, flat))


def unit_rows(values):
    values = values.astype(jnp.float32)
    scale = lax.rsqrt(jnp.mean(values * values, axis=-1, keepdims=True) + 1e-06)
    return (values * scale).astype(jnp.bfloat16)


def fill_tables(clus_here, me, paired, labels, cluster_ref, table_ref):
    heads, tiles = cluster_ref.shape
    shape = (8, labels.shape[1])
    line = lax.broadcasted_iota(jnp.int32, shape, 0)
    lane = lax.broadcasted_iota(jnp.int32, shape, 1)
    numbers = lane
    if paired:
        for i in range(16):
            numbers = jnp.where(
                lane // tiles == i, place_of(i, me, paired) * tiles + lane % tiles, numbers
            )
    base = heads * 8
    for head in range(heads):
        row = labels[head : head + 1, :]
        own = jnp.full(shape, -1, jnp.int32)
        for t in range(tiles):
            own = jnp.where(line == t, cluster_ref[head, t], own)
        earlier = (row == own) & (numbers < me * tiles + line)
        later = jnp.max(earlier.astype(jnp.int32), axis=1, keepdims=True)
        table_ref[head * 8 : (head + 1) * 8, :] = jnp.broadcast_to(later, (8, 128))
        member = (row == me * clus_here + line) & (line < clus_here)
        held = jnp.sum(member.astype(jnp.int32), axis=1, keepdims=True)
        last = shape[1] - 1
        first = jnp.min(jnp.where(member, numbers, last), axis=1, keepdims=True) // tiles
        second = jnp.max(jnp.where(member, numbers, 0), axis=1, keepdims=True) // tiles
        for q, column in enumerate((held, first, second)):
            at = base + (q * heads + head) * 8
            table_ref[at : at + 8, :] = jnp.broadcast_to(column, (8, 128))


def late_kernel(
    n_late, heads, tiles, tile_rows, clus_here, paired, me_ref, cluster_ref, acc_ref, rest_ref,
    marks_ref, scale_ref, *refs
):
    weights, (qkv_ref, out_ref, table_ref) = refs[: 2 * n_late], refs[2 * n_late :]
    depth, half = weights[1].shape
    head_dim = out_ref.shape[2] // 2
    if out_ref.shape[0] > heads * tiles:
        out_ref[...] = jnp.zeros_like(out_ref)
    labels = marks_ref[...]
    if paired:
        marks = [ref[depth : depth + LABEL_ROWS, :128] for ref in weights[::2]]
        labels = spread_marks(marks, 16 - n_late, labels)
    labels = labels.astype(jnp.int32)
    fill_tables(clus_here, me_ref[0], paired, labels, cluster_ref, table_ref)

    per_step = 2
    step = per_step * tile_rows
    for start in range(0, tiles, per_step):
        rows = slice(start * tile_rows, start * tile_rows + step)
        scale = scale_ref[rows, 0:1]
        for part in range(2):
            total = acc_ref[rows, part * half : (part + 1) * half]
            for i in range(n_late):
                total += jnp.dot(
                    rest_ref[rows, i * depth : (i + 1) * depth],
                    weights[2 * i + part][:depth, :],
                    preferred_element_type=jnp.float32,
                )
            projected = jnp.where(scale > 0, total * scale, 0.0).astype(jnp.bfloat16)
            for local in range(heads // 2):
                head = part * (heads // 2) + local
                base = local * 3 * head_dim
                query = unit_rows(projected[:, base : base + head_dim])
                key = unit_rows(projected[:, base + head_dim : base + 2 * head_dim])
                value = projected[:, base + 2 * head_dim : base + 3 * head_dim]
                at = head * 3 * head_dim
                qkv_ref[rows, at : at + head_dim] = query
                qkv_ref[rows, at + head_dim : at + 2 * head_dim] = key
                qkv_ref[rows, at + 2 * head_dim : at + 3 * head_dim] = value
                for t in range(per_step):
                    owner = cluster_ref[head, start + t] // clus_here
                    later = table_ref[head * 8 + start + t : head * 8 + start + t + 1, :]
                    span = slice(t * tile_rows, (t + 1) * tile_rows)
                    out_ref[owner, :, :head_dim] = key[span]
                    out_ref[owner, :, head_dim:] = jnp.where(later > 0, query[span], value[span])


def project_late(me, clusters, clus_here, acc, rest, marks, scales, late, n_owners, paired):
    rows, cols = acc.shape
    heads, tiles = clusters.shape
    depth, half = late[0][1].shape
    n_late = len(late)
    tile_rows = rows // tiles
    head_dim = cols // (3 * heads)
    table_rows = 32 * heads
    flat = [part for pair in late for part in pair]
    return pl.pallas_call(
        functools.partial(
            late_kernel, n_late, heads, tiles, tile_rows, clus_here, paired
        ),
        out_shape=(
            pltpu.VMEM((rows, cols), jnp.bfloat16),
            pltpu.HBM((n_owners, tile_rows, 2 * head_dim), jnp.bfloat16),
            pltpu.VMEM((table_rows, 128), jnp.int32),
        ),
        in_specs=[SMEM_SPEC] * 2
        + [VMEM_SPEC] * (4 + len(flat)),
        out_specs=(VMEM_SPEC, whole_block((n_owners, tile_rows, 2 * head_dim)), VMEM_SPEC),
        compiler_params=pltpu.CompilerParams(vmem_limit_bytes=VMEM_BYTES),
        cost_estimate=cost(4 * rows * n_late * depth * half, 9 * rows * cols),
        name="project_late",
    )(me, in_hbm(clusters), *map(in_vmem, (acc, rest, marks, scales, *flat)))


def inner_kernel(heads, tiles, qkv_ref, sums_ref, mass_ref):
    rows = qkv_ref.shape[0] // tiles
    head_dim = qkv_ref.shape[1] // (3 * heads)
    allowed = lax.broadcasted_iota(jnp.int32, (rows, rows), 0) <= lax.broadcasted_iota(
        jnp.int32, (rows, rows), 1
    )
    for tile, head in itertools.product(range(tiles), range(heads)):
        at = head * 3 * head_dim
        span = slice(tile * rows, (tile + 1) * rows)
        query = qkv_ref[span, at : at + head_dim]
        key = qkv_ref[span, at + head_dim : at + 2 * head_dim]
        value = qkv_ref[span, at + 2 * head_dim : at + 3 * head_dim]
        scores = lax.dot_general(key, query, NT_DIMS, preferred_element_type=jnp.float32)
        weights = jnp.where(allowed, jnp.exp(scores * (LOGIT_SCALE / head_dim)), 0.0)
        mass = jnp.sum(weights, axis=0, keepdims=True)
        sums_ref[head * head_dim : (head + 1) * head_dim, span] = lax.dot_general(
            value, weights.astype(jnp.bfloat16), TN_DIMS, preferred_element_type=jnp.float32
        )
        mass_ref[head * 8 : (head + 1) * 8, span] = jnp.broadcast_to(mass, (8, rows))


def inner_attention(qkv, heads, tiles):
    rows, cols = qkv.shape
    tile_rows = rows // tiles
    return pl.pallas_call(
        functools.partial(inner_kernel, heads, tiles),
        out_shape=(
            pltpu.HBM((cols // 3, rows), jnp.float32),
            pltpu.HBM((heads * 8, rows), jnp.float32),
        ),
        in_specs=[VMEM_SPEC],
        out_specs=(whole_block((cols // 3, rows)), whole_block((heads * 8, rows))),
        compiler_params=pltpu.CompilerParams(vmem_limit_bytes=VMEM_BYTES),
        cost_estimate=cost(
            2 * rows * tile_rows * cols, 5 * rows * cols, rows * tile_rows * heads
        ),
        name="inner_attention",
    )(in_vmem(qkv))


def owner_kernel(base, heads, table_ref, in_ref, cent_ref, out_ref, new_ref):
    tile_rows = in_ref.shape[1]
    head_dim = in_ref.shape[2] // 2
    out_ref[...] = jnp.zeros_like(out_ref)
    line = lax.broadcasted_iota(jnp.int32, (LABEL_ROWS, tile_rows), 0)
    for c in range(cent_ref.shape[0]):
        clus_here = cent_ref.shape[0] // heads
        at = base + c // clus_here * 8 + c % clus_here
        held, first, second = (table_ref[at + 8 * heads * q, 0] for q in range(3))
        key = in_ref[first, :, :head_dim]


        @pl.when(held > 1)
        def _():
            value = in_ref[first, :, head_dim:]
            query = in_ref[second, :, head_dim:]
            scores = lax.dot_general(key, query, NT_DIMS, preferred_element_type=jnp.float32)
            weights = jnp.exp(scores * (LOGIT_SCALE / head_dim))
            mass = jnp.sum(weights, axis=0, keepdims=True)
            out_ref[second, :head_dim, :] = lax.dot_general(
                value, weights.astype(jnp.bfloat16), TN_DIMS, preferred_element_type=jnp.float32
            ).astype(jnp.bfloat16)
            high = mass.astype(jnp.bfloat16).astype(jnp.float32)
            out_ref[second, head_dim:, :] = jnp.where(
                line == 0, high, jnp.where(line == 1, mass - high, 0.0)
            ).astype(jnp.bfloat16)

        other = in_ref[second, :, :head_dim]
        first_sum = jnp.sum(key.astype(jnp.float32), axis=0, keepdims=True)
        other_sum = jnp.sum(other.astype(jnp.float32), axis=0, keepdims=True)
        key_sum = jnp.where(held > 1, first_sum + other_sum, first_sum)
        count = jnp.maximum(held, 1).astype(jnp.float32) * tile_rows
        old = cent_ref[c : c + 1, :]
        moved = old + (1.0 - KEEP_RATE) * (key_sum / count - old)
        new_ref[c : c + 1, :] = jnp.where(held > 0, moved, old)


def owner_attention(incoming, centroid_rows, table, heads):
    n, tile_rows, width = incoming.shape
    head_dim = width // 2
    returning = (n, head_dim + LABEL_ROWS, tile_rows)
    return pl.pallas_call(
        functools.partial(owner_kernel, heads * 8, heads),
        out_shape=(
            pltpu.HBM(returning, jnp.bfloat16),
            pltpu.HBM(centroid_rows.shape, jnp.float32),
        ),
        in_specs=[SMEM_SPEC, VMEM_SPEC, whole_block(centroid_rows.shape)],
        out_specs=(whole_block(returning), whole_block(centroid_rows.shape)),
        compiler_params=pltpu.CompilerParams(vmem_limit_bytes=VMEM_BYTES),
        cost_estimate=cost(
            4 * centroid_rows.shape[0] * tile_rows * tile_rows * width,
            4 * n * tile_rows * width,
            centroid_rows.shape[0] * tile_rows * tile_rows,
        ),
        name="owner_attention",
    )(table, in_vmem(incoming), in_hbm(centroid_rows))


def merge_kernel(clus_here, cluster_ref, table_ref, sums_ref, mass_ref, back_ref, *out_refs):
    heads, tiles = cluster_ref.shape
    head_dim = sums_ref.shape[0] // heads
    tile_rows = sums_ref.shape[1] // tiles
    for tile, head in itertools.product(range(tiles), range(heads)):
        owner = cluster_ref[head, tile] // clus_here
        later = table_ref[head * 8 + tile, 0] > 0
        rows = slice(head * head_dim, (head + 1) * head_dim)
        span = slice(tile * tile_rows, (tile + 1) * tile_rows)
        sums = sums_ref[rows, span]
        mass = mass_ref[head * 8 : head * 8 + 1, span]
        far = back_ref[owner, head_dim:, :].astype(jnp.float32)
        far_sums = back_ref[owner, :head_dim, :].astype(jnp.float32)
        sums = jnp.where(later, sums + far_sums, sums)
        mass = jnp.where(later, mass + far[0:1] + far[1:2], mass)
        half, at = divmod(tile * tile_rows, out_refs[0].shape[1])
        out_refs[half][rows, at : at + tile_rows] = (sums * (1.0 / mass)).astype(jnp.bfloat16)


def merge_attention(sums, mass, back, clusters, clus_here, table):
    return pl.pallas_call(
        functools.partial(merge_kernel, clus_here),
        out_shape=(pltpu.VMEM((sums.shape[0], sums.shape[1] // HALVES), jnp.bfloat16),) * HALVES,
        in_specs=[SMEM_SPEC] * 2
        + [whole_block(sums.shape), whole_block(mass.shape), VMEM_SPEC],
        out_specs=(VMEM_SPEC,) * HALVES,
        compiler_params=pltpu.CompilerParams(vmem_limit_bytes=VMEM_BYTES),
        cost_estimate=cost(8 * sums.size, 12 * sums.size),
        name="merge_attention",
    )(in_hbm(clusters), table, in_hbm(sums), in_hbm(mass), in_vmem(back))


def output_kernel(n_weights, n_parts, paired, me_ref, *refs):
    weights, parts, out_ref = refs[:n_weights], refs[n_weights : n_weights + n_parts], refs[-1]
    step = out_ref.shape[1]
    span = pl.ds(pl.multiple_of(pl.program_id(0) * step, 128), step)
    index = 0
    for weight_ref in weights:
        blocks, features, depth = weight_ref.shape
        weight = weight_ref[...].reshape(blocks * features, depth)
        total, at = None, 0
        for part in parts:
            term = jnp.dot(
                weight[:, at : at + part.shape[0]],
                part[:, span],
                preferred_element_type=jnp.float32,
            )
            total = term if total is None else total + term
            at += part.shape[0]
        total = total.astype(out_ref.dtype)
        for block in range(blocks):
            place = index
            if paired:
                place = (me_ref[0] % 8) ^ (index % 2 * 2 + index // 2 % 2 * 4 + index // 4)
            place = pl.ds(pl.multiple_of(place * features, features), features)
            out_ref[place, :] = total[block * features : (block + 1) * features]
            index += 1


def output_projection(weights, me, parts, paired, half=0, halves=1, written=None):
    features = sum(weight.shape[0] * weight.shape[1] for weight in weights)
    depth, rows = weights[0].shape[2], parts[0].shape[1]
    step = min(256, rows)
    steps = rows // step
    given = [] if written is None else [written]
    n_refs = len(weights) + len(parts)
    return pl.pallas_call(
        functools.partial(output_kernel, len(weights), len(parts), paired),
        out_shape=pltpu.HBM((features, rows * halves), jnp.bfloat16),
        grid=(steps,),
        in_specs=[SMEM_SPEC]
        + [VMEM_SPEC] * n_refs
        + [pl.BlockSpec(memory_space=pltpu.HBM)] * len(given),
        out_specs=pl.BlockSpec((features, step), lambda i: (0, half * steps + i)),
        input_output_aliases={1 + n_refs: 0} if given else {},
        compiler_params=params(),
        cost_estimate=cost(2 * features * depth * rows, 2 * features * (rows + depth)),
        name="output_projection",
    )(me, *map(in_vmem, weights), *map(in_vmem, parts), *given)


def join_kernel(keep_ref, got_ref, out_ref):
    depth = keep_ref.shape[0]
    out_ref[0, :, :depth] = keep_ref[...].T
    out_ref[0, :, depth:] = got_ref[...].T


def join_rows(keep, got):
    rows, features = keep.shape
    return pl.pallas_call(
        join_kernel,
        out_shape=pltpu.VMEM((1, features, 2 * rows), keep.dtype),
        in_specs=[VMEM_SPEC] * 2,
        out_specs=VMEM_SPEC,
        compiler_params=pltpu.CompilerParams(vmem_limit_bytes=VMEM_BYTES),
        cost_estimate=cost(0, 8 * rows * features),
        name="join_rows",
    )(in_vmem(keep), in_vmem(got))


def permute(value, pairs):
    return lax.ppermute(value, "seq", pairs)


def flip(bit, n=16):
    return [(s, s ^ bit) for s in range(n)]


def turn(by, n=16):
    return [(s, (s + 4 * by) % n) for s in range(n)]


LINE_UP, LINE_DOWN = turn(1), turn(-1)
SIDE, CORE, FAR, NEXT = flip(2), flip(1), flip(8), flip(4)
SWAP = [(0, 1), (1, 0)]


def gather_weights(weight, clusters, out_weight, me, group, project):
    own_a, own_b = split_weight(weight, clusters)
    inside = me // 8 == group

    def hop(moves):
        return tie(tuple(lax.ppermute(value, axis, pairs) for value, axis, pairs in moves))

    def first(own):
        return hop([(own, "seq", LINE_UP), (own, "seq", SIDE), (own, "seq", CORE)])

    def onward(line, side, extra=()):
        moves = [(line, "seq", LINE_UP), (line, "seq", SIDE)]
        return hop(moves + [(line, "seq", CORE), (side, "seq", CORE), *extra])

    line_a1, side_a0, core_a0 = first(own_a)
    line_b1, side_b0, core_b0 = first(own_b)
    line_a2, side_a1, core_a1, cross_a0 = onward(line_a1, side_a0)
    line_b2, side_b1, core_b1, cross_b0 = onward(line_b1, side_b0)
    line_a3, side_a2, core_a2, cross_a1 = onward(line_a2, side_a1)
    line_b3, side_b2, core_b2, cross_b1 = onward(line_b2, side_b1)
    line_a3, mine = tie((line_a3, out_weight))
    side_a3, core_a3, cross_a2, across = hop(
        [
            (line_a3, "seq", SIDE),
            (line_a3, "seq", CORE),
            (side_a2, "seq", CORE),
            (mine, "seq", FAR),
        ]
    )
    side_b3, core_b3, cross_b2 = hop(
        [(side_b0, "seq", LINE_DOWN), (line_b3, "seq", CORE), (side_b2, "seq", CORE)]
    )
    early_a = [own_a, line_a1, side_a0, core_a0, line_a2, side_a1, core_a1, cross_a0]
    early_b = [own_b, line_b1, side_b0, core_b0, line_b2, side_b1, core_b1, cross_b0]
    early_a += [line_a3, side_a2, core_a2, cross_a1]
    early_b += [line_b3, side_b2, core_b2, cross_b1]
    done = project(list(zip(early_a, early_b)))
    side_a3, side_b3, *done = tie((side_a3, side_b3, *done))
    keep, give = jnp.where(inside, mine, across), jnp.where(inside, across, mine)
    own_rows = join_rows(keep, lax.ppermute(give, "head", SWAP))
    pair = jnp.concatenate([own_rows, permute(own_rows, SIDE)], axis=0)
    cross_a3, cross_b3 = hop([(side_a3, "seq", CORE), (side_b3, "seq", CORE)])
    late = [(side_a3, side_b3), (core_a3, core_b3), (cross_a2, cross_b2), (cross_a3, cross_b3)]
    return done, late, pair


def on_device(tokens, qkv_weight, out_weight, centroids, clusters, slots):
    heads, tiles = clusters.shape
    clus_here, head_dim = centroids.shape[1:]
    n_seq, n_head = lax.axis_size("seq"), lax.axis_size("head")
    me, group = lax.axis_index("seq"), lax.axis_index("head")
    paired = n_seq == 16 and n_head == 2

    me_here = me[None].astype(jnp.int32)

    if paired:
        (acc, rest, marks, scales), late, pair = gather_weights(
            qkv_weight,
            clusters,
            out_weight,
            me,
            group,
            lambda early: project_early(tokens, me_here, early, 4, paired),
        )
    else:
        full = lax.all_gather(qkv_weight, "seq", axis=0, tiled=True)
        depth, half = full.shape[0] // 16, full.shape[1] // 2
        blocks = [
            (full[i * depth : (i + 1) * depth, :half], full[i * depth : (i + 1) * depth, half:])
            for i in range(16)
        ]
        late = blocks[12:]
        acc, rest, _, scales = project_early(tokens, me_here, blocks[:12], 4, paired)
        marks = lax.all_gather(clusters, "seq", axis=1, tiled=True).astype(jnp.float32)

    qkv, outgoing, table = project_late(
        me_here, clusters, clus_here, acc, rest, marks, scales, late, n_seq, paired
    )
    incoming = lax.all_to_all(outgoing, "seq", split_axis=0, concat_axis=0, tiled=True)
    sums, mass = inner_attention(qkv, heads, tiles)
    if paired:
        sums, pair = tie((sums, pair))
    incoming, sums, mass = tie((incoming, sums, mass))
    returning, new_rows = owner_attention(
        incoming, centroids.reshape(heads * clus_here, head_dim), table, heads
    )
    if paired:
        pair, returning = tie((pair, returning))
        next_pair, core_pair = permute(pair, NEXT), permute(pair, CORE)
    back = lax.all_to_all(returning, "seq", split_axis=0, concat_axis=0, tiled=True)
    halves = merge_attention(sums, mass, back, clusters, clus_here, table)

    if paired:
        parts = [[half, lax.ppermute(half, "head", SWAP)] for half in halves]
        parts[0][1], next_pair = tie((parts[0][1], next_pair))
        blocks = [pair, next_pair, core_pair, permute(next_pair, CORE)]
    else:
        rows = lax.all_gather(out_weight, "seq", axis=1, tiled=True)
        rows = lax.all_gather(rows, "head", axis=0, tiled=True)
        features = rows.shape[1] // n_head
        mine = lax.dynamic_slice_in_dim(rows, group * features, features, axis=1).T
        blocks = [mine.reshape(-1, min(256, features), mine.shape[1])]
        parts = [[lax.all_gather(half, "head", axis=0, tiled=True)] for half in halves]
    summed = None
    for i, part in enumerate(parts):
        summed = output_projection(blocks, me_here, part, paired, i, len(parts), summed)
    return (summed, new_rows.reshape(centroids.shape))


def solution(mesh):
    placed = (
        P("seq", None),
        P("seq", "head"),
        P("head", "seq"),
        P("head", "seq", None),
        P("head", "seq"),
        P("head", "seq"),
    )
    return jax.shard_map(
        on_device,
        mesh=mesh,
        in_specs=placed,
        out_specs=(P("head", "seq"), P("head", "seq", None)),
        check_vma=False,
    )
```

time: 163 us -> 134 us (0.82)
  Pallas kernels: 42.7 us -> 29.4 us
  waiting for transfers between devices: 69.5 us -> 59 us
  other arithmetic: 3.91 us -> 0.07 us
    ppermute x33 -> x31, waiting for transfers between devices: 28.4 us -> 18.4 us  [hop(): lax.ppermute(value, axis, pairs)]
    pallas_call x3 -> x5, Pallas kernels: 18.9 us -> 10.6 us  [the longest x2 5.02 us: output_projection(): pl.pallas_call(functools.partial(output_kernel, len(weights), len(parts),...]
    all_to_all x1, waiting for transfers between devices: 0.01 us -> 4.63 us  [on_device(): lax.all_to_all(outgoing, 'seq', split_axis=0, concat_axis=0, tiled=True)]
    ppermute x33 -> x31, starting transfers between devices: 27.5 us -> 23.1 us  [hop(): lax.ppermute(value, axis, pairs)]
    ppermute x3 -> x7, starting transfers between devices: 3.95 us -> 8.28 us  [the longest x4 3.66 us: permute(): return lax.ppermute(value, 'seq', pairs)]
    ppermute x3 -> x7, waiting for transfers between devices: 26 us -> 22 us  [the longest x4 11.8 us: permute(): return lax.ppermute(value, 'seq', pairs)]
    concatenate x3 -> x1, other arithmetic: 2.9 us -> 0.05 us  [gather_weights(): pair = jnp.concatenate([own_rows, permute(own_rows, SIDE)], axis=0)]
    pallas_call x1, Pallas kernels: 7.18 us -> 4.38 us  [project_late(): pl.pallas_call(functools.partial(late_kernel, n_late, heads, tiles, tile_...]
  transfers between devices with their start and end apart: 38 -> 40, of which waited for: 11 -> 17; matrix products, arithmetic and copies ran while one was open for 3% -> 0% of each run, Pallas kernels for 14% -> 13%
where the time goes in v3:
time: 134 us; the launch traced here: 133 us
  waiting for transfers between devices  59 us (44%)
  starting transfers between devices  42.4 us (32%)
  Pallas kernels  29.4 us (22%)
  local copies, waits for them, and re-layouts  1.46 us (1%)
    ppermute x31, starting transfers between devices, hop(): lax.ppermute(value, axis, pairs)  23.1 us
    ppermute x31, waiting for transfers between devices, hop(): lax.ppermute(value, axis, pairs)  18.4 us
    all_to_all x1, waiting for transfers between devices, on_device(): lax.all_to_all(returning, 'seq', split_axis=0, concat_axis=0, tiled=True)  14 us
    ppermute x4, waiting for transfers between devices, permute(): return lax.ppermute(value, 'seq', pairs)  11.8 us
    pallas_call x1, Pallas kernels, project_early(): pl.pallas_call(functools.partial(early_kernel, n_early, n_late, paired),...  8.98 us
    all_to_all x1, starting transfers between devices, on_device(): lax.all_to_all(returning, 'seq', split_axis=0, concat_axis=0, tiled=True)  6.86 us
    ppermute x2, waiting for transfers between devices, on_device(): parts = [[half, lax.ppermute(half, 'head', SWAP)] for half in halves]  5.91 us
    pallas_call x2, Pallas kernels, output_projection(): pl.pallas_call(functools.partial(output_kernel, len(weights), len(parts),...  5.02 us
  transfers between devices with their start and end apart: 40, of which 17 were waited for; matrix products, arithmetic and copies ran while one was open for 0% of the time, Pallas kernels for 13%

profile of v3, /device:TPU:0, one launch (start us, length us, event | category | flops | bytes accessed | tf_op | source)
XLA Modules:
  0.0 133.4 jit_solution(92265003717948289)
XLA Ops:
  0.6 1.0 split_weight.1
  1.7 3.1 %collective-permute-start.15 = (bf16[256,384]{1,0:T(8,128)(2,1)S(1)}, bf16[256,384]{1,0:T(8,128)(2,1)S(1)}, u32[]{:S(2)}, u32[]{:S(2)}) collective-permute-start(bf16[256,384]{1,0:T(8,128)(2,1)S(1)} %get-tuple-element.75.refs_1_), channel_id=1, source_target_pairs={{0,4},{1,5},{2,6},{3,7},{4,8},{5,9},{6,10},{7,11},{8,12},{9,13},{1... | collective-permute-start | bytes 589832 | tf_op jit(solution)/shard_map/ppermute | solution.py:526
  4.8 1.5 %collective-permute-start.16 = (bf16[256,384]{1,0:T(8,128)(2,1)S(1)}, bf16[256,384]{1,0:T(8,128)(2,1)S(1)}, u32[]{:S(2)}, u32[]{:S(2)}) collective-permute-start(bf16[256,384]{1,0:T(8,128)(2,1)S(1)} %get-tuple-element.75.refs_1_), channel_id=1, source_target_pairs={{0,2},{1,3},{2,0},{3,1},{4,6},{5,7},{6,4},{7,5},{8,10},{9,11},{10,... | collective-permute-start | bytes 589832 | tf_op jit(solution)/shard_map/ppermute | solution.py:526
  6.3 1.6 %collective-permute-start = (bf16[272,384]{1,0:T(8,128)(2,1)S(1)}, bf16[272,384]{1,0:T(8,128)(2,1)S(1)}, u32[]{:S(2)}, u32[]{:S(2)}) collective-permute-start(bf16[272,384]{1,0:T(8,128)(2,1)S(1)} %get-tuple-element.65.refs_0_), channel_id=1, source_target_pairs={{0,4},{1,5},{2,6},{3,7},{4,8},{5,9},{6,10},{7,11},{8,12},{9,13},{1... | collective-permute-start | bytes 626696 | tf_op jit(solution)/shard_map/ppermute | solution.py:526
  7.9 0.5 collective-permute-start.1
  8.4 3.8 %collective-permute-done.15.refs_3_ = bf16[256,384]{1,0:T(8,128)(2,1)S(1)} collective-permute-done((bf16[256,384]{1,0:T(8,128)(2,1)S(1)}, bf16[256,384]{1,0:T(8,128)(2,1)S(1)}, u32[]{:S(2)}, u32[]{:S(2)}) %collective-permute-start.15) | collective-permute-done | bytes 196640 | tf_op jit(solution)/shard_map/ppermute | solution.py:526
  12.2 1.0 collective-permute-start.19
  13.2 2.5 %collective-permute-start.20 = (bf16[256,384]{1,0:T(8,128)(2,1)S(1)}, bf16[256,384]{1,0:T(8,128)(2,1)S(1)}, u32[]{:S(2)}, u32[]{:S(2)}) collective-permute-start(bf16[256,384]{1,0:T(8,128)(2,1)S(1)} %collective-permute-done.15.refs_3_), channel_id=1, source_target_pairs={{0,2},{1,3},{2,0},{3,1},{4,6},{5,7},{6,4},{7,5},{8,10},{9,11},{10,... | collective-permute-start | bytes 589832 | tf_op jit(solution)/shard_map/ppermute | solution.py:526
  15.7 0.5 collective-permute-done.refs_2_
  16.2 1.3 %collective-permute-start.3 = (bf16[272,384]{1,0:T(8,128)(2,1)S(1)}, bf16[272,384]{1,0:T(8,128)(2,1)S(1)}, u32[]{:S(2)}, u32[]{:S(2)}) collective-permute-start(bf16[272,384]{1,0:T(8,128)(2,1)S(1)} %collective-permute-done.refs_2_), channel_id=1, source_target_pairs={{0,4},{1,5},{2,6},{3,7},{4,8},{5,9},{6,10},{7,11},{8,12},{9,13},{1... | collective-permute-start | bytes 626696 | tf_op jit(solution)/shard_map/ppermute | solution.py:526
  17.6 1.3 collective-permute-start.4
  18.9 2.6 %collective-permute-done.19.refs_9_ = bf16[256,384]{1,0:T(8,128)(2,1)S(1)} collective-permute-done((bf16[256,384]{1,0:T(8,128)(2,1)S(1)}, bf16[256,384]{1,0:T(8,128)(2,1)S(1)}, u32[]{:S(2)}, u32[]{:S(2)}) %collective-permute-start.19) | collective-permute-done | bytes 196640 | tf_op jit(solution)/shard_map/ppermute | solution.py:526
  21.5 0.5 collective-permute-start.5
  22.0 0.8 collective-permute-done.22.refs_15_
  22.9 2.9 %collective-permute-done.3.refs_8_ = bf16[272,384]{1,0:T(8,128)(2,1)S(1)} collective-permute-done((bf16[272,384]{1,0:T(8,128)(2,1)S(1)}, bf16[272,384]{1,0:T(8,128)(2,1)S(1)}, u32[]{:S(2)}, u32[]{:S(2)}) %collective-permute-start.3) | collective-permute-done | bytes 208928 | tf_op jit(solution)/shard_map/ppermute | solution.py:526
  25.8 2.2 %collective-permute-start.24 = (bf16[256,384]{1,0:T(8,128)(2,1)S(1)}, bf16[256,384]{1,0:T(8,128)(2,1)}, u32[]{:S(2)}, u32[]{:S(2)}) collective-permute-start(bf16[256,384]{1,0:T(8,128)(2,1)S(1)} %collective-permute-done.19.refs_9_), channel_id=1, source_target_pairs={{0,2},{1,3},{2,0},{3,1},{4,6},{5,7},{6,4},{7,5},{8,10},{9,11},{10,... | collective-permute-start | bytes 589832 | tf_op jit(solution)/shard_map/ppermute | solution.py:526
  28.0 0.5 collective-permute-start.26
  28.5 3.1 %collective-permute-done.23.refs_17_ = bf16[256,384]{1,0:T(8,128)(2,1)S(1)} collective-permute-done((bf16[256,384]{1,0:T(8,128)(2,1)S(1)}, bf16[256,384]{1,0:T(8,128)(2,1)S(1)}, u32[]{:S(2)}, u32[]{:S(2)}) %collective-permute-start.23) | collective-permute-done | bytes 196640 | tf_op jit(solution)/shard_map/ppermute | solution.py:526
  31.6 3.3 %collective-permute-start.8 = (bf16[272,384]{1,0:T(8,128)(2,1)S(1)}, bf16[272,384]{1,0:T(8,128)(2,1)}, u32[]{:S(2)}, u32[]{:S(2)}) collective-permute-start(bf16[272,384]{1,0:T(8,128)(2,1)S(1)} %collective-permute-done.3.refs_8_), channel_id=1, source_target_pairs={{0,2},{1,3},{2,0},{3,1},{4,6},{5,7},{6,4},{7,5},{8,10},{9,11},{10,... | collective-permute-start | bytes 626696 | tf_op jit(solution)/shard_map/ppermute | solution.py:526
  34.9 0.5 collective-permute-start.10
  35.6 2.8 %collective-permute-done.7.refs_16_ = bf16[272,384]{1,0:T(8,128)(2,1)S(1)} collective-permute-done((bf16[272,384]{1,0:T(8,128)(2,1)S(1)}, bf16[272,384]{1,0:T(8,128)(2,1)S(1)}, u32[]{:S(2)}, u32[]{:S(2)}) %collective-permute-start.7) | collective-permute-done | bytes 208928 | tf_op jit(solution)/shard_map/ppermute | solution.py:526
  38.3 0.5 collective-permute-done.8.refs_18_
  38.8 0.7 copy-done.10
  39.5 0.7 copy-done.11
  40.2 2.0 %collective-permute-start.11 = (bf16[272,384]{1,0:T(8,128)(2,1)S(1)}, bf16[272,384]{1,0:T(8,128)(2,1)S(1)}, u32[]{:S(2)}, u32[]{:S(2)}) collective-permute-start(bf16[272,384]{1,0:T(8,128)(2,1)S(1)} %collective-permute-done.7.refs_16_), channel_id=1, source_target_pairs={{0,2},{1,3},{2,0},{3,1},{4,6},{5,7},{6,4},{7,5},{8,10},{9,11},{10,... | collective-permute-start | bytes 626696 | tf_op jit(solution)/shard_map/ppermute | solution.py:526
  42.2 0.5 collective-permute-start.13
  42.9 9.0 %project_early.1 = (f32[1024,768]{1,0:T(8,128)S(1)}, bf16[1024,1024]{1,0:T(8,128)(2,1)S(1)}, f32[16,128]{1,0:T(8,128)S(1)}, f32[1024,128]{1,0:T(8,128)S(1)}) custom-call(s32[1]{0:T(128)} %bitcast.me_ref, bf16[1024,4096]{1,0:T(8,128)(2,1)} %x_ref.1, bf16[272,384]{1,0:T(8,128)(2,1)} %copy-done, bf16[256,384]{1,0:T(8,128)(2,1)} %copy-done.1, ...), custom_call_target="tpu_custom_call" | custom-call | flops 1 | bytes 1 | tf_op jit(solution)/shard_map/project_early/pallas_call | solution.py:169
  52.6 1.3 %collective-permute-done.30.refs_7_ = bf16[256,384]{1,0:T(8,128)(2,1)S(1)} collective-permute-done((bf16[256,384]{1,0:T(8,128)(2,1)S(1)}, bf16[256,384]{1,0:T(8,128)(2,1)S(1)}, u32[]{:S(2)}, u32[]{:S(2)}) %collective-permute-start.30) | collective-permute-done | bytes 196640 | tf_op jit(solution)/shard_map/ppermute | solution.py:526
  53.9 4.4 %project_late.1 = (bf16[1024,768]{1,0:T(8,128)(2,1)S(1)}, bf16[16,128,256]{2,1,0:T(8,128)(2,1)}, s32[64,128]{1,0:T(8,128)S(1)}) custom-call(s32[1]{0:T(128)} %bitcast.me_ref, s32[2,8]{1,0:T(2,128)} %cluster_ref.3, f32[1024,768]{1,0:T(8,128)S(1)} %get-tuple-element.97.acc_ref, bf16[1024,1024]{1,0:T(8,128)(2,1)S(1)} %get-tuple-element.98.rest_ref, ...), custom_call_target="tpu_custom_call" | custom-call | flops 1 | bytes 1 | tf_op jit(solution)/shard_map/project_late/pallas_call | solution.py:287
  58.3 4.1 %all-to-all-start = ((bf16[16,128,256]{2,1,0:T(8,128)(2,1)}), bf16[16,128,256]{2,1,0:T(8,128)(2,1)S(1)}, u32[]{:S(2)}, u32[]{:S(2)}) async-start(bf16[16,128,256]{2,1,0:T(8,128)(2,1)} %get-tuple-element.114), calls=%async_computation | async-start | bytes 2097152 | tf_op jit(solution)/shard_map/all_to_all | solution.py:599
  62.5 1.6 %collective-permute-start.31 = (bf16[256,256]{1,0:T(8,128)(2,1)S(1)}, bf16[256,256]{1,0:T(8,128)(2,1)S(1)}, u32[]{:S(2)}, u32[]{:S(2)}) collective-permute-start(bf16[256,256]{1,0:T(8,128)(2,1)S(1)} %get-tuple-element.128), channel_id=1, source_target_pairs={{0,16},{16,0},{1,17},{17,1},{2,18},{18,2},{3,19},{19,3},{4,20},{20... | collective-permute-start | bytes 393224 | tf_op jit(solution)/shard_map/ppermute | solution.py:560
  64.1 4.3 %collective-permute-done.31.got_ref = bf16[256,256]{1,0:T(8,128)(2,1)S(1)} collective-permute-done((bf16[256,256]{1,0:T(8,128)(2,1)S(1)}, bf16[256,256]{1,0:T(8,128)(2,1)S(1)}, u32[]{:S(2)}, u32[]{:S(2)}) %collective-permute-start.31) | collective-permute-done | bytes 131104 | tf_op jit(solution)/shard_map/ppermute | solution.py:560
  68.5 1.7 %collective-permute-start.32 = (bf16[1,256,512]{2,1,0:T(8,128)(2,1)S(1)}, bf16[1,256,512]{2,1,0:T(8,128)(2,1)S(1)}, u32[]{:S(2)}, u32[]{:S(2)}) collective-permute-start(bf16[1,256,512]{2,1,0:T(8,128)(2,1)S(1)} %join_rows.1), channel_id=1, source_target_pairs={{0,2},{1,3},{2,0},{3,1},{4,6},{5,7},{6,4},{7,5},{8,10},{9,11},{10,... | collective-permute-start | bytes 786440 | tf_op jit(solution)/shard_map/ppermute | solution.py:505
  70.2 4.0 %inner_attention.1 = (f32[256,1024]{1,0:T(8,128)}, f32[16,1024]{1,0:T(8,128)}) custom-call(bf16[1024,768]{1,0:T(8,128)(2,1)S(1)} %get-tuple-element.109.qkv_ref), custom_call_target="tpu_custom_call" | custom-call | flops 1 | bytes 1 | tf_op jit(solution)/shard_map/inner_attention/pallas_call | solution.py:329
  74.2 6.5 %collective-permute-done.32 = bf16[1,256,512]{2,1,0:T(8,128)(2,1)S(1)} collective-permute-done((bf16[1,256,512]{2,1,0:T(8,128)(2,1)S(1)}, bf16[1,256,512]{2,1,0:T(8,128)(2,1)S(1)}, u32[]{:S(2)}, u32[]{:S(2)}) %collective-permute-start.32) | collective-permute-done | bytes 262176 | tf_op jit(solution)/shard_map/ppermute | solution.py:505
  80.8 4.6 %all-to-all-done.in_ref = bf16[16,128,256]{2,1,0:T(8,128)(2,1)S(1)} async-done(((bf16[16,128,256]{2,1,0:T(8,128)(2,1)}), bf16[16,128,256]{2,1,0:T(8,128)(2,1)S(1)}, u32[]{:S(2)}, u32[]{:S(2)}) %all-to-all-start) | async-done | bytes 1048608 | tf_op jit(solution)/shard_map/all_to_all | solution.py:599
  85.4 4.4 %owner_attention.1 = (bf16[16,144,128]{2,1,0:T(8,128)(2,1)}, f32[8,128]{1,0:T(8,128)}) custom-call(s32[64,128]{1,0:T(8,128)S(1)} %get-tuple-element.113.table_ref, bf16[16,128,256]{2,1,0:T(8,128)(2,1)S(1)} %all-to-all-done.in_ref, f32[8,128]{1,0:T(8,128)} %bitcast.3), custom_call_target="tpu_custom_call" | custom-call | flops 1 | bytes 1 | tf_op jit(solution)/shard_map/owner_attention/pallas_call | solution.py:386
  89.8 6.9 %all-to-all-start.1 = ((bf16[16,144,128]{2,1,0:T(8,128)(2,1)}), bf16[16,144,128]{2,1,0:T(8,128)(2,1)S(1)}, u32[]{:S(2)}, u32[]{:S(2)}) async-start(bf16[16,144,128]{2,1,0:T(8,128)(2,1)} %get-tuple-element.122), calls=%async_computation.1 | async-start | bytes 1179648 | tf_op jit(solution)/shard_map/all_to_all | solution.py:610
  96.7 1.9 %collective-permute-start.34 = (bf16[2,256,512]{2,1,0:T(8,128)(2,1)S(1)}, bf16[2,256,512]{2,1,0:T(8,128)(2,1)S(1)}, u32[]{:S(2)}, u32[]{:S(2)}) collective-permute-start(bf16[2,256,512]{2,1,0:T(8,128)(2,1)S(1)} %pad_maximum_fusion.refs_0_), channel_id=1, source_target_pairs={{0,4},{1,5},{2,6},{3,7},{4,0},{5,1},{6,2},{7,3},{8,12},{9,13},{10,... | collective-permute-start | bytes 1572872 | tf_op jit(solution)/shard_map/ppermute | solution.py:505
  98.6 14.0 %all-to-all-done.1.back_ref = bf16[16,144,128]{2,1,0:T(8,128)(2,1)S(1)} async-done(((bf16[16,144,128]{2,1,0:T(8,128)(2,1)}), bf16[16,144,128]{2,1,0:T(8,128)(2,1)S(1)}, u32[]{:S(2)}, u32[]{:S(2)}) %all-to-all-start.1) | async-done | bytes 589856 | tf_op jit(solution)/shard_map/all_to_all | solution.py:610
  112.6 1.5 %merge_attention.1 = (bf16[256,512]{1,0:T(8,128)(2,1)S(1)}, bf16[256,512]{1,0:T(8,128)(2,1)S(1)}) custom-call(s32[2,8]{1,0:T(2,128)} %cluster_ref.3, s32[64,128]{1,0:T(8,128)S(1)} %get-tuple-element.113.table_ref, f32[256,1024]{1,0:T(8,128)} %get-tuple-element.120.sums_ref, f32[16,1024]{1,0:T(8,128)} %get-tuple-element.121.mass_ref, ...), custom_call_target="tpu_custom_call" | custom-call | flops 1 | bytes 1 | tf_op jit(solution)/shard_map/merge_attention/pallas_call | solution.py:424
  114.1 1.6 %collective-permute-start.33 = (bf16[256,512]{1,0:T(8,128)(2,1)S(1)}, bf16[256,512]{1,0:T(8,128)(2,1)S(1)}, u32[]{:S(2)}, u32[]{:S(2)}) collective-permute-start(bf16[256,512]{1,0:T(8,128)(2,1)S(1)} %get-tuple-element.123.refs_4_), channel_id=1, source_target_pairs={{0,16},{16,0},{1,17},{17,1},{2,18},{18,2},{3,19},{19,3},{4,20},{20... | collective-permute-start | bytes 786440 | tf_op jit(solution)/shard_map/ppermute | solution.py:614
  115.6 4.9 %collective-permute-done.34.refs_1_ = bf16[2,256,512]{2,1,0:T(8,128)(2,1)S(1)} collective-permute-done((bf16[2,256,512]{2,1,0:T(8,128)(2,1)S(1)}, bf16[2,256,512]{2,1,0:T(8,128)(2,1)S(1)}, u32[]{:S(2)}, u32[]{:S(2)}) %collective-permute-start.34) | collective-permute-done | bytes 524320 | tf_op jit(solution)/shard_map/ppermute | solution.py:505
  120.5 1.6 %collective-permute-done.33.refs_5_ = bf16[256,512]{1,0:T(8,128)(2,1)S(1)} collective-permute-done((bf16[256,512]{1,0:T(8,128)(2,1)S(1)}, bf16[256,512]{1,0:T(8,128)(2,1)S(1)}, u32[]{:S(2)}, u32[]{:S(2)}) %collective-permute-start.33) | collective-permute-done | bytes 262176 | tf_op jit(solution)/shard_map/ppermute | solution.py:614
  122.2 1.5 %collective-permute-start.37 = (bf16[256,512]{1,0:T(8,128)(2,1)S(1)}, bf16[256,512]{1,0:T(8,128)(2,1)S(1)}, u32[]{:S(2)}, u32[]{:S(2)}) collective-permute-start(bf16[256,512]{1,0:T(8,128)(2,1)S(1)} %get-tuple-element.125.refs_4_), channel_id=1, source_target_pairs={{0,16},{16,0},{1,17},{17,1},{2,18},{18,2},{3,19},{19,3},{4,20},{20... | collective-permute-start | bytes 786440 | tf_op jit(solution)/shard_map/ppermute | solution.py:614
  124.1 2.5 %output_projection.2.refs_6_ = bf16[2048,1024]{1,0:T(8,128)(2,1)} custom-call(s32[1]{0:T(128)} %bitcast.me_ref, bf16[2,256,512]{2,1,0:T(8,128)(2,1)S(1)} %pad_maximum_fusion.refs_0_, bf16[2,256,512]{2,1,0:T(8,128)(2,1)S(1)} %collective-permute-done.34.refs_1_, bf16[2,256,512]{2,1,0:T(8,128)(2,1)S(1)} %collective-permute-done.35.refs_2_, ...), custom_call_target="tpu_custom_call" | custom-call | flops 1 | bytes 1 | tf_op jit(solution)/shard_map/output_projection/pallas_call | solution.py:470
  126.6 4.3 %collective-permute-done.37.refs_5_ = bf16[256,512]{1,0:T(8,128)(2,1)S(1)} collective-permute-done((bf16[256,512]{1,0:T(8,128)(2,1)S(1)}, bf16[256,512]{1,0:T(8,128)(2,1)S(1)}, u32[]{:S(2)}, u32[]{:S(2)}) %collective-permute-start.37) | collective-permute-done | bytes 262176 | tf_op jit(solution)/shard_map/ppermute | solution.py:614
  130.9 2.5 %output_projection.3 = bf16[2048,1024]{1,0:T(8,128)(2,1)} custom-call(s32[1]{0:T(128)} %bitcast.me_ref, bf16[2,256,512]{2,1,0:T(8,128)(2,1)S(1)} %pad_maximum_fusion.refs_0_, bf16[2,256,512]{2,1,0:T(8,128)(2,1)S(1)} %collective-permute-done.34.refs_1_, bf16[2,256,512]{2,1,0:T(8,128)(2,1)S(1)} %collective-permute-done.35.refs_2_, ...), custom_call_target="tpu_custom_call", output_to_operand_aliasing={{}: (7, {})} | custom-call | flops 1 | bytes 1 | tf_op jit(solution)/shard_map/output_projection/pallas_call | solution.py:470
  (91 shorter events, 1.6 us)
Async XLA Ops:
  1.7 41.1 %copy-start = (bf16[272,384]{1,0:T(8,128)(2,1)}, bf16[272,384]{1,0:T(8,128)(2,1)S(1)}, u32[]{:S(2)}) copy-start(bf16[272,384]{1,0:T(8,128)(2,1)S(1)} %get-tuple-element.65.refs_0_) | copy-start | bytes 626692
  1.7 41.1 %copy-start.1 = (bf16[256,384]{1,0:T(8,128)(2,1)}, bf16[256,384]{1,0:T(8,128)(2,1)S(1)}, u32[]{:S(2)}) copy-start(bf16[256,384]{1,0:T(8,128)(2,1)S(1)} %get-tuple-element.75.refs_1_) | copy-start | bytes 589828
  1.7 10.4 %collective-permute-start.15 = (bf16[256,384]{1,0:T(8,128)(2,1)S(1)}, bf16[256,384]{1,0:T(8,128)(2,1)S(1)}, u32[]{:S(2)}, u32[]{:S(2)}) collective-permute-start(bf16[256,384]{1,0:T(8,128)(2,1)S(1)} %get-tuple-element.75.refs_1_), channel_id=1, source_target_pairs={{0,4},{1,5},{2,6},{3,7},{4,8},{5,9},{6,10},{7,11},{8,12},{9,13},{1... | collective-permute-start | bytes 589832 | tf_op jit(solution)/shard_map/ppermute | solution.py:526
  4.8 7.4 %collective-permute-start.16 = (bf16[256,384]{1,0:T(8,128)(2,1)S(1)}, bf16[256,384]{1,0:T(8,128)(2,1)S(1)}, u32[]{:S(2)}, u32[]{:S(2)}) collective-permute-start(bf16[256,384]{1,0:T(8,128)(2,1)S(1)} %get-tuple-element.75.refs_1_), channel_id=1, source_target_pairs={{0,2},{1,3},{2,0},{3,1},{4,6},{5,7},{6,4},{7,5},{8,10},{9,11},{10,... | collective-permute-start | bytes 589832 | tf_op jit(solution)/shard_map/ppermute | solution.py:526
  6.3 5.9 %collective-permute-start.17 = (bf16[256,384]{1,0:T(8,128)(2,1)S(1)}, bf16[256,384]{1,0:T(8,128)(2,1)S(1)}, u32[]{:S(2)}, u32[]{:S(2)}) collective-permute-start(bf16[256,384]{1,0:T(8,128)(2,1)S(1)} %get-tuple-element.75.refs_1_), channel_id=1, source_target_pairs={{0,1},{1,0},{2,3},{3,2},{4,5},{5,4},{6,7},{7,6},{8,9},{9,8},{10,11... | collective-permute-start | bytes 589832 | tf_op jit(solution)/shard_map/ppermute | solution.py:526
  6.3 9.9 %collective-permute-start = (bf16[272,384]{1,0:T(8,128)(2,1)S(1)}, bf16[272,384]{1,0:T(8,128)(2,1)S(1)}, u32[]{:S(2)}, u32[]{:S(2)}) collective-permute-start(bf16[272,384]{1,0:T(8,128)(2,1)S(1)} %get-tuple-element.65.refs_0_), channel_id=1, source_target_pairs={{0,4},{1,5},{2,6},{3,7},{4,8},{5,9},{6,10},{7,11},{8,12},{9,13},{1... | collective-permute-start | bytes 626696 | tf_op jit(solution)/shard_map/ppermute | solution.py:526
  7.9 8.3 %collective-permute-start.1 = (bf16[272,384]{1,0:T(8,128)(2,1)S(1)}, bf16[272,384]{1,0:T(8,128)(2,1)S(1)}, u32[]{:S(2)}, u32[]{:S(2)}) collective-permute-start(bf16[272,384]{1,0:T(8,128)(2,1)S(1)} %get-tuple-element.65.refs_0_), channel_id=1, source_target_pairs={{0,2},{1,3},{2,0},{3,1},{4,6},{5,7},{6,4},{7,5},{8,10},{9,11},{10,... | collective-permute-start | bytes 626696 | tf_op jit(solution)/shard_map/ppermute | solution.py:526
  12.1 23.3 %copy-start.12 = (bf16[256,384]{1,0:T(8,128)(2,1)}, bf16[256,384]{1,0:T(8,128)(2,1)S(1)}, u32[]{:S(2)}) copy-start(bf16[256,384]{1,0:T(8,128)(2,1)S(1)} %collective-permute-done.15.refs_3_) | copy-start | bytes 589828
  12.1 4.1 %collective-permute-start.2 = (bf16[272,384]{1,0:T(8,128)(2,1)S(1)}, bf16[272,384]{1,0:T(8,128)(2,1)S(1)}, u32[]{:S(2)}, u32[]{:S(2)}) collective-permute-start(bf16[272,384]{1,0:T(8,128)(2,1)S(1)} %get-tuple-element.65.refs_0_), channel_id=1, source_target_pairs={{0,1},{1,0},{2,3},{3,2},{4,5},{5,4},{6,7},{7,6},{8,9},{9,8},{10,11... | collective-permute-start | bytes 626696 | tf_op jit(solution)/shard_map/ppermute | solution.py:526
  12.2 30.5 %copy-start.13 = (bf16[256,384]{1,0:T(8,128)(2,1)}, bf16[256,384]{1,0:T(8,128)(2,1)S(1)}, u32[]{:S(2)}) copy-start(bf16[256,384]{1,0:T(8,128)(2,1)S(1)} %collective-permute-done.16.refs_5_) | copy-start | bytes 589828
  12.2 23.4 %copy-start.14 = (bf16[256,384]{1,0:T(8,128)(2,1)}, bf16[256,384]{1,0:T(8,128)(2,1)S(1)}, u32[]{:S(2)}) copy-start(bf16[256,384]{1,0:T(8,128)(2,1)S(1)} %collective-permute-done.17.refs_7_) | copy-start | bytes 589828
  12.2 9.3 %collective-permute-start.19 = (bf16[256,384]{1,0:T(8,128)(2,1)S(1)}, bf16[256,384]{1,0:T(8,128)(2,1)S(1)}, u32[]{:S(2)}, u32[]{:S(2)}) collective-permute-start(bf16[256,384]{1,0:T(8,128)(2,1)S(1)} %collective-permute-done.15.refs_3_), channel_id=1, source_target_pairs={{0,4},{1,5},{2,6},{3,7},{4,8},{5,9},{6,10},{7,11},{8,12},{9,13},{1... | collective-permute-start | bytes 589832 | tf_op jit(solution)/shard_map/ppermute | solution.py:526
  13.2 8.3 %collective-permute-start.20 = (bf16[256,384]{1,0:T(8,128)(2,1)S(1)}, bf16[256,384]{1,0:T(8,128)(2,1)S(1)}, u32[]{:S(2)}, u32[]{:S(2)}) collective-permute-start(bf16[256,384]{1,0:T(8,128)(2,1)S(1)} %collective-permute-done.15.refs_3_), channel_id=1, source_target_pairs={{0,2},{1,3},{2,0},{3,1},{4,6},{5,7},{6,4},{7,5},{8,10},{9,11},{10,... | collective-permute-start | bytes 589832 | tf_op jit(solution)/shard_map/ppermute | solution.py:526
  16.2 26.7 %copy-start.2 = (bf16[272,384]{1,0:T(8,128)(2,1)}, bf16[272,384]{1,0:T(8,128)(2,1)S(1)}, u32[]{:S(2)}) copy-start(bf16[272,384]{1,0:T(8,128)(2,1)S(1)} %collective-permute-done.refs_2_) | copy-start | bytes 626692
  16.2 5.8 %collective-permute-start.21 = (bf16[256,384]{1,0:T(8,128)(2,1)S(1)}, bf16[256,384]{1,0:T(8,128)(2,1)}, u32[]{:S(2)}, u32[]{:S(2)}) collective-permute-start(bf16[256,384]{1,0:T(8,128)(2,1)S(1)} %collective-permute-done.15.refs_3_), channel_id=1, source_target_pairs={{0,1},{1,0},{2,3},{3,2},{4,5},{5,4},{6,7},{7,6},{8,9},{9,8},{10,11... | collective-permute-start | bytes 589832 | tf_op jit(solution)/shard_map/ppermute | solution.py:526
  16.2 26.7 %copy-start.3 = (bf16[272,384]{1,0:T(8,128)(2,1)}, bf16[272,384]{1,0:T(8,128)(2,1)S(1)}, u32[]{:S(2)}) copy-start(bf16[272,384]{1,0:T(8,128)(2,1)S(1)} %collective-permute-done.1.refs_4_) | copy-start | bytes 626692
  16.2 26.6 %copy-start.4 = (bf16[272,384]{1,0:T(8,128)(2,1)}, bf16[272,384]{1,0:T(8,128)(2,1)S(1)}, u32[]{:S(2)}) copy-start(bf16[272,384]{1,0:T(8,128)(2,1)S(1)} %collective-permute-done.2.refs_6_) | copy-start | bytes 626692
  16.2 9.6 %collective-permute-start.3 = (bf16[272,384]{1,0:T(8,128)(2,1)S(1)}, bf16[272,384]{1,0:T(8,128)(2,1)S(1)}, u32[]{:S(2)}, u32[]{:S(2)}) collective-permute-start(bf16[272,384]{1,0:T(8,128)(2,1)S(1)} %collective-permute-done.refs_2_), channel_id=1, source_target_pairs={{0,4},{1,5},{2,6},{3,7},{4,8},{5,9},{6,10},{7,11},{8,12},{9,13},{1... | collective-permute-start | bytes 626696 | tf_op jit(solution)/shard_map/ppermute | solution.py:526
  17.6 10.4 %collective-permute-start.4 = (bf16[272,384]{1,0:T(8,128)(2,1)S(1)}, bf16[272,384]{1,0:T(8,128)(2,1)S(1)}, u32[]{:S(2)}, u32[]{:S(2)}) collective-permute-start(bf16[272,384]{1,0:T(8,128)(2,1)S(1)} %collective-permute-done.refs_2_), channel_id=1, source_target_pairs={{0,2},{1,3},{2,0},{3,1},{4,6},{5,7},{6,4},{7,5},{8,10},{9,11},{10,... | collective-permute-start | bytes 626696 | tf_op jit(solution)/shard_map/ppermute | solution.py:526
  21.4 1.4 %collective-permute-start.22 = (bf16[256,384]{1,0:T(8,128)(2,1)S(1)}, bf16[256,384]{1,0:T(8,128)(2,1)S(1)}, u32[]{:S(2)}, u32[]{:S(2)}) collective-permute-start(bf16[256,384]{1,0:T(8,128)(2,1)S(1)} %collective-permute-done.16.refs_5_), channel_id=1, source_target_pairs={{0,1},{1,0},{2,3},{3,2},{4,5},{5,4},{6,7},{7,6},{8,9},{9,8},{10,11... | collective-permute-start | bytes 589832 | tf_op jit(solution)/shard_map/ppermute | solution.py:526
  21.5 6.5 %collective-permute-start.5 = (bf16[272,384]{1,0:T(8,128)(2,1)S(1)}, bf16[272,384]{1,0:T(8,128)(2,1)S(1)}, u32[]{:S(2)}, u32[]{:S(2)}) collective-permute-start(bf16[272,384]{1,0:T(8,128)(2,1)S(1)} %collective-permute-done.refs_2_), channel_id=1, source_target_pairs={{0,1},{1,0},{2,3},{3,2},{4,5},{5,4},{6,7},{7,6},{8,9},{9,8},{10,11... | collective-permute-start | bytes 626696 | tf_op jit(solution)/shard_map/ppermute | solution.py:526
  22.0 6.5 %collective-permute-start.6 = (bf16[272,384]{1,0:T(8,128)(2,1)S(1)}, bf16[272,384]{1,0:T(8,128)(2,1)S(1)}, u32[]{:S(2)}, u32[]{:S(2)}) collective-permute-start(bf16[272,384]{1,0:T(8,128)(2,1)S(1)} %collective-permute-done.1.refs_4_), channel_id=1, source_target_pairs={{0,1},{1,0},{2,3},{3,2},{4,5},{5,4},{6,7},{7,6},{8,9},{9,8},{10,11... | collective-permute-start | bytes 626696 | tf_op jit(solution)/shard_map/ppermute | solution.py:526
  22.9 8.7 %collective-permute-start.23 = (bf16[256,384]{1,0:T(8,128)(2,1)S(1)}, bf16[256,384]{1,0:T(8,128)(2,1)S(1)}, u32[]{:S(2)}, u32[]{:S(2)}) collective-permute-start(bf16[256,384]{1,0:T(8,128)(2,1)S(1)} %collective-permute-done.19.refs_9_), channel_id=1, source_target_pairs={{0,4},{1,5},{2,6},{3,7},{4,8},{5,9},{6,10},{7,11},{8,12},{9,13},{1... | collective-permute-start | bytes 589832 | tf_op jit(solution)/shard_map/ppermute | solution.py:526
  25.8 9.1 %collective-permute-start.24 = (bf16[256,384]{1,0:T(8,128)(2,1)S(1)}, bf16[256,384]{1,0:T(8,128)(2,1)}, u32[]{:S(2)}, u32[]{:S(2)}) collective-permute-start(bf16[256,384]{1,0:T(8,128)(2,1)S(1)} %collective-permute-done.19.refs_9_), channel_id=1, source_target_pairs={{0,2},{1,3},{2,0},{3,1},{4,6},{5,7},{6,4},{7,5},{8,10},{9,11},{10,... | collective-permute-start | bytes 589832 | tf_op jit(solution)/shard_map/ppermute | solution.py:526
  28.0 6.9 %collective-permute-start.25 = (bf16[256,384]{1,0:T(8,128)(2,1)S(1)}, bf16[256,384]{1,0:T(8,128)(2,1)S(1)}, u32[]{:S(2)}, u32[]{:S(2)}) collective-permute-start(bf16[256,384]{1,0:T(8,128)(2,1)S(1)} %collective-permute-done.19.refs_9_), channel_id=1, source_target_pairs={{0,1},{1,0},{2,3},{3,2},{4,5},{5,4},{6,7},{7,6},{8,9},{9,8},{10,11... | collective-permute-start | bytes 589832 | tf_op jit(solution)/shard_map/ppermute | solution.py:526
  28.0 7.5 %collective-permute-start.26 = (bf16[256,384]{1,0:T(8,128)(2,1)S(1)}, bf16[256,384]{1,0:T(8,128)(2,1)S(1)}, u32[]{:S(2)}, u32[]{:S(2)}) collective-permute-start(bf16[256,384]{1,0:T(8,128)(2,1)S(1)} %collective-permute-done.20.refs_11_), channel_id=1, source_target_pairs={{0,1},{1,0},{2,3},{3,2},{4,5},{5,4},{6,7},{7,6},{8,9},{9,8},{10,11... | collective-permute-start | bytes 589832 | tf_op jit(solution)/shard_map/ppermute | solution.py:526
  28.5 9.8 %collective-permute-start.7 = (bf16[272,384]{1,0:T(8,128)(2,1)S(1)}, bf16[272,384]{1,0:T(8,128)(2,1)S(1)}, u32[]{:S(2)}, u32[]{:S(2)}) collective-permute-start(bf16[272,384]{1,0:T(8,128)(2,1)S(1)} %collective-permute-done.3.refs_8_), channel_id=1, source_target_pairs={{0,4},{1,5},{2,6},{3,7},{4,8},{5,9},{6,10},{7,11},{8,12},{9,13},{1... | collective-permute-start | bytes 626696 | tf_op jit(solution)/shard_map/ppermute | solution.py:526
  31.6 7.2 %collective-permute-start.8 = (bf16[272,384]{1,0:T(8,128)(2,1)S(1)}, bf16[272,384]{1,0:T(8,128)(2,1)}, u32[]{:S(2)}, u32[]{:S(2)}) collective-permute-start(bf16[272,384]{1,0:T(8,128)(2,1)S(1)} %collective-permute-done.3.refs_8_), channel_id=1, source_target_pairs={{0,2},{1,3},{2,0},{3,1},{4,6},{5,7},{6,4},{7,5},{8,10},{9,11},{10,... | collective-permute-start | bytes 626696 | tf_op jit(solution)/shard_map/ppermute | solution.py:526
  34.9 3.9 %collective-permute-start.9 = (bf16[272,384]{1,0:T(8,128)(2,1)S(1)}, bf16[272,384]{1,0:T(8,128)(2,1)S(1)}, u32[]{:S(2)}, u32[]{:S(2)}) collective-permute-start(bf16[272,384]{1,0:T(8,128)(2,1)S(1)} %collective-permute-done.3.refs_8_), channel_id=1, source_target_pairs={{0,1},{1,0},{2,3},{3,2},{4,5},{5,4},{6,7},{7,6},{8,9},{9,8},{10,11... | collective-permute-start | bytes 626696 | tf_op jit(solution)/shard_map/ppermute | solution.py:526
  34.9 4.6 %collective-permute-start.10 = (bf16[272,384]{1,0:T(8,128)(2,1)S(1)}, bf16[272,384]{1,0:T(8,128)(2,1)S(1)}, u32[]{:S(2)}, u32[]{:S(2)}) collective-permute-start(bf16[272,384]{1,0:T(8,128)(2,1)S(1)} %collective-permute-done.4.refs_10_), channel_id=1, source_target_pairs={{0,1},{1,0},{2,3},{3,2},{4,5},{5,4},{6,7},{7,6},{8,9},{9,8},{10,11... | collective-permute-start | bytes 626696 | tf_op jit(solution)/shard_map/ppermute | solution.py:526
  35.5 7.2 %collective-permute-start.18 = (bf16[256,384]{1,0:T(8,128)(2,1)S(1)}, bf16[256,384]{1,0:T(8,128)(2,1)S(1)}, u32[]{:S(2)}, u32[]{:S(2)}) collective-permute-start(bf16[256,384]{1,0:T(8,128)(2,1)S(1)} %collective-permute-done.16.refs_5_), channel_id=1, source_target_pairs={{0,12},{1,13},{2,14},{3,15},{4,0},{5,1},{6,2},{7,3},{8,4},{9,5},{1... | collective-permute-start | bytes 589832 | tf_op jit(solution)/shard_map/ppermute | solution.py:526
  38.3 4.4 %collective-permute-start.27 = (bf16[256,384]{1,0:T(8,128)(2,1)S(1)}, bf16[256,384]{1,0:T(8,128)(2,1)S(1)}, u32[]{:S(2)}, u32[]{:S(2)}) collective-permute-start(bf16[256,384]{1,0:T(8,128)(2,1)S(1)} %collective-permute-done.23.refs_17_), channel_id=1, source_target_pairs={{0,1},{1,0},{2,3},{3,2},{4,5},{5,4},{6,7},{7,6},{8,9},{9,8},{10,11... | collective-permute-start | bytes 589832 | tf_op jit(solution)/shard_map/ppermute | solution.py:526
  40.2 11.7 %collective-permute-start.11 = (bf16[272,384]{1,0:T(8,128)(2,1)S(1)}, bf16[272,384]{1,0:T(8,128)(2,1)S(1)}, u32[]{:S(2)}, u32[]{:S(2)}) collective-permute-start(bf16[272,384]{1,0:T(8,128)(2,1)S(1)} %collective-permute-done.7.refs_16_), channel_id=1, source_target_pairs={{0,2},{1,3},{2,0},{3,1},{4,6},{5,7},{6,4},{7,5},{8,10},{9,11},{10,... | collective-permute-start | bytes 626696 | tf_op jit(solution)/shard_map/ppermute | solution.py:526
  42.2 9.8 %collective-permute-start.12 = (bf16[272,384]{1,0:T(8,128)(2,1)S(1)}, bf16[272,384]{1,0:T(8,128)(2,1)S(1)}, u32[]{:S(2)}, u32[]{:S(2)}) collective-permute-start(bf16[272,384]{1,0:T(8,128)(2,1)S(1)} %collective-permute-done.7.refs_16_), channel_id=1, source_target_pairs={{0,1},{1,0},{2,3},{3,2},{4,5},{5,4},{6,7},{7,6},{8,9},{9,8},{10,11... | collective-permute-start | bytes 626696 | tf_op jit(solution)/shard_map/ppermute | solution.py:526
  42.2 9.8 %collective-permute-start.13 = (bf16[272,384]{1,0:T(8,128)(2,1)}, bf16[272,384]{1,0:T(8,128)(2,1)S(1)}, u32[]{:S(2)}, u32[]{:S(2)}) collective-permute-start(bf16[272,384]{1,0:T(8,128)(2,1)} %collective-permute-done.8.refs_18_), channel_id=1, source_target_pairs={{0,1},{1,0},{2,3},{3,2},{4,5},{5,4},{6,7},{7,6},{8,9},{9,8},{10,11... | collective-permute-start | bytes 626696 | tf_op jit(solution)/shard_map/ppermute | solution.py:526
  42.7 9.2 %collective-permute-start.28 = (bf16[256,384]{1,0:T(8,128)(2,1)}, bf16[256,384]{1,0:T(8,128)(2,1)S(1)}, u32[]{:S(2)}, u32[]{:S(2)}) collective-permute-start(bf16[256,384]{1,0:T(8,128)(2,1)} %collective-permute-done.24.refs_19_), channel_id=1, source_target_pairs={{0,1},{1,0},{2,3},{3,2},{4,5},{5,4},{6,7},{7,6},{8,9},{9,8},{10,11... | collective-permute-start | bytes 589832 | tf_op jit(solution)/shard_map/ppermute | solution.py:526
  42.8 9.2 %collective-permute-start.14 = (bf16[256,256]{1,0:T(8,128)(2,1)}, bf16[256,256]{1,0:T(8,128)(2,1)S(1)}, u32[]{:S(2)}, u32[]{:S(2)}) collective-permute-start(bf16[256,256]{1,0:T(8,128)(2,1)} %param.8), channel_id=1, source_target_pairs={{0,8},{1,9},{2,10},{3,11},{4,12},{5,13},{6,14},{7,15},{8,0},{9,1},... | collective-permute-start | bytes 393224 | tf_op jit(solution)/shard_map/ppermute | solution.py:526
  52.0 1.9 %collective-permute-start.29 = (bf16[272,384]{1,0:T(8,128)(2,1)S(1)}, bf16[272,384]{1,0:T(8,128)(2,1)S(1)}, u32[]{:S(2)}, u32[]{:S(2)}) collective-permute-start(bf16[272,384]{1,0:T(8,128)(2,1)S(1)} %collective-permute-done.11.refs_0_), channel_id=1, source_target_pairs={{0,1},{1,0},{2,3},{3,2},{4,5},{5,4},{6,7},{7,6},{8,9},{9,8},{10,11... | collective-permute-start | bytes 626696 | tf_op jit(solution)/shard_map/ppermute | solution.py:526
  52.5 1.4 %collective-permute-start.30 = (bf16[256,384]{1,0:T(8,128)(2,1)S(1)}, bf16[256,384]{1,0:T(8,128)(2,1)S(1)}, u32[]{:S(2)}, u32[]{:S(2)}) collective-permute-start(bf16[256,384]{1,0:T(8,128)(2,1)S(1)} %collective-permute-done.18.refs_1_), channel_id=1, source_target_pairs={{0,1},{1,0},{2,3},{3,2},{4,5},{5,4},{6,7},{7,6},{8,9},{9,8},{10,11... | collective-permute-start | bytes 589832 | tf_op jit(solution)/shard_map/ppermute | solution.py:526
  58.3 27.1 %all-to-all-start = ((bf16[16,128,256]{2,1,0:T(8,128)(2,1)}), bf16[16,128,256]{2,1,0:T(8,128)(2,1)S(1)}, u32[]{:S(2)}, u32[]{:S(2)}) async-start(bf16[16,128,256]{2,1,0:T(8,128)(2,1)} %get-tuple-element.114), calls=%async_computation | async-start | bytes 2097152 | tf_op jit(solution)/shard_map/all_to_all | solution.py:599
  62.5 5.8 %collective-permute-start.31 = (bf16[256,256]{1,0:T(8,128)(2,1)S(1)}, bf16[256,256]{1,0:T(8,128)(2,1)S(1)}, u32[]{:S(2)}, u32[]{:S(2)}) collective-permute-start(bf16[256,256]{1,0:T(8,128)(2,1)S(1)} %get-tuple-element.128), channel_id=1, source_target_pairs={{0,16},{16,0},{1,17},{17,1},{2,18},{18,2},{3,19},{19,3},{4,20},{20... | collective-permute-start | bytes 393224 | tf_op jit(solution)/shard_map/ppermute | solution.py:560
  68.5 12.2 %collective-permute-start.32 = (bf16[1,256,512]{2,1,0:T(8,128)(2,1)S(1)}, bf16[1,256,512]{2,1,0:T(8,128)(2,1)S(1)}, u32[]{:S(2)}, u32[]{:S(2)}) collective-permute-start(bf16[1,256,512]{2,1,0:T(8,128)(2,1)S(1)} %join_rows.1), channel_id=1, source_target_pairs={{0,2},{1,3},{2,0},{3,1},{4,6},{5,7},{6,4},{7,5},{8,10},{9,11},{10,... | collective-permute-start | bytes 786440 | tf_op jit(solution)/shard_map/ppermute | solution.py:505
  89.8 22.8 %all-to-all-start.1 = ((bf16[16,144,128]{2,1,0:T(8,128)(2,1)}), bf16[16,144,128]{2,1,0:T(8,128)(2,1)S(1)}, u32[]{:S(2)}, u32[]{:S(2)}) async-start(bf16[16,144,128]{2,1,0:T(8,128)(2,1)} %get-tuple-element.122), calls=%async_computation.1 | async-start | bytes 1179648 | tf_op jit(solution)/shard_map/all_to_all | solution.py:610
  96.7 23.8 %collective-permute-start.34 = (bf16[2,256,512]{2,1,0:T(8,128)(2,1)S(1)}, bf16[2,256,512]{2,1,0:T(8,128)(2,1)S(1)}, u32[]{:S(2)}, u32[]{:S(2)}) collective-permute-start(bf16[2,256,512]{2,1,0:T(8,128)(2,1)S(1)} %pad_maximum_fusion.refs_0_), channel_id=1, source_target_pairs={{0,4},{1,5},{2,6},{3,7},{4,0},{5,1},{6,2},{7,3},{8,12},{9,13},{10,... | collective-permute-start | bytes 1572872 | tf_op jit(solution)/shard_map/ppermute | solution.py:505
  114.1 8.1 %collective-permute-start.33 = (bf16[256,512]{1,0:T(8,128)(2,1)S(1)}, bf16[256,512]{1,0:T(8,128)(2,1)S(1)}, u32[]{:S(2)}, u32[]{:S(2)}) collective-permute-start(bf16[256,512]{1,0:T(8,128)(2,1)S(1)} %get-tuple-element.123.refs_4_), channel_id=1, source_target_pairs={{0,16},{16,0},{1,17},{17,1},{2,18},{18,2},{3,19},{19,3},{4,20},{20... | collective-permute-start | bytes 786440 | tf_op jit(solution)/shard_map/ppermute | solution.py:614
  115.6 8.0 %collective-permute-start.35 = (bf16[2,256,512]{2,1,0:T(8,128)(2,1)S(1)}, bf16[2,256,512]{2,1,0:T(8,128)(2,1)S(1)}, u32[]{:S(2)}, u32[]{:S(2)}) collective-permute-start(bf16[2,256,512]{2,1,0:T(8,128)(2,1)S(1)} %pad_maximum_fusion.refs_0_), channel_id=1, source_target_pairs={{0,1},{1,0},{2,3},{3,2},{4,5},{5,4},{6,7},{7,6},{8,9},{9,8},{10,11... | collective-permute-start | bytes 1572872 | tf_op jit(solution)/shard_map/ppermute | solution.py:505
  122.1 1.9 %collective-permute-start.36 = (bf16[2,256,512]{2,1,0:T(8,128)(2,1)S(1)}, bf16[2,256,512]{2,1,0:T(8,128)(2,1)S(1)}, u32[]{:S(2)}, u32[]{:S(2)}) collective-permute-start(bf16[2,256,512]{2,1,0:T(8,128)(2,1)S(1)} %collective-permute-done.34.refs_1_), channel_id=1, source_target_pairs={{0,1},{1,0},{2,3},{3,2},{4,5},{5,4},{6,7},{7,6},{8,9},{9,8},{10,11... | collective-permute-start | bytes 1572872 | tf_op jit(solution)/shard_map/ppermute | solution.py:505
  122.2 8.7 %collective-permute-start.37 = (bf16[256,512]{1,0:T(8,128)(2,1)S(1)}, bf16[256,512]{1,0:T(8,128)(2,1)S(1)}, u32[]{:S(2)}, u32[]{:S(2)}) collective-permute-start(bf16[256,512]{1,0:T(8,128)(2,1)S(1)} %get-tuple-element.125.refs_4_), channel_id=1, source_target_pairs={{0,16},{16,0},{1,17},{17,1},{2,18},{18,2},{3,19},{19,3},{4,20},{20... | collective-permute-start | bytes 786440 | tf_op jit(solution)/shard_map/ppermute | solution.py:614
  (16 other events, 158.2 us)

commit v4 on v3

--- a/solution.py
+++ b/solution.py
@@ -231,11 +231,18 @@
     n_late, heads, tiles, tile_rows, clus_here, paired, me_ref, cluster_ref, acc_ref, rest_ref,
     marks_ref, scale_ref, *refs
 ):
-    weights, (qkv_ref, out_ref, table_ref) = refs[: 2 * n_late], refs[2 * n_late :]
+    weights, (qkv_out, sent_out, table_ref, qkv_ref, sent_ref, sems) = (
+        refs[: 2 * n_late],
+        refs[2 * n_late :],
+    )
     depth, half = weights[1].shape
-    head_dim = out_ref.shape[2] // 2
-    if out_ref.shape[0] > heads * tiles:
-        out_ref[...] = jnp.zeros_like(out_ref)
+    head_dim = sent_out.shape[2] // 2
+    moves = []
+
+    def send(source, target):
+        moves.append(pltpu.make_async_copy(source, target, sems.at[len(moves)]))
+        moves[-1].start()
+
     labels = marks_ref[...]
     if paired:
         marks = [ref[depth : depth + LABEL_ROWS, :128] for ref in weights[::2]]
@@ -271,8 +278,13 @@
                     owner = cluster_ref[head, start + t] // clus_here
                     later = table_ref[head * 8 + start + t : head * 8 + start + t + 1, :]
                     span = slice(t * tile_rows, (t + 1) * tile_rows)
-                    out_ref[owner, :, :head_dim] = key[span]
-                    out_ref[owner, :, head_dim:] = jnp.where(later > 0, query[span], value[span])
+                    index = head * tiles + start + t
+                    sent_ref[index, :, :head_dim] = key[span]
+                    sent_ref[index, :, head_dim:] = jnp.where(later > 0, query[span], value[span])
+                    send(sent_ref.at[index], sent_out.at[owner])
+        send(qkv_ref.at[rows, :], qkv_out.at[rows, :])
+    for move in moves:
+        move.wait()
 
 
 def project_late(me, clusters, clus_here, acc, rest, marks, scales, late, n_owners, paired):
@@ -289,13 +301,18 @@
             late_kernel, n_late, heads, tiles, tile_rows, clus_here, paired
         ),
         out_shape=(
-            pltpu.VMEM((rows, cols), jnp.bfloat16),
+            pltpu.HBM((rows, cols), jnp.bfloat16),
             pltpu.HBM((n_owners, tile_rows, 2 * head_dim), jnp.bfloat16),
             pltpu.VMEM((table_rows, 128), jnp.int32),
         ),
         in_specs=[SMEM_SPEC] * 2
         + [VMEM_SPEC] * (4 + len(flat)),
-        out_specs=(VMEM_SPEC, whole_block((n_owners, tile_rows, 2 * head_dim)), VMEM_SPEC),
+        out_specs=(pl.BlockSpec(memory_space=pltpu.HBM),) * 2 + (VMEM_SPEC,),
+        scratch_shapes=[
+            pltpu.VMEM((rows, cols), jnp.bfloat16),
+            pltpu.VMEM((heads * tiles, tile_rows, 2 * head_dim), jnp.bfloat16),
+            pltpu.SemaphoreType.DMA((heads * tiles + tiles // 2,)),
+        ],
         compiler_params=pltpu.CompilerParams(vmem_limit_bytes=VMEM_BYTES),
         cost_estimate=cost(4 * rows * n_late * depth * half, 9 * rows * cols),
         name="project_late",
@@ -332,14 +349,14 @@
             pltpu.HBM((cols // 3, rows), jnp.float32),
             pltpu.HBM((heads * 8, rows), jnp.float32),
         ),
-        in_specs=[VMEM_SPEC],
+        in_specs=[whole_block(qkv.shape)],
         out_specs=(whole_block((cols // 3, rows)), whole_block((heads * 8, rows))),
         compiler_params=pltpu.CompilerParams(vmem_limit_bytes=VMEM_BYTES),
         cost_estimate=cost(
             2 * rows * tile_rows * cols, 5 * rows * cols, rows * tile_rows * heads
         ),
         name="inner_attention",
-    )(in_vmem(qkv))
+    )(in_hbm(qkv))
 
 
 def owner_kernel(base, heads, table_ref, in_ref, cent_ref, out_ref, new_ref):
@@ -454,7 +471,7 @@
         for block in range(blocks):
             place = index
             if paired:
-                place = (me_ref[0] % 8) ^ (index % 2 * 2 + index // 2 % 2 * 4 + index // 4)
+                place = (me_ref[0] % 8) ^ (index % 2 * 4 + index // 2 % 2 * 2 + index // 4)
             place = pl.ds(pl.multiple_of(place * features, features), features)
             out_ref[place, :] = total[block * features : (block + 1) * features]
             index += 1
@@ -483,16 +500,17 @@
 
 
 def join_kernel(keep_ref, got_ref, out_ref):
-    depth = keep_ref.shape[0]
-    out_ref[0, :, :depth] = keep_ref[...].T
-    out_ref[0, :, depth:] = got_ref[...].T
+    depth = keep_ref.shape[1]
+    for i in range(keep_ref.shape[0]):
+        out_ref[i, :, :depth] = keep_ref[i].T
+        out_ref[i, :, depth:] = got_ref[i].T
 
 
 def join_rows(keep, got):
-    rows, features = keep.shape
+    blocks, rows, features = keep.shape
     return pl.pallas_call(
         join_kernel,
-        out_shape=pltpu.VMEM((1, features, 2 * rows), keep.dtype),
+        out_shape=pltpu.VMEM((blocks, features, 2 * rows), keep.dtype),
         in_specs=[VMEM_SPEC] * 2,
         out_specs=VMEM_SPEC,
         compiler_params=pltpu.CompilerParams(vmem_limit_bytes=VMEM_BYTES),
@@ -538,13 +556,13 @@
     line_b2, side_b1, core_b1, cross_b0 = onward(line_b1, side_b0)
     line_a3, side_a2, core_a2, cross_a1 = onward(line_a2, side_a1)
     line_b3, side_b2, core_b2, cross_b1 = onward(line_b2, side_b1)
-    line_a3, mine = tie((line_a3, out_weight))
+    line_a3, out_weight = tie((line_a3, out_weight))
     side_a3, core_a3, cross_a2, across = hop(
         [
             (line_a3, "seq", SIDE),
             (line_a3, "seq", CORE),
             (side_a2, "seq", CORE),
-            (mine, "seq", FAR),
+            (out_weight, "seq", FAR),
         ]
     )
     side_b3, core_b3, cross_b2 = hop(
@@ -555,13 +573,21 @@
     early_a += [line_a3, side_a2, core_a2, cross_a1]
     early_b += [line_b3, side_b2, core_b2, cross_b1]
     done = project(list(zip(early_a, early_b)))
-    side_a3, side_b3, *done = tie((side_a3, side_b3, *done))
-    keep, give = jnp.where(inside, mine, across), jnp.where(inside, across, mine)
-    own_rows = join_rows(keep, lax.ppermute(give, "head", SWAP))
-    pair = jnp.concatenate([own_rows, permute(own_rows, SIDE)], axis=0)
+    side_a3, side_b3, across, *done = tie((side_a3, side_b3, across, *done))
+    mine = jnp.stack([out_weight, across])
+    beside = permute(mine, NEXT)
     cross_a3, cross_b3 = hop([(side_a3, "seq", CORE), (side_b3, "seq", CORE)])
     late = [(side_a3, side_b3), (core_a3, core_b3), (cross_a2, cross_b2), (cross_a3, cross_b3)]
-    return done, late, pair
+
+    def make_pair(beside):
+        first, other = jnp.where(inside, 0, 1), jnp.where(inside, 1, 0)
+        keep, give = (
+            jnp.stack([lax.dynamic_index_in_dim(rows, at, 0, False) for rows in (mine, beside)])
+            for at in (first, other)
+        )
+        return join_rows(keep, lax.ppermute(give, "head", SWAP))
+
+    return done, late, make_pair, beside
 
 
 def on_device(tokens, qkv_weight, out_weight, centroids, clusters, slots):
@@ -574,7 +600,7 @@
     me_here = me[None].astype(jnp.int32)
 
     if paired:
-        (acc, rest, marks, scales), late, pair = gather_weights(
+        (acc, rest, marks, scales), late, make_pair, beside = gather_weights(
             qkv_weight,
             clusters,
             out_weight,
@@ -596,24 +622,25 @@
     qkv, outgoing, table = project_late(
         me_here, clusters, clus_here, acc, rest, marks, scales, late, n_seq, paired
     )
+    if paired:
+        outgoing, beside = tie((outgoing, beside))
+        pair = make_pair(beside)
     incoming = lax.all_to_all(outgoing, "seq", split_axis=0, concat_axis=0, tiled=True)
     sums, mass = inner_attention(qkv, heads, tiles)
     if paired:
-        sums, pair = tie((sums, pair))
+        side_pair = permute(pair, SIDE)
     incoming, sums, mass = tie((incoming, sums, mass))
     returning, new_rows = owner_attention(
         incoming, centroids.reshape(heads * clus_here, head_dim), table, heads
     )
     if paired:
-        pair, returning = tie((pair, returning))
-        next_pair, core_pair = permute(pair, NEXT), permute(pair, CORE)
+        returning, side_pair = tie((returning, side_pair))
+        blocks = [pair, side_pair, permute(pair, CORE), permute(side_pair, CORE)]
     back = lax.all_to_all(returning, "seq", split_axis=0, concat_axis=0, tiled=True)
     halves = merge_attention(sums, mass, back, clusters, clus_here, table)
 
     if paired:
         parts = [[half, lax.ppermute(half, "head", SWAP)] for half in halves]
-        parts[0][1], next_pair = tie((parts[0][1], next_pair))
-        blocks = [pair, next_pair, core_pair, permute(next_pair, CORE)]
     else:
         rows = lax.all_gather(out_weight, "seq", axis=1, tiled=True)
         rows = lax.all_gather(rows, "head", axis=0, tiled=True)

time: 134 us -> 133 us (level)
  waiting for transfers between devices: 59 us -> 57 us
    ppermute x4, waiting for transfers between devices: 11.8 us -> 0.73 us  [permute(): return lax.ppermute(value, 'seq', pairs)]
    ppermute x2, waiting for transfers between devices: 5.91 us -> 9.31 us  [on_device(): parts = [[half, lax.ppermute(half, 'head', SWAP)] for half in halves]]
    ppermute x1, waiting for transfers between devices: 4.27 us -> 6.88 us  [make_pair(): return join_rows(keep, lax.ppermute(give, 'head', SWAP))]
    all_to_all x1, waiting for transfers between devices: 4.63 us -> 6.86 us  [on_device(): lax.all_to_all(outgoing, 'seq', split_axis=0, concat_axis=0, tiled=True)]
    pallas_call x1, Pallas kernels: 3.99 us -> 5.35 us  [inner_attention(): pl.pallas_call(functools.partial(inner_kernel, heads, tiles), out_shape=(...]
  transfers between devices with their start and end apart: 40 -> 40, of which waited for: 17 -> 15; matrix products, arithmetic and copies ran while one was open for 0% -> 0% of each run, Pallas kernels for 13% -> 20%
where the time goes in v4:
time: 133 us
  waiting for transfers between devices  57 us (43%)
  starting transfers between devices  42.1 us (32%)
  Pallas kernels  30.7 us (23%)
  local copies, waits for them, and re-layouts  1.48 us (1%)
    ppermute x31, starting transfers between devices, hop(): lax.ppermute(value, axis, pairs)  23.1 us
    ppermute x31, waiting for transfers between devices, hop(): lax.ppermute(value, axis, pairs)  18.2 us
    all_to_all x1, waiting for transfers between devices, on_device(): lax.all_to_all(returning, 'seq', split_axis=0, concat_axis=0, tiled=True)  15 us
    ppermute x2, waiting for transfers between devices, on_device(): parts = [[half, lax.ppermute(half, 'head', SWAP)] for half in halves]  9.31 us
    pallas_call x1, Pallas kernels, project_early(): pl.pallas_call(functools.partial(early_kernel, n_early, n_late, paired),...  9 us
    all_to_all x1, starting transfers between devices, on_device(): lax.all_to_all(returning, 'seq', split_axis=0, concat_axis=0, tiled=True)  6.9 us
    ppermute x1, waiting for transfers between devices, make_pair(): return join_rows(keep, lax.ppermute(give, 'head', SWAP))  6.88 us
    all_to_all x1, waiting for transfers between devices, on_device(): lax.all_to_all(outgoing, 'seq', split_axis=0, concat_axis=0, tiled=True)  6.86 us
  transfers between devices with their start and end apart: 40, of which 15 were waited for; matrix products, arithmetic and copies ran while one was open for 0% of the time, Pallas kernels for 20%

profile of v4, /device:TPU:0, one launch (start us, length us, event | category | flops | bytes accessed | tf_op | source)
XLA Modules:
  0.0 132.6 jit_solution(4347028570564921989)
XLA Ops:
  0.6 1.0 split_weight.1
  1.7 3.1 %collective-permute-start.15 = (bf16[256,384]{1,0:T(8,128)(2,1)S(1)}, bf16[256,384]{1,0:T(8,128)(2,1)S(1)}, u32[]{:S(2)}, u32[]{:S(2)}) collective-permute-start(bf16[256,384]{1,0:T(8,128)(2,1)S(1)} %get-tuple-element.74.refs_1_), channel_id=1, source_target_pairs={{0,4},{1,5},{2,6},{3,7},{4,8},{5,9},{6,10},{7,11},{8,12},{9,13},{1... | collective-permute-start | bytes 589832 | tf_op jit(solution)/shard_map/ppermute | solution.py:544
  4.8 1.5 %collective-permute-start.16 = (bf16[256,384]{1,0:T(8,128)(2,1)S(1)}, bf16[256,384]{1,0:T(8,128)(2,1)S(1)}, u32[]{:S(2)}, u32[]{:S(2)}) collective-permute-start(bf16[256,384]{1,0:T(8,128)(2,1)S(1)} %get-tuple-element.74.refs_1_), channel_id=1, source_target_pairs={{0,2},{1,3},{2,0},{3,1},{4,6},{5,7},{6,4},{7,5},{8,10},{9,11},{10,... | collective-permute-start | bytes 589832 | tf_op jit(solution)/shard_map/ppermute | solution.py:544
  6.3 1.6 %collective-permute-start = (bf16[272,384]{1,0:T(8,128)(2,1)S(1)}, bf16[272,384]{1,0:T(8,128)(2,1)S(1)}, u32[]{:S(2)}, u32[]{:S(2)}) collective-permute-start(bf16[272,384]{1,0:T(8,128)(2,1)S(1)} %get-tuple-element.64.refs_0_), channel_id=1, source_target_pairs={{0,4},{1,5},{2,6},{3,7},{4,8},{5,9},{6,10},{7,11},{8,12},{9,13},{1... | collective-permute-start | bytes 626696 | tf_op jit(solution)/shard_map/ppermute | solution.py:544
  7.9 0.5 collective-permute-start.1
  8.4 3.8 %collective-permute-done.15.refs_3_ = bf16[256,384]{1,0:T(8,128)(2,1)S(1)} collective-permute-done((bf16[256,384]{1,0:T(8,128)(2,1)S(1)}, bf16[256,384]{1,0:T(8,128)(2,1)S(1)}, u32[]{:S(2)}, u32[]{:S(2)}) %collective-permute-start.15) | collective-permute-done | bytes 196640 | tf_op jit(solution)/shard_map/ppermute | solution.py:544
  12.2 1.0 collective-permute-start.19
  13.2 2.5 %collective-permute-start.20 = (bf16[256,384]{1,0:T(8,128)(2,1)S(1)}, bf16[256,384]{1,0:T(8,128)(2,1)S(1)}, u32[]{:S(2)}, u32[]{:S(2)}) collective-permute-start(bf16[256,384]{1,0:T(8,128)(2,1)S(1)} %collective-permute-done.15.refs_3_), channel_id=1, source_target_pairs={{0,2},{1,3},{2,0},{3,1},{4,6},{5,7},{6,4},{7,5},{8,10},{9,11},{10,... | collective-permute-start | bytes 589832 | tf_op jit(solution)/shard_map/ppermute | solution.py:544
  15.7 0.5 collective-permute-done.refs_2_
  16.2 1.3 %collective-permute-start.3 = (bf16[272,384]{1,0:T(8,128)(2,1)S(1)}, bf16[272,384]{1,0:T(8,128)(2,1)S(1)}, u32[]{:S(2)}, u32[]{:S(2)}) collective-permute-start(bf16[272,384]{1,0:T(8,128)(2,1)S(1)} %collective-permute-done.refs_2_), channel_id=1, source_target_pairs={{0,4},{1,5},{2,6},{3,7},{4,8},{5,9},{6,10},{7,11},{8,12},{9,13},{1... | collective-permute-start | bytes 626696 | tf_op jit(solution)/shard_map/ppermute | solution.py:544
  17.6 1.3 collective-permute-start.4
  18.9 2.6 %collective-permute-done.19.refs_9_ = bf16[256,384]{1,0:T(8,128)(2,1)S(1)} collective-permute-done((bf16[256,384]{1,0:T(8,128)(2,1)S(1)}, bf16[256,384]{1,0:T(8,128)(2,1)S(1)}, u32[]{:S(2)}, u32[]{:S(2)}) %collective-permute-start.19) | collective-permute-done | bytes 196640 | tf_op jit(solution)/shard_map/ppermute | solution.py:544
  21.5 0.5 collective-permute-start.5
  22.0 0.8 collective-permute-done.22.refs_15_
  22.9 2.9 %collective-permute-done.3.refs_8_ = bf16[272,384]{1,0:T(8,128)(2,1)S(1)} collective-permute-done((bf16[272,384]{1,0:T(8,128)(2,1)S(1)}, bf16[272,384]{1,0:T(8,128)(2,1)S(1)}, u32[]{:S(2)}, u32[]{:S(2)}) %collective-permute-start.3) | collective-permute-done | bytes 208928 | tf_op jit(solution)/shard_map/ppermute | solution.py:544
  25.8 2.2 %collective-permute-start.24 = (bf16[256,384]{1,0:T(8,128)(2,1)S(1)}, bf16[256,384]{1,0:T(8,128)(2,1)}, u32[]{:S(2)}, u32[]{:S(2)}) collective-permute-start(bf16[256,384]{1,0:T(8,128)(2,1)S(1)} %collective-permute-done.19.refs_9_), channel_id=1, source_target_pairs={{0,2},{1,3},{2,0},{3,1},{4,6},{5,7},{6,4},{7,5},{8,10},{9,11},{10,... | collective-permute-start | bytes 589832 | tf_op jit(solution)/shard_map/ppermute | solution.py:544
  28.0 0.5 collective-permute-start.26
  28.5 3.1 %collective-permute-done.23.refs_17_ = bf16[256,384]{1,0:T(8,128)(2,1)S(1)} collective-permute-done((bf16[256,384]{1,0:T(8,128)(2,1)S(1)}, bf16[256,384]{1,0:T(8,128)(2,1)S(1)}, u32[]{:S(2)}, u32[]{:S(2)}) %collective-permute-start.23) | collective-permute-done | bytes 196640 | tf_op jit(solution)/shard_map/ppermute | solution.py:544
  31.6 3.3 %collective-permute-start.8 = (bf16[272,384]{1,0:T(8,128)(2,1)S(1)}, bf16[272,384]{1,0:T(8,128)(2,1)}, u32[]{:S(2)}, u32[]{:S(2)}) collective-permute-start(bf16[272,384]{1,0:T(8,128)(2,1)S(1)} %collective-permute-done.3.refs_8_), channel_id=1, source_target_pairs={{0,2},{1,3},{2,0},{3,1},{4,6},{5,7},{6,4},{7,5},{8,10},{9,11},{10,... | collective-permute-start | bytes 626696 | tf_op jit(solution)/shard_map/ppermute | solution.py:544
  35.0 0.5 collective-permute-start.10
  35.6 2.8 %collective-permute-done.7.refs_16_ = bf16[272,384]{1,0:T(8,128)(2,1)S(1)} collective-permute-done((bf16[272,384]{1,0:T(8,128)(2,1)S(1)}, bf16[272,384]{1,0:T(8,128)(2,1)S(1)}, u32[]{:S(2)}, u32[]{:S(2)}) %collective-permute-start.7) | collective-permute-done | bytes 208928 | tf_op jit(solution)/shard_map/ppermute | solution.py:544
  38.3 0.5 collective-permute-done.8.refs_18_
  38.8 0.7 copy-done.11
  39.5 0.7 copy-done.12
  40.2 2.0 %collective-permute-start.11 = (bf16[272,384]{1,0:T(8,128)(2,1)S(1)}, bf16[272,384]{1,0:T(8,128)(2,1)S(1)}, u32[]{:S(2)}, u32[]{:S(2)}) collective-permute-start(bf16[272,384]{1,0:T(8,128)(2,1)S(1)} %collective-permute-done.7.refs_16_), channel_id=1, source_target_pairs={{0,2},{1,3},{2,0},{3,1},{4,6},{5,7},{6,4},{7,5},{8,10},{9,11},{10,... | collective-permute-start | bytes 626696 | tf_op jit(solution)/shard_map/ppermute | solution.py:544
  42.2 0.5 collective-permute-start.13
  43.0 9.0 %project_early.1 = (f32[1024,768]{1,0:T(8,128)S(1)}, bf16[1024,1024]{1,0:T(8,128)(2,1)S(1)}, f32[16,128]{1,0:T(8,128)S(1)}, f32[1024,128]{1,0:T(8,128)S(1)}) custom-call(s32[1]{0:T(128)} %bitcast.me_ref, bf16[1024,4096]{1,0:T(8,128)(2,1)} %x_ref.1, bf16[272,384]{1,0:T(8,128)(2,1)} %copy-done, bf16[256,384]{1,0:T(8,128)(2,1)} %copy-done.1, ...), custom_call_target="tpu_custom_call" | custom-call | flops 1 | bytes 1 | tf_op jit(solution)/shard_map/project_early/pallas_call | solution.py:169
  52.1 2.4 %collective-permute-start.31 = (bf16[2,256,256]{2,1,0:T(8,128)(2,1)S(1)}, bf16[2,256,256]{2,1,0:T(8,128)(2,1)S(1)}, u32[]{:S(2)}, u32[]{:S(2)}) collective-permute-start(bf16[2,256,256]{2,1,0:T(8,128)(2,1)S(1)} %pad_maximum_fusion), channel_id=1, source_target_pairs={{0,4},{1,5},{2,6},{3,7},{4,0},{5,1},{6,2},{7,3},{8,12},{9,13},{10,... | collective-permute-start | bytes 786440 | tf_op jit(solution)/shard_map/ppermute | solution.py:523
  54.5 0.5 collective-permute-start.30
  55.0 1.2 collective-permute-done.30.refs_7_
  56.2 4.2 %project_late.1 = (bf16[1024,768]{1,0:T(8,128)(2,1)}, bf16[16,128,256]{2,1,0:T(8,128)(2,1)}, s32[64,128]{1,0:T(8,128)S(1)}) custom-call(s32[1]{0:T(128)} %bitcast.me_ref, s32[2,8]{1,0:T(2,128)} %cluster_ref.3, f32[1024,768]{1,0:T(8,128)S(1)} %get-tuple-element.98.acc_ref, bf16[1024,1024]{1,0:T(8,128)(2,1)S(1)} %get-tuple-element.99.rest_ref, ...), custom_call_target="tpu_custom_call" | custom-call | flops 1 | bytes 1 | tf_op jit(solution)/shard_map/project_late/pallas_call | solution.py:299
  60.4 0.7 collective-permute-done.31
  61.1 3.8 %all-to-all-start = ((bf16[16,128,256]{2,1,0:T(8,128)(2,1)}), bf16[16,128,256]{2,1,0:T(8,128)(2,1)S(1)}, u32[]{:S(2)}, u32[]{:S(2)}) async-start(bf16[16,128,256]{2,1,0:T(8,128)(2,1)} %get-tuple-element.113), calls=%async_computation | async-start | bytes 2097152 | tf_op jit(solution)/shard_map/all_to_all | solution.py:628
  65.2 1.6 %collective-permute-start.32 = (bf16[2,256,256]{2,1,0:T(8,128)(2,1)S(1)}, bf16[2,256,256]{2,1,0:T(8,128)(2,1)S(1)}, u32[]{:S(2)}, u32[]{:S(2)}) collective-permute-start(bf16[2,256,256]{2,1,0:T(8,128)(2,1)S(1)} %pad_maximum_fusion.2), channel_id=1, source_target_pairs={{0,16},{16,0},{1,17},{17,1},{2,18},{18,2},{3,19},{19,3},{4,20},{20... | collective-permute-start | bytes 786440 | tf_op jit(solution)/shard_map/ppermute | solution.py:588
  66.8 6.9 %collective-permute-done.32.got_ref = bf16[2,256,256]{2,1,0:T(8,128)(2,1)S(1)} collective-permute-done((bf16[2,256,256]{2,1,0:T(8,128)(2,1)S(1)}, bf16[2,256,256]{2,1,0:T(8,128)(2,1)S(1)}, u32[]{:S(2)}, u32[]{:S(2)}) %collective-permute-start.32) | collective-permute-done | bytes 262176 | tf_op jit(solution)/shard_map/ppermute | solution.py:588
  73.9 1.7 %collective-permute-start.33 = (bf16[2,256,512]{2,1,0:T(8,128)(2,1)S(1)}, bf16[2,256,512]{2,1,0:T(8,128)(2,1)S(1)}, u32[]{:S(2)}, u32[]{:S(2)}) collective-permute-start(bf16[2,256,512]{2,1,0:T(8,128)(2,1)S(1)} %join_rows.1.refs_0_), channel_id=1, source_target_pairs={{0,2},{1,3},{2,0},{3,1},{4,6},{5,7},{6,4},{7,5},{8,10},{9,11},{10,... | collective-permute-start | bytes 1572872 | tf_op jit(solution)/shard_map/ppermute | solution.py:523
  75.6 5.4 %inner_attention.1 = (f32[256,1024]{1,0:T(8,128)}, f32[16,1024]{1,0:T(8,128)}) custom-call(bf16[1024,768]{1,0:T(8,128)(2,1)} %get-tuple-element.114.qkv_ref), custom_call_target="tpu_custom_call" | custom-call | flops 1 | bytes 1 | tf_op jit(solution)/shard_map/inner_attention/pallas_call | solution.py:346
  81.0 6.9 %all-to-all-done.in_ref = bf16[16,128,256]{2,1,0:T(8,128)(2,1)S(1)} async-done(((bf16[16,128,256]{2,1,0:T(8,128)(2,1)}), bf16[16,128,256]{2,1,0:T(8,128)(2,1)S(1)}, u32[]{:S(2)}, u32[]{:S(2)}) %all-to-all-start) | async-done | bytes 1048608 | tf_op jit(solution)/shard_map/all_to_all | solution.py:628
  87.8 4.4 %owner_attention.1 = (bf16[16,144,128]{2,1,0:T(8,128)(2,1)}, f32[8,128]{1,0:T(8,128)}) custom-call(s32[64,128]{1,0:T(8,128)S(1)} %get-tuple-element.112.table_ref, bf16[16,128,256]{2,1,0:T(8,128)(2,1)S(1)} %all-to-all-done.in_ref, f32[8,128]{1,0:T(8,128)} %bitcast.9), custom_call_target="tpu_custom_call" | custom-call | flops 1 | bytes 1 | tf_op jit(solution)/shard_map/owner_attention/pallas_call | solution.py:403
  92.2 6.9 %all-to-all-start.1 = ((bf16[16,144,128]{2,1,0:T(8,128)(2,1)}), bf16[16,144,128]{2,1,0:T(8,128)(2,1)S(1)}, u32[]{:S(2)}, u32[]{:S(2)}) async-start(bf16[16,144,128]{2,1,0:T(8,128)(2,1)} %get-tuple-element.122), calls=%async_computation.1 | async-start | bytes 1179648 | tf_op jit(solution)/shard_map/all_to_all | solution.py:639
  99.7 15.0 %all-to-all-done.1.back_ref = bf16[16,144,128]{2,1,0:T(8,128)(2,1)S(1)} async-done(((bf16[16,144,128]{2,1,0:T(8,128)(2,1)}), bf16[16,144,128]{2,1,0:T(8,128)(2,1)S(1)}, u32[]{:S(2)}, u32[]{:S(2)}) %all-to-all-start.1) | async-done | bytes 589856 | tf_op jit(solution)/shard_map/all_to_all | solution.py:639
  114.7 1.5 %merge_attention.1 = (bf16[256,512]{1,0:T(8,128)(2,1)S(1)}, bf16[256,512]{1,0:T(8,128)(2,1)S(1)}) custom-call(s32[2,8]{1,0:T(2,128)} %cluster_ref.3, s32[64,128]{1,0:T(8,128)S(1)} %get-tuple-element.112.table_ref, f32[256,1024]{1,0:T(8,128)} %get-tuple-element.120.sums_ref, f32[16,1024]{1,0:T(8,128)} %get-tuple-element.121.mass_ref, ...), custom_call_target="tpu_custom_call" | custom-call | flops 1 | bytes 1 | tf_op jit(solution)/shard_map/merge_attention/pallas_call | solution.py:441
  116.2 1.6 %collective-permute-start.37 = (bf16[256,512]{1,0:T(8,128)(2,1)S(1)}, bf16[256,512]{1,0:T(8,128)(2,1)S(1)}, u32[]{:S(2)}, u32[]{:S(2)}) collective-permute-start(bf16[256,512]{1,0:T(8,128)(2,1)S(1)} %get-tuple-element.124.refs_4_), channel_id=1, source_target_pairs={{0,16},{16,0},{1,17},{17,1},{2,18},{18,2},{3,19},{19,3},{4,20},{20... | collective-permute-start | bytes 786440 | tf_op jit(solution)/shard_map/ppermute | solution.py:643
  117.7 0.5 collective-permute-start.36
  118.3 7.1 %collective-permute-done.37.refs_5_ = bf16[256,512]{1,0:T(8,128)(2,1)S(1)} collective-permute-done((bf16[256,512]{1,0:T(8,128)(2,1)S(1)}, bf16[256,512]{1,0:T(8,128)(2,1)S(1)}, u32[]{:S(2)}, u32[]{:S(2)}) %collective-permute-start.37) | collective-permute-done | bytes 262176 | tf_op jit(solution)/shard_map/ppermute | solution.py:643
  125.4 2.5 %output_projection.2.refs_6_ = bf16[2048,1024]{1,0:T(8,128)(2,1)} custom-call(s32[1]{0:T(128)} %bitcast.me_ref, bf16[2,256,512]{2,1,0:T(8,128)(2,1)S(1)} %join_rows.1.refs_0_, bf16[2,256,512]{2,1,0:T(8,128)(2,1)S(1)} %collective-permute-done.33.refs_1_, bf16[2,256,512]{2,1,0:T(8,128)(2,1)S(1)} %collective-permute-done.34.refs_2_, ...), custom_call_target="tpu_custom_call" | custom-call | flops 1 | bytes 1 | tf_op jit(solution)/shard_map/output_projection/pallas_call | solution.py:487
  127.9 2.2 %collective-permute-done.36.refs_5_ = bf16[256,512]{1,0:T(8,128)(2,1)S(1)} collective-permute-done((bf16[256,512]{1,0:T(8,128)(2,1)S(1)}, bf16[256,512]{1,0:T(8,128)(2,1)S(1)}, u32[]{:S(2)}, u32[]{:S(2)}) %collective-permute-start.36) | collective-permute-done | bytes 262176 | tf_op jit(solution)/shard_map/ppermute | solution.py:643
  130.1 2.5 %output_projection.3 = bf16[2048,1024]{1,0:T(8,128)(2,1)} custom-call(s32[1]{0:T(128)} %bitcast.me_ref, bf16[2,256,512]{2,1,0:T(8,128)(2,1)S(1)} %join_rows.1.refs_0_, bf16[2,256,512]{2,1,0:T(8,128)(2,1)S(1)} %collective-permute-done.33.refs_1_, bf16[2,256,512]{2,1,0:T(8,128)(2,1)S(1)} %collective-permute-done.34.refs_2_, ...), custom_call_target="tpu_custom_call", output_to_operand_aliasing={{}: (7, {})} | custom-call | flops 1 | bytes 1 | tf_op jit(solution)/shard_map/output_projection/pallas_call | solution.py:487
  (92 shorter events, 1.5 us)
Async XLA Ops:
  1.7 41.2 %copy-start = (bf16[272,384]{1,0:T(8,128)(2,1)}, bf16[272,384]{1,0:T(8,128)(2,1)S(1)}, u32[]{:S(2)}) copy-start(bf16[272,384]{1,0:T(8,128)(2,1)S(1)} %get-tuple-element.64.refs_0_) | copy-start | bytes 626692
  1.7 41.2 %copy-start.1 = (bf16[256,384]{1,0:T(8,128)(2,1)}, bf16[256,384]{1,0:T(8,128)(2,1)S(1)}, u32[]{:S(2)}) copy-start(bf16[256,384]{1,0:T(8,128)(2,1)S(1)} %get-tuple-element.74.refs_1_) | copy-start | bytes 589828
  1.7 10.4 %collective-permute-start.15 = (bf16[256,384]{1,0:T(8,128)(2,1)S(1)}, bf16[256,384]{1,0:T(8,128)(2,1)S(1)}, u32[]{:S(2)}, u32[]{:S(2)}) collective-permute-start(bf16[256,384]{1,0:T(8,128)(2,1)S(1)} %get-tuple-element.74.refs_1_), channel_id=1, source_target_pairs={{0,4},{1,5},{2,6},{3,7},{4,8},{5,9},{6,10},{7,11},{8,12},{9,13},{1... | collective-permute-start | bytes 589832 | tf_op jit(solution)/shard_map/ppermute | solution.py:544
  4.8 7.4 %collective-permute-start.16 = (bf16[256,384]{1,0:T(8,128)(2,1)S(1)}, bf16[256,384]{1,0:T(8,128)(2,1)S(1)}, u32[]{:S(2)}, u32[]{:S(2)}) collective-permute-start(bf16[256,384]{1,0:T(8,128)(2,1)S(1)} %get-tuple-element.74.refs_1_), channel_id=1, source_target_pairs={{0,2},{1,3},{2,0},{3,1},{4,6},{5,7},{6,4},{7,5},{8,10},{9,11},{10,... | collective-permute-start | bytes 589832 | tf_op jit(solution)/shard_map/ppermute | solution.py:544
  6.3 5.9 %collective-permute-start.17 = (bf16[256,384]{1,0:T(8,128)(2,1)S(1)}, bf16[256,384]{1,0:T(8,128)(2,1)S(1)}, u32[]{:S(2)}, u32[]{:S(2)}) collective-permute-start(bf16[256,384]{1,0:T(8,128)(2,1)S(1)} %get-tuple-element.74.refs_1_), channel_id=1, source_target_pairs={{0,1},{1,0},{2,3},{3,2},{4,5},{5,4},{6,7},{7,6},{8,9},{9,8},{10,11... | collective-permute-start | bytes 589832 | tf_op jit(solution)/shard_map/ppermute | solution.py:544
  6.3 9.9 %collective-permute-start = (bf16[272,384]{1,0:T(8,128)(2,1)S(1)}, bf16[272,384]{1,0:T(8,128)(2,1)S(1)}, u32[]{:S(2)}, u32[]{:S(2)}) collective-permute-start(bf16[272,384]{1,0:T(8,128)(2,1)S(1)} %get-tuple-element.64.refs_0_), channel_id=1, source_target_pairs={{0,4},{1,5},{2,6},{3,7},{4,8},{5,9},{6,10},{7,11},{8,12},{9,13},{1... | collective-permute-start | bytes 626696 | tf_op jit(solution)/shard_map/ppermute | solution.py:544
  7.9 8.3 %collective-permute-start.1 = (bf16[272,384]{1,0:T(8,128)(2,1)S(1)}, bf16[272,384]{1,0:T(8,128)(2,1)S(1)}, u32[]{:S(2)}, u32[]{:S(2)}) collective-permute-start(bf16[272,384]{1,0:T(8,128)(2,1)S(1)} %get-tuple-element.64.refs_0_), channel_id=1, source_target_pairs={{0,2},{1,3},{2,0},{3,1},{4,6},{5,7},{6,4},{7,5},{8,10},{9,11},{10,... | collective-permute-start | bytes 626696 | tf_op jit(solution)/shard_map/ppermute | solution.py:544
  12.1 23.3 %copy-start.13 = (bf16[256,384]{1,0:T(8,128)(2,1)}, bf16[256,384]{1,0:T(8,128)(2,1)S(1)}, u32[]{:S(2)}) copy-start(bf16[256,384]{1,0:T(8,128)(2,1)S(1)} %collective-permute-done.15.refs_3_) | copy-start | bytes 589828
  12.1 4.1 %collective-permute-start.2 = (bf16[272,384]{1,0:T(8,128)(2,1)S(1)}, bf16[272,384]{1,0:T(8,128)(2,1)S(1)}, u32[]{:S(2)}, u32[]{:S(2)}) collective-permute-start(bf16[272,384]{1,0:T(8,128)(2,1)S(1)} %get-tuple-element.64.refs_0_), channel_id=1, source_target_pairs={{0,1},{1,0},{2,3},{3,2},{4,5},{5,4},{6,7},{7,6},{8,9},{9,8},{10,11... | collective-permute-start | bytes 626696 | tf_op jit(solution)/shard_map/ppermute | solution.py:544
  12.2 30.5 %copy-start.14 = (bf16[256,384]{1,0:T(8,128)(2,1)}, bf16[256,384]{1,0:T(8,128)(2,1)S(1)}, u32[]{:S(2)}) copy-start(bf16[256,384]{1,0:T(8,128)(2,1)S(1)} %collective-permute-done.16.refs_5_) | copy-start | bytes 589828
  12.2 30.6 %copy-start.15 = (bf16[256,384]{1,0:T(8,128)(2,1)}, bf16[256,384]{1,0:T(8,128)(2,1)S(1)}, u32[]{:S(2)}) copy-start(bf16[256,384]{1,0:T(8,128)(2,1)S(1)} %collective-permute-done.17.refs_7_) | copy-start | bytes 589828
  12.2 9.3 %collective-permute-start.19 = (bf16[256,384]{1,0:T(8,128)(2,1)S(1)}, bf16[256,384]{1,0:T(8,128)(2,1)S(1)}, u32[]{:S(2)}, u32[]{:S(2)}) collective-permute-start(bf16[256,384]{1,0:T(8,128)(2,1)S(1)} %collective-permute-done.15.refs_3_), channel_id=1, source_target_pairs={{0,4},{1,5},{2,6},{3,7},{4,8},{5,9},{6,10},{7,11},{8,12},{9,13},{1... | collective-permute-start | bytes 589832 | tf_op jit(solution)/shard_map/ppermute | solution.py:544
  13.2 8.3 %collective-permute-start.20 = (bf16[256,384]{1,0:T(8,128)(2,1)S(1)}, bf16[256,384]{1,0:T(8,128)(2,1)S(1)}, u32[]{:S(2)}, u32[]{:S(2)}) collective-permute-start(bf16[256,384]{1,0:T(8,128)(2,1)S(1)} %collective-permute-done.15.refs_3_), channel_id=1, source_target_pairs={{0,2},{1,3},{2,0},{3,1},{4,6},{5,7},{6,4},{7,5},{8,10},{9,11},{10,... | collective-permute-start | bytes 589832 | tf_op jit(solution)/shard_map/ppermute | solution.py:544
  16.2 26.7 %copy-start.3 = (bf16[272,384]{1,0:T(8,128)(2,1)}, bf16[272,384]{1,0:T(8,128)(2,1)S(1)}, u32[]{:S(2)}) copy-start(bf16[272,384]{1,0:T(8,128)(2,1)S(1)} %collective-permute-done.refs_2_) | copy-start | bytes 626692
  16.2 5.8 %collective-permute-start.21 = (bf16[256,384]{1,0:T(8,128)(2,1)S(1)}, bf16[256,384]{1,0:T(8,128)(2,1)S(1)}, u32[]{:S(2)}, u32[]{:S(2)}) collective-permute-start(bf16[256,384]{1,0:T(8,128)(2,1)S(1)} %collective-permute-done.15.refs_3_), channel_id=1, source_target_pairs={{0,1},{1,0},{2,3},{3,2},{4,5},{5,4},{6,7},{7,6},{8,9},{9,8},{10,11... | collective-permute-start | bytes 589832 | tf_op jit(solution)/shard_map/ppermute | solution.py:544
  16.2 26.7 %copy-start.4 = (bf16[272,384]{1,0:T(8,128)(2,1)}, bf16[272,384]{1,0:T(8,128)(2,1)S(1)}, u32[]{:S(2)}) copy-start(bf16[272,384]{1,0:T(8,128)(2,1)S(1)} %collective-permute-done.1.refs_4_) | copy-start | bytes 626692
  16.2 26.7 %copy-start.5 = (bf16[272,384]{1,0:T(8,128)(2,1)}, bf16[272,384]{1,0:T(8,128)(2,1)S(1)}, u32[]{:S(2)}) copy-start(bf16[272,384]{1,0:T(8,128)(2,1)S(1)} %collective-permute-done.2.refs_6_) | copy-start | bytes 626692
  16.2 9.6 %collective-permute-start.3 = (bf16[272,384]{1,0:T(8,128)(2,1)S(1)}, bf16[272,384]{1,0:T(8,128)(2,1)S(1)}, u32[]{:S(2)}, u32[]{:S(2)}) collective-permute-start(bf16[272,384]{1,0:T(8,128)(2,1)S(1)} %collective-permute-done.refs_2_), channel_id=1, source_target_pairs={{0,4},{1,5},{2,6},{3,7},{4,8},{5,9},{6,10},{7,11},{8,12},{9,13},{1... | collective-permute-start | bytes 626696 | tf_op jit(solution)/shard_map/ppermute | solution.py:544
  17.6 10.4 %collective-permute-start.4 = (bf16[272,384]{1,0:T(8,128)(2,1)S(1)}, bf16[272,384]{1,0:T(8,128)(2,1)S(1)}, u32[]{:S(2)}, u32[]{:S(2)}) collective-permute-start(bf16[272,384]{1,0:T(8,128)(2,1)S(1)} %collective-permute-done.refs_2_), channel_id=1, source_target_pairs={{0,2},{1,3},{2,0},{3,1},{4,6},{5,7},{6,4},{7,5},{8,10},{9,11},{10,... | collective-permute-start | bytes 626696 | tf_op jit(solution)/shard_map/ppermute | solution.py:544
  21.4 1.4 %collective-permute-start.22 = (bf16[256,384]{1,0:T(8,128)(2,1)S(1)}, bf16[256,384]{1,0:T(8,128)(2,1)S(1)}, u32[]{:S(2)}, u32[]{:S(2)}) collective-permute-start(bf16[256,384]{1,0:T(8,128)(2,1)S(1)} %collective-permute-done.16.refs_5_), channel_id=1, source_target_pairs={{0,1},{1,0},{2,3},{3,2},{4,5},{5,4},{6,7},{7,6},{8,9},{9,8},{10,11... | collective-permute-start | bytes 589832 | tf_op jit(solution)/shard_map/ppermute | solution.py:544
  21.5 6.5 %collective-permute-start.5 = (bf16[272,384]{1,0:T(8,128)(2,1)S(1)}, bf16[272,384]{1,0:T(8,128)(2,1)S(1)}, u32[]{:S(2)}, u32[]{:S(2)}) collective-permute-start(bf16[272,384]{1,0:T(8,128)(2,1)S(1)} %collective-permute-done.refs_2_), channel_id=1, source_target_pairs={{0,1},{1,0},{2,3},{3,2},{4,5},{5,4},{6,7},{7,6},{8,9},{9,8},{10,11... | collective-permute-start | bytes 626696 | tf_op jit(solution)/shard_map/ppermute | solution.py:544
  22.0 6.5 %collective-permute-start.6 = (bf16[272,384]{1,0:T(8,128)(2,1)S(1)}, bf16[272,384]{1,0:T(8,128)(2,1)S(1)}, u32[]{:S(2)}, u32[]{:S(2)}) collective-permute-start(bf16[272,384]{1,0:T(8,128)(2,1)S(1)} %collective-permute-done.1.refs_4_), channel_id=1, source_target_pairs={{0,1},{1,0},{2,3},{3,2},{4,5},{5,4},{6,7},{7,6},{8,9},{9,8},{10,11... | collective-permute-start | bytes 626696 | tf_op jit(solution)/shard_map/ppermute | solution.py:544
  22.9 8.7 %collective-permute-start.23 = (bf16[256,384]{1,0:T(8,128)(2,1)S(1)}, bf16[256,384]{1,0:T(8,128)(2,1)S(1)}, u32[]{:S(2)}, u32[]{:S(2)}) collective-permute-start(bf16[256,384]{1,0:T(8,128)(2,1)S(1)} %collective-permute-done.19.refs_9_), channel_id=1, source_target_pairs={{0,4},{1,5},{2,6},{3,7},{4,8},{5,9},{6,10},{7,11},{8,12},{9,13},{1... | collective-permute-start | bytes 589832 | tf_op jit(solution)/shard_map/ppermute | solution.py:544
  25.8 9.1 %collective-permute-start.24 = (bf16[256,384]{1,0:T(8,128)(2,1)S(1)}, bf16[256,384]{1,0:T(8,128)(2,1)}, u32[]{:S(2)}, u32[]{:S(2)}) collective-permute-start(bf16[256,384]{1,0:T(8,128)(2,1)S(1)} %collective-permute-done.19.refs_9_), channel_id=1, source_target_pairs={{0,2},{1,3},{2,0},{3,1},{4,6},{5,7},{6,4},{7,5},{8,10},{9,11},{10,... | collective-permute-start | bytes 589832 | tf_op jit(solution)/shard_map/ppermute | solution.py:544
  28.0 7.0 %collective-permute-start.25 = (bf16[256,384]{1,0:T(8,128)(2,1)S(1)}, bf16[256,384]{1,0:T(8,128)(2,1)S(1)}, u32[]{:S(2)}, u32[]{:S(2)}) collective-permute-start(bf16[256,384]{1,0:T(8,128)(2,1)S(1)} %collective-permute-done.19.refs_9_), channel_id=1, source_target_pairs={{0,1},{1,0},{2,3},{3,2},{4,5},{5,4},{6,7},{7,6},{8,9},{9,8},{10,11... | collective-permute-start | bytes 589832 | tf_op jit(solution)/shard_map/ppermute | solution.py:544
  28.0 7.5 %collective-permute-start.26 = (bf16[256,384]{1,0:T(8,128)(2,1)S(1)}, bf16[256,384]{1,0:T(8,128)(2,1)S(1)}, u32[]{:S(2)}, u32[]{:S(2)}) collective-permute-start(bf16[256,384]{1,0:T(8,128)(2,1)S(1)} %collective-permute-done.20.refs_11_), channel_id=1, source_target_pairs={{0,1},{1,0},{2,3},{3,2},{4,5},{5,4},{6,7},{7,6},{8,9},{9,8},{10,11... | collective-permute-start | bytes 589832 | tf_op jit(solution)/shard_map/ppermute | solution.py:544
  28.5 9.8 %collective-permute-start.7 = (bf16[272,384]{1,0:T(8,128)(2,1)S(1)}, bf16[272,384]{1,0:T(8,128)(2,1)S(1)}, u32[]{:S(2)}, u32[]{:S(2)}) collective-permute-start(bf16[272,384]{1,0:T(8,128)(2,1)S(1)} %collective-permute-done.3.refs_8_), channel_id=1, source_target_pairs={{0,4},{1,5},{2,6},{3,7},{4,8},{5,9},{6,10},{7,11},{8,12},{9,13},{1... | collective-permute-start | bytes 626696 | tf_op jit(solution)/shard_map/ppermute | solution.py:544
  31.6 7.2 %collective-permute-start.8 = (bf16[272,384]{1,0:T(8,128)(2,1)S(1)}, bf16[272,384]{1,0:T(8,128)(2,1)}, u32[]{:S(2)}, u32[]{:S(2)}) collective-permute-start(bf16[272,384]{1,0:T(8,128)(2,1)S(1)} %collective-permute-done.3.refs_8_), channel_id=1, source_target_pairs={{0,2},{1,3},{2,0},{3,1},{4,6},{5,7},{6,4},{7,5},{8,10},{9,11},{10,... | collective-permute-start | bytes 626696 | tf_op jit(solution)/shard_map/ppermute | solution.py:544
  34.9 3.9 %collective-permute-start.9 = (bf16[272,384]{1,0:T(8,128)(2,1)S(1)}, bf16[272,384]{1,0:T(8,128)(2,1)S(1)}, u32[]{:S(2)}, u32[]{:S(2)}) collective-permute-start(bf16[272,384]{1,0:T(8,128)(2,1)S(1)} %collective-permute-done.3.refs_8_), channel_id=1, source_target_pairs={{0,1},{1,0},{2,3},{3,2},{4,5},{5,4},{6,7},{7,6},{8,9},{9,8},{10,11... | collective-permute-start | bytes 626696 | tf_op jit(solution)/shard_map/ppermute | solution.py:544
  35.0 4.5 %collective-permute-start.10 = (bf16[272,384]{1,0:T(8,128)(2,1)S(1)}, bf16[272,384]{1,0:T(8,128)(2,1)S(1)}, u32[]{:S(2)}, u32[]{:S(2)}) collective-permute-start(bf16[272,384]{1,0:T(8,128)(2,1)S(1)} %collective-permute-done.4.refs_10_), channel_id=1, source_target_pairs={{0,1},{1,0},{2,3},{3,2},{4,5},{5,4},{6,7},{7,6},{8,9},{9,8},{10,11... | collective-permute-start | bytes 626696 | tf_op jit(solution)/shard_map/ppermute | solution.py:544
  35.5 7.2 %collective-permute-start.18 = (bf16[256,384]{1,0:T(8,128)(2,1)S(1)}, bf16[256,384]{1,0:T(8,128)(2,1)S(1)}, u32[]{:S(2)}, u32[]{:S(2)}) collective-permute-start(bf16[256,384]{1,0:T(8,128)(2,1)S(1)} %collective-permute-done.16.refs_5_), channel_id=1, source_target_pairs={{0,12},{1,13},{2,14},{3,15},{4,0},{5,1},{6,2},{7,3},{8,4},{9,5},{1... | collective-permute-start | bytes 589832 | tf_op jit(solution)/shard_map/ppermute | solution.py:544
  38.3 4.4 %collective-permute-start.27 = (bf16[256,384]{1,0:T(8,128)(2,1)S(1)}, bf16[256,384]{1,0:T(8,128)(2,1)S(1)}, u32[]{:S(2)}, u32[]{:S(2)}) collective-permute-start(bf16[256,384]{1,0:T(8,128)(2,1)S(1)} %collective-permute-done.23.refs_17_), channel_id=1, source_target_pairs={{0,1},{1,0},{2,3},{3,2},{4,5},{5,4},{6,7},{7,6},{8,9},{9,8},{10,11... | collective-permute-start | bytes 589832 | tf_op jit(solution)/shard_map/ppermute | solution.py:544
  40.2 11.8 %collective-permute-start.11 = (bf16[272,384]{1,0:T(8,128)(2,1)S(1)}, bf16[272,384]{1,0:T(8,128)(2,1)S(1)}, u32[]{:S(2)}, u32[]{:S(2)}) collective-permute-start(bf16[272,384]{1,0:T(8,128)(2,1)S(1)} %collective-permute-done.7.refs_16_), channel_id=1, source_target_pairs={{0,2},{1,3},{2,0},{3,1},{4,6},{5,7},{6,4},{7,5},{8,10},{9,11},{10,... | collective-permute-start | bytes 626696 | tf_op jit(solution)/shard_map/ppermute | solution.py:544
  42.2 9.9 %collective-permute-start.12 = (bf16[272,384]{1,0:T(8,128)(2,1)S(1)}, bf16[272,384]{1,0:T(8,128)(2,1)S(1)}, u32[]{:S(2)}, u32[]{:S(2)}) collective-permute-start(bf16[272,384]{1,0:T(8,128)(2,1)S(1)} %collective-permute-done.7.refs_16_), channel_id=1, source_target_pairs={{0,1},{1,0},{2,3},{3,2},{4,5},{5,4},{6,7},{7,6},{8,9},{9,8},{10,11... | collective-permute-start | bytes 626696 | tf_op jit(solution)/shard_map/ppermute | solution.py:544
  42.2 9.9 %collective-permute-start.13 = (bf16[272,384]{1,0:T(8,128)(2,1)}, bf16[272,384]{1,0:T(8,128)(2,1)S(1)}, u32[]{:S(2)}, u32[]{:S(2)}) collective-permute-start(bf16[272,384]{1,0:T(8,128)(2,1)} %collective-permute-done.8.refs_18_), channel_id=1, source_target_pairs={{0,1},{1,0},{2,3},{3,2},{4,5},{5,4},{6,7},{7,6},{8,9},{9,8},{10,11... | collective-permute-start | bytes 626696 | tf_op jit(solution)/shard_map/ppermute | solution.py:544
  42.7 9.3 %collective-permute-start.28 = (bf16[256,384]{1,0:T(8,128)(2,1)}, bf16[256,384]{1,0:T(8,128)(2,1)S(1)}, u32[]{:S(2)}, u32[]{:S(2)}) collective-permute-start(bf16[256,384]{1,0:T(8,128)(2,1)} %collective-permute-done.24.refs_19_), channel_id=1, source_target_pairs={{0,1},{1,0},{2,3},{3,2},{4,5},{5,4},{6,7},{7,6},{8,9},{9,8},{10,11... | collective-permute-start | bytes 589832 | tf_op jit(solution)/shard_map/ppermute | solution.py:544
  42.8 9.2 %collective-permute-start.14 = (bf16[256,256]{1,0:T(8,128)(2,1)}, bf16[256,256]{1,0:T(8,128)(2,1)S(1)}, u32[]{:S(2)}, u32[]{:S(2)}) collective-permute-start(bf16[256,256]{1,0:T(8,128)(2,1)} %param.8), channel_id=1, source_target_pairs={{0,8},{1,9},{2,10},{3,11},{4,12},{5,13},{6,14},{7,15},{8,0},{9,1},... | collective-permute-start | bytes 393224 | tf_op jit(solution)/shard_map/ppermute | solution.py:544
  52.1 9.0 %collective-permute-start.31 = (bf16[2,256,256]{2,1,0:T(8,128)(2,1)S(1)}, bf16[2,256,256]{2,1,0:T(8,128)(2,1)S(1)}, u32[]{:S(2)}, u32[]{:S(2)}) collective-permute-start(bf16[2,256,256]{2,1,0:T(8,128)(2,1)S(1)} %pad_maximum_fusion), channel_id=1, source_target_pairs={{0,4},{1,5},{2,6},{3,7},{4,0},{5,1},{6,2},{7,3},{8,12},{9,13},{10,... | collective-permute-start | bytes 786440 | tf_op jit(solution)/shard_map/ppermute | solution.py:523
  54.5 1.7 %collective-permute-start.29 = (bf16[272,384]{1,0:T(8,128)(2,1)S(1)}, bf16[272,384]{1,0:T(8,128)(2,1)S(1)}, u32[]{:S(2)}, u32[]{:S(2)}) collective-permute-start(bf16[272,384]{1,0:T(8,128)(2,1)S(1)} %collective-permute-done.11.refs_0_), channel_id=1, source_target_pairs={{0,1},{1,0},{2,3},{3,2},{4,5},{5,4},{6,7},{7,6},{8,9},{9,8},{10,11... | collective-permute-start | bytes 626696 | tf_op jit(solution)/shard_map/ppermute | solution.py:544
  54.5 1.7 %collective-permute-start.30 = (bf16[256,384]{1,0:T(8,128)(2,1)S(1)}, bf16[256,384]{1,0:T(8,128)(2,1)S(1)}, u32[]{:S(2)}, u32[]{:S(2)}) collective-permute-start(bf16[256,384]{1,0:T(8,128)(2,1)S(1)} %collective-permute-done.18.refs_1_), channel_id=1, source_target_pairs={{0,1},{1,0},{2,3},{3,2},{4,5},{5,4},{6,7},{7,6},{8,9},{9,8},{10,11... | collective-permute-start | bytes 589832 | tf_op jit(solution)/shard_map/ppermute | solution.py:544
  61.1 26.7 %all-to-all-start = ((bf16[16,128,256]{2,1,0:T(8,128)(2,1)}), bf16[16,128,256]{2,1,0:T(8,128)(2,1)S(1)}, u32[]{:S(2)}, u32[]{:S(2)}) async-start(bf16[16,128,256]{2,1,0:T(8,128)(2,1)} %get-tuple-element.113), calls=%async_computation | async-start | bytes 2097152 | tf_op jit(solution)/shard_map/all_to_all | solution.py:628
  65.2 8.5 %collective-permute-start.32 = (bf16[2,256,256]{2,1,0:T(8,128)(2,1)S(1)}, bf16[2,256,256]{2,1,0:T(8,128)(2,1)S(1)}, u32[]{:S(2)}, u32[]{:S(2)}) collective-permute-start(bf16[2,256,256]{2,1,0:T(8,128)(2,1)S(1)} %pad_maximum_fusion.2), channel_id=1, source_target_pairs={{0,16},{16,0},{1,17},{17,1},{2,18},{18,2},{3,19},{19,3},{4,20},{20... | collective-permute-start | bytes 786440 | tf_op jit(solution)/shard_map/ppermute | solution.py:588
  73.9 18.4 %collective-permute-start.33 = (bf16[2,256,512]{2,1,0:T(8,128)(2,1)S(1)}, bf16[2,256,512]{2,1,0:T(8,128)(2,1)S(1)}, u32[]{:S(2)}, u32[]{:S(2)}) collective-permute-start(bf16[2,256,512]{2,1,0:T(8,128)(2,1)S(1)} %join_rows.1.refs_0_), channel_id=1, source_target_pairs={{0,2},{1,3},{2,0},{3,1},{4,6},{5,7},{6,4},{7,5},{8,10},{9,11},{10,... | collective-permute-start | bytes 1572872 | tf_op jit(solution)/shard_map/ppermute | solution.py:523
  92.2 22.5 %all-to-all-start.1 = ((bf16[16,144,128]{2,1,0:T(8,128)(2,1)}), bf16[16,144,128]{2,1,0:T(8,128)(2,1)S(1)}, u32[]{:S(2)}, u32[]{:S(2)}) async-start(bf16[16,144,128]{2,1,0:T(8,128)(2,1)} %get-tuple-element.122), calls=%async_computation.1 | async-start | bytes 1179648 | tf_op jit(solution)/shard_map/all_to_all | solution.py:639
  99.2 19.1 %collective-permute-start.34 = (bf16[2,256,512]{2,1,0:T(8,128)(2,1)S(1)}, bf16[2,256,512]{2,1,0:T(8,128)(2,1)S(1)}, u32[]{:S(2)}, u32[]{:S(2)}) collective-permute-start(bf16[2,256,512]{2,1,0:T(8,128)(2,1)S(1)} %join_rows.1.refs_0_), channel_id=1, source_target_pairs={{0,1},{1,0},{2,3},{3,2},{4,5},{5,4},{6,7},{7,6},{8,9},{9,8},{10,11... | collective-permute-start | bytes 1572872 | tf_op jit(solution)/shard_map/ppermute | solution.py:523
  99.6 18.7 %collective-permute-start.35 = (bf16[2,256,512]{2,1,0:T(8,128)(2,1)S(1)}, bf16[2,256,512]{2,1,0:T(8,128)(2,1)S(1)}, u32[]{:S(2)}, u32[]{:S(2)}) collective-permute-start(bf16[2,256,512]{2,1,0:T(8,128)(2,1)S(1)} %collective-permute-done.33.refs_1_), channel_id=1, source_target_pairs={{0,1},{1,0},{2,3},{3,2},{4,5},{5,4},{6,7},{7,6},{8,9},{9,8},{10,11... | collective-permute-start | bytes 1572872 | tf_op jit(solution)/shard_map/ppermute | solution.py:523
  116.2 9.2 %collective-permute-start.37 = (bf16[256,512]{1,0:T(8,128)(2,1)S(1)}, bf16[256,512]{1,0:T(8,128)(2,1)S(1)}, u32[]{:S(2)}, u32[]{:S(2)}) collective-permute-start(bf16[256,512]{1,0:T(8,128)(2,1)S(1)} %get-tuple-element.124.refs_4_), channel_id=1, source_target_pairs={{0,16},{16,0},{1,17},{17,1},{2,18},{18,2},{3,19},{19,3},{4,20},{20... | collective-permute-start | bytes 786440 | tf_op jit(solution)/shard_map/ppermute | solution.py:643
  117.7 12.4 %collective-permute-start.36 = (bf16[256,512]{1,0:T(8,128)(2,1)S(1)}, bf16[256,512]{1,0:T(8,128)(2,1)S(1)}, u32[]{:S(2)}, u32[]{:S(2)}) collective-permute-start(bf16[256,512]{1,0:T(8,128)(2,1)S(1)} %get-tuple-element.123.refs_4_), channel_id=1, source_target_pairs={{0,16},{16,0},{1,17},{17,1},{2,18},{18,2},{3,19},{19,3},{4,20},{20... | collective-permute-start | bytes 786440 | tf_op jit(solution)/shard_map/ppermute | solution.py:643
  (15 other events, 162.8 us)

commit v5 on v4

--- a/solution.py
+++ b/solution.py
@@ -12,7 +12,7 @@
 KEEP_RATE = 0.75
 VMEM_BYTES = 8 * 1024 * 1024
 LABEL_ROWS = 16
-HALVES = 2
+HALVES = 4
 NT_DIMS = (((1,), (1,)), ((), ()))
 TN_DIMS = (((0,), (0,)), ((), ()))
 tie = lax.optimization_barrier
@@ -111,6 +111,9 @@
         at = pl.multiple_of(place_of(i, me, paired) * depth, depth)
         return pltpu.make_async_copy(x_ref.at[:, pl.ds(at, depth)], target, x_sems.at[i])
 
+    groups = 6
+    size = n_early // groups
+    step = min(512, rows)
     moves = []
     for i in range(n_early):
         span = slice(i * depth, (i + 1) * depth)
@@ -127,19 +130,22 @@
     for i in range(n_late):
         target = rest_ref.at[:, i * depth : (i + 1) * depth]
         moves.append([columns(n_early + i, target)])
-    for move in itertools.chain(*moves):
-        move.start()
+    def begin(group):
+        last = group == groups - 1
+        for move in itertools.chain(*moves[group * size :][: None if last else size]):
+            move.start()
 
     def squares(x):
         x = x.astype(jnp.float32)
         return sum(x[:, at : at + 128] * x[:, at : at + 128] for at in range(0, x.shape[1], 128))
 
-    groups = 3
-    size = n_early // groups
-    step = min(512, rows)
+    for group in range(2):
+        begin(group)
     for group in range(groups):
         for move in itertools.chain(*moves[group * size : (group + 1) * size]):
             move.wait()
+        if group + 2 < groups:
+            begin(group + 2)
         span = slice(group * size * depth, (group + 1) * size * depth)
         for start in range(0, rows, step):
             here = slice(start, start + step)
@@ -208,7 +214,9 @@
             numbers = jnp.where(
                 lane // tiles == i, place_of(i, me, paired) * tiles + lane % tiles, numbers
             )
-    base = heads * 8
+    slot = lax.broadcasted_iota(jnp.int32, (8, 128), 1)
+    down = lax.broadcasted_iota(jnp.int32, (8, 128), 0)
+    rows, laters = [0] * 4, []
     for head in range(heads):
         row = labels[head : head + 1, :]
         own = jnp.full(shape, -1, jnp.int32)
@@ -216,15 +224,17 @@
             own = jnp.where(line == t, cluster_ref[head, t], own)
         earlier = (row == own) & (numbers < me * tiles + line)
         later = jnp.max(earlier.astype(jnp.int32), axis=1, keepdims=True)
-        table_ref[head * 8 : (head + 1) * 8, :] = jnp.broadcast_to(later, (8, 128))
+        laters.append(jnp.broadcast_to(later, (8, 128)))
         member = (row == me * clus_here + line) & (line < clus_here)
         held = jnp.sum(member.astype(jnp.int32), axis=1, keepdims=True)
         last = shape[1] - 1
         first = jnp.min(jnp.where(member, numbers, last), axis=1, keepdims=True) // tiles
         second = jnp.max(jnp.where(member, numbers, 0), axis=1, keepdims=True) // tiles
-        for q, column in enumerate((held, first, second)):
-            at = base + (q * heads + head) * 8
-            table_ref[at : at + 8, :] = jnp.broadcast_to(column, (8, 128))
+        for q, column in enumerate((later, held, first, second)):
+            rows[q] += jnp.sum(jnp.where(slot == head * 8 + down, column, 0), axis=0, keepdims=True)
+    for q in range(4):
+        table_ref[q : q + 1, :] = rows[q]
+    return laters
 
 
 def late_kernel(
@@ -248,7 +258,7 @@
         marks = [ref[depth : depth + LABEL_ROWS, :128] for ref in weights[::2]]
         labels = spread_marks(marks, 16 - n_late, labels)
     labels = labels.astype(jnp.int32)
-    fill_tables(clus_here, me_ref[0], paired, labels, cluster_ref, table_ref)
+    laters = fill_tables(clus_here, me_ref[0], paired, labels, cluster_ref, table_ref)
 
     per_step = 2
     step = per_step * tile_rows
@@ -276,7 +286,7 @@
                 qkv_ref[rows, at + 2 * head_dim : at + 3 * head_dim] = value
                 for t in range(per_step):
                     owner = cluster_ref[head, start + t] // clus_here
-                    later = table_ref[head * 8 + start + t : head * 8 + start + t + 1, :]
+                    later = laters[head][start + t : start + t + 1, :]
                     span = slice(t * tile_rows, (t + 1) * tile_rows)
                     index = head * tiles + start + t
                     sent_ref[index, :, :head_dim] = key[span]
@@ -294,7 +304,6 @@
     n_late = len(late)
     tile_rows = rows // tiles
     head_dim = cols // (3 * heads)
-    table_rows = 32 * heads
     flat = [part for pair in late for part in pair]
     return pl.pallas_call(
         functools.partial(
@@ -303,7 +312,7 @@
         out_shape=(
             pltpu.HBM((rows, cols), jnp.bfloat16),
             pltpu.HBM((n_owners, tile_rows, 2 * head_dim), jnp.bfloat16),
-            pltpu.VMEM((table_rows, 128), jnp.int32),
+            pltpu.VMEM((8, 128), jnp.int32),
         ),
         in_specs=[SMEM_SPEC] * 2
         + [VMEM_SPEC] * (4 + len(flat)),
@@ -359,61 +368,80 @@
     )(in_hbm(qkv))
 
 
-def owner_kernel(base, heads, table_ref, in_ref, cent_ref, out_ref, new_ref):
+def owner_kernel(heads, full, table_ref, in_ref, cent_ref, out_ref, new_ref, held_ref, sems):
     tile_rows = in_ref.shape[1]
     head_dim = in_ref.shape[2] // 2
-    out_ref[...] = jnp.zeros_like(out_ref)
+    clus_here = cent_ref.shape[0] // heads
     line = lax.broadcasted_iota(jnp.int32, (LABEL_ROWS, tile_rows), 0)
+    entries, waits = [], []
     for c in range(cent_ref.shape[0]):
-        clus_here = cent_ref.shape[0] // heads
-        at = base + c // clus_here * 8 + c % clus_here
-        held, first, second = (table_ref[at + 8 * heads * q, 0] for q in range(3))
-        key = in_ref[first, :, :head_dim]
-
-
-        @pl.when(held > 1)
-        def _():
+        at = c // clus_here * 8 + c % clus_here
+        held, first, second = (table_ref[q, at] for q in (1, 2, 3))
+        entries.append((held, first, second))
+        move = pltpu.make_async_copy(held_ref.at[c], out_ref.at[second], sems.at[c])
+
+        def attend(c=c, first=first, second=second, move=move):
+            key = in_ref[first, :, :head_dim]
             value = in_ref[first, :, head_dim:]
             query = in_ref[second, :, head_dim:]
             scores = lax.dot_general(key, query, NT_DIMS, preferred_element_type=jnp.float32)
             weights = jnp.exp(scores * (LOGIT_SCALE / head_dim))
             mass = jnp.sum(weights, axis=0, keepdims=True)
-            out_ref[second, :head_dim, :] = lax.dot_general(
+            held_ref[c, :head_dim, :] = lax.dot_general(
                 value, weights.astype(jnp.bfloat16), TN_DIMS, preferred_element_type=jnp.float32
             ).astype(jnp.bfloat16)
             high = mass.astype(jnp.bfloat16).astype(jnp.float32)
-            out_ref[second, head_dim:, :] = jnp.where(
+            held_ref[c, head_dim:, :] = jnp.where(
                 line == 0, high, jnp.where(line == 1, mass - high, 0.0)
             ).astype(jnp.bfloat16)
-
-        other = in_ref[second, :, :head_dim]
-        first_sum = jnp.sum(key.astype(jnp.float32), axis=0, keepdims=True)
-        other_sum = jnp.sum(other.astype(jnp.float32), axis=0, keepdims=True)
+            if not full:
+                move.start()
+
+        if full:
+            attend()
+            waits.append(move)
+        else:
+            pl.when(held > 1)(attend)
+            waits.append((held > 1, move.wait))
+    if full:
+        for move in waits:
+            move.start()
+    for c, (held, first, second) in enumerate(entries):
+        first_sum, other_sum = (
+            jnp.sum(in_ref[source, :, :head_dim].astype(jnp.float32), axis=0, keepdims=True)
+            for source in (first, second)
+        )
         key_sum = jnp.where(held > 1, first_sum + other_sum, first_sum)
         count = jnp.maximum(held, 1).astype(jnp.float32) * tile_rows
         old = cent_ref[c : c + 1, :]
         moved = old + (1.0 - KEEP_RATE) * (key_sum / count - old)
         new_ref[c : c + 1, :] = jnp.where(held > 0, moved, old)
-
-
-def owner_attention(incoming, centroid_rows, table, heads):
+    for move in waits:
+        if full:
+            move.wait()
+        else:
+            pl.when(move[0])(move[1])
+
+
+def owner_attention(incoming, centroid_rows, table, heads, full):
     n, tile_rows, width = incoming.shape
     head_dim = width // 2
     returning = (n, head_dim + LABEL_ROWS, tile_rows)
+    clusters = centroid_rows.shape[0]
     return pl.pallas_call(
-        functools.partial(owner_kernel, heads * 8, heads),
+        functools.partial(owner_kernel, heads, full),
         out_shape=(
             pltpu.HBM(returning, jnp.bfloat16),
             pltpu.HBM(centroid_rows.shape, jnp.float32),
         ),
         in_specs=[SMEM_SPEC, VMEM_SPEC, whole_block(centroid_rows.shape)],
-        out_specs=(whole_block(returning), whole_block(centroid_rows.shape)),
+        out_specs=(pl.BlockSpec(memory_space=pltpu.HBM), whole_block(centroid_rows.shape)),
+        scratch_shapes=[
+            pltpu.VMEM((clusters, *returning[1:]), jnp.bfloat16),
+            pltpu.SemaphoreType.DMA((clusters,)),
+        ],
         compiler_params=pltpu.CompilerParams(vmem_limit_bytes=VMEM_BYTES),
-        cost_estimate=cost(
-            4 * centroid_rows.shape[0] * tile_rows * tile_rows * width,
-            4 * n * tile_rows * width,
-            centroid_rows.shape[0] * tile_rows * tile_rows,
-        ),
+        cost_estimate=cost(8 * tile_rows * tile_rows * width, 4 * n * tile_rows * width),
         name="owner_attention",
     )(table, in_vmem(incoming), in_hbm(centroid_rows))
 
@@ -424,7 +452,7 @@
     tile_rows = sums_ref.shape[1] // tiles
     for tile, head in itertools.product(range(tiles), range(heads)):
         owner = cluster_ref[head, tile] // clus_here
-        later = table_ref[head * 8 + tile, 0] > 0
+        later = table_ref[0, head * 8 + tile] > 0
         rows = slice(head * head_dim, (head + 1) * head_dim)
         span = slice(tile * tile_rows, (tile + 1) * tile_rows)
         sums = sums_ref[rows, span]
@@ -630,8 +658,9 @@
     if paired:
         side_pair = permute(pair, SIDE)
     incoming, sums, mass = tie((incoming, sums, mass))
+    full = heads * tiles == n_seq and 2 * heads * clus_here == n_seq
     returning, new_rows = owner_attention(
-        incoming, centroids.reshape(heads * clus_here, head_dim), table, heads
+        incoming, centroids.reshape(heads * clus_here, head_dim), table, heads, full
     )
     if paired:
         returning, side_pair = tie((returning, side_pair))

time: 133 us -> 131 us (0.985)
  waiting for transfers between devices: 57 us -> 52.9 us
  starting transfers between devices: 42.1 us -> 43.5 us
    ppermute x2 -> x4, waiting for transfers between devices: 9.31 us -> 4.59 us  [on_device(): parts = [[half, lax.ppermute(half, 'head', SWAP)] for half in halves]]
    ppermute x2 -> x4, starting transfers between devices: 2.09 us -> 4.12 us  [on_device(): parts = [[half, lax.ppermute(half, 'head', SWAP)] for half in halves]]
    pallas_call x2 -> x4, Pallas kernels: 5.02 us -> 6.92 us  [output_projection(): pl.pallas_call(functools.partial(output_kernel, len(weights), len(parts),...]
  transfers between devices with their start and end apart: 40 -> 42, of which waited for: 15 -> 19; matrix products, arithmetic and copies ran while one was open for 0% -> 0% of each run, Pallas kernels for 20% -> 22%
where the time goes in v5:
time: 131 us; the launch traced here: 130 us
  waiting for transfers between devices  52.9 us (40%)
  starting transfers between devices  43.5 us (33%)
  Pallas kernels  31.3 us (24%)
  local copies, waits for them, and re-layouts  1.48 us (1%)
    ppermute x31, starting transfers between devices, hop(): lax.ppermute(value, axis, pairs)  23.1 us
    ppermute x31, waiting for transfers between devices, hop(): lax.ppermute(value, axis, pairs)  18.5 us
    all_to_all x1, waiting for transfers between devices, on_device(): lax.all_to_all(returning, 'seq', split_axis=0, concat_axis=0, tiled=True)  15 us
    pallas_call x1, Pallas kernels, project_early(): pl.pallas_call(functools.partial(early_kernel, n_early, n_late, paired),...  8.48 us
    pallas_call x4, Pallas kernels, output_projection(): pl.pallas_call(functools.partial(output_kernel, len(weights), len(parts),...  6.92 us
    ppermute x1, waiting for transfers between devices, make_pair(): return join_rows(keep, lax.ppermute(give, 'head', SWAP))  6.89 us
    all_to_all x1, waiting for transfers between devices, on_device(): lax.all_to_all(outgoing, 'seq', split_axis=0, concat_axis=0, tiled=True)  6.85 us
    all_to_all x1, starting transfers between devices, on_device(): lax.all_to_all(returning, 'seq', split_axis=0, concat_axis=0, tiled=True)  6.53 us
  transfers between devices with their start and end apart: 42, of which 19 were waited for; matrix products, arithmetic and copies ran while one was open for 0% of the time, Pallas kernels for 22%

profile of v5, /device:TPU:0, one launch (start us, length us, event | category | flops | bytes accessed | tf_op | source)
XLA Modules:
  0.0 130.5 jit_solution(5604592106921536672)
XLA Ops:
  0.6 1.0 split_weight.1
  1.7 3.1 %collective-permute-start.15 = (bf16[256,384]{1,0:T(8,128)(2,1)S(1)}, bf16[256,384]{1,0:T(8,128)(2,1)S(1)}, u32[]{:S(2)}, u32[]{:S(2)}) collective-permute-start(bf16[256,384]{1,0:T(8,128)(2,1)S(1)} %get-tuple-element.76.refs_1_), channel_id=1, source_target_pairs={{0,4},{1,5},{2,6},{3,7},{4,8},{5,9},{6,10},{7,11},{8,12},{9,13},{1... | collective-permute-start | bytes 589832 | tf_op jit(solution)/shard_map/ppermute | solution.py:572
  4.8 1.5 %collective-permute-start.16 = (bf16[256,384]{1,0:T(8,128)(2,1)S(1)}, bf16[256,384]{1,0:T(8,128)(2,1)S(1)}, u32[]{:S(2)}, u32[]{:S(2)}) collective-permute-start(bf16[256,384]{1,0:T(8,128)(2,1)S(1)} %get-tuple-element.76.refs_1_), channel_id=1, source_target_pairs={{0,2},{1,3},{2,0},{3,1},{4,6},{5,7},{6,4},{7,5},{8,10},{9,11},{10,... | collective-permute-start | bytes 589832 | tf_op jit(solution)/shard_map/ppermute | solution.py:572
  6.3 1.6 %collective-permute-start = (bf16[272,384]{1,0:T(8,128)(2,1)S(1)}, bf16[272,384]{1,0:T(8,128)(2,1)S(1)}, u32[]{:S(2)}, u32[]{:S(2)}) collective-permute-start(bf16[272,384]{1,0:T(8,128)(2,1)S(1)} %get-tuple-element.66.refs_0_), channel_id=1, source_target_pairs={{0,4},{1,5},{2,6},{3,7},{4,8},{5,9},{6,10},{7,11},{8,12},{9,13},{1... | collective-permute-start | bytes 626696 | tf_op jit(solution)/shard_map/ppermute | solution.py:572
  7.9 0.5 collective-permute-start.1
  8.4 3.8 %collective-permute-done.15.refs_3_ = bf16[256,384]{1,0:T(8,128)(2,1)S(1)} collective-permute-done((bf16[256,384]{1,0:T(8,128)(2,1)S(1)}, bf16[256,384]{1,0:T(8,128)(2,1)S(1)}, u32[]{:S(2)}, u32[]{:S(2)}) %collective-permute-start.15) | collective-permute-done | bytes 196640 | tf_op jit(solution)/shard_map/ppermute | solution.py:572
  12.2 1.0 collective-permute-start.19
  13.2 2.5 %collective-permute-start.20 = (bf16[256,384]{1,0:T(8,128)(2,1)S(1)}, bf16[256,384]{1,0:T(8,128)(2,1)S(1)}, u32[]{:S(2)}, u32[]{:S(2)}) collective-permute-start(bf16[256,384]{1,0:T(8,128)(2,1)S(1)} %collective-permute-done.15.refs_3_), channel_id=1, source_target_pairs={{0,2},{1,3},{2,0},{3,1},{4,6},{5,7},{6,4},{7,5},{8,10},{9,11},{10,... | collective-permute-start | bytes 589832 | tf_op jit(solution)/shard_map/ppermute | solution.py:572
  16.2 1.3 %collective-permute-start.3 = (bf16[272,384]{1,0:T(8,128)(2,1)S(1)}, bf16[272,384]{1,0:T(8,128)(2,1)S(1)}, u32[]{:S(2)}, u32[]{:S(2)}) collective-permute-start(bf16[272,384]{1,0:T(8,128)(2,1)S(1)} %collective-permute-done.refs_2_), channel_id=1, source_target_pairs={{0,4},{1,5},{2,6},{3,7},{4,8},{5,9},{6,10},{7,11},{8,12},{9,13},{1... | collective-permute-start | bytes 626696 | tf_op jit(solution)/shard_map/ppermute | solution.py:572
  17.6 1.3 collective-permute-start.4
  18.9 2.6 %collective-permute-done.19.refs_9_ = bf16[256,384]{1,0:T(8,128)(2,1)S(1)} collective-permute-done((bf16[256,384]{1,0:T(8,128)(2,1)S(1)}, bf16[256,384]{1,0:T(8,128)(2,1)S(1)}, u32[]{:S(2)}, u32[]{:S(2)}) %collective-permute-start.19) | collective-permute-done | bytes 196640 | tf_op jit(solution)/shard_map/ppermute | solution.py:572
  22.0 0.8 collective-permute-done.22.refs_15_
  22.9 2.9 %collective-permute-done.3.refs_8_ = bf16[272,384]{1,0:T(8,128)(2,1)S(1)} collective-permute-done((bf16[272,384]{1,0:T(8,128)(2,1)S(1)}, bf16[272,384]{1,0:T(8,128)(2,1)S(1)}, u32[]{:S(2)}, u32[]{:S(2)}) %collective-permute-start.3) | collective-permute-done | bytes 208928 | tf_op jit(solution)/shard_map/ppermute | solution.py:572
  25.8 2.2 %collective-permute-start.24 = (bf16[256,384]{1,0:T(8,128)(2,1)S(1)}, bf16[256,384]{1,0:T(8,128)(2,1)}, u32[]{:S(2)}, u32[]{:S(2)}) collective-permute-start(bf16[256,384]{1,0:T(8,128)(2,1)S(1)} %collective-permute-done.19.refs_9_), channel_id=1, source_target_pairs={{0,2},{1,3},{2,0},{3,1},{4,6},{5,7},{6,4},{7,5},{8,10},{9,11},{10,... | collective-permute-start | bytes 589832 | tf_op jit(solution)/shard_map/ppermute | solution.py:572
  28.5 3.1 %collective-permute-done.23.refs_17_ = bf16[256,384]{1,0:T(8,128)(2,1)S(1)} collective-permute-done((bf16[256,384]{1,0:T(8,128)(2,1)S(1)}, bf16[256,384]{1,0:T(8,128)(2,1)S(1)}, u32[]{:S(2)}, u32[]{:S(2)}) %collective-permute-start.23) | collective-permute-done | bytes 196640 | tf_op jit(solution)/shard_map/ppermute | solution.py:572
  31.6 3.3 %collective-permute-start.8 = (bf16[272,384]{1,0:T(8,128)(2,1)S(1)}, bf16[272,384]{1,0:T(8,128)(2,1)}, u32[]{:S(2)}, u32[]{:S(2)}) collective-permute-start(bf16[272,384]{1,0:T(8,128)(2,1)S(1)} %collective-permute-done.3.refs_8_), channel_id=1, source_target_pairs={{0,2},{1,3},{2,0},{3,1},{4,6},{5,7},{6,4},{7,5},{8,10},{9,11},{10,... | collective-permute-start | bytes 626696 | tf_op jit(solution)/shard_map/ppermute | solution.py:572
  35.6 2.8 %collective-permute-done.7.refs_16_ = bf16[272,384]{1,0:T(8,128)(2,1)S(1)} collective-permute-done((bf16[272,384]{1,0:T(8,128)(2,1)S(1)}, bf16[272,384]{1,0:T(8,128)(2,1)S(1)}, u32[]{:S(2)}, u32[]{:S(2)}) %collective-permute-start.7) | collective-permute-done | bytes 208928 | tf_op jit(solution)/shard_map/ppermute | solution.py:572
  38.8 0.7 copy-done.11
  39.5 0.7 copy-done.12
  40.2 2.0 %collective-permute-start.11 = (bf16[272,384]{1,0:T(8,128)(2,1)S(1)}, bf16[272,384]{1,0:T(8,128)(2,1)S(1)}, u32[]{:S(2)}, u32[]{:S(2)}) collective-permute-start(bf16[272,384]{1,0:T(8,128)(2,1)S(1)} %collective-permute-done.7.refs_16_), channel_id=1, source_target_pairs={{0,2},{1,3},{2,0},{3,1},{4,6},{5,7},{6,4},{7,5},{8,10},{9,11},{10,... | collective-permute-start | bytes 626696 | tf_op jit(solution)/shard_map/ppermute | solution.py:572
  42.2 0.5 collective-permute-start.13
  43.0 8.5 %project_early.1 = (f32[1024,768]{1,0:T(8,128)S(1)}, bf16[1024,1024]{1,0:T(8,128)(2,1)S(1)}, f32[16,128]{1,0:T(8,128)S(1)}, f32[1024,128]{1,0:T(8,128)S(1)}) custom-call(s32[1]{0:T(128)} %bitcast.me_ref, bf16[1024,4096]{1,0:T(8,128)(2,1)} %x_ref.1, bf16[272,384]{1,0:T(8,128)(2,1)} %copy-done, bf16[256,384]{1,0:T(8,128)(2,1)} %copy-done.1, ...), custom_call_target="tpu_custom_call" | custom-call | flops 1 | bytes 1 | tf_op jit(solution)/shard_map/project_early/pallas_call | solution.py:175
  51.9 2.1 %collective-permute-start.31 = (bf16[2,256,256]{2,1,0:T(8,128)(2,1)S(1)}, bf16[2,256,256]{2,1,0:T(8,128)(2,1)S(1)}, u32[]{:S(2)}, u32[]{:S(2)}) collective-permute-start(bf16[2,256,256]{2,1,0:T(8,128)(2,1)S(1)} %pad_maximum_fusion), channel_id=1, source_target_pairs={{0,4},{1,5},{2,6},{3,7},{4,0},{5,1},{6,2},{7,3},{8,12},{9,13},{10,... | collective-permute-start | bytes 786440 | tf_op jit(solution)/shard_map/ppermute | solution.py:551
  53.9 0.5 collective-permute-start.30
  54.4 1.2 collective-permute-done.30.refs_7_
  55.7 4.2 %project_late.1 = (bf16[1024,768]{1,0:T(8,128)(2,1)}, bf16[16,128,256]{2,1,0:T(8,128)(2,1)}, s32[8,128]{1,0:T(8,128)S(1)}) custom-call(s32[1]{0:T(128)} %bitcast.me_ref, s32[2,8]{1,0:T(2,128)} %cluster_ref.3, f32[1024,768]{1,0:T(8,128)S(1)} %get-tuple-element.100.acc_ref, bf16[1024,1024]{1,0:T(8,128)(2,1)S(1)} %get-tuple-element.101.rest_ref, ...), custom_call_target="tpu_custom_call" | custom-call | flops 1 | bytes 1 | tf_op jit(solution)/shard_map/project_late/pallas_call | solution.py:308
  59.9 0.7 collective-permute-done.31
  60.6 3.8 %all-to-all-start = ((bf16[16,128,256]{2,1,0:T(8,128)(2,1)}), bf16[16,128,256]{2,1,0:T(8,128)(2,1)S(1)}, u32[]{:S(2)}, u32[]{:S(2)}) async-start(bf16[16,128,256]{2,1,0:T(8,128)(2,1)} %get-tuple-element.115), calls=%async_computation | async-start | bytes 2097152 | tf_op jit(solution)/shard_map/all_to_all | solution.py:656
  64.7 1.6 %collective-permute-start.32 = (bf16[2,256,256]{2,1,0:T(8,128)(2,1)S(1)}, bf16[2,256,256]{2,1,0:T(8,128)(2,1)S(1)}, u32[]{:S(2)}, u32[]{:S(2)}) collective-permute-start(bf16[2,256,256]{2,1,0:T(8,128)(2,1)S(1)} %pad_maximum_fusion.2), channel_id=1, source_target_pairs={{0,16},{16,0},{1,17},{17,1},{2,18},{18,2},{3,19},{19,3},{4,20},{20... | collective-permute-start | bytes 786440 | tf_op jit(solution)/shard_map/ppermute | solution.py:616
  66.3 6.9 %collective-permute-done.32.got_ref = bf16[2,256,256]{2,1,0:T(8,128)(2,1)S(1)} collective-permute-done((bf16[2,256,256]{2,1,0:T(8,128)(2,1)S(1)}, bf16[2,256,256]{2,1,0:T(8,128)(2,1)S(1)}, u32[]{:S(2)}, u32[]{:S(2)}) %collective-permute-start.32) | collective-permute-done | bytes 262176 | tf_op jit(solution)/shard_map/ppermute | solution.py:616
  73.3 1.7 %collective-permute-start.33 = (bf16[2,256,512]{2,1,0:T(8,128)(2,1)S(1)}, bf16[2,256,512]{2,1,0:T(8,128)(2,1)S(1)}, u32[]{:S(2)}, u32[]{:S(2)}) collective-permute-start(bf16[2,256,512]{2,1,0:T(8,128)(2,1)S(1)} %join_rows.1.refs_0_), channel_id=1, source_target_pairs={{0,2},{1,3},{2,0},{3,1},{4,6},{5,7},{6,4},{7,5},{8,10},{9,11},{10,... | collective-permute-start | bytes 1572872 | tf_op jit(solution)/shard_map/ppermute | solution.py:551
  75.1 5.4 %inner_attention.1 = (f32[256,1024]{1,0:T(8,128)}, f32[16,1024]{1,0:T(8,128)}) custom-call(bf16[1024,768]{1,0:T(8,128)(2,1)} %get-tuple-element.116.qkv_ref), custom_call_target="tpu_custom_call" | custom-call | flops 1 | bytes 1 | tf_op jit(solution)/shard_map/inner_attention/pallas_call | solution.py:355
  80.4 6.9 %all-to-all-done.in_ref = bf16[16,128,256]{2,1,0:T(8,128)(2,1)S(1)} async-done(((bf16[16,128,256]{2,1,0:T(8,128)(2,1)}), bf16[16,128,256]{2,1,0:T(8,128)(2,1)S(1)}, u32[]{:S(2)}, u32[]{:S(2)}) %all-to-all-start) | async-done | bytes 1048608 | tf_op jit(solution)/shard_map/all_to_all | solution.py:656
  87.3 3.6 %owner_attention.1 = (bf16[16,144,128]{2,1,0:T(8,128)(2,1)}, f32[8,128]{1,0:T(8,128)}) custom-call(s32[8,128]{1,0:T(8,128)S(1)} %get-tuple-element.114.table_ref, bf16[16,128,256]{2,1,0:T(8,128)(2,1)S(1)} %all-to-all-done.in_ref, f32[8,128]{1,0:T(8,128)} %bitcast.9), custom_call_target="tpu_custom_call" | custom-call | flops 1 | bytes 1 | tf_op jit(solution)/shard_map/owner_attention/pallas_call | solution.py:431
  91.3 6.5 %all-to-all-start.1 = ((bf16[16,144,128]{2,1,0:T(8,128)(2,1)}), bf16[16,144,128]{2,1,0:T(8,128)(2,1)S(1)}, u32[]{:S(2)}, u32[]{:S(2)}) async-start(bf16[16,144,128]{2,1,0:T(8,128)(2,1)} %get-tuple-element.124), calls=%async_computation.1 | async-start | bytes 1179648 | tf_op jit(solution)/shard_map/all_to_all | solution.py:668
  98.4 15.0 %all-to-all-done.1.back_ref = bf16[16,144,128]{2,1,0:T(8,128)(2,1)S(1)} async-done(((bf16[16,144,128]{2,1,0:T(8,128)(2,1)}), bf16[16,144,128]{2,1,0:T(8,128)(2,1)S(1)}, u32[]{:S(2)}, u32[]{:S(2)}) %all-to-all-start.1) | async-done | bytes 589856 | tf_op jit(solution)/shard_map/all_to_all | solution.py:668
  113.4 1.5 %merge_attention.1 = (bf16[256,256]{1,0:T(8,128)(2,1)S(1)}, bf16[256,256]{1,0:T(8,128)(2,1)S(1)}, bf16[256,256]{1,0:T(8,128)(2,1)S(1)}, bf16[256,256]{1,0:T(8,128)(2,1)S(1)}) custom-call(s32[2,8]{1,0:T(2,128)} %cluster_ref.3, s32[8,128]{1,0:T(8,128)S(1)} %get-tuple-element.114.table_ref, f32[256,1024]{1,0:T(8,128)} %get-tuple-element.122.sums_ref, ...), custom_call_target="tpu_custom_call" | custom-call | flops 1 | bytes 1 | tf_op jit(solution)/shard_map/merge_attention/pallas_call | solution.py:469
  114.8 1.6 %collective-permute-start.39 = (bf16[256,256]{1,0:T(8,128)(2,1)S(1)}, bf16[256,256]{1,0:T(8,128)(2,1)S(1)}, u32[]{:S(2)}, u32[]{:S(2)}) collective-permute-start(bf16[256,256]{1,0:T(8,128)(2,1)S(1)} %get-tuple-element.128.refs_4_), channel_id=1, source_target_pairs={{0,16},{16,0},{1,17},{17,1},{2,18},{18,2},{3,19},{19,3},{4,20},{20... | collective-permute-start | bytes 393224 | tf_op jit(solution)/shard_map/ppermute | solution.py:672
  116.4 0.5 collective-permute-start.38
  116.9 1.5 %collective-permute-start.37 = (bf16[256,256]{1,0:T(8,128)(2,1)S(1)}, bf16[256,256]{1,0:T(8,128)(2,1)S(1)}, u32[]{:S(2)}, u32[]{:S(2)}) collective-permute-start(bf16[256,256]{1,0:T(8,128)(2,1)S(1)} %get-tuple-element.126.refs_4_), channel_id=1, source_target_pairs={{0,16},{16,0},{1,17},{17,1},{2,18},{18,2},{3,19},{19,3},{4,20},{20... | collective-permute-start | bytes 393224 | tf_op jit(solution)/shard_map/ppermute | solution.py:672
  118.4 0.5 collective-permute-start.36
  119.0 2.3 %collective-permute-done.39.refs_5_ = bf16[256,256]{1,0:T(8,128)(2,1)S(1)} collective-permute-done((bf16[256,256]{1,0:T(8,128)(2,1)S(1)}, bf16[256,256]{1,0:T(8,128)(2,1)S(1)}, u32[]{:S(2)}, u32[]{:S(2)}) %collective-permute-start.39) | collective-permute-done | bytes 131104 | tf_op jit(solution)/shard_map/ppermute | solution.py:672
  121.3 1.7 %output_projection.4.refs_6_ = bf16[2048,1024]{1,0:T(8,128)(2,1)} custom-call(s32[1]{0:T(128)} %bitcast.me_ref, bf16[2,256,512]{2,1,0:T(8,128)(2,1)S(1)} %join_rows.1.refs_0_, bf16[2,256,512]{2,1,0:T(8,128)(2,1)S(1)} %collective-permute-done.33.refs_1_, bf16[2,256,512]{2,1,0:T(8,128)(2,1)S(1)} %collective-permute-done.34.refs_2_, ...), custom_call_target="tpu_custom_call" | custom-call | flops 1 | bytes 1 | tf_op jit(solution)/shard_map/output_projection/pallas_call | solution.py:515
  123.0 1.1 collective-permute-done.38.refs_5_
  124.1 1.7 %output_projection.5.refs_6_ = bf16[2048,1024]{1,0:T(8,128)(2,1)} custom-call(s32[1]{0:T(128)} %bitcast.me_ref, bf16[2,256,512]{2,1,0:T(8,128)(2,1)S(1)} %join_rows.1.refs_0_, bf16[2,256,512]{2,1,0:T(8,128)(2,1)S(1)} %collective-permute-done.33.refs_1_, bf16[2,256,512]{2,1,0:T(8,128)(2,1)S(1)} %collective-permute-done.34.refs_2_, ...), custom_call_target="tpu_custom_call", output_to_operand_aliasing={{}: (7, {})} | custom-call | flops 1 | bytes 1 | tf_op jit(solution)/shard_map/output_projection/pallas_call | solution.py:515
  125.8 1.1 collective-permute-done.37.refs_5_
  126.9 1.7 %output_projection.6.refs_6_ = bf16[2048,1024]{1,0:T(8,128)(2,1)} custom-call(s32[1]{0:T(128)} %bitcast.me_ref, bf16[2,256,512]{2,1,0:T(8,128)(2,1)S(1)} %join_rows.1.refs_0_, bf16[2,256,512]{2,1,0:T(8,128)(2,1)S(1)} %collective-permute-done.33.refs_1_, bf16[2,256,512]{2,1,0:T(8,128)(2,1)S(1)} %collective-permute-done.34.refs_2_, ...), custom_call_target="tpu_custom_call", output_to_operand_aliasing={{}: (7, {})} | custom-call | flops 1 | bytes 1 | tf_op jit(solution)/shard_map/output_projection/pallas_call | solution.py:515
  128.7 1.7 %output_projection.7 = bf16[2048,1024]{1,0:T(8,128)(2,1)} custom-call(s32[1]{0:T(128)} %bitcast.me_ref, bf16[2,256,512]{2,1,0:T(8,128)(2,1)S(1)} %join_rows.1.refs_0_, bf16[2,256,512]{2,1,0:T(8,128)(2,1)S(1)} %collective-permute-done.33.refs_1_, bf16[2,256,512]{2,1,0:T(8,128)(2,1)S(1)} %collective-permute-done.34.refs_2_, ...), custom_call_target="tpu_custom_call", output_to_operand_aliasing={{}: (7, {})} | custom-call | flops 1 | bytes 1 | tf_op jit(solution)/shard_map/output_projection/pallas_call | solution.py:515
  (98 shorter events, 4.8 us)
Async XLA Ops:
  1.7 41.2 %copy-start = (bf16[272,384]{1,0:T(8,128)(2,1)}, bf16[272,384]{1,0:T(8,128)(2,1)S(1)}, u32[]{:S(2)}) copy-start(bf16[272,384]{1,0:T(8,128)(2,1)S(1)} %get-tuple-element.66.refs_0_) | copy-start | bytes 626692
  1.7 41.2 %copy-start.1 = (bf16[256,384]{1,0:T(8,128)(2,1)}, bf16[256,384]{1,0:T(8,128)(2,1)S(1)}, u32[]{:S(2)}) copy-start(bf16[256,384]{1,0:T(8,128)(2,1)S(1)} %get-tuple-element.76.refs_1_) | copy-start | bytes 589828
  1.7 10.4 %collective-permute-start.15 = (bf16[256,384]{1,0:T(8,128)(2,1)S(1)}, bf16[256,384]{1,0:T(8,128)(2,1)S(1)}, u32[]{:S(2)}, u32[]{:S(2)}) collective-permute-start(bf16[256,384]{1,0:T(8,128)(2,1)S(1)} %get-tuple-element.76.refs_1_), channel_id=1, source_target_pairs={{0,4},{1,5},{2,6},{3,7},{4,8},{5,9},{6,10},{7,11},{8,12},{9,13},{1... | collective-permute-start | bytes 589832 | tf_op jit(solution)/shard_map/ppermute | solution.py:572
  4.8 7.4 %collective-permute-start.16 = (bf16[256,384]{1,0:T(8,128)(2,1)S(1)}, bf16[256,384]{1,0:T(8,128)(2,1)S(1)}, u32[]{:S(2)}, u32[]{:S(2)}) collective-permute-start(bf16[256,384]{1,0:T(8,128)(2,1)S(1)} %get-tuple-element.76.refs_1_), channel_id=1, source_target_pairs={{0,2},{1,3},{2,0},{3,1},{4,6},{5,7},{6,4},{7,5},{8,10},{9,11},{10,... | collective-permute-start | bytes 589832 | tf_op jit(solution)/shard_map/ppermute | solution.py:572
  6.3 5.9 %collective-permute-start.17 = (bf16[256,384]{1,0:T(8,128)(2,1)S(1)}, bf16[256,384]{1,0:T(8,128)(2,1)S(1)}, u32[]{:S(2)}, u32[]{:S(2)}) collective-permute-start(bf16[256,384]{1,0:T(8,128)(2,1)S(1)} %get-tuple-element.76.refs_1_), channel_id=1, source_target_pairs={{0,1},{1,0},{2,3},{3,2},{4,5},{5,4},{6,7},{7,6},{8,9},{9,8},{10,11... | collective-permute-start | bytes 589832 | tf_op jit(solution)/shard_map/ppermute | solution.py:572
  6.3 9.9 %collective-permute-start = (bf16[272,384]{1,0:T(8,128)(2,1)S(1)}, bf16[272,384]{1,0:T(8,128)(2,1)S(1)}, u32[]{:S(2)}, u32[]{:S(2)}) collective-permute-start(bf16[272,384]{1,0:T(8,128)(2,1)S(1)} %get-tuple-element.66.refs_0_), channel_id=1, source_target_pairs={{0,4},{1,5},{2,6},{3,7},{4,8},{5,9},{6,10},{7,11},{8,12},{9,13},{1... | collective-permute-start | bytes 626696 | tf_op jit(solution)/shard_map/ppermute | solution.py:572
  7.9 8.3 %collective-permute-start.1 = (bf16[272,384]{1,0:T(8,128)(2,1)S(1)}, bf16[272,384]{1,0:T(8,128)(2,1)S(1)}, u32[]{:S(2)}, u32[]{:S(2)}) collective-permute-start(bf16[272,384]{1,0:T(8,128)(2,1)S(1)} %get-tuple-element.66.refs_0_), channel_id=1, source_target_pairs={{0,2},{1,3},{2,0},{3,1},{4,6},{5,7},{6,4},{7,5},{8,10},{9,11},{10,... | collective-permute-start | bytes 626696 | tf_op jit(solution)/shard_map/ppermute | solution.py:572
  12.1 4.1 %collective-permute-start.2 = (bf16[272,384]{1,0:T(8,128)(2,1)S(1)}, bf16[272,384]{1,0:T(8,128)(2,1)S(1)}, u32[]{:S(2)}, u32[]{:S(2)}) collective-permute-start(bf16[272,384]{1,0:T(8,128)(2,1)S(1)} %get-tuple-element.66.refs_0_), channel_id=1, source_target_pairs={{0,1},{1,0},{2,3},{3,2},{4,5},{5,4},{6,7},{7,6},{8,9},{9,8},{10,11... | collective-permute-start | bytes 626696 | tf_op jit(solution)/shard_map/ppermute | solution.py:572
  12.2 30.5 %copy-start.14 = (bf16[256,384]{1,0:T(8,128)(2,1)}, bf16[256,384]{1,0:T(8,128)(2,1)S(1)}, u32[]{:S(2)}) copy-start(bf16[256,384]{1,0:T(8,128)(2,1)S(1)} %collective-permute-done.16.refs_5_) | copy-start | bytes 589828
  12.2 30.6 %copy-start.15 = (bf16[256,384]{1,0:T(8,128)(2,1)}, bf16[256,384]{1,0:T(8,128)(2,1)S(1)}, u32[]{:S(2)}) copy-start(bf16[256,384]{1,0:T(8,128)(2,1)S(1)} %collective-permute-done.17.refs_7_) | copy-start | bytes 589828
  12.2 9.3 %collective-permute-start.19 = (bf16[256,384]{1,0:T(8,128)(2,1)S(1)}, bf16[256,384]{1,0:T(8,128)(2,1)S(1)}, u32[]{:S(2)}, u32[]{:S(2)}) collective-permute-start(bf16[256,384]{1,0:T(8,128)(2,1)S(1)} %collective-permute-done.15.refs_3_), channel_id=1, source_target_pairs={{0,4},{1,5},{2,6},{3,7},{4,8},{5,9},{6,10},{7,11},{8,12},{9,13},{1... | collective-permute-start | bytes 589832 | tf_op jit(solution)/shard_map/ppermute | solution.py:572
  13.2 8.3 %collective-permute-start.20 = (bf16[256,384]{1,0:T(8,128)(2,1)S(1)}, bf16[256,384]{1,0:T(8,128)(2,1)S(1)}, u32[]{:S(2)}, u32[]{:S(2)}) collective-permute-start(bf16[256,384]{1,0:T(8,128)(2,1)S(1)} %collective-permute-done.15.refs_3_), channel_id=1, source_target_pairs={{0,2},{1,3},{2,0},{3,1},{4,6},{5,7},{6,4},{7,5},{8,10},{9,11},{10,... | collective-permute-start | bytes 589832 | tf_op jit(solution)/shard_map/ppermute | solution.py:572
  16.2 26.7 %copy-start.3 = (bf16[272,384]{1,0:T(8,128)(2,1)}, bf16[272,384]{1,0:T(8,128)(2,1)S(1)}, u32[]{:S(2)}) copy-start(bf16[272,384]{1,0:T(8,128)(2,1)S(1)} %collective-permute-done.refs_2_) | copy-start | bytes 626692
  16.2 5.8 %collective-permute-start.21 = (bf16[256,384]{1,0:T(8,128)(2,1)S(1)}, bf16[256,384]{1,0:T(8,128)(2,1)S(1)}, u32[]{:S(2)}, u32[]{:S(2)}) collective-permute-start(bf16[256,384]{1,0:T(8,128)(2,1)S(1)} %collective-permute-done.15.refs_3_), channel_id=1, source_target_pairs={{0,1},{1,0},{2,3},{3,2},{4,5},{5,4},{6,7},{7,6},{8,9},{9,8},{10,11... | collective-permute-start | bytes 589832 | tf_op jit(solution)/shard_map/ppermute | solution.py:572
  16.2 26.7 %copy-start.4 = (bf16[272,384]{1,0:T(8,128)(2,1)}, bf16[272,384]{1,0:T(8,128)(2,1)S(1)}, u32[]{:S(2)}) copy-start(bf16[272,384]{1,0:T(8,128)(2,1)S(1)} %collective-permute-done.1.refs_4_) | copy-start | bytes 626692
  16.2 9.6 %collective-permute-start.3 = (bf16[272,384]{1,0:T(8,128)(2,1)S(1)}, bf16[272,384]{1,0:T(8,128)(2,1)S(1)}, u32[]{:S(2)}, u32[]{:S(2)}) collective-permute-start(bf16[272,384]{1,0:T(8,128)(2,1)S(1)} %collective-permute-done.refs_2_), channel_id=1, source_target_pairs={{0,4},{1,5},{2,6},{3,7},{4,8},{5,9},{6,10},{7,11},{8,12},{9,13},{1... | collective-permute-start | bytes 626696 | tf_op jit(solution)/shard_map/ppermute | solution.py:572
  17.6 10.4 %collective-permute-start.4 = (bf16[272,384]{1,0:T(8,128)(2,1)S(1)}, bf16[272,384]{1,0:T(8,128)(2,1)S(1)}, u32[]{:S(2)}, u32[]{:S(2)}) collective-permute-start(bf16[272,384]{1,0:T(8,128)(2,1)S(1)} %collective-permute-done.refs_2_), channel_id=1, source_target_pairs={{0,2},{1,3},{2,0},{3,1},{4,6},{5,7},{6,4},{7,5},{8,10},{9,11},{10,... | collective-permute-start | bytes 626696 | tf_op jit(solution)/shard_map/ppermute | solution.py:572
  21.4 1.4 %collective-permute-start.22 = (bf16[256,384]{1,0:T(8,128)(2,1)S(1)}, bf16[256,384]{1,0:T(8,128)(2,1)S(1)}, u32[]{:S(2)}, u32[]{:S(2)}) collective-permute-start(bf16[256,384]{1,0:T(8,128)(2,1)S(1)} %collective-permute-done.16.refs_5_), channel_id=1, source_target_pairs={{0,1},{1,0},{2,3},{3,2},{4,5},{5,4},{6,7},{7,6},{8,9},{9,8},{10,11... | collective-permute-start | bytes 589832 | tf_op jit(solution)/shard_map/ppermute | solution.py:572
  21.5 6.5 %collective-permute-start.5 = (bf16[272,384]{1,0:T(8,128)(2,1)S(1)}, bf16[272,384]{1,0:T(8,128)(2,1)S(1)}, u32[]{:S(2)}, u32[]{:S(2)}) collective-permute-start(bf16[272,384]{1,0:T(8,128)(2,1)S(1)} %collective-permute-done.refs_2_), channel_id=1, source_target_pairs={{0,1},{1,0},{2,3},{3,2},{4,5},{5,4},{6,7},{7,6},{8,9},{9,8},{10,11... | collective-permute-start | bytes 626696 | tf_op jit(solution)/shard_map/ppermute | solution.py:572
  22.0 6.5 %collective-permute-start.6 = (bf16[272,384]{1,0:T(8,128)(2,1)S(1)}, bf16[272,384]{1,0:T(8,128)(2,1)S(1)}, u32[]{:S(2)}, u32[]{:S(2)}) collective-permute-start(bf16[272,384]{1,0:T(8,128)(2,1)S(1)} %collective-permute-done.1.refs_4_), channel_id=1, source_target_pairs={{0,1},{1,0},{2,3},{3,2},{4,5},{5,4},{6,7},{7,6},{8,9},{9,8},{10,11... | collective-permute-start | bytes 626696 | tf_op jit(solution)/shard_map/ppermute | solution.py:572
  22.9 8.7 %collective-permute-start.23 = (bf16[256,384]{1,0:T(8,128)(2,1)S(1)}, bf16[256,384]{1,0:T(8,128)(2,1)S(1)}, u32[]{:S(2)}, u32[]{:S(2)}) collective-permute-start(bf16[256,384]{1,0:T(8,128)(2,1)S(1)} %collective-permute-done.19.refs_9_), channel_id=1, source_target_pairs={{0,4},{1,5},{2,6},{3,7},{4,8},{5,9},{6,10},{7,11},{8,12},{9,13},{1... | collective-permute-start | bytes 589832 | tf_op jit(solution)/shard_map/ppermute | solution.py:572
  25.8 9.1 %collective-permute-start.24 = (bf16[256,384]{1,0:T(8,128)(2,1)S(1)}, bf16[256,384]{1,0:T(8,128)(2,1)}, u32[]{:S(2)}, u32[]{:S(2)}) collective-permute-start(bf16[256,384]{1,0:T(8,128)(2,1)S(1)} %collective-permute-done.19.refs_9_), channel_id=1, source_target_pairs={{0,2},{1,3},{2,0},{3,1},{4,6},{5,7},{6,4},{7,5},{8,10},{9,11},{10,... | collective-permute-start | bytes 589832 | tf_op jit(solution)/shard_map/ppermute | solution.py:572
  28.0 7.0 %collective-permute-start.25 = (bf16[256,384]{1,0:T(8,128)(2,1)S(1)}, bf16[256,384]{1,0:T(8,128)(2,1)S(1)}, u32[]{:S(2)}, u32[]{:S(2)}) collective-permute-start(bf16[256,384]{1,0:T(8,128)(2,1)S(1)} %collective-permute-done.19.refs_9_), channel_id=1, source_target_pairs={{0,1},{1,0},{2,3},{3,2},{4,5},{5,4},{6,7},{7,6},{8,9},{9,8},{10,11... | collective-permute-start | bytes 589832 | tf_op jit(solution)/shard_map/ppermute | solution.py:572
  28.0 7.5 %collective-permute-start.26 = (bf16[256,384]{1,0:T(8,128)(2,1)S(1)}, bf16[256,384]{1,0:T(8,128)(2,1)S(1)}, u32[]{:S(2)}, u32[]{:S(2)}) collective-permute-start(bf16[256,384]{1,0:T(8,128)(2,1)S(1)} %collective-permute-done.20.refs_11_), channel_id=1, source_target_pairs={{0,1},{1,0},{2,3},{3,2},{4,5},{5,4},{6,7},{7,6},{8,9},{9,8},{10,11... | collective-permute-start | bytes 589832 | tf_op jit(solution)/shard_map/ppermute | solution.py:572
  28.5 9.8 %collective-permute-start.7 = (bf16[272,384]{1,0:T(8,128)(2,1)S(1)}, bf16[272,384]{1,0:T(8,128)(2,1)S(1)}, u32[]{:S(2)}, u32[]{:S(2)}) collective-permute-start(bf16[272,384]{1,0:T(8,128)(2,1)S(1)} %collective-permute-done.3.refs_8_), channel_id=1, source_target_pairs={{0,4},{1,5},{2,6},{3,7},{4,8},{5,9},{6,10},{7,11},{8,12},{9,13},{1... | collective-permute-start | bytes 626696 | tf_op jit(solution)/shard_map/ppermute | solution.py:572
  31.6 7.2 %collective-permute-start.8 = (bf16[272,384]{1,0:T(8,128)(2,1)S(1)}, bf16[272,384]{1,0:T(8,128)(2,1)}, u32[]{:S(2)}, u32[]{:S(2)}) collective-permute-start(bf16[272,384]{1,0:T(8,128)(2,1)S(1)} %collective-permute-done.3.refs_8_), channel_id=1, source_target_pairs={{0,2},{1,3},{2,0},{3,1},{4,6},{5,7},{6,4},{7,5},{8,10},{9,11},{10,... | collective-permute-start | bytes 626696 | tf_op jit(solution)/shard_map/ppermute | solution.py:572
  34.9 3.9 %collective-permute-start.9 = (bf16[272,384]{1,0:T(8,128)(2,1)S(1)}, bf16[272,384]{1,0:T(8,128)(2,1)S(1)}, u32[]{:S(2)}, u32[]{:S(2)}) collective-permute-start(bf16[272,384]{1,0:T(8,128)(2,1)S(1)} %collective-permute-done.3.refs_8_), channel_id=1, source_target_pairs={{0,1},{1,0},{2,3},{3,2},{4,5},{5,4},{6,7},{7,6},{8,9},{9,8},{10,11... | collective-permute-start | bytes 626696 | tf_op jit(solution)/shard_map/ppermute | solution.py:572
  35.0 4.5 %collective-permute-start.10 = (bf16[272,384]{1,0:T(8,128)(2,1)S(1)}, bf16[272,384]{1,0:T(8,128)(2,1)S(1)}, u32[]{:S(2)}, u32[]{:S(2)}) collective-permute-start(bf16[272,384]{1,0:T(8,128)(2,1)S(1)} %collective-permute-done.4.refs_10_), channel_id=1, source_target_pairs={{0,1},{1,0},{2,3},{3,2},{4,5},{5,4},{6,7},{7,6},{8,9},{9,8},{10,11... | collective-permute-start | bytes 626696 | tf_op jit(solution)/shard_map/ppermute | solution.py:572
  35.5 7.2 %collective-permute-start.18 = (bf16[256,384]{1,0:T(8,128)(2,1)S(1)}, bf16[256,384]{1,0:T(8,128)(2,1)S(1)}, u32[]{:S(2)}, u32[]{:S(2)}) collective-permute-start(bf16[256,384]{1,0:T(8,128)(2,1)S(1)} %collective-permute-done.16.refs_5_), channel_id=1, source_target_pairs={{0,12},{1,13},{2,14},{3,15},{4,0},{5,1},{6,2},{7,3},{8,4},{9,5},{1... | collective-permute-start | bytes 589832 | tf_op jit(solution)/shard_map/ppermute | solution.py:572
  38.3 4.4 %collective-permute-start.27 = (bf16[256,384]{1,0:T(8,128)(2,1)S(1)}, bf16[256,384]{1,0:T(8,128)(2,1)S(1)}, u32[]{:S(2)}, u32[]{:S(2)}) collective-permute-start(bf16[256,384]{1,0:T(8,128)(2,1)S(1)} %collective-permute-done.23.refs_17_), channel_id=1, source_target_pairs={{0,1},{1,0},{2,3},{3,2},{4,5},{5,4},{6,7},{7,6},{8,9},{9,8},{10,11... | collective-permute-start | bytes 589832 | tf_op jit(solution)/shard_map/ppermute | solution.py:572
  40.2 11.6 %collective-permute-start.11 = (bf16[272,384]{1,0:T(8,128)(2,1)S(1)}, bf16[272,384]{1,0:T(8,128)(2,1)S(1)}, u32[]{:S(2)}, u32[]{:S(2)}) collective-permute-start(bf16[272,384]{1,0:T(8,128)(2,1)S(1)} %collective-permute-done.7.refs_16_), channel_id=1, source_target_pairs={{0,2},{1,3},{2,0},{3,1},{4,6},{5,7},{6,4},{7,5},{8,10},{9,11},{10,... | collective-permute-start | bytes 626696 | tf_op jit(solution)/shard_map/ppermute | solution.py:572
  42.2 9.6 %collective-permute-start.12 = (bf16[272,384]{1,0:T(8,128)(2,1)S(1)}, bf16[272,384]{1,0:T(8,128)(2,1)S(1)}, u32[]{:S(2)}, u32[]{:S(2)}) collective-permute-start(bf16[272,384]{1,0:T(8,128)(2,1)S(1)} %collective-permute-done.7.refs_16_), channel_id=1, source_target_pairs={{0,1},{1,0},{2,3},{3,2},{4,5},{5,4},{6,7},{7,6},{8,9},{9,8},{10,11... | collective-permute-start | bytes 626696 | tf_op jit(solution)/shard_map/ppermute | solution.py:572
  42.2 9.6 %collective-permute-start.13 = (bf16[272,384]{1,0:T(8,128)(2,1)}, bf16[272,384]{1,0:T(8,128)(2,1)S(1)}, u32[]{:S(2)}, u32[]{:S(2)}) collective-permute-start(bf16[272,384]{1,0:T(8,128)(2,1)} %collective-permute-done.8.refs_18_), channel_id=1, source_target_pairs={{0,1},{1,0},{2,3},{3,2},{4,5},{5,4},{6,7},{7,6},{8,9},{9,8},{10,11... | collective-permute-start | bytes 626696 | tf_op jit(solution)/shard_map/ppermute | solution.py:572
  42.7 8.8 %collective-permute-start.28 = (bf16[256,384]{1,0:T(8,128)(2,1)}, bf16[256,384]{1,0:T(8,128)(2,1)S(1)}, u32[]{:S(2)}, u32[]{:S(2)}) collective-permute-start(bf16[256,384]{1,0:T(8,128)(2,1)} %collective-permute-done.24.refs_19_), channel_id=1, source_target_pairs={{0,1},{1,0},{2,3},{3,2},{4,5},{5,4},{6,7},{7,6},{8,9},{9,8},{10,11... | collective-permute-start | bytes 589832 | tf_op jit(solution)/shard_map/ppermute | solution.py:572
  42.8 9.0 %collective-permute-start.14 = (bf16[256,256]{1,0:T(8,128)(2,1)}, bf16[256,256]{1,0:T(8,128)(2,1)S(1)}, u32[]{:S(2)}, u32[]{:S(2)}) collective-permute-start(bf16[256,256]{1,0:T(8,128)(2,1)} %param.8), channel_id=1, source_target_pairs={{0,8},{1,9},{2,10},{3,11},{4,12},{5,13},{6,14},{7,15},{8,0},{9,1},... | collective-permute-start | bytes 393224 | tf_op jit(solution)/shard_map/ppermute | solution.py:572
  51.9 8.8 %collective-permute-start.31 = (bf16[2,256,256]{2,1,0:T(8,128)(2,1)S(1)}, bf16[2,256,256]{2,1,0:T(8,128)(2,1)S(1)}, u32[]{:S(2)}, u32[]{:S(2)}) collective-permute-start(bf16[2,256,256]{2,1,0:T(8,128)(2,1)S(1)} %pad_maximum_fusion), channel_id=1, source_target_pairs={{0,4},{1,5},{2,6},{3,7},{4,0},{5,1},{6,2},{7,3},{8,12},{9,13},{10,... | collective-permute-start | bytes 786440 | tf_op jit(solution)/shard_map/ppermute | solution.py:551
  53.9 1.7 %collective-permute-start.29 = (bf16[272,384]{1,0:T(8,128)(2,1)S(1)}, bf16[272,384]{1,0:T(8,128)(2,1)S(1)}, u32[]{:S(2)}, u32[]{:S(2)}) collective-permute-start(bf16[272,384]{1,0:T(8,128)(2,1)S(1)} %collective-permute-done.11.refs_0_), channel_id=1, source_target_pairs={{0,1},{1,0},{2,3},{3,2},{4,5},{5,4},{6,7},{7,6},{8,9},{9,8},{10,11... | collective-permute-start | bytes 626696 | tf_op jit(solution)/shard_map/ppermute | solution.py:572
  53.9 1.7 %collective-permute-start.30 = (bf16[256,384]{1,0:T(8,128)(2,1)S(1)}, bf16[256,384]{1,0:T(8,128)(2,1)S(1)}, u32[]{:S(2)}, u32[]{:S(2)}) collective-permute-start(bf16[256,384]{1,0:T(8,128)(2,1)S(1)} %collective-permute-done.18.refs_1_), channel_id=1, source_target_pairs={{0,1},{1,0},{2,3},{3,2},{4,5},{5,4},{6,7},{7,6},{8,9},{9,8},{10,11... | collective-permute-start | bytes 589832 | tf_op jit(solution)/shard_map/ppermute | solution.py:572
  60.6 26.7 %all-to-all-start = ((bf16[16,128,256]{2,1,0:T(8,128)(2,1)}), bf16[16,128,256]{2,1,0:T(8,128)(2,1)S(1)}, u32[]{:S(2)}, u32[]{:S(2)}) async-start(bf16[16,128,256]{2,1,0:T(8,128)(2,1)} %get-tuple-element.115), calls=%async_computation | async-start | bytes 2097152 | tf_op jit(solution)/shard_map/all_to_all | solution.py:656
  64.7 8.5 %collective-permute-start.32 = (bf16[2,256,256]{2,1,0:T(8,128)(2,1)S(1)}, bf16[2,256,256]{2,1,0:T(8,128)(2,1)S(1)}, u32[]{:S(2)}, u32[]{:S(2)}) collective-permute-start(bf16[2,256,256]{2,1,0:T(8,128)(2,1)S(1)} %pad_maximum_fusion.2), channel_id=1, source_target_pairs={{0,16},{16,0},{1,17},{17,1},{2,18},{18,2},{3,19},{19,3},{4,20},{20... | collective-permute-start | bytes 786440 | tf_op jit(solution)/shard_map/ppermute | solution.py:616
  73.3 17.9 %collective-permute-start.33 = (bf16[2,256,512]{2,1,0:T(8,128)(2,1)S(1)}, bf16[2,256,512]{2,1,0:T(8,128)(2,1)S(1)}, u32[]{:S(2)}, u32[]{:S(2)}) collective-permute-start(bf16[2,256,512]{2,1,0:T(8,128)(2,1)S(1)} %join_rows.1.refs_0_), channel_id=1, source_target_pairs={{0,2},{1,3},{2,0},{3,1},{4,6},{5,7},{6,4},{7,5},{8,10},{9,11},{10,... | collective-permute-start | bytes 1572872 | tf_op jit(solution)/shard_map/ppermute | solution.py:551
  91.3 22.1 %all-to-all-start.1 = ((bf16[16,144,128]{2,1,0:T(8,128)(2,1)}), bf16[16,144,128]{2,1,0:T(8,128)(2,1)S(1)}, u32[]{:S(2)}, u32[]{:S(2)}) async-start(bf16[16,144,128]{2,1,0:T(8,128)(2,1)} %get-tuple-element.124), calls=%async_computation.1 | async-start | bytes 1179648 | tf_op jit(solution)/shard_map/all_to_all | solution.py:668
  97.8 20.6 %collective-permute-start.34 = (bf16[2,256,512]{2,1,0:T(8,128)(2,1)S(1)}, bf16[2,256,512]{2,1,0:T(8,128)(2,1)S(1)}, u32[]{:S(2)}, u32[]{:S(2)}) collective-permute-start(bf16[2,256,512]{2,1,0:T(8,128)(2,1)S(1)} %join_rows.1.refs_0_), channel_id=1, source_target_pairs={{0,1},{1,0},{2,3},{3,2},{4,5},{5,4},{6,7},{7,6},{8,9},{9,8},{10,11... | collective-permute-start | bytes 1572872 | tf_op jit(solution)/shard_map/ppermute | solution.py:551
  98.2 20.7 %collective-permute-start.35 = (bf16[2,256,512]{2,1,0:T(8,128)(2,1)S(1)}, bf16[2,256,512]{2,1,0:T(8,128)(2,1)S(1)}, u32[]{:S(2)}, u32[]{:S(2)}) collective-permute-start(bf16[2,256,512]{2,1,0:T(8,128)(2,1)S(1)} %collective-permute-done.33.refs_1_), channel_id=1, source_target_pairs={{0,1},{1,0},{2,3},{3,2},{4,5},{5,4},{6,7},{7,6},{8,9},{9,8},{10,11... | collective-permute-start | bytes 1572872 | tf_op jit(solution)/shard_map/ppermute | solution.py:551
  114.8 6.4 %collective-permute-start.39 = (bf16[256,256]{1,0:T(8,128)(2,1)S(1)}, bf16[256,256]{1,0:T(8,128)(2,1)S(1)}, u32[]{:S(2)}, u32[]{:S(2)}) collective-permute-start(bf16[256,256]{1,0:T(8,128)(2,1)S(1)} %get-tuple-element.128.refs_4_), channel_id=1, source_target_pairs={{0,16},{16,0},{1,17},{17,1},{2,18},{18,2},{3,19},{19,3},{4,20},{20... | collective-permute-start | bytes 393224 | tf_op jit(solution)/shard_map/ppermute | solution.py:672
  116.4 7.7 %collective-permute-start.38 = (bf16[256,256]{1,0:T(8,128)(2,1)S(1)}, bf16[256,256]{1,0:T(8,128)(2,1)S(1)}, u32[]{:S(2)}, u32[]{:S(2)}) collective-permute-start(bf16[256,256]{1,0:T(8,128)(2,1)S(1)} %get-tuple-element.127.refs_4_), channel_id=1, source_target_pairs={{0,16},{16,0},{1,17},{17,1},{2,18},{18,2},{3,19},{19,3},{4,20},{20... | collective-permute-start | bytes 393224 | tf_op jit(solution)/shard_map/ppermute | solution.py:672
  116.9 10.0 %collective-permute-start.37 = (bf16[256,256]{1,0:T(8,128)(2,1)S(1)}, bf16[256,256]{1,0:T(8,128)(2,1)S(1)}, u32[]{:S(2)}, u32[]{:S(2)}) collective-permute-start(bf16[256,256]{1,0:T(8,128)(2,1)S(1)} %get-tuple-element.126.refs_4_), channel_id=1, source_target_pairs={{0,16},{16,0},{1,17},{17,1},{2,18},{18,2},{3,19},{19,3},{4,20},{20... | collective-permute-start | bytes 393224 | tf_op jit(solution)/shard_map/ppermute | solution.py:672
  118.4 10.3 %collective-permute-start.36 = (bf16[256,256]{1,0:T(8,128)(2,1)S(1)}, bf16[256,256]{1,0:T(8,128)(2,1)S(1)}, u32[]{:S(2)}, u32[]{:S(2)}) collective-permute-start(bf16[256,256]{1,0:T(8,128)(2,1)S(1)} %get-tuple-element.125.refs_4_), channel_id=1, source_target_pairs={{0,16},{16,0},{1,17},{17,1},{2,18},{18,2},{3,19},{19,3},{4,20},{20... | collective-permute-start | bytes 393224 | tf_op jit(solution)/shard_map/ppermute | solution.py:672
  (17 other events, 212.6 us)

commit v6 on v5

--- a/solution.py
+++ b/solution.py
@@ -13,6 +13,7 @@
 VMEM_BYTES = 8 * 1024 * 1024
 LABEL_ROWS = 16
 HALVES = 4
+SETTLED = 20
 NT_DIMS = (((1,), (1,)), ((), ()))
 TN_DIMS = (((0,), (0,)), ((), ()))
 tie = lax.optimization_barrier
@@ -180,7 +181,7 @@
             pltpu.VMEM((LABEL_ROWS, 128), jnp.float32),
             pltpu.VMEM((rows, 128), jnp.float32),
         ),
-        in_specs=[SMEM_SPEC] + [in_place] * (1 + len(flat)),
+        in_specs=[SMEM_SPEC] + [in_place] * (1 + SETTLED) + [VMEM_SPEC] * (len(flat) - SETTLED),
         out_specs=(VMEM_SPEC,) * 4,
         scratch_shapes=[
             pltpu.VMEM((n_early * depth, 2 * half), jnp.bfloat16),
@@ -194,7 +195,12 @@
             4 * rows * n_early * depth * half, 2 * rows * width + 8 * rows * half
         ),
         name="project_early",
-    )(me, in_hbm(tokens), *map(in_hbm, flat))
+    )(
+        me,
+        in_hbm(tokens),
+        *map(in_hbm, flat[:SETTLED]),
+        *map(in_vmem, flat[SETTLED:]),
+    )
 
 
 def unit_rows(values):

time: 131 us -> 131 us (level)
  local copies, waits for them, and re-layouts: 1.48 us -> 0.1 us
    unnamed x46 -> x34, local copies, waits for them, and re-layouts: 1.46 us -> 0.07 us
  transfers between devices with their start and end apart: 42 -> 42, of which waited for: 19 -> 20; matrix products, arithmetic and copies ran while one was open for 0% -> 0% of each run, Pallas kernels for 22% -> 22%
where the time goes in v6:
time: 131 us; the launch traced here: 130 us
  waiting for transfers between devices  54 us (41%)
  starting transfers between devices  43.6 us (33%)
  Pallas kernels  31.4 us (24%)
    ppermute x31, starting transfers between devices, hop(): lax.ppermute(value, axis, pairs)  23.1 us
    ppermute x31, waiting for transfers between devices, hop(): lax.ppermute(value, axis, pairs)  19.7 us
    all_to_all x1, waiting for transfers between devices, on_device(): lax.all_to_all(returning, 'seq', split_axis=0, concat_axis=0, tiled=True)  15 us
    pallas_call x1, Pallas kernels, project_early(): pl.pallas_call(functools.partial(early_kernel, n_early, n_late, paired),...  8.56 us
    pallas_call x4, Pallas kernels, output_projection(): pl.pallas_call(functools.partial(output_kernel, len(weights), len(parts),...  6.91 us
    all_to_all x1, waiting for transfers between devices, on_device(): lax.all_to_all(outgoing, 'seq', split_axis=0, concat_axis=0, tiled=True)  6.87 us
    ppermute x1, waiting for transfers between devices, make_pair(): return join_rows(keep, lax.ppermute(give, 'head', SWAP))  6.83 us
    all_to_all x1, starting transfers between devices, on_device(): lax.all_to_all(returning, 'seq', split_axis=0, concat_axis=0, tiled=True)  6.57 us
  transfers between devices with their start and end apart: 42, of which 20 were waited for; matrix products, arithmetic and copies ran while one was open for 0% of the time, Pallas kernels for 22%

profile of v6, /device:TPU:0, one launch (start us, length us, event | category | flops | bytes accessed | tf_op | source)
XLA Modules:
  0.0 130.3 jit_solution(12499361189185273152)
XLA Ops:
  0.6 1.0 split_weight.1
  1.7 3.1 %collective-permute-start.15 = (bf16[256,384]{1,0:T(8,128)(2,1)S(1)}, bf16[256,384]{1,0:T(8,128)(2,1)S(1)}, u32[]{:S(2)}, u32[]{:S(2)}) collective-permute-start(bf16[256,384]{1,0:T(8,128)(2,1)S(1)} %get-tuple-element.76.refs_1_), channel_id=1, source_target_pairs={{0,4},{1,5},{2,6},{3,7},{4,8},{5,9},{6,10},{7,11},{8,12},{9,13},{1... | collective-permute-start | bytes 589832 | tf_op jit(solution)/shard_map/ppermute | solution.py:578
  4.8 1.5 %collective-permute-start.16 = (bf16[256,384]{1,0:T(8,128)(2,1)S(1)}, bf16[256,384]{1,0:T(8,128)(2,1)S(1)}, u32[]{:S(2)}, u32[]{:S(2)}) collective-permute-start(bf16[256,384]{1,0:T(8,128)(2,1)S(1)} %get-tuple-element.76.refs_1_), channel_id=1, source_target_pairs={{0,2},{1,3},{2,0},{3,1},{4,6},{5,7},{6,4},{7,5},{8,10},{9,11},{10,... | collective-permute-start | bytes 589832 | tf_op jit(solution)/shard_map/ppermute | solution.py:578
  6.3 1.6 %collective-permute-start = (bf16[272,384]{1,0:T(8,128)(2,1)S(1)}, bf16[272,384]{1,0:T(8,128)(2,1)S(1)}, u32[]{:S(2)}, u32[]{:S(2)}) collective-permute-start(bf16[272,384]{1,0:T(8,128)(2,1)S(1)} %get-tuple-element.66.refs_0_), channel_id=1, source_target_pairs={{0,4},{1,5},{2,6},{3,7},{4,8},{5,9},{6,10},{7,11},{8,12},{9,13},{1... | collective-permute-start | bytes 626696 | tf_op jit(solution)/shard_map/ppermute | solution.py:578
  8.4 3.8 %collective-permute-done.15.refs_3_ = bf16[256,384]{1,0:T(8,128)(2,1)S(1)} collective-permute-done((bf16[256,384]{1,0:T(8,128)(2,1)S(1)}, bf16[256,384]{1,0:T(8,128)(2,1)S(1)}, u32[]{:S(2)}, u32[]{:S(2)}) %collective-permute-start.15) | collective-permute-done | bytes 196640 | tf_op jit(solution)/shard_map/ppermute | solution.py:578
  12.2 1.0 collective-permute-start.19
  13.2 2.5 %collective-permute-start.20 = (bf16[256,384]{1,0:T(8,128)(2,1)S(1)}, bf16[256,384]{1,0:T(8,128)(2,1)S(1)}, u32[]{:S(2)}, u32[]{:S(2)}) collective-permute-start(bf16[256,384]{1,0:T(8,128)(2,1)S(1)} %collective-permute-done.15.refs_3_), channel_id=1, source_target_pairs={{0,2},{1,3},{2,0},{3,1},{4,6},{5,7},{6,4},{7,5},{8,10},{9,11},{10,... | collective-permute-start | bytes 589832 | tf_op jit(solution)/shard_map/ppermute | solution.py:578
  16.2 1.3 %collective-permute-start.3 = (bf16[272,384]{1,0:T(8,128)(2,1)S(1)}, bf16[272,384]{1,0:T(8,128)(2,1)S(1)}, u32[]{:S(2)}, u32[]{:S(2)}) collective-permute-start(bf16[272,384]{1,0:T(8,128)(2,1)S(1)} %collective-permute-done.refs_2_), channel_id=1, source_target_pairs={{0,4},{1,5},{2,6},{3,7},{4,8},{5,9},{6,10},{7,11},{8,12},{9,13},{1... | collective-permute-start | bytes 626696 | tf_op jit(solution)/shard_map/ppermute | solution.py:578
  17.6 1.3 collective-permute-start.4
  18.9 2.6 %collective-permute-done.19.refs_9_ = bf16[256,384]{1,0:T(8,128)(2,1)S(1)} collective-permute-done((bf16[256,384]{1,0:T(8,128)(2,1)S(1)}, bf16[256,384]{1,0:T(8,128)(2,1)S(1)}, u32[]{:S(2)}, u32[]{:S(2)}) %collective-permute-start.19) | collective-permute-done | bytes 196640 | tf_op jit(solution)/shard_map/ppermute | solution.py:578
  21.5 0.6 collective-permute-start.5
  22.1 0.8 collective-permute-done.22.refs_15_
  22.9 2.9 %collective-permute-done.3.refs_8_ = bf16[272,384]{1,0:T(8,128)(2,1)S(1)} collective-permute-done((bf16[272,384]{1,0:T(8,128)(2,1)S(1)}, bf16[272,384]{1,0:T(8,128)(2,1)S(1)}, u32[]{:S(2)}, u32[]{:S(2)}) %collective-permute-start.3) | collective-permute-done | bytes 208928 | tf_op jit(solution)/shard_map/ppermute | solution.py:578
  25.8 2.2 %collective-permute-start.24 = (bf16[256,384]{1,0:T(8,128)(2,1)S(1)}, bf16[256,384]{1,0:T(8,128)(2,1)}, u32[]{:S(2)}, u32[]{:S(2)}) collective-permute-start(bf16[256,384]{1,0:T(8,128)(2,1)S(1)} %collective-permute-done.19.refs_9_), channel_id=1, source_target_pairs={{0,2},{1,3},{2,0},{3,1},{4,6},{5,7},{6,4},{7,5},{8,10},{9,11},{10,... | collective-permute-start | bytes 589832 | tf_op jit(solution)/shard_map/ppermute | solution.py:578
  28.1 0.5 collective-permute-start.26
  28.6 3.0 %collective-permute-done.23.refs_17_ = bf16[256,384]{1,0:T(8,128)(2,1)S(1)} collective-permute-done((bf16[256,384]{1,0:T(8,128)(2,1)S(1)}, bf16[256,384]{1,0:T(8,128)(2,1)S(1)}, u32[]{:S(2)}, u32[]{:S(2)}) %collective-permute-start.23) | collective-permute-done | bytes 196640 | tf_op jit(solution)/shard_map/ppermute | solution.py:578
  31.6 3.3 %collective-permute-start.8 = (bf16[272,384]{1,0:T(8,128)(2,1)S(1)}, bf16[272,384]{1,0:T(8,128)(2,1)}, u32[]{:S(2)}, u32[]{:S(2)}) collective-permute-start(bf16[272,384]{1,0:T(8,128)(2,1)S(1)} %collective-permute-done.3.refs_8_), channel_id=1, source_target_pairs={{0,2},{1,3},{2,0},{3,1},{4,6},{5,7},{6,4},{7,5},{8,10},{9,11},{10,... | collective-permute-start | bytes 626696 | tf_op jit(solution)/shard_map/ppermute | solution.py:578
  35.4 3.1 %collective-permute-done.7.refs_16_ = bf16[272,384]{1,0:T(8,128)(2,1)} collective-permute-done((bf16[272,384]{1,0:T(8,128)(2,1)S(1)}, bf16[272,384]{1,0:T(8,128)(2,1)}, u32[]{:S(2)}, u32[]{:S(2)}) %collective-permute-start.7) | collective-permute-done | bytes 208928 | tf_op jit(solution)/shard_map/ppermute | solution.py:578
  38.9 2.0 %collective-permute-start.11 = (bf16[272,384]{1,0:T(8,128)(2,1)}, bf16[272,384]{1,0:T(8,128)(2,1)S(1)}, u32[]{:S(2)}, u32[]{:S(2)}) collective-permute-start(bf16[272,384]{1,0:T(8,128)(2,1)} %collective-permute-done.7.refs_16_), channel_id=1, source_target_pairs={{0,2},{1,3},{2,0},{3,1},{4,6},{5,7},{6,4},{7,5},{8,10},{9,11},{10,... | collective-permute-start | bytes 626696 | tf_op jit(solution)/shard_map/ppermute | solution.py:578
  40.9 0.5 collective-permute-start.13
  41.4 1.1 collective-permute-done.18.refs_1_
  42.7 8.6 %project_early.1 = (f32[1024,768]{1,0:T(8,128)S(1)}, bf16[1024,1024]{1,0:T(8,128)(2,1)S(1)}, f32[16,128]{1,0:T(8,128)S(1)}, f32[1024,128]{1,0:T(8,128)S(1)}) custom-call(s32[1]{0:T(128)} %bitcast.me_ref, bf16[1024,4096]{1,0:T(8,128)(2,1)} %x_ref.1, bf16[272,384]{1,0:T(8,128)(2,1)} %copy-done, bf16[256,384]{1,0:T(8,128)(2,1)} %copy-done.1, ...), custom_call_target="tpu_custom_call" | custom-call | flops 1 | bytes 1 | tf_op jit(solution)/shard_map/project_early/pallas_call | solution.py:176
  51.8 2.0 %collective-permute-start.31 = (bf16[2,256,256]{2,1,0:T(8,128)(2,1)S(1)}, bf16[2,256,256]{2,1,0:T(8,128)(2,1)S(1)}, u32[]{:S(2)}, u32[]{:S(2)}) collective-permute-start(bf16[2,256,256]{2,1,0:T(8,128)(2,1)S(1)} %pad_maximum_fusion), channel_id=1, source_target_pairs={{0,4},{1,5},{2,6},{3,7},{4,0},{5,1},{6,2},{7,3},{8,12},{9,13},{10,... | collective-permute-start | bytes 786440 | tf_op jit(solution)/shard_map/ppermute | solution.py:557
  53.8 0.5 collective-permute-start.30
  54.3 1.2 collective-permute-done.30.refs_7_
  55.5 4.3 %project_late.1 = (bf16[1024,768]{1,0:T(8,128)(2,1)}, bf16[16,128,256]{2,1,0:T(8,128)(2,1)}, s32[8,128]{1,0:T(8,128)S(1)}) custom-call(s32[1]{0:T(128)} %bitcast.me_ref, s32[2,8]{1,0:T(2,128)} %cluster_ref.3, f32[1024,768]{1,0:T(8,128)S(1)} %get-tuple-element.100.acc_ref, bf16[1024,1024]{1,0:T(8,128)(2,1)S(1)} %get-tuple-element.101.rest_ref, ...), custom_call_target="tpu_custom_call" | custom-call | flops 1 | bytes 1 | tf_op jit(solution)/shard_map/project_late/pallas_call | solution.py:314
  59.8 0.7 collective-permute-done.31
  60.5 3.8 %all-to-all-start = ((bf16[16,128,256]{2,1,0:T(8,128)(2,1)}), bf16[16,128,256]{2,1,0:T(8,128)(2,1)S(1)}, u32[]{:S(2)}, u32[]{:S(2)}) async-start(bf16[16,128,256]{2,1,0:T(8,128)(2,1)} %get-tuple-element.115), calls=%async_computation | async-start | bytes 2097152 | tf_op jit(solution)/shard_map/all_to_all | solution.py:662
  64.5 1.6 %collective-permute-start.32 = (bf16[2,256,256]{2,1,0:T(8,128)(2,1)S(1)}, bf16[2,256,256]{2,1,0:T(8,128)(2,1)S(1)}, u32[]{:S(2)}, u32[]{:S(2)}) collective-permute-start(bf16[2,256,256]{2,1,0:T(8,128)(2,1)S(1)} %pad_maximum_fusion.2), channel_id=1, source_target_pairs={{0,16},{16,0},{1,17},{17,1},{2,18},{18,2},{3,19},{19,3},{4,20},{20... | collective-permute-start | bytes 786440 | tf_op jit(solution)/shard_map/ppermute | solution.py:622
  66.1 6.8 %collective-permute-done.32.got_ref = bf16[2,256,256]{2,1,0:T(8,128)(2,1)S(1)} collective-permute-done((bf16[2,256,256]{2,1,0:T(8,128)(2,1)S(1)}, bf16[2,256,256]{2,1,0:T(8,128)(2,1)S(1)}, u32[]{:S(2)}, u32[]{:S(2)}) %collective-permute-start.32) | collective-permute-done | bytes 262176 | tf_op jit(solution)/shard_map/ppermute | solution.py:622
  73.1 1.7 %collective-permute-start.33 = (bf16[2,256,512]{2,1,0:T(8,128)(2,1)S(1)}, bf16[2,256,512]{2,1,0:T(8,128)(2,1)S(1)}, u32[]{:S(2)}, u32[]{:S(2)}) collective-permute-start(bf16[2,256,512]{2,1,0:T(8,128)(2,1)S(1)} %join_rows.1.refs_0_), channel_id=1, source_target_pairs={{0,2},{1,3},{2,0},{3,1},{4,6},{5,7},{6,4},{7,5},{8,10},{9,11},{10,... | collective-permute-start | bytes 1572872 | tf_op jit(solution)/shard_map/ppermute | solution.py:557
  74.9 5.4 %inner_attention.1 = (f32[256,1024]{1,0:T(8,128)}, f32[16,1024]{1,0:T(8,128)}) custom-call(bf16[1024,768]{1,0:T(8,128)(2,1)} %get-tuple-element.116.qkv_ref), custom_call_target="tpu_custom_call" | custom-call | flops 1 | bytes 1 | tf_op jit(solution)/shard_map/inner_attention/pallas_call | solution.py:361
  80.2 6.9 %all-to-all-done.in_ref = bf16[16,128,256]{2,1,0:T(8,128)(2,1)S(1)} async-done(((bf16[16,128,256]{2,1,0:T(8,128)(2,1)}), bf16[16,128,256]{2,1,0:T(8,128)(2,1)S(1)}, u32[]{:S(2)}, u32[]{:S(2)}) %all-to-all-start) | async-done | bytes 1048608 | tf_op jit(solution)/shard_map/all_to_all | solution.py:662
  87.1 3.6 %owner_attention.1 = (bf16[16,144,128]{2,1,0:T(8,128)(2,1)}, f32[8,128]{1,0:T(8,128)}) custom-call(s32[8,128]{1,0:T(8,128)S(1)} %get-tuple-element.114.table_ref, bf16[16,128,256]{2,1,0:T(8,128)(2,1)S(1)} %all-to-all-done.in_ref, f32[8,128]{1,0:T(8,128)} %bitcast.9), custom_call_target="tpu_custom_call" | custom-call | flops 1 | bytes 1 | tf_op jit(solution)/shard_map/owner_attention/pallas_call | solution.py:437
  91.1 6.6 %all-to-all-start.1 = ((bf16[16,144,128]{2,1,0:T(8,128)(2,1)}), bf16[16,144,128]{2,1,0:T(8,128)(2,1)S(1)}, u32[]{:S(2)}, u32[]{:S(2)}) async-start(bf16[16,144,128]{2,1,0:T(8,128)(2,1)} %get-tuple-element.124), calls=%async_computation.1 | async-start | bytes 1179648 | tf_op jit(solution)/shard_map/all_to_all | solution.py:674
  98.2 15.0 %all-to-all-done.1.back_ref = bf16[16,144,128]{2,1,0:T(8,128)(2,1)S(1)} async-done(((bf16[16,144,128]{2,1,0:T(8,128)(2,1)}), bf16[16,144,128]{2,1,0:T(8,128)(2,1)S(1)}, u32[]{:S(2)}, u32[]{:S(2)}) %all-to-all-start.1) | async-done | bytes 589856 | tf_op jit(solution)/shard_map/all_to_all | solution.py:674
  113.2 1.5 %merge_attention.1 = (bf16[256,256]{1,0:T(8,128)(2,1)S(1)}, bf16[256,256]{1,0:T(8,128)(2,1)S(1)}, bf16[256,256]{1,0:T(8,128)(2,1)S(1)}, bf16[256,256]{1,0:T(8,128)(2,1)S(1)}) custom-call(s32[2,8]{1,0:T(2,128)} %cluster_ref.3, s32[8,128]{1,0:T(8,128)S(1)} %get-tuple-element.114.table_ref, f32[256,1024]{1,0:T(8,128)} %get-tuple-element.122.sums_ref, ...), custom_call_target="tpu_custom_call" | custom-call | flops 1 | bytes 1 | tf_op jit(solution)/shard_map/merge_attention/pallas_call | solution.py:475
  114.6 1.6 %collective-permute-start.39 = (bf16[256,256]{1,0:T(8,128)(2,1)S(1)}, bf16[256,256]{1,0:T(8,128)(2,1)S(1)}, u32[]{:S(2)}, u32[]{:S(2)}) collective-permute-start(bf16[256,256]{1,0:T(8,128)(2,1)S(1)} %get-tuple-element.128.refs_4_), channel_id=1, source_target_pairs={{0,16},{16,0},{1,17},{17,1},{2,18},{18,2},{3,19},{19,3},{4,20},{20... | collective-permute-start | bytes 393224 | tf_op jit(solution)/shard_map/ppermute | solution.py:678
  116.2 0.5 collective-permute-start.38
  116.7 1.5 %collective-permute-start.37 = (bf16[256,256]{1,0:T(8,128)(2,1)S(1)}, bf16[256,256]{1,0:T(8,128)(2,1)S(1)}, u32[]{:S(2)}, u32[]{:S(2)}) collective-permute-start(bf16[256,256]{1,0:T(8,128)(2,1)S(1)} %get-tuple-element.126.refs_4_), channel_id=1, source_target_pairs={{0,16},{16,0},{1,17},{17,1},{2,18},{18,2},{3,19},{19,3},{4,20},{20... | collective-permute-start | bytes 393224 | tf_op jit(solution)/shard_map/ppermute | solution.py:678
  118.2 0.5 collective-permute-start.36
  118.8 2.3 %collective-permute-done.39.refs_5_ = bf16[256,256]{1,0:T(8,128)(2,1)S(1)} collective-permute-done((bf16[256,256]{1,0:T(8,128)(2,1)S(1)}, bf16[256,256]{1,0:T(8,128)(2,1)S(1)}, u32[]{:S(2)}, u32[]{:S(2)}) %collective-permute-start.39) | collective-permute-done | bytes 131104 | tf_op jit(solution)/shard_map/ppermute | solution.py:678
  121.1 1.7 %output_projection.4.refs_6_ = bf16[2048,1024]{1,0:T(8,128)(2,1)} custom-call(s32[1]{0:T(128)} %bitcast.me_ref, bf16[2,256,512]{2,1,0:T(8,128)(2,1)S(1)} %join_rows.1.refs_0_, bf16[2,256,512]{2,1,0:T(8,128)(2,1)S(1)} %collective-permute-done.33.refs_1_, bf16[2,256,512]{2,1,0:T(8,128)(2,1)S(1)} %collective-permute-done.34.refs_2_, ...), custom_call_target="tpu_custom_call" | custom-call | flops 1 | bytes 1 | tf_op jit(solution)/shard_map/output_projection/pallas_call | solution.py:521
  122.8 1.1 collective-permute-done.38.refs_5_
  123.9 1.7 %output_projection.5.refs_6_ = bf16[2048,1024]{1,0:T(8,128)(2,1)} custom-call(s32[1]{0:T(128)} %bitcast.me_ref, bf16[2,256,512]{2,1,0:T(8,128)(2,1)S(1)} %join_rows.1.refs_0_, bf16[2,256,512]{2,1,0:T(8,128)(2,1)S(1)} %collective-permute-done.33.refs_1_, bf16[2,256,512]{2,1,0:T(8,128)(2,1)S(1)} %collective-permute-done.34.refs_2_, ...), custom_call_target="tpu_custom_call", output_to_operand_aliasing={{}: (7, {})} | custom-call | flops 1 | bytes 1 | tf_op jit(solution)/shard_map/output_projection/pallas_call | solution.py:521
  125.6 1.1 collective-permute-done.37.refs_5_
  126.7 1.7 %output_projection.6.refs_6_ = bf16[2048,1024]{1,0:T(8,128)(2,1)} custom-call(s32[1]{0:T(128)} %bitcast.me_ref, bf16[2,256,512]{2,1,0:T(8,128)(2,1)S(1)} %join_rows.1.refs_0_, bf16[2,256,512]{2,1,0:T(8,128)(2,1)S(1)} %collective-permute-done.33.refs_1_, bf16[2,256,512]{2,1,0:T(8,128)(2,1)S(1)} %collective-permute-done.34.refs_2_, ...), custom_call_target="tpu_custom_call", output_to_operand_aliasing={{}: (7, {})} | custom-call | flops 1 | bytes 1 | tf_op jit(solution)/shard_map/output_projection/pallas_call | solution.py:521
  128.6 1.7 %output_projection.7 = bf16[2048,1024]{1,0:T(8,128)(2,1)} custom-call(s32[1]{0:T(128)} %bitcast.me_ref, bf16[2,256,512]{2,1,0:T(8,128)(2,1)S(1)} %join_rows.1.refs_0_, bf16[2,256,512]{2,1,0:T(8,128)(2,1)S(1)} %collective-permute-done.33.refs_1_, bf16[2,256,512]{2,1,0:T(8,128)(2,1)S(1)} %collective-permute-done.34.refs_2_, ...), custom_call_target="tpu_custom_call", output_to_operand_aliasing={{}: (7, {})} | custom-call | flops 1 | bytes 1 | tf_op jit(solution)/shard_map/output_projection/pallas_call | solution.py:521
  (86 shorter events, 4.1 us)
Async XLA Ops:
  1.7 40.9 %copy-start = (bf16[272,384]{1,0:T(8,128)(2,1)}, bf16[272,384]{1,0:T(8,128)(2,1)S(1)}, u32[]{:S(2)}) copy-start(bf16[272,384]{1,0:T(8,128)(2,1)S(1)} %get-tuple-element.66.refs_0_) | copy-start | bytes 626692
  1.7 40.9 %copy-start.1 = (bf16[256,384]{1,0:T(8,128)(2,1)}, bf16[256,384]{1,0:T(8,128)(2,1)S(1)}, u32[]{:S(2)}) copy-start(bf16[256,384]{1,0:T(8,128)(2,1)S(1)} %get-tuple-element.76.refs_1_) | copy-start | bytes 589828
  1.7 10.4 %collective-permute-start.15 = (bf16[256,384]{1,0:T(8,128)(2,1)S(1)}, bf16[256,384]{1,0:T(8,128)(2,1)S(1)}, u32[]{:S(2)}, u32[]{:S(2)}) collective-permute-start(bf16[256,384]{1,0:T(8,128)(2,1)S(1)} %get-tuple-element.76.refs_1_), channel_id=1, source_target_pairs={{0,4},{1,5},{2,6},{3,7},{4,8},{5,9},{6,10},{7,11},{8,12},{9,13},{1... | collective-permute-start | bytes 589832 | tf_op jit(solution)/shard_map/ppermute | solution.py:578
  4.8 7.4 %collective-permute-start.16 = (bf16[256,384]{1,0:T(8,128)(2,1)S(1)}, bf16[256,384]{1,0:T(8,128)(2,1)S(1)}, u32[]{:S(2)}, u32[]{:S(2)}) collective-permute-start(bf16[256,384]{1,0:T(8,128)(2,1)S(1)} %get-tuple-element.76.refs_1_), channel_id=1, source_target_pairs={{0,2},{1,3},{2,0},{3,1},{4,6},{5,7},{6,4},{7,5},{8,10},{9,11},{10,... | collective-permute-start | bytes 589832 | tf_op jit(solution)/shard_map/ppermute | solution.py:578
  6.3 5.9 %collective-permute-start.17 = (bf16[256,384]{1,0:T(8,128)(2,1)S(1)}, bf16[256,384]{1,0:T(8,128)(2,1)S(1)}, u32[]{:S(2)}, u32[]{:S(2)}) collective-permute-start(bf16[256,384]{1,0:T(8,128)(2,1)S(1)} %get-tuple-element.76.refs_1_), channel_id=1, source_target_pairs={{0,1},{1,0},{2,3},{3,2},{4,5},{5,4},{6,7},{7,6},{8,9},{9,8},{10,11... | collective-permute-start | bytes 589832 | tf_op jit(solution)/shard_map/ppermute | solution.py:578
  6.3 9.9 %collective-permute-start = (bf16[272,384]{1,0:T(8,128)(2,1)S(1)}, bf16[272,384]{1,0:T(8,128)(2,1)S(1)}, u32[]{:S(2)}, u32[]{:S(2)}) collective-permute-start(bf16[272,384]{1,0:T(8,128)(2,1)S(1)} %get-tuple-element.66.refs_0_), channel_id=1, source_target_pairs={{0,4},{1,5},{2,6},{3,7},{4,8},{5,9},{6,10},{7,11},{8,12},{9,13},{1... | collective-permute-start | bytes 626696 | tf_op jit(solution)/shard_map/ppermute | solution.py:578
  7.9 8.3 %collective-permute-start.1 = (bf16[272,384]{1,0:T(8,128)(2,1)S(1)}, bf16[272,384]{1,0:T(8,128)(2,1)S(1)}, u32[]{:S(2)}, u32[]{:S(2)}) collective-permute-start(bf16[272,384]{1,0:T(8,128)(2,1)S(1)} %get-tuple-element.66.refs_0_), channel_id=1, source_target_pairs={{0,2},{1,3},{2,0},{3,1},{4,6},{5,7},{6,4},{7,5},{8,10},{9,11},{10,... | collective-permute-start | bytes 626696 | tf_op jit(solution)/shard_map/ppermute | solution.py:578
  12.1 4.1 %collective-permute-start.2 = (bf16[272,384]{1,0:T(8,128)(2,1)S(1)}, bf16[272,384]{1,0:T(8,128)(2,1)S(1)}, u32[]{:S(2)}, u32[]{:S(2)}) collective-permute-start(bf16[272,384]{1,0:T(8,128)(2,1)S(1)} %get-tuple-element.66.refs_0_), channel_id=1, source_target_pairs={{0,1},{1,0},{2,3},{3,2},{4,5},{5,4},{6,7},{7,6},{8,9},{9,8},{10,11... | collective-permute-start | bytes 626696 | tf_op jit(solution)/shard_map/ppermute | solution.py:578
  12.2 29.2 %copy-start.11 = (bf16[256,384]{1,0:T(8,128)(2,1)}, bf16[256,384]{1,0:T(8,128)(2,1)S(1)}, u32[]{:S(2)}) copy-start(bf16[256,384]{1,0:T(8,128)(2,1)S(1)} %collective-permute-done.16.refs_5_) | copy-start | bytes 589828
  12.2 9.3 %collective-permute-start.19 = (bf16[256,384]{1,0:T(8,128)(2,1)S(1)}, bf16[256,384]{1,0:T(8,128)(2,1)S(1)}, u32[]{:S(2)}, u32[]{:S(2)}) collective-permute-start(bf16[256,384]{1,0:T(8,128)(2,1)S(1)} %collective-permute-done.15.refs_3_), channel_id=1, source_target_pairs={{0,4},{1,5},{2,6},{3,7},{4,8},{5,9},{6,10},{7,11},{8,12},{9,13},{1... | collective-permute-start | bytes 589832 | tf_op jit(solution)/shard_map/ppermute | solution.py:578
  13.2 8.3 %collective-permute-start.20 = (bf16[256,384]{1,0:T(8,128)(2,1)S(1)}, bf16[256,384]{1,0:T(8,128)(2,1)S(1)}, u32[]{:S(2)}, u32[]{:S(2)}) collective-permute-start(bf16[256,384]{1,0:T(8,128)(2,1)S(1)} %collective-permute-done.15.refs_3_), channel_id=1, source_target_pairs={{0,2},{1,3},{2,0},{3,1},{4,6},{5,7},{6,4},{7,5},{8,10},{9,11},{10,... | collective-permute-start | bytes 589832 | tf_op jit(solution)/shard_map/ppermute | solution.py:578
  16.2 26.4 %copy-start.3 = (bf16[272,384]{1,0:T(8,128)(2,1)}, bf16[272,384]{1,0:T(8,128)(2,1)S(1)}, u32[]{:S(2)}) copy-start(bf16[272,384]{1,0:T(8,128)(2,1)S(1)} %collective-permute-done.refs_2_) | copy-start | bytes 626692
  16.2 5.8 %collective-permute-start.21 = (bf16[256,384]{1,0:T(8,128)(2,1)S(1)}, bf16[256,384]{1,0:T(8,128)(2,1)}, u32[]{:S(2)}, u32[]{:S(2)}) collective-permute-start(bf16[256,384]{1,0:T(8,128)(2,1)S(1)} %collective-permute-done.15.refs_3_), channel_id=1, source_target_pairs={{0,1},{1,0},{2,3},{3,2},{4,5},{5,4},{6,7},{7,6},{8,9},{9,8},{10,11... | collective-permute-start | bytes 589832 | tf_op jit(solution)/shard_map/ppermute | solution.py:578
  16.2 26.4 %copy-start.4 = (bf16[272,384]{1,0:T(8,128)(2,1)}, bf16[272,384]{1,0:T(8,128)(2,1)S(1)}, u32[]{:S(2)}) copy-start(bf16[272,384]{1,0:T(8,128)(2,1)S(1)} %collective-permute-done.1.refs_4_) | copy-start | bytes 626692
  16.2 26.4 %copy-start.5 = (bf16[272,384]{1,0:T(8,128)(2,1)}, bf16[272,384]{1,0:T(8,128)(2,1)S(1)}, u32[]{:S(2)}) copy-start(bf16[272,384]{1,0:T(8,128)(2,1)S(1)} %collective-permute-done.2.refs_6_) | copy-start | bytes 626692
  16.2 9.6 %collective-permute-start.3 = (bf16[272,384]{1,0:T(8,128)(2,1)S(1)}, bf16[272,384]{1,0:T(8,128)(2,1)S(1)}, u32[]{:S(2)}, u32[]{:S(2)}) collective-permute-start(bf16[272,384]{1,0:T(8,128)(2,1)S(1)} %collective-permute-done.refs_2_), channel_id=1, source_target_pairs={{0,4},{1,5},{2,6},{3,7},{4,8},{5,9},{6,10},{7,11},{8,12},{9,13},{1... | collective-permute-start | bytes 626696 | tf_op jit(solution)/shard_map/ppermute | solution.py:578
  17.6 10.4 %collective-permute-start.4 = (bf16[272,384]{1,0:T(8,128)(2,1)S(1)}, bf16[272,384]{1,0:T(8,128)(2,1)S(1)}, u32[]{:S(2)}, u32[]{:S(2)}) collective-permute-start(bf16[272,384]{1,0:T(8,128)(2,1)S(1)} %collective-permute-done.refs_2_), channel_id=1, source_target_pairs={{0,2},{1,3},{2,0},{3,1},{4,6},{5,7},{6,4},{7,5},{8,10},{9,11},{10,... | collective-permute-start | bytes 626696 | tf_op jit(solution)/shard_map/ppermute | solution.py:578
  21.4 1.4 %collective-permute-start.22 = (bf16[256,384]{1,0:T(8,128)(2,1)S(1)}, bf16[256,384]{1,0:T(8,128)(2,1)S(1)}, u32[]{:S(2)}, u32[]{:S(2)}) collective-permute-start(bf16[256,384]{1,0:T(8,128)(2,1)S(1)} %collective-permute-done.16.refs_5_), channel_id=1, source_target_pairs={{0,1},{1,0},{2,3},{3,2},{4,5},{5,4},{6,7},{7,6},{8,9},{9,8},{10,11... | collective-permute-start | bytes 589832 | tf_op jit(solution)/shard_map/ppermute | solution.py:578
  21.5 6.6 %collective-permute-start.5 = (bf16[272,384]{1,0:T(8,128)(2,1)S(1)}, bf16[272,384]{1,0:T(8,128)(2,1)S(1)}, u32[]{:S(2)}, u32[]{:S(2)}) collective-permute-start(bf16[272,384]{1,0:T(8,128)(2,1)S(1)} %collective-permute-done.refs_2_), channel_id=1, source_target_pairs={{0,1},{1,0},{2,3},{3,2},{4,5},{5,4},{6,7},{7,6},{8,9},{9,8},{10,11... | collective-permute-start | bytes 626696 | tf_op jit(solution)/shard_map/ppermute | solution.py:578
  22.0 6.6 %collective-permute-start.6 = (bf16[272,384]{1,0:T(8,128)(2,1)S(1)}, bf16[272,384]{1,0:T(8,128)(2,1)S(1)}, u32[]{:S(2)}, u32[]{:S(2)}) collective-permute-start(bf16[272,384]{1,0:T(8,128)(2,1)S(1)} %collective-permute-done.1.refs_4_), channel_id=1, source_target_pairs={{0,1},{1,0},{2,3},{3,2},{4,5},{5,4},{6,7},{7,6},{8,9},{9,8},{10,11... | collective-permute-start | bytes 626696 | tf_op jit(solution)/shard_map/ppermute | solution.py:578
  22.9 8.7 %collective-permute-start.23 = (bf16[256,384]{1,0:T(8,128)(2,1)S(1)}, bf16[256,384]{1,0:T(8,128)(2,1)S(1)}, u32[]{:S(2)}, u32[]{:S(2)}) collective-permute-start(bf16[256,384]{1,0:T(8,128)(2,1)S(1)} %collective-permute-done.19.refs_9_), channel_id=1, source_target_pairs={{0,4},{1,5},{2,6},{3,7},{4,8},{5,9},{6,10},{7,11},{8,12},{9,13},{1... | collective-permute-start | bytes 589832 | tf_op jit(solution)/shard_map/ppermute | solution.py:578
  25.8 9.1 %collective-permute-start.24 = (bf16[256,384]{1,0:T(8,128)(2,1)S(1)}, bf16[256,384]{1,0:T(8,128)(2,1)}, u32[]{:S(2)}, u32[]{:S(2)}) collective-permute-start(bf16[256,384]{1,0:T(8,128)(2,1)S(1)} %collective-permute-done.19.refs_9_), channel_id=1, source_target_pairs={{0,2},{1,3},{2,0},{3,1},{4,6},{5,7},{6,4},{7,5},{8,10},{9,11},{10,... | collective-permute-start | bytes 589832 | tf_op jit(solution)/shard_map/ppermute | solution.py:578
  28.0 6.9 %collective-permute-start.25 = (bf16[256,384]{1,0:T(8,128)(2,1)S(1)}, bf16[256,384]{1,0:T(8,128)(2,1)S(1)}, u32[]{:S(2)}, u32[]{:S(2)}) collective-permute-start(bf16[256,384]{1,0:T(8,128)(2,1)S(1)} %collective-permute-done.19.refs_9_), channel_id=1, source_target_pairs={{0,1},{1,0},{2,3},{3,2},{4,5},{5,4},{6,7},{7,6},{8,9},{9,8},{10,11... | collective-permute-start | bytes 589832 | tf_op jit(solution)/shard_map/ppermute | solution.py:578
  28.1 7.3 %collective-permute-start.26 = (bf16[256,384]{1,0:T(8,128)(2,1)S(1)}, bf16[256,384]{1,0:T(8,128)(2,1)S(1)}, u32[]{:S(2)}, u32[]{:S(2)}) collective-permute-start(bf16[256,384]{1,0:T(8,128)(2,1)S(1)} %collective-permute-done.20.refs_11_), channel_id=1, source_target_pairs={{0,1},{1,0},{2,3},{3,2},{4,5},{5,4},{6,7},{7,6},{8,9},{9,8},{10,11... | collective-permute-start | bytes 589832 | tf_op jit(solution)/shard_map/ppermute | solution.py:578
  28.6 9.9 %collective-permute-start.7 = (bf16[272,384]{1,0:T(8,128)(2,1)S(1)}, bf16[272,384]{1,0:T(8,128)(2,1)}, u32[]{:S(2)}, u32[]{:S(2)}) collective-permute-start(bf16[272,384]{1,0:T(8,128)(2,1)S(1)} %collective-permute-done.3.refs_8_), channel_id=1, source_target_pairs={{0,4},{1,5},{2,6},{3,7},{4,8},{5,9},{6,10},{7,11},{8,12},{9,13},{1... | collective-permute-start | bytes 626696 | tf_op jit(solution)/shard_map/ppermute | solution.py:578
  31.6 7.2 %collective-permute-start.8 = (bf16[272,384]{1,0:T(8,128)(2,1)S(1)}, bf16[272,384]{1,0:T(8,128)(2,1)}, u32[]{:S(2)}, u32[]{:S(2)}) collective-permute-start(bf16[272,384]{1,0:T(8,128)(2,1)S(1)} %collective-permute-done.3.refs_8_), channel_id=1, source_target_pairs={{0,2},{1,3},{2,0},{3,1},{4,6},{5,7},{6,4},{7,5},{8,10},{9,11},{10,... | collective-permute-start | bytes 626696 | tf_op jit(solution)/shard_map/ppermute | solution.py:578
  34.9 3.9 %collective-permute-start.9 = (bf16[272,384]{1,0:T(8,128)(2,1)S(1)}, bf16[272,384]{1,0:T(8,128)(2,1)S(1)}, u32[]{:S(2)}, u32[]{:S(2)}) collective-permute-start(bf16[272,384]{1,0:T(8,128)(2,1)S(1)} %collective-permute-done.3.refs_8_), channel_id=1, source_target_pairs={{0,1},{1,0},{2,3},{3,2},{4,5},{5,4},{6,7},{7,6},{8,9},{9,8},{10,11... | collective-permute-start | bytes 626696 | tf_op jit(solution)/shard_map/ppermute | solution.py:578
  34.9 3.9 %collective-permute-start.10 = (bf16[272,384]{1,0:T(8,128)(2,1)S(1)}, bf16[272,384]{1,0:T(8,128)(2,1)S(1)}, u32[]{:S(2)}, u32[]{:S(2)}) collective-permute-start(bf16[272,384]{1,0:T(8,128)(2,1)S(1)} %collective-permute-done.4.refs_10_), channel_id=1, source_target_pairs={{0,1},{1,0},{2,3},{3,2},{4,5},{5,4},{6,7},{7,6},{8,9},{9,8},{10,11... | collective-permute-start | bytes 626696 | tf_op jit(solution)/shard_map/ppermute | solution.py:578
  35.4 7.1 %collective-permute-start.18 = (bf16[256,384]{1,0:T(8,128)(2,1)S(1)}, bf16[256,384]{1,0:T(8,128)(2,1)S(1)}, u32[]{:S(2)}, u32[]{:S(2)}) collective-permute-start(bf16[256,384]{1,0:T(8,128)(2,1)S(1)} %collective-permute-done.16.refs_5_), channel_id=1, source_target_pairs={{0,12},{1,13},{2,14},{3,15},{4,0},{5,1},{6,2},{7,3},{8,4},{9,5},{1... | collective-permute-start | bytes 589832 | tf_op jit(solution)/shard_map/ppermute | solution.py:578
  38.6 3.9 %collective-permute-start.27 = (bf16[256,384]{1,0:T(8,128)(2,1)S(1)}, bf16[256,384]{1,0:T(8,128)(2,1)S(1)}, u32[]{:S(2)}, u32[]{:S(2)}) collective-permute-start(bf16[256,384]{1,0:T(8,128)(2,1)S(1)} %collective-permute-done.23.refs_17_), channel_id=1, source_target_pairs={{0,1},{1,0},{2,3},{3,2},{4,5},{5,4},{6,7},{7,6},{8,9},{9,8},{10,11... | collective-permute-start | bytes 589832 | tf_op jit(solution)/shard_map/ppermute | solution.py:578
  38.9 12.8 %collective-permute-start.11 = (bf16[272,384]{1,0:T(8,128)(2,1)}, bf16[272,384]{1,0:T(8,128)(2,1)S(1)}, u32[]{:S(2)}, u32[]{:S(2)}) collective-permute-start(bf16[272,384]{1,0:T(8,128)(2,1)} %collective-permute-done.7.refs_16_), channel_id=1, source_target_pairs={{0,2},{1,3},{2,0},{3,1},{4,6},{5,7},{6,4},{7,5},{8,10},{9,11},{10,... | collective-permute-start | bytes 626696 | tf_op jit(solution)/shard_map/ppermute | solution.py:578
  40.9 10.8 %collective-permute-start.12 = (bf16[272,384]{1,0:T(8,128)(2,1)}, bf16[272,384]{1,0:T(8,128)(2,1)S(1)}, u32[]{:S(2)}, u32[]{:S(2)}) collective-permute-start(bf16[272,384]{1,0:T(8,128)(2,1)} %collective-permute-done.7.refs_16_), channel_id=1, source_target_pairs={{0,1},{1,0},{2,3},{3,2},{4,5},{5,4},{6,7},{7,6},{8,9},{9,8},{10,11... | collective-permute-start | bytes 626696 | tf_op jit(solution)/shard_map/ppermute | solution.py:578
  40.9 10.8 %collective-permute-start.13 = (bf16[272,384]{1,0:T(8,128)(2,1)}, bf16[272,384]{1,0:T(8,128)(2,1)S(1)}, u32[]{:S(2)}, u32[]{:S(2)}) collective-permute-start(bf16[272,384]{1,0:T(8,128)(2,1)} %collective-permute-done.8.refs_18_), channel_id=1, source_target_pairs={{0,1},{1,0},{2,3},{3,2},{4,5},{5,4},{6,7},{7,6},{8,9},{9,8},{10,11... | collective-permute-start | bytes 626696 | tf_op jit(solution)/shard_map/ppermute | solution.py:578
  42.5 8.7 %collective-permute-start.28 = (bf16[256,384]{1,0:T(8,128)(2,1)}, bf16[256,384]{1,0:T(8,128)(2,1)S(1)}, u32[]{:S(2)}, u32[]{:S(2)}) collective-permute-start(bf16[256,384]{1,0:T(8,128)(2,1)} %collective-permute-done.24.refs_19_), channel_id=1, source_target_pairs={{0,1},{1,0},{2,3},{3,2},{4,5},{5,4},{6,7},{7,6},{8,9},{9,8},{10,11... | collective-permute-start | bytes 589832 | tf_op jit(solution)/shard_map/ppermute | solution.py:578
  42.5 9.2 %collective-permute-start.14 = (bf16[256,256]{1,0:T(8,128)(2,1)}, bf16[256,256]{1,0:T(8,128)(2,1)S(1)}, u32[]{:S(2)}, u32[]{:S(2)}) collective-permute-start(bf16[256,256]{1,0:T(8,128)(2,1)} %param.8), channel_id=1, source_target_pairs={{0,8},{1,9},{2,10},{3,11},{4,12},{5,13},{6,14},{7,15},{8,0},{9,1},... | collective-permute-start | bytes 393224 | tf_op jit(solution)/shard_map/ppermute | solution.py:578
  51.8 8.7 %collective-permute-start.31 = (bf16[2,256,256]{2,1,0:T(8,128)(2,1)S(1)}, bf16[2,256,256]{2,1,0:T(8,128)(2,1)S(1)}, u32[]{:S(2)}, u32[]{:S(2)}) collective-permute-start(bf16[2,256,256]{2,1,0:T(8,128)(2,1)S(1)} %pad_maximum_fusion), channel_id=1, source_target_pairs={{0,4},{1,5},{2,6},{3,7},{4,0},{5,1},{6,2},{7,3},{8,12},{9,13},{10,... | collective-permute-start | bytes 786440 | tf_op jit(solution)/shard_map/ppermute | solution.py:557
  53.8 1.7 %collective-permute-start.29 = (bf16[272,384]{1,0:T(8,128)(2,1)S(1)}, bf16[272,384]{1,0:T(8,128)(2,1)S(1)}, u32[]{:S(2)}, u32[]{:S(2)}) collective-permute-start(bf16[272,384]{1,0:T(8,128)(2,1)S(1)} %collective-permute-done.11.refs_0_), channel_id=1, source_target_pairs={{0,1},{1,0},{2,3},{3,2},{4,5},{5,4},{6,7},{7,6},{8,9},{9,8},{10,11... | collective-permute-start | bytes 626696 | tf_op jit(solution)/shard_map/ppermute | solution.py:578
  53.8 1.7 %collective-permute-start.30 = (bf16[256,384]{1,0:T(8,128)(2,1)S(1)}, bf16[256,384]{1,0:T(8,128)(2,1)S(1)}, u32[]{:S(2)}, u32[]{:S(2)}) collective-permute-start(bf16[256,384]{1,0:T(8,128)(2,1)S(1)} %collective-permute-done.18.refs_1_), channel_id=1, source_target_pairs={{0,1},{1,0},{2,3},{3,2},{4,5},{5,4},{6,7},{7,6},{8,9},{9,8},{10,11... | collective-permute-start | bytes 589832 | tf_op jit(solution)/shard_map/ppermute | solution.py:578
  60.5 26.6 %all-to-all-start = ((bf16[16,128,256]{2,1,0:T(8,128)(2,1)}), bf16[16,128,256]{2,1,0:T(8,128)(2,1)S(1)}, u32[]{:S(2)}, u32[]{:S(2)}) async-start(bf16[16,128,256]{2,1,0:T(8,128)(2,1)} %get-tuple-element.115), calls=%async_computation | async-start | bytes 2097152 | tf_op jit(solution)/shard_map/all_to_all | solution.py:662
  64.5 8.4 %collective-permute-start.32 = (bf16[2,256,256]{2,1,0:T(8,128)(2,1)S(1)}, bf16[2,256,256]{2,1,0:T(8,128)(2,1)S(1)}, u32[]{:S(2)}, u32[]{:S(2)}) collective-permute-start(bf16[2,256,256]{2,1,0:T(8,128)(2,1)S(1)} %pad_maximum_fusion.2), channel_id=1, source_target_pairs={{0,16},{16,0},{1,17},{17,1},{2,18},{18,2},{3,19},{19,3},{4,20},{20... | collective-permute-start | bytes 786440 | tf_op jit(solution)/shard_map/ppermute | solution.py:622
  73.1 17.9 %collective-permute-start.33 = (bf16[2,256,512]{2,1,0:T(8,128)(2,1)S(1)}, bf16[2,256,512]{2,1,0:T(8,128)(2,1)S(1)}, u32[]{:S(2)}, u32[]{:S(2)}) collective-permute-start(bf16[2,256,512]{2,1,0:T(8,128)(2,1)S(1)} %join_rows.1.refs_0_), channel_id=1, source_target_pairs={{0,2},{1,3},{2,0},{3,1},{4,6},{5,7},{6,4},{7,5},{8,10},{9,11},{10,... | collective-permute-start | bytes 1572872 | tf_op jit(solution)/shard_map/ppermute | solution.py:557
  91.1 22.1 %all-to-all-start.1 = ((bf16[16,144,128]{2,1,0:T(8,128)(2,1)}), bf16[16,144,128]{2,1,0:T(8,128)(2,1)S(1)}, u32[]{:S(2)}, u32[]{:S(2)}) async-start(bf16[16,144,128]{2,1,0:T(8,128)(2,1)} %get-tuple-element.124), calls=%async_computation.1 | async-start | bytes 1179648 | tf_op jit(solution)/shard_map/all_to_all | solution.py:674
  97.6 20.6 %collective-permute-start.34 = (bf16[2,256,512]{2,1,0:T(8,128)(2,1)S(1)}, bf16[2,256,512]{2,1,0:T(8,128)(2,1)S(1)}, u32[]{:S(2)}, u32[]{:S(2)}) collective-permute-start(bf16[2,256,512]{2,1,0:T(8,128)(2,1)S(1)} %join_rows.1.refs_0_), channel_id=1, source_target_pairs={{0,1},{1,0},{2,3},{3,2},{4,5},{5,4},{6,7},{7,6},{8,9},{9,8},{10,11... | collective-permute-start | bytes 1572872 | tf_op jit(solution)/shard_map/ppermute | solution.py:557
  98.0 20.7 %collective-permute-start.35 = (bf16[2,256,512]{2,1,0:T(8,128)(2,1)S(1)}, bf16[2,256,512]{2,1,0:T(8,128)(2,1)S(1)}, u32[]{:S(2)}, u32[]{:S(2)}) collective-permute-start(bf16[2,256,512]{2,1,0:T(8,128)(2,1)S(1)} %collective-permute-done.33.refs_1_), channel_id=1, source_target_pairs={{0,1},{1,0},{2,3},{3,2},{4,5},{5,4},{6,7},{7,6},{8,9},{9,8},{10,11... | collective-permute-start | bytes 1572872 | tf_op jit(solution)/shard_map/ppermute | solution.py:557
  114.6 6.4 %collective-permute-start.39 = (bf16[256,256]{1,0:T(8,128)(2,1)S(1)}, bf16[256,256]{1,0:T(8,128)(2,1)S(1)}, u32[]{:S(2)}, u32[]{:S(2)}) collective-permute-start(bf16[256,256]{1,0:T(8,128)(2,1)S(1)} %get-tuple-element.128.refs_4_), channel_id=1, source_target_pairs={{0,16},{16,0},{1,17},{17,1},{2,18},{18,2},{3,19},{19,3},{4,20},{20... | collective-permute-start | bytes 393224 | tf_op jit(solution)/shard_map/ppermute | solution.py:678
  116.2 7.7 %collective-permute-start.38 = (bf16[256,256]{1,0:T(8,128)(2,1)S(1)}, bf16[256,256]{1,0:T(8,128)(2,1)S(1)}, u32[]{:S(2)}, u32[]{:S(2)}) collective-permute-start(bf16[256,256]{1,0:T(8,128)(2,1)S(1)} %get-tuple-element.127.refs_4_), channel_id=1, source_target_pairs={{0,16},{16,0},{1,17},{17,1},{2,18},{18,2},{3,19},{19,3},{4,20},{20... | collective-permute-start | bytes 393224 | tf_op jit(solution)/shard_map/ppermute | solution.py:678
  116.7 10.0 %collective-permute-start.37 = (bf16[256,256]{1,0:T(8,128)(2,1)S(1)}, bf16[256,256]{1,0:T(8,128)(2,1)S(1)}, u32[]{:S(2)}, u32[]{:S(2)}) collective-permute-start(bf16[256,256]{1,0:T(8,128)(2,1)S(1)} %get-tuple-element.126.refs_4_), channel_id=1, source_target_pairs={{0,16},{16,0},{1,17},{17,1},{2,18},{18,2},{3,19},{19,3},{4,20},{20... | collective-permute-start | bytes 393224 | tf_op jit(solution)/shard_map/ppermute | solution.py:678
  118.2 10.3 %collective-permute-start.36 = (bf16[256,256]{1,0:T(8,128)(2,1)S(1)}, bf16[256,256]{1,0:T(8,128)(2,1)S(1)}, u32[]{:S(2)}, u32[]{:S(2)}) collective-permute-start(bf16[256,256]{1,0:T(8,128)(2,1)S(1)} %get-tuple-element.125.refs_4_), channel_id=1, source_target_pairs={{0,16},{16,0},{1,17},{17,1},{2,18},{18,2},{3,19},{19,3},{4,20},{20... | collective-permute-start | bytes 393224 | tf_op jit(solution)/shard_map/ppermute | solution.py:678
  (11 other events, 135.9 us)

commit v7 on v6

--- a/solution.py
+++ b/solution.py
@@ -484,50 +484,56 @@
     )(in_hbm(clusters), table, in_hbm(sums), in_hbm(mass), in_vmem(back))
 
 
-def output_kernel(n_weights, n_parts, paired, me_ref, *refs):
-    weights, parts, out_ref = refs[:n_weights], refs[n_weights : n_weights + n_parts], refs[-1]
-    step = out_ref.shape[1]
-    span = pl.ds(pl.multiple_of(pl.program_id(0) * step, 128), step)
-    index = 0
+def output_kernel(n_weights, n_parts, n_given, paired, half, me_ref, *refs):
+    weights, parts = refs[:n_weights], refs[n_weights : n_weights + n_parts]
+    out_ref, held_ref, sems = refs[n_weights + n_parts + n_given :]
+    columns = parts[0].shape[1]
+    span = slice(half * columns, (half + 1) * columns)
+    moves = []
     for weight_ref in weights:
         blocks, features, depth = weight_ref.shape
         weight = weight_ref[...].reshape(blocks * features, depth)
         total, at = None, 0
         for part in parts:
             term = jnp.dot(
-                weight[:, at : at + part.shape[0]],
-                part[:, span],
-                preferred_element_type=jnp.float32,
+                weight[:, at : at + part.shape[0]], part[...], preferred_element_type=jnp.float32
             )
             total = term if total is None else total + term
             at += part.shape[0]
         total = total.astype(out_ref.dtype)
         for block in range(blocks):
-            place = index
+            index = place = len(moves)
             if paired:
                 place = (me_ref[0] % 8) ^ (index % 2 * 4 + index // 2 % 2 * 2 + index // 4)
+            held = held_ref.at[index * features : (index + 1) * features, :]
+            held[...] = total[block * features : (block + 1) * features]
             place = pl.ds(pl.multiple_of(place * features, features), features)
-            out_ref[place, :] = total[block * features : (block + 1) * features]
-            index += 1
+            moves.append(pltpu.make_async_copy(held, out_ref.at[place, span], sems.at[index]))
+            moves[-1].start()
+    for move in moves:
+        move.wait()
 
 
 def output_projection(weights, me, parts, paired, half=0, halves=1, written=None):
-    features = sum(weight.shape[0] * weight.shape[1] for weight in weights)
+    blocks = sum(weight.shape[0] for weight in weights)
+    features = blocks * weights[0].shape[1]
     depth, rows = weights[0].shape[2], parts[0].shape[1]
-    step = min(256, rows)
-    steps = rows // step
     given = [] if written is None else [written]
     n_refs = len(weights) + len(parts)
+    in_place = pl.BlockSpec(memory_space=pltpu.HBM)
     return pl.pallas_call(
-        functools.partial(output_kernel, len(weights), len(parts), paired),
+        functools.partial(
+            output_kernel, len(weights), len(parts), len(given), paired, half
+        ),
         out_shape=pltpu.HBM((features, rows * halves), jnp.bfloat16),
-        grid=(steps,),
-        in_specs=[SMEM_SPEC]
-        + [VMEM_SPEC] * n_refs
-        + [pl.BlockSpec(memory_space=pltpu.HBM)] * len(given),
-        out_specs=pl.BlockSpec((features, step), lambda i: (0, half * steps + i)),
+        in_specs=[SMEM_SPEC] + [VMEM_SPEC] * n_refs + [in_place] * len(given),
+        out_specs=in_place,
+        scratch_shapes=[
+            pltpu.VMEM((features, rows), jnp.bfloat16),
+            pltpu.SemaphoreType.DMA((blocks,)),
+        ],
         input_output_aliases={1 + n_refs: 0} if given else {},
-        compiler_params=params(),
+        compiler_params=pltpu.CompilerParams(vmem_limit_bytes=VMEM_BYTES),
         cost_estimate=cost(2 * features * depth * rows, 2 * features * (rows + depth)),
         name="output_projection",
     )(me, *map(in_vmem, weights), *map(in_vmem, parts), *given)

time: 131 us -> 131 us (level)
  no operation moved by 1% of the time
where the time goes in v7:
time: 131 us; the launch traced here: 130 us
  waiting for transfers between devices  54.5 us (42%)
  starting transfers between devices  43.6 us (33%)
  Pallas kernels  30.7 us (23%)
    ppermute x31, starting transfers between devices, hop(): lax.ppermute(value, axis, pairs)  23.1 us
    ppermute x31, waiting for transfers between devices, hop(): lax.ppermute(value, axis, pairs)  19.7 us
    all_to_all x1, waiting for transfers between devices, on_device(): lax.all_to_all(returning, 'seq', split_axis=0, concat_axis=0, tiled=True)  15 us
    pallas_call x1, Pallas kernels, project_early(): pl.pallas_call(functools.partial(early_kernel, n_early, n_late, paired),...  8.56 us
    all_to_all x1, waiting for transfers between devices, on_device(): lax.all_to_all(outgoing, 'seq', split_axis=0, concat_axis=0, tiled=True)  6.87 us
    ppermute x1, waiting for transfers between devices, make_pair(): return join_rows(keep, lax.ppermute(give, 'head', SWAP))  6.83 us
    all_to_all x1, starting transfers between devices, on_device(): lax.all_to_all(returning, 'seq', split_axis=0, concat_axis=0, tiled=True)  6.57 us
    pallas_call x4, Pallas kernels, output_projection(): pl.pallas_call(functools.partial(output_kernel, len(weights), len(parts),...  6.22 us
  transfers between devices with their start and end apart: 42, of which 20 were waited for; matrix products, arithmetic and copies ran while one was open for 0% of the time, Pallas kernels for 22%

profile of v7, /device:TPU:0, one launch (start us, length us, event | category | flops | bytes accessed | tf_op | source)
XLA Modules:
  0.0 130.3 jit_solution(5233263950852002827)
XLA Ops:
  0.6 1.0 split_weight.1
  1.7 3.1 %collective-permute-start.15 = (bf16[256,384]{1,0:T(8,128)(2,1)S(1)}, bf16[256,384]{1,0:T(8,128)(2,1)S(1)}, u32[]{:S(2)}, u32[]{:S(2)}) collective-permute-start(bf16[256,384]{1,0:T(8,128)(2,1)S(1)} %get-tuple-element.76.refs_1_), channel_id=1, source_target_pairs={{0,4},{1,5},{2,6},{3,7},{4,8},{5,9},{6,10},{7,11},{8,12},{9,13},{1... | collective-permute-start | bytes 589832 | tf_op jit(solution)/shard_map/ppermute | solution.py:584
  4.8 1.5 %collective-permute-start.16 = (bf16[256,384]{1,0:T(8,128)(2,1)S(1)}, bf16[256,384]{1,0:T(8,128)(2,1)S(1)}, u32[]{:S(2)}, u32[]{:S(2)}) collective-permute-start(bf16[256,384]{1,0:T(8,128)(2,1)S(1)} %get-tuple-element.76.refs_1_), channel_id=1, source_target_pairs={{0,2},{1,3},{2,0},{3,1},{4,6},{5,7},{6,4},{7,5},{8,10},{9,11},{10,... | collective-permute-start | bytes 589832 | tf_op jit(solution)/shard_map/ppermute | solution.py:584
  6.3 1.6 %collective-permute-start = (bf16[272,384]{1,0:T(8,128)(2,1)S(1)}, bf16[272,384]{1,0:T(8,128)(2,1)S(1)}, u32[]{:S(2)}, u32[]{:S(2)}) collective-permute-start(bf16[272,384]{1,0:T(8,128)(2,1)S(1)} %get-tuple-element.66.refs_0_), channel_id=1, source_target_pairs={{0,4},{1,5},{2,6},{3,7},{4,8},{5,9},{6,10},{7,11},{8,12},{9,13},{1... | collective-permute-start | bytes 626696 | tf_op jit(solution)/shard_map/ppermute | solution.py:584
  8.4 3.8 %collective-permute-done.15.refs_3_ = bf16[256,384]{1,0:T(8,128)(2,1)S(1)} collective-permute-done((bf16[256,384]{1,0:T(8,128)(2,1)S(1)}, bf16[256,384]{1,0:T(8,128)(2,1)S(1)}, u32[]{:S(2)}, u32[]{:S(2)}) %collective-permute-start.15) | collective-permute-done | bytes 196640 | tf_op jit(solution)/shard_map/ppermute | solution.py:584
  12.2 1.0 collective-permute-start.19
  13.2 2.5 %collective-permute-start.20 = (bf16[256,384]{1,0:T(8,128)(2,1)S(1)}, bf16[256,384]{1,0:T(8,128)(2,1)S(1)}, u32[]{:S(2)}, u32[]{:S(2)}) collective-permute-start(bf16[256,384]{1,0:T(8,128)(2,1)S(1)} %collective-permute-done.15.refs_3_), channel_id=1, source_target_pairs={{0,2},{1,3},{2,0},{3,1},{4,6},{5,7},{6,4},{7,5},{8,10},{9,11},{10,... | collective-permute-start | bytes 589832 | tf_op jit(solution)/shard_map/ppermute | solution.py:584
  16.2 1.3 %collective-permute-start.3 = (bf16[272,384]{1,0:T(8,128)(2,1)S(1)}, bf16[272,384]{1,0:T(8,128)(2,1)S(1)}, u32[]{:S(2)}, u32[]{:S(2)}) collective-permute-start(bf16[272,384]{1,0:T(8,128)(2,1)S(1)} %collective-permute-done.refs_2_), channel_id=1, source_target_pairs={{0,4},{1,5},{2,6},{3,7},{4,8},{5,9},{6,10},{7,11},{8,12},{9,13},{1... | collective-permute-start | bytes 626696 | tf_op jit(solution)/shard_map/ppermute | solution.py:584
  17.6 1.3 collective-permute-start.4
  18.9 2.6 %collective-permute-done.19.refs_9_ = bf16[256,384]{1,0:T(8,128)(2,1)S(1)} collective-permute-done((bf16[256,384]{1,0:T(8,128)(2,1)S(1)}, bf16[256,384]{1,0:T(8,128)(2,1)S(1)}, u32[]{:S(2)}, u32[]{:S(2)}) %collective-permute-start.19) | collective-permute-done | bytes 196640 | tf_op jit(solution)/shard_map/ppermute | solution.py:584
  21.5 0.6 collective-permute-start.5
  22.1 0.8 collective-permute-done.22.refs_15_
  22.9 2.9 %collective-permute-done.3.refs_8_ = bf16[272,384]{1,0:T(8,128)(2,1)S(1)} collective-permute-done((bf16[272,384]{1,0:T(8,128)(2,1)S(1)}, bf16[272,384]{1,0:T(8,128)(2,1)S(1)}, u32[]{:S(2)}, u32[]{:S(2)}) %collective-permute-start.3) | collective-permute-done | bytes 208928 | tf_op jit(solution)/shard_map/ppermute | solution.py:584
  25.8 2.2 %collective-permute-start.24 = (bf16[256,384]{1,0:T(8,128)(2,1)S(1)}, bf16[256,384]{1,0:T(8,128)(2,1)}, u32[]{:S(2)}, u32[]{:S(2)}) collective-permute-start(bf16[256,384]{1,0:T(8,128)(2,1)S(1)} %collective-permute-done.19.refs_9_), channel_id=1, source_target_pairs={{0,2},{1,3},{2,0},{3,1},{4,6},{5,7},{6,4},{7,5},{8,10},{9,11},{10,... | collective-permute-start | bytes 589832 | tf_op jit(solution)/shard_map/ppermute | solution.py:584
  28.1 0.5 collective-permute-start.26
  28.6 3.0 %collective-permute-done.23.refs_17_ = bf16[256,384]{1,0:T(8,128)(2,1)S(1)} collective-permute-done((bf16[256,384]{1,0:T(8,128)(2,1)S(1)}, bf16[256,384]{1,0:T(8,128)(2,1)S(1)}, u32[]{:S(2)}, u32[]{:S(2)}) %collective-permute-start.23) | collective-permute-done | bytes 196640 | tf_op jit(solution)/shard_map/ppermute | solution.py:584
  31.6 3.3 %collective-permute-start.8 = (bf16[272,384]{1,0:T(8,128)(2,1)S(1)}, bf16[272,384]{1,0:T(8,128)(2,1)}, u32[]{:S(2)}, u32[]{:S(2)}) collective-permute-start(bf16[272,384]{1,0:T(8,128)(2,1)S(1)} %collective-permute-done.3.refs_8_), channel_id=1, source_target_pairs={{0,2},{1,3},{2,0},{3,1},{4,6},{5,7},{6,4},{7,5},{8,10},{9,11},{10,... | collective-permute-start | bytes 626696 | tf_op jit(solution)/shard_map/ppermute | solution.py:584
  35.4 3.1 %collective-permute-done.7.refs_16_ = bf16[272,384]{1,0:T(8,128)(2,1)} collective-permute-done((bf16[272,384]{1,0:T(8,128)(2,1)S(1)}, bf16[272,384]{1,0:T(8,128)(2,1)}, u32[]{:S(2)}, u32[]{:S(2)}) %collective-permute-start.7) | collective-permute-done | bytes 208928 | tf_op jit(solution)/shard_map/ppermute | solution.py:584
  38.9 2.0 %collective-permute-start.11 = (bf16[272,384]{1,0:T(8,128)(2,1)}, bf16[272,384]{1,0:T(8,128)(2,1)S(1)}, u32[]{:S(2)}, u32[]{:S(2)}) collective-permute-start(bf16[272,384]{1,0:T(8,128)(2,1)} %collective-permute-done.7.refs_16_), channel_id=1, source_target_pairs={{0,2},{1,3},{2,0},{3,1},{4,6},{5,7},{6,4},{7,5},{8,10},{9,11},{10,... | collective-permute-start | bytes 626696 | tf_op jit(solution)/shard_map/ppermute | solution.py:584
  40.9 0.5 collective-permute-start.13
  41.4 1.1 collective-permute-done.18.refs_1_
  42.7 8.6 %project_early.1 = (f32[1024,768]{1,0:T(8,128)S(1)}, bf16[1024,1024]{1,0:T(8,128)(2,1)S(1)}, f32[16,128]{1,0:T(8,128)S(1)}, f32[1024,128]{1,0:T(8,128)S(1)}) custom-call(s32[1]{0:T(128)} %bitcast.me_ref, bf16[1024,4096]{1,0:T(8,128)(2,1)} %x_ref.1, bf16[272,384]{1,0:T(8,128)(2,1)} %copy-done, bf16[256,384]{1,0:T(8,128)(2,1)} %copy-done.1, ...), custom_call_target="tpu_custom_call" | custom-call | flops 1 | bytes 1 | tf_op jit(solution)/shard_map/project_early/pallas_call | solution.py:176
  51.8 2.0 %collective-permute-start.31 = (bf16[2,256,256]{2,1,0:T(8,128)(2,1)S(1)}, bf16[2,256,256]{2,1,0:T(8,128)(2,1)S(1)}, u32[]{:S(2)}, u32[]{:S(2)}) collective-permute-start(bf16[2,256,256]{2,1,0:T(8,128)(2,1)S(1)} %pad_maximum_fusion), channel_id=1, source_target_pairs={{0,4},{1,5},{2,6},{3,7},{4,0},{5,1},{6,2},{7,3},{8,12},{9,13},{10,... | collective-permute-start | bytes 786440 | tf_op jit(solution)/shard_map/ppermute | solution.py:563
  53.8 0.5 collective-permute-start.30
  54.3 1.2 collective-permute-done.30.refs_7_
  55.5 4.3 %project_late.1 = (bf16[1024,768]{1,0:T(8,128)(2,1)}, bf16[16,128,256]{2,1,0:T(8,128)(2,1)}, s32[8,128]{1,0:T(8,128)S(1)}) custom-call(s32[1]{0:T(128)} %bitcast.me_ref, s32[2,8]{1,0:T(2,128)} %cluster_ref.3, f32[1024,768]{1,0:T(8,128)S(1)} %get-tuple-element.100.acc_ref, bf16[1024,1024]{1,0:T(8,128)(2,1)S(1)} %get-tuple-element.101.rest_ref, ...), custom_call_target="tpu_custom_call" | custom-call | flops 1 | bytes 1 | tf_op jit(solution)/shard_map/project_late/pallas_call | solution.py:314
  59.8 0.7 collective-permute-done.31
  60.5 3.8 %all-to-all-start = ((bf16[16,128,256]{2,1,0:T(8,128)(2,1)}), bf16[16,128,256]{2,1,0:T(8,128)(2,1)S(1)}, u32[]{:S(2)}, u32[]{:S(2)}) async-start(bf16[16,128,256]{2,1,0:T(8,128)(2,1)} %get-tuple-element.115), calls=%async_computation | async-start | bytes 2097152 | tf_op jit(solution)/shard_map/all_to_all | solution.py:668
  64.5 1.6 %collective-permute-start.32 = (bf16[2,256,256]{2,1,0:T(8,128)(2,1)S(1)}, bf16[2,256,256]{2,1,0:T(8,128)(2,1)S(1)}, u32[]{:S(2)}, u32[]{:S(2)}) collective-permute-start(bf16[2,256,256]{2,1,0:T(8,128)(2,1)S(1)} %pad_maximum_fusion.2), channel_id=1, source_target_pairs={{0,16},{16,0},{1,17},{17,1},{2,18},{18,2},{3,19},{19,3},{4,20},{20... | collective-permute-start | bytes 786440 | tf_op jit(solution)/shard_map/ppermute | solution.py:628
  66.1 6.8 %collective-permute-done.32.got_ref = bf16[2,256,256]{2,1,0:T(8,128)(2,1)S(1)} collective-permute-done((bf16[2,256,256]{2,1,0:T(8,128)(2,1)S(1)}, bf16[2,256,256]{2,1,0:T(8,128)(2,1)S(1)}, u32[]{:S(2)}, u32[]{:S(2)}) %collective-permute-start.32) | collective-permute-done | bytes 262176 | tf_op jit(solution)/shard_map/ppermute | solution.py:628
  73.1 1.7 %collective-permute-start.33 = (bf16[2,256,512]{2,1,0:T(8,128)(2,1)S(1)}, bf16[2,256,512]{2,1,0:T(8,128)(2,1)S(1)}, u32[]{:S(2)}, u32[]{:S(2)}) collective-permute-start(bf16[2,256,512]{2,1,0:T(8,128)(2,1)S(1)} %join_rows.1.refs_0_), channel_id=1, source_target_pairs={{0,2},{1,3},{2,0},{3,1},{4,6},{5,7},{6,4},{7,5},{8,10},{9,11},{10,... | collective-permute-start | bytes 1572872 | tf_op jit(solution)/shard_map/ppermute | solution.py:563
  74.9 5.4 %inner_attention.1 = (f32[256,1024]{1,0:T(8,128)}, f32[16,1024]{1,0:T(8,128)}) custom-call(bf16[1024,768]{1,0:T(8,128)(2,1)} %get-tuple-element.116.qkv_ref), custom_call_target="tpu_custom_call" | custom-call | flops 1 | bytes 1 | tf_op jit(solution)/shard_map/inner_attention/pallas_call | solution.py:361
  80.2 6.9 %all-to-all-done.in_ref = bf16[16,128,256]{2,1,0:T(8,128)(2,1)S(1)} async-done(((bf16[16,128,256]{2,1,0:T(8,128)(2,1)}), bf16[16,128,256]{2,1,0:T(8,128)(2,1)S(1)}, u32[]{:S(2)}, u32[]{:S(2)}) %all-to-all-start) | async-done | bytes 1048608 | tf_op jit(solution)/shard_map/all_to_all | solution.py:668
  87.1 3.6 %owner_attention.1 = (bf16[16,144,128]{2,1,0:T(8,128)(2,1)}, f32[8,128]{1,0:T(8,128)}) custom-call(s32[8,128]{1,0:T(8,128)S(1)} %get-tuple-element.114.table_ref, bf16[16,128,256]{2,1,0:T(8,128)(2,1)S(1)} %all-to-all-done.in_ref, f32[8,128]{1,0:T(8,128)} %bitcast.9), custom_call_target="tpu_custom_call" | custom-call | flops 1 | bytes 1 | tf_op jit(solution)/shard_map/owner_attention/pallas_call | solution.py:437
  91.1 6.6 %all-to-all-start.1 = ((bf16[16,144,128]{2,1,0:T(8,128)(2,1)}), bf16[16,144,128]{2,1,0:T(8,128)(2,1)S(1)}, u32[]{:S(2)}, u32[]{:S(2)}) async-start(bf16[16,144,128]{2,1,0:T(8,128)(2,1)} %get-tuple-element.124), calls=%async_computation.1 | async-start | bytes 1179648 | tf_op jit(solution)/shard_map/all_to_all | solution.py:680
  98.2 15.0 %all-to-all-done.1.back_ref = bf16[16,144,128]{2,1,0:T(8,128)(2,1)S(1)} async-done(((bf16[16,144,128]{2,1,0:T(8,128)(2,1)}), bf16[16,144,128]{2,1,0:T(8,128)(2,1)S(1)}, u32[]{:S(2)}, u32[]{:S(2)}) %all-to-all-start.1) | async-done | bytes 589856 | tf_op jit(solution)/shard_map/all_to_all | solution.py:680
  113.2 1.5 %merge_attention.1 = (bf16[256,256]{1,0:T(8,128)(2,1)S(1)}, bf16[256,256]{1,0:T(8,128)(2,1)S(1)}, bf16[256,256]{1,0:T(8,128)(2,1)S(1)}, bf16[256,256]{1,0:T(8,128)(2,1)S(1)}) custom-call(s32[2,8]{1,0:T(2,128)} %cluster_ref.3, s32[8,128]{1,0:T(8,128)S(1)} %get-tuple-element.114.table_ref, f32[256,1024]{1,0:T(8,128)} %get-tuple-element.122.sums_ref, ...), custom_call_target="tpu_custom_call" | custom-call | flops 1 | bytes 1 | tf_op jit(solution)/shard_map/merge_attention/pallas_call | solution.py:475
  114.6 1.6 %collective-permute-start.39 = (bf16[256,256]{1,0:T(8,128)(2,1)S(1)}, bf16[256,256]{1,0:T(8,128)(2,1)S(1)}, u32[]{:S(2)}, u32[]{:S(2)}) collective-permute-start(bf16[256,256]{1,0:T(8,128)(2,1)S(1)} %get-tuple-element.128.refs_4_), channel_id=1, source_target_pairs={{0,16},{16,0},{1,17},{17,1},{2,18},{18,2},{3,19},{19,3},{4,20},{20... | collective-permute-start | bytes 393224 | tf_op jit(solution)/shard_map/ppermute | solution.py:684
  116.2 0.5 collective-permute-start.38
  116.7 1.5 %collective-permute-start.37 = (bf16[256,256]{1,0:T(8,128)(2,1)S(1)}, bf16[256,256]{1,0:T(8,128)(2,1)S(1)}, u32[]{:S(2)}, u32[]{:S(2)}) collective-permute-start(bf16[256,256]{1,0:T(8,128)(2,1)S(1)} %get-tuple-element.126.refs_4_), channel_id=1, source_target_pairs={{0,16},{16,0},{1,17},{17,1},{2,18},{18,2},{3,19},{19,3},{4,20},{20... | collective-permute-start | bytes 393224 | tf_op jit(solution)/shard_map/ppermute | solution.py:684
  118.2 0.5 collective-permute-start.36
  118.8 2.3 %collective-permute-done.39.refs_5_ = bf16[256,256]{1,0:T(8,128)(2,1)S(1)} collective-permute-done((bf16[256,256]{1,0:T(8,128)(2,1)S(1)}, bf16[256,256]{1,0:T(8,128)(2,1)S(1)}, u32[]{:S(2)}, u32[]{:S(2)}) %collective-permute-start.39) | collective-permute-done | bytes 131104 | tf_op jit(solution)/shard_map/ppermute | solution.py:684
  121.1 1.6 %output_projection.4.refs_6_ = bf16[2048,1024]{1,0:T(8,128)(2,1)} custom-call(s32[1]{0:T(128)} %bitcast.me_ref, bf16[2,256,512]{2,1,0:T(8,128)(2,1)S(1)} %join_rows.1.refs_0_, bf16[2,256,512]{2,1,0:T(8,128)(2,1)S(1)} %collective-permute-done.33.refs_1_, bf16[2,256,512]{2,1,0:T(8,128)(2,1)S(1)} %collective-permute-done.34.refs_2_, ...), custom_call_target="tpu_custom_call" | custom-call | flops 1 | bytes 1 | tf_op jit(solution)/shard_map/output_projection/pallas_call | solution.py:524
  122.6 1.2 collective-permute-done.38.refs_5_
  123.9 1.6 %output_projection.5.refs_6_ = bf16[2048,1024]{1,0:T(8,128)(2,1)} custom-call(s32[1]{0:T(128)} %bitcast.me_ref, bf16[2,256,512]{2,1,0:T(8,128)(2,1)S(1)} %join_rows.1.refs_0_, bf16[2,256,512]{2,1,0:T(8,128)(2,1)S(1)} %collective-permute-done.33.refs_1_, bf16[2,256,512]{2,1,0:T(8,128)(2,1)S(1)} %collective-permute-done.34.refs_2_, ...), custom_call_target="tpu_custom_call", output_to_operand_aliasing={{}: (7, {})} | custom-call | flops 1 | bytes 1 | tf_op jit(solution)/shard_map/output_projection/pallas_call | solution.py:524
  125.4 1.2 collective-permute-done.37.refs_5_
  126.7 1.6 %output_projection.6.refs_6_ = bf16[2048,1024]{1,0:T(8,128)(2,1)} custom-call(s32[1]{0:T(128)} %bitcast.me_ref, bf16[2,256,512]{2,1,0:T(8,128)(2,1)S(1)} %join_rows.1.refs_0_, bf16[2,256,512]{2,1,0:T(8,128)(2,1)S(1)} %collective-permute-done.33.refs_1_, bf16[2,256,512]{2,1,0:T(8,128)(2,1)S(1)} %collective-permute-done.34.refs_2_, ...), custom_call_target="tpu_custom_call", output_to_operand_aliasing={{}: (7, {})} | custom-call | flops 1 | bytes 1 | tf_op jit(solution)/shard_map/output_projection/pallas_call | solution.py:524
  128.6 1.6 %output_projection.7 = bf16[2048,1024]{1,0:T(8,128)(2,1)} custom-call(s32[1]{0:T(128)} %bitcast.me_ref, bf16[2,256,512]{2,1,0:T(8,128)(2,1)S(1)} %join_rows.1.refs_0_, bf16[2,256,512]{2,1,0:T(8,128)(2,1)S(1)} %collective-permute-done.33.refs_1_, bf16[2,256,512]{2,1,0:T(8,128)(2,1)S(1)} %collective-permute-done.34.refs_2_, ...), custom_call_target="tpu_custom_call", output_to_operand_aliasing={{}: (7, {})} | custom-call | flops 1 | bytes 1 | tf_op jit(solution)/shard_map/output_projection/pallas_call | solution.py:524
  (86 shorter events, 4.2 us)
Async XLA Ops:
  1.7 40.9 %copy-start = (bf16[272,384]{1,0:T(8,128)(2,1)}, bf16[272,384]{1,0:T(8,128)(2,1)S(1)}, u32[]{:S(2)}) copy-start(bf16[272,384]{1,0:T(8,128)(2,1)S(1)} %get-tuple-element.66.refs_0_) | copy-start | bytes 626692
  1.7 40.9 %copy-start.1 = (bf16[256,384]{1,0:T(8,128)(2,1)}, bf16[256,384]{1,0:T(8,128)(2,1)S(1)}, u32[]{:S(2)}) copy-start(bf16[256,384]{1,0:T(8,128)(2,1)S(1)} %get-tuple-element.76.refs_1_) | copy-start | bytes 589828
  1.7 10.4 %collective-permute-start.15 = (bf16[256,384]{1,0:T(8,128)(2,1)S(1)}, bf16[256,384]{1,0:T(8,128)(2,1)S(1)}, u32[]{:S(2)}, u32[]{:S(2)}) collective-permute-start(bf16[256,384]{1,0:T(8,128)(2,1)S(1)} %get-tuple-element.76.refs_1_), channel_id=1, source_target_pairs={{0,4},{1,5},{2,6},{3,7},{4,8},{5,9},{6,10},{7,11},{8,12},{9,13},{1... | collective-permute-start | bytes 589832 | tf_op jit(solution)/shard_map/ppermute | solution.py:584
  4.8 7.4 %collective-permute-start.16 = (bf16[256,384]{1,0:T(8,128)(2,1)S(1)}, bf16[256,384]{1,0:T(8,128)(2,1)S(1)}, u32[]{:S(2)}, u32[]{:S(2)}) collective-permute-start(bf16[256,384]{1,0:T(8,128)(2,1)S(1)} %get-tuple-element.76.refs_1_), channel_id=1, source_target_pairs={{0,2},{1,3},{2,0},{3,1},{4,6},{5,7},{6,4},{7,5},{8,10},{9,11},{10,... | collective-permute-start | bytes 589832 | tf_op jit(solution)/shard_map/ppermute | solution.py:584
  6.3 5.9 %collective-permute-start.17 = (bf16[256,384]{1,0:T(8,128)(2,1)S(1)}, bf16[256,384]{1,0:T(8,128)(2,1)S(1)}, u32[]{:S(2)}, u32[]{:S(2)}) collective-permute-start(bf16[256,384]{1,0:T(8,128)(2,1)S(1)} %get-tuple-element.76.refs_1_), channel_id=1, source_target_pairs={{0,1},{1,0},{2,3},{3,2},{4,5},{5,4},{6,7},{7,6},{8,9},{9,8},{10,11... | collective-permute-start | bytes 589832 | tf_op jit(solution)/shard_map/ppermute | solution.py:584
  6.3 9.9 %collective-permute-start = (bf16[272,384]{1,0:T(8,128)(2,1)S(1)}, bf16[272,384]{1,0:T(8,128)(2,1)S(1)}, u32[]{:S(2)}, u32[]{:S(2)}) collective-permute-start(bf16[272,384]{1,0:T(8,128)(2,1)S(1)} %get-tuple-element.66.refs_0_), channel_id=1, source_target_pairs={{0,4},{1,5},{2,6},{3,7},{4,8},{5,9},{6,10},{7,11},{8,12},{9,13},{1... | collective-permute-start | bytes 626696 | tf_op jit(solution)/shard_map/ppermute | solution.py:584
  7.9 8.3 %collective-permute-start.1 = (bf16[272,384]{1,0:T(8,128)(2,1)S(1)}, bf16[272,384]{1,0:T(8,128)(2,1)S(1)}, u32[]{:S(2)}, u32[]{:S(2)}) collective-permute-start(bf16[272,384]{1,0:T(8,128)(2,1)S(1)} %get-tuple-element.66.refs_0_), channel_id=1, source_target_pairs={{0,2},{1,3},{2,0},{3,1},{4,6},{5,7},{6,4},{7,5},{8,10},{9,11},{10,... | collective-permute-start | bytes 626696 | tf_op jit(solution)/shard_map/ppermute | solution.py:584
  12.1 4.1 %collective-permute-start.2 = (bf16[272,384]{1,0:T(8,128)(2,1)S(1)}, bf16[272,384]{1,0:T(8,128)(2,1)S(1)}, u32[]{:S(2)}, u32[]{:S(2)}) collective-permute-start(bf16[272,384]{1,0:T(8,128)(2,1)S(1)} %get-tuple-element.66.refs_0_), channel_id=1, source_target_pairs={{0,1},{1,0},{2,3},{3,2},{4,5},{5,4},{6,7},{7,6},{8,9},{9,8},{10,11... | collective-permute-start | bytes 626696 | tf_op jit(solution)/shard_map/ppermute | solution.py:584
  12.2 29.2 %copy-start.11 = (bf16[256,384]{1,0:T(8,128)(2,1)}, bf16[256,384]{1,0:T(8,128)(2,1)S(1)}, u32[]{:S(2)}) copy-start(bf16[256,384]{1,0:T(8,128)(2,1)S(1)} %collective-permute-done.16.refs_5_) | copy-start | bytes 589828
  12.2 9.3 %collective-permute-start.19 = (bf16[256,384]{1,0:T(8,128)(2,1)S(1)}, bf16[256,384]{1,0:T(8,128)(2,1)S(1)}, u32[]{:S(2)}, u32[]{:S(2)}) collective-permute-start(bf16[256,384]{1,0:T(8,128)(2,1)S(1)} %collective-permute-done.15.refs_3_), channel_id=1, source_target_pairs={{0,4},{1,5},{2,6},{3,7},{4,8},{5,9},{6,10},{7,11},{8,12},{9,13},{1... | collective-permute-start | bytes 589832 | tf_op jit(solution)/shard_map/ppermute | solution.py:584
  13.2 8.3 %collective-permute-start.20 = (bf16[256,384]{1,0:T(8,128)(2,1)S(1)}, bf16[256,384]{1,0:T(8,128)(2,1)S(1)}, u32[]{:S(2)}, u32[]{:S(2)}) collective-permute-start(bf16[256,384]{1,0:T(8,128)(2,1)S(1)} %collective-permute-done.15.refs_3_), channel_id=1, source_target_pairs={{0,2},{1,3},{2,0},{3,1},{4,6},{5,7},{6,4},{7,5},{8,10},{9,11},{10,... | collective-permute-start | bytes 589832 | tf_op jit(solution)/shard_map/ppermute | solution.py:584
  16.2 26.4 %copy-start.3 = (bf16[272,384]{1,0:T(8,128)(2,1)}, bf16[272,384]{1,0:T(8,128)(2,1)S(1)}, u32[]{:S(2)}) copy-start(bf16[272,384]{1,0:T(8,128)(2,1)S(1)} %collective-permute-done.refs_2_) | copy-start | bytes 626692
  16.2 5.8 %collective-permute-start.21 = (bf16[256,384]{1,0:T(8,128)(2,1)S(1)}, bf16[256,384]{1,0:T(8,128)(2,1)}, u32[]{:S(2)}, u32[]{:S(2)}) collective-permute-start(bf16[256,384]{1,0:T(8,128)(2,1)S(1)} %collective-permute-done.15.refs_3_), channel_id=1, source_target_pairs={{0,1},{1,0},{2,3},{3,2},{4,5},{5,4},{6,7},{7,6},{8,9},{9,8},{10,11... | collective-permute-start | bytes 589832 | tf_op jit(solution)/shard_map/ppermute | solution.py:584
  16.2 26.4 %copy-start.4 = (bf16[272,384]{1,0:T(8,128)(2,1)}, bf16[272,384]{1,0:T(8,128)(2,1)S(1)}, u32[]{:S(2)}) copy-start(bf16[272,384]{1,0:T(8,128)(2,1)S(1)} %collective-permute-done.1.refs_4_) | copy-start | bytes 626692
  16.2 26.4 %copy-start.5 = (bf16[272,384]{1,0:T(8,128)(2,1)}, bf16[272,384]{1,0:T(8,128)(2,1)S(1)}, u32[]{:S(2)}) copy-start(bf16[272,384]{1,0:T(8,128)(2,1)S(1)} %collective-permute-done.2.refs_6_) | copy-start | bytes 626692
  16.2 9.6 %collective-permute-start.3 = (bf16[272,384]{1,0:T(8,128)(2,1)S(1)}, bf16[272,384]{1,0:T(8,128)(2,1)S(1)}, u32[]{:S(2)}, u32[]{:S(2)}) collective-permute-start(bf16[272,384]{1,0:T(8,128)(2,1)S(1)} %collective-permute-done.refs_2_), channel_id=1, source_target_pairs={{0,4},{1,5},{2,6},{3,7},{4,8},{5,9},{6,10},{7,11},{8,12},{9,13},{1... | collective-permute-start | bytes 626696 | tf_op jit(solution)/shard_map/ppermute | solution.py:584
  17.6 10.4 %collective-permute-start.4 = (bf16[272,384]{1,0:T(8,128)(2,1)S(1)}, bf16[272,384]{1,0:T(8,128)(2,1)S(1)}, u32[]{:S(2)}, u32[]{:S(2)}) collective-permute-start(bf16[272,384]{1,0:T(8,128)(2,1)S(1)} %collective-permute-done.refs_2_), channel_id=1, source_target_pairs={{0,2},{1,3},{2,0},{3,1},{4,6},{5,7},{6,4},{7,5},{8,10},{9,11},{10,... | collective-permute-start | bytes 626696 | tf_op jit(solution)/shard_map/ppermute | solution.py:584
  21.4 1.4 %collective-permute-start.22 = (bf16[256,384]{1,0:T(8,128)(2,1)S(1)}, bf16[256,384]{1,0:T(8,128)(2,1)S(1)}, u32[]{:S(2)}, u32[]{:S(2)}) collective-permute-start(bf16[256,384]{1,0:T(8,128)(2,1)S(1)} %collective-permute-done.16.refs_5_), channel_id=1, source_target_pairs={{0,1},{1,0},{2,3},{3,2},{4,5},{5,4},{6,7},{7,6},{8,9},{9,8},{10,11... | collective-permute-start | bytes 589832 | tf_op jit(solution)/shard_map/ppermute | solution.py:584
  21.5 6.6 %collective-permute-start.5 = (bf16[272,384]{1,0:T(8,128)(2,1)S(1)}, bf16[272,384]{1,0:T(8,128)(2,1)S(1)}, u32[]{:S(2)}, u32[]{:S(2)}) collective-permute-start(bf16[272,384]{1,0:T(8,128)(2,1)S(1)} %collective-permute-done.refs_2_), channel_id=1, source_target_pairs={{0,1},{1,0},{2,3},{3,2},{4,5},{5,4},{6,7},{7,6},{8,9},{9,8},{10,11... | collective-permute-start | bytes 626696 | tf_op jit(solution)/shard_map/ppermute | solution.py:584
  22.0 6.6 %collective-permute-start.6 = (bf16[272,384]{1,0:T(8,128)(2,1)S(1)}, bf16[272,384]{1,0:T(8,128)(2,1)S(1)}, u32[]{:S(2)}, u32[]{:S(2)}) collective-permute-start(bf16[272,384]{1,0:T(8,128)(2,1)S(1)} %collective-permute-done.1.refs_4_), channel_id=1, source_target_pairs={{0,1},{1,0},{2,3},{3,2},{4,5},{5,4},{6,7},{7,6},{8,9},{9,8},{10,11... | collective-permute-start | bytes 626696 | tf_op jit(solution)/shard_map/ppermute | solution.py:584
  22.9 8.7 %collective-permute-start.23 = (bf16[256,384]{1,0:T(8,128)(2,1)S(1)}, bf16[256,384]{1,0:T(8,128)(2,1)S(1)}, u32[]{:S(2)}, u32[]{:S(2)}) collective-permute-start(bf16[256,384]{1,0:T(8,128)(2,1)S(1)} %collective-permute-done.19.refs_9_), channel_id=1, source_target_pairs={{0,4},{1,5},{2,6},{3,7},{4,8},{5,9},{6,10},{7,11},{8,12},{9,13},{1... | collective-permute-start | bytes 589832 | tf_op jit(solution)/shard_map/ppermute | solution.py:584
  25.8 9.1 %collective-permute-start.24 = (bf16[256,384]{1,0:T(8,128)(2,1)S(1)}, bf16[256,384]{1,0:T(8,128)(2,1)}, u32[]{:S(2)}, u32[]{:S(2)}) collective-permute-start(bf16[256,384]{1,0:T(8,128)(2,1)S(1)} %collective-permute-done.19.refs_9_), channel_id=1, source_target_pairs={{0,2},{1,3},{2,0},{3,1},{4,6},{5,7},{6,4},{7,5},{8,10},{9,11},{10,... | collective-permute-start | bytes 589832 | tf_op jit(solution)/shard_map/ppermute | solution.py:584
  28.0 6.9 %collective-permute-start.25 = (bf16[256,384]{1,0:T(8,128)(2,1)S(1)}, bf16[256,384]{1,0:T(8,128)(2,1)S(1)}, u32[]{:S(2)}, u32[]{:S(2)}) collective-permute-start(bf16[256,384]{1,0:T(8,128)(2,1)S(1)} %collective-permute-done.19.refs_9_), channel_id=1, source_target_pairs={{0,1},{1,0},{2,3},{3,2},{4,5},{5,4},{6,7},{7,6},{8,9},{9,8},{10,11... | collective-permute-start | bytes 589832 | tf_op jit(solution)/shard_map/ppermute | solution.py:584
  28.1 7.3 %collective-permute-start.26 = (bf16[256,384]{1,0:T(8,128)(2,1)S(1)}, bf16[256,384]{1,0:T(8,128)(2,1)S(1)}, u32[]{:S(2)}, u32[]{:S(2)}) collective-permute-start(bf16[256,384]{1,0:T(8,128)(2,1)S(1)} %collective-permute-done.20.refs_11_), channel_id=1, source_target_pairs={{0,1},{1,0},{2,3},{3,2},{4,5},{5,4},{6,7},{7,6},{8,9},{9,8},{10,11... | collective-permute-start | bytes 589832 | tf_op jit(solution)/shard_map/ppermute | solution.py:584
  28.6 9.9 %collective-permute-start.7 = (bf16[272,384]{1,0:T(8,128)(2,1)S(1)}, bf16[272,384]{1,0:T(8,128)(2,1)}, u32[]{:S(2)}, u32[]{:S(2)}) collective-permute-start(bf16[272,384]{1,0:T(8,128)(2,1)S(1)} %collective-permute-done.3.refs_8_), channel_id=1, source_target_pairs={{0,4},{1,5},{2,6},{3,7},{4,8},{5,9},{6,10},{7,11},{8,12},{9,13},{1... | collective-permute-start | bytes 626696 | tf_op jit(solution)/shard_map/ppermute | solution.py:584
  31.6 7.2 %collective-permute-start.8 = (bf16[272,384]{1,0:T(8,128)(2,1)S(1)}, bf16[272,384]{1,0:T(8,128)(2,1)}, u32[]{:S(2)}, u32[]{:S(2)}) collective-permute-start(bf16[272,384]{1,0:T(8,128)(2,1)S(1)} %collective-permute-done.3.refs_8_), channel_id=1, source_target_pairs={{0,2},{1,3},{2,0},{3,1},{4,6},{5,7},{6,4},{7,5},{8,10},{9,11},{10,... | collective-permute-start | bytes 626696 | tf_op jit(solution)/shard_map/ppermute | solution.py:584
  34.9 3.9 %collective-permute-start.9 = (bf16[272,384]{1,0:T(8,128)(2,1)S(1)}, bf16[272,384]{1,0:T(8,128)(2,1)S(1)}, u32[]{:S(2)}, u32[]{:S(2)}) collective-permute-start(bf16[272,384]{1,0:T(8,128)(2,1)S(1)} %collective-permute-done.3.refs_8_), channel_id=1, source_target_pairs={{0,1},{1,0},{2,3},{3,2},{4,5},{5,4},{6,7},{7,6},{8,9},{9,8},{10,11... | collective-permute-start | bytes 626696 | tf_op jit(solution)/shard_map/ppermute | solution.py:584
  34.9 3.9 %collective-permute-start.10 = (bf16[272,384]{1,0:T(8,128)(2,1)S(1)}, bf16[272,384]{1,0:T(8,128)(2,1)S(1)}, u32[]{:S(2)}, u32[]{:S(2)}) collective-permute-start(bf16[272,384]{1,0:T(8,128)(2,1)S(1)} %collective-permute-done.4.refs_10_), channel_id=1, source_target_pairs={{0,1},{1,0},{2,3},{3,2},{4,5},{5,4},{6,7},{7,6},{8,9},{9,8},{10,11... | collective-permute-start | bytes 626696 | tf_op jit(solution)/shard_map/ppermute | solution.py:584
  35.4 7.1 %collective-permute-start.18 = (bf16[256,384]{1,0:T(8,128)(2,1)S(1)}, bf16[256,384]{1,0:T(8,128)(2,1)S(1)}, u32[]{:S(2)}, u32[]{:S(2)}) collective-permute-start(bf16[256,384]{1,0:T(8,128)(2,1)S(1)} %collective-permute-done.16.refs_5_), channel_id=1, source_target_pairs={{0,12},{1,13},{2,14},{3,15},{4,0},{5,1},{6,2},{7,3},{8,4},{9,5},{1... | collective-permute-start | bytes 589832 | tf_op jit(solution)/shard_map/ppermute | solution.py:584
  38.6 3.9 %collective-permute-start.27 = (bf16[256,384]{1,0:T(8,128)(2,1)S(1)}, bf16[256,384]{1,0:T(8,128)(2,1)S(1)}, u32[]{:S(2)}, u32[]{:S(2)}) collective-permute-start(bf16[256,384]{1,0:T(8,128)(2,1)S(1)} %collective-permute-done.23.refs_17_), channel_id=1, source_target_pairs={{0,1},{1,0},{2,3},{3,2},{4,5},{5,4},{6,7},{7,6},{8,9},{9,8},{10,11... | collective-permute-start | bytes 589832 | tf_op jit(solution)/shard_map/ppermute | solution.py:584
  38.9 12.8 %collective-permute-start.11 = (bf16[272,384]{1,0:T(8,128)(2,1)}, bf16[272,384]{1,0:T(8,128)(2,1)S(1)}, u32[]{:S(2)}, u32[]{:S(2)}) collective-permute-start(bf16[272,384]{1,0:T(8,128)(2,1)} %collective-permute-done.7.refs_16_), channel_id=1, source_target_pairs={{0,2},{1,3},{2,0},{3,1},{4,6},{5,7},{6,4},{7,5},{8,10},{9,11},{10,... | collective-permute-start | bytes 626696 | tf_op jit(solution)/shard_map/ppermute | solution.py:584
  40.9 10.8 %collective-permute-start.12 = (bf16[272,384]{1,0:T(8,128)(2,1)}, bf16[272,384]{1,0:T(8,128)(2,1)S(1)}, u32[]{:S(2)}, u32[]{:S(2)}) collective-permute-start(bf16[272,384]{1,0:T(8,128)(2,1)} %collective-permute-done.7.refs_16_), channel_id=1, source_target_pairs={{0,1},{1,0},{2,3},{3,2},{4,5},{5,4},{6,7},{7,6},{8,9},{9,8},{10,11... | collective-permute-start | bytes 626696 | tf_op jit(solution)/shard_map/ppermute | solution.py:584
  40.9 10.8 %collective-permute-start.13 = (bf16[272,384]{1,0:T(8,128)(2,1)}, bf16[272,384]{1,0:T(8,128)(2,1)S(1)}, u32[]{:S(2)}, u32[]{:S(2)}) collective-permute-start(bf16[272,384]{1,0:T(8,128)(2,1)} %collective-permute-done.8.refs_18_), channel_id=1, source_target_pairs={{0,1},{1,0},{2,3},{3,2},{4,5},{5,4},{6,7},{7,6},{8,9},{9,8},{10,11... | collective-permute-start | bytes 626696 | tf_op jit(solution)/shard_map/ppermute | solution.py:584
  42.5 8.7 %collective-permute-start.28 = (bf16[256,384]{1,0:T(8,128)(2,1)}, bf16[256,384]{1,0:T(8,128)(2,1)S(1)}, u32[]{:S(2)}, u32[]{:S(2)}) collective-permute-start(bf16[256,384]{1,0:T(8,128)(2,1)} %collective-permute-done.24.refs_19_), channel_id=1, source_target_pairs={{0,1},{1,0},{2,3},{3,2},{4,5},{5,4},{6,7},{7,6},{8,9},{9,8},{10,11... | collective-permute-start | bytes 589832 | tf_op jit(solution)/shard_map/ppermute | solution.py:584
  42.5 9.2 %collective-permute-start.14 = (bf16[256,256]{1,0:T(8,128)(2,1)}, bf16[256,256]{1,0:T(8,128)(2,1)S(1)}, u32[]{:S(2)}, u32[]{:S(2)}) collective-permute-start(bf16[256,256]{1,0:T(8,128)(2,1)} %param.8), channel_id=1, source_target_pairs={{0,8},{1,9},{2,10},{3,11},{4,12},{5,13},{6,14},{7,15},{8,0},{9,1},... | collective-permute-start | bytes 393224 | tf_op jit(solution)/shard_map/ppermute | solution.py:584
  51.8 8.7 %collective-permute-start.31 = (bf16[2,256,256]{2,1,0:T(8,128)(2,1)S(1)}, bf16[2,256,256]{2,1,0:T(8,128)(2,1)S(1)}, u32[]{:S(2)}, u32[]{:S(2)}) collective-permute-start(bf16[2,256,256]{2,1,0:T(8,128)(2,1)S(1)} %pad_maximum_fusion), channel_id=1, source_target_pairs={{0,4},{1,5},{2,6},{3,7},{4,0},{5,1},{6,2},{7,3},{8,12},{9,13},{10,... | collective-permute-start | bytes 786440 | tf_op jit(solution)/shard_map/ppermute | solution.py:563
  53.8 1.7 %collective-permute-start.29 = (bf16[272,384]{1,0:T(8,128)(2,1)S(1)}, bf16[272,384]{1,0:T(8,128)(2,1)S(1)}, u32[]{:S(2)}, u32[]{:S(2)}) collective-permute-start(bf16[272,384]{1,0:T(8,128)(2,1)S(1)} %collective-permute-done.11.refs_0_), channel_id=1, source_target_pairs={{0,1},{1,0},{2,3},{3,2},{4,5},{5,4},{6,7},{7,6},{8,9},{9,8},{10,11... | collective-permute-start | bytes 626696 | tf_op jit(solution)/shard_map/ppermute | solution.py:584
  53.8 1.7 %collective-permute-start.30 = (bf16[256,384]{1,0:T(8,128)(2,1)S(1)}, bf16[256,384]{1,0:T(8,128)(2,1)S(1)}, u32[]{:S(2)}, u32[]{:S(2)}) collective-permute-start(bf16[256,384]{1,0:T(8,128)(2,1)S(1)} %collective-permute-done.18.refs_1_), channel_id=1, source_target_pairs={{0,1},{1,0},{2,3},{3,2},{4,5},{5,4},{6,7},{7,6},{8,9},{9,8},{10,11... | collective-permute-start | bytes 589832 | tf_op jit(solution)/shard_map/ppermute | solution.py:584
  60.5 26.6 %all-to-all-start = ((bf16[16,128,256]{2,1,0:T(8,128)(2,1)}), bf16[16,128,256]{2,1,0:T(8,128)(2,1)S(1)}, u32[]{:S(2)}, u32[]{:S(2)}) async-start(bf16[16,128,256]{2,1,0:T(8,128)(2,1)} %get-tuple-element.115), calls=%async_computation | async-start | bytes 2097152 | tf_op jit(solution)/shard_map/all_to_all | solution.py:668
  64.5 8.4 %collective-permute-start.32 = (bf16[2,256,256]{2,1,0:T(8,128)(2,1)S(1)}, bf16[2,256,256]{2,1,0:T(8,128)(2,1)S(1)}, u32[]{:S(2)}, u32[]{:S(2)}) collective-permute-start(bf16[2,256,256]{2,1,0:T(8,128)(2,1)S(1)} %pad_maximum_fusion.2), channel_id=1, source_target_pairs={{0,16},{16,0},{1,17},{17,1},{2,18},{18,2},{3,19},{19,3},{4,20},{20... | collective-permute-start | bytes 786440 | tf_op jit(solution)/shard_map/ppermute | solution.py:628
  73.1 17.9 %collective-permute-start.33 = (bf16[2,256,512]{2,1,0:T(8,128)(2,1)S(1)}, bf16[2,256,512]{2,1,0:T(8,128)(2,1)S(1)}, u32[]{:S(2)}, u32[]{:S(2)}) collective-permute-start(bf16[2,256,512]{2,1,0:T(8,128)(2,1)S(1)} %join_rows.1.refs_0_), channel_id=1, source_target_pairs={{0,2},{1,3},{2,0},{3,1},{4,6},{5,7},{6,4},{7,5},{8,10},{9,11},{10,... | collective-permute-start | bytes 1572872 | tf_op jit(solution)/shard_map/ppermute | solution.py:563
  91.1 22.1 %all-to-all-start.1 = ((bf16[16,144,128]{2,1,0:T(8,128)(2,1)}), bf16[16,144,128]{2,1,0:T(8,128)(2,1)S(1)}, u32[]{:S(2)}, u32[]{:S(2)}) async-start(bf16[16,144,128]{2,1,0:T(8,128)(2,1)} %get-tuple-element.124), calls=%async_computation.1 | async-start | bytes 1179648 | tf_op jit(solution)/shard_map/all_to_all | solution.py:680
  97.6 20.6 %collective-permute-start.34 = (bf16[2,256,512]{2,1,0:T(8,128)(2,1)S(1)}, bf16[2,256,512]{2,1,0:T(8,128)(2,1)S(1)}, u32[]{:S(2)}, u32[]{:S(2)}) collective-permute-start(bf16[2,256,512]{2,1,0:T(8,128)(2,1)S(1)} %join_rows.1.refs_0_), channel_id=1, source_target_pairs={{0,1},{1,0},{2,3},{3,2},{4,5},{5,4},{6,7},{7,6},{8,9},{9,8},{10,11... | collective-permute-start | bytes 1572872 | tf_op jit(solution)/shard_map/ppermute | solution.py:563
  98.0 20.7 %collective-permute-start.35 = (bf16[2,256,512]{2,1,0:T(8,128)(2,1)S(1)}, bf16[2,256,512]{2,1,0:T(8,128)(2,1)S(1)}, u32[]{:S(2)}, u32[]{:S(2)}) collective-permute-start(bf16[2,256,512]{2,1,0:T(8,128)(2,1)S(1)} %collective-permute-done.33.refs_1_), channel_id=1, source_target_pairs={{0,1},{1,0},{2,3},{3,2},{4,5},{5,4},{6,7},{7,6},{8,9},{9,8},{10,11... | collective-permute-start | bytes 1572872 | tf_op jit(solution)/shard_map/ppermute | solution.py:563
  114.6 6.4 %collective-permute-start.39 = (bf16[256,256]{1,0:T(8,128)(2,1)S(1)}, bf16[256,256]{1,0:T(8,128)(2,1)S(1)}, u32[]{:S(2)}, u32[]{:S(2)}) collective-permute-start(bf16[256,256]{1,0:T(8,128)(2,1)S(1)} %get-tuple-element.128.refs_4_), channel_id=1, source_target_pairs={{0,16},{16,0},{1,17},{17,1},{2,18},{18,2},{3,19},{19,3},{4,20},{20... | collective-permute-start | bytes 393224 | tf_op jit(solution)/shard_map/ppermute | solution.py:684
  116.2 7.7 %collective-permute-start.38 = (bf16[256,256]{1,0:T(8,128)(2,1)S(1)}, bf16[256,256]{1,0:T(8,128)(2,1)S(1)}, u32[]{:S(2)}, u32[]{:S(2)}) collective-permute-start(bf16[256,256]{1,0:T(8,128)(2,1)S(1)} %get-tuple-element.127.refs_4_), channel_id=1, source_target_pairs={{0,16},{16,0},{1,17},{17,1},{2,18},{18,2},{3,19},{19,3},{4,20},{20... | collective-permute-start | bytes 393224 | tf_op jit(solution)/shard_map/ppermute | solution.py:684
  116.7 10.0 %collective-permute-start.37 = (bf16[256,256]{1,0:T(8,128)(2,1)S(1)}, bf16[256,256]{1,0:T(8,128)(2,1)S(1)}, u32[]{:S(2)}, u32[]{:S(2)}) collective-permute-start(bf16[256,256]{1,0:T(8,128)(2,1)S(1)} %get-tuple-element.126.refs_4_), channel_id=1, source_target_pairs={{0,16},{16,0},{1,17},{17,1},{2,18},{18,2},{3,19},{19,3},{4,20},{20... | collective-permute-start | bytes 393224 | tf_op jit(solution)/shard_map/ppermute | solution.py:684
  118.2 10.3 %collective-permute-start.36 = (bf16[256,256]{1,0:T(8,128)(2,1)S(1)}, bf16[256,256]{1,0:T(8,128)(2,1)S(1)}, u32[]{:S(2)}, u32[]{:S(2)}) collective-permute-start(bf16[256,256]{1,0:T(8,128)(2,1)S(1)} %get-tuple-element.125.refs_4_), channel_id=1, source_target_pairs={{0,16},{16,0},{1,17},{17,1},{2,18},{18,2},{3,19},{19,3},{4,20},{20... | collective-permute-start | bytes 393224 | tf_op jit(solution)/shard_map/ppermute | solution.py:684
  (11 other events, 135.9 us)

commit v8 on v7

--- a/solution.py
+++ b/solution.py
@@ -400,8 +400,7 @@
             held_ref[c, head_dim:, :] = jnp.where(
                 line == 0, high, jnp.where(line == 1, mass - high, 0.0)
             ).astype(jnp.bfloat16)
-            if not full:
-                move.start()
+            move.start()
 
         if full:
             attend()
@@ -409,9 +408,6 @@
         else:
             pl.when(held > 1)(attend)
             waits.append((held > 1, move.wait))
-    if full:
-        for move in waits:
-            move.start()
     for c, (held, first, second) in enumerate(entries):
         first_sum, other_sum = (
             jnp.sum(in_ref[source, :, :head_dim].astype(jnp.float32), axis=0, keepdims=True)

time: 131 us -> 131 us (level)
  no operation moved by 1% of the time
where the time goes in v8:
time: 131 us; the launch traced here: 130 us
  waiting for transfers between devices  54.6 us (42%)
  starting transfers between devices  43.5 us (33%)
  Pallas kernels  30.6 us (23%)
    ppermute x31, starting transfers between devices, hop(): lax.ppermute(value, axis, pairs)  23.1 us
    ppermute x31, waiting for transfers between devices, hop(): lax.ppermute(value, axis, pairs)  19.7 us
    all_to_all x1, waiting for transfers between devices, on_device(): lax.all_to_all(returning, 'seq', split_axis=0, concat_axis=0, tiled=True)  15 us
    pallas_call x1, Pallas kernels, project_early(): pl.pallas_call(functools.partial(early_kernel, n_early, n_late, paired),...  8.56 us
    all_to_all x1, waiting for transfers between devices, on_device(): lax.all_to_all(outgoing, 'seq', split_axis=0, concat_axis=0, tiled=True)  6.87 us
    ppermute x1, waiting for transfers between devices, make_pair(): return join_rows(keep, lax.ppermute(give, 'head', SWAP))  6.83 us
    all_to_all x1, starting transfers between devices, on_device(): lax.all_to_all(returning, 'seq', split_axis=0, concat_axis=0, tiled=True)  6.49 us
    pallas_call x4, Pallas kernels, output_projection(): pl.pallas_call(functools.partial(output_kernel, len(weights), len(parts),...  6.21 us
  transfers between devices with their start and end apart: 42, of which 20 were waited for; matrix products, arithmetic and copies ran while one was open for 0% of the time, Pallas kernels for 22%

profile of v8, /device:TPU:0, one launch (start us, length us, event | category | flops | bytes accessed | tf_op | source)
XLA Modules:
  0.0 130.2 jit_solution(17939760396616022501)
XLA Ops:
  0.6 1.0 split_weight.1
  1.7 3.1 %collective-permute-start.15 = (bf16[256,384]{1,0:T(8,128)(2,1)S(1)}, bf16[256,384]{1,0:T(8,128)(2,1)S(1)}, u32[]{:S(2)}, u32[]{:S(2)}) collective-permute-start(bf16[256,384]{1,0:T(8,128)(2,1)S(1)} %get-tuple-element.76.refs_1_), channel_id=1, source_target_pairs={{0,4},{1,5},{2,6},{3,7},{4,8},{5,9},{6,10},{7,11},{8,12},{9,13},{1... | collective-permute-start | bytes 589832 | tf_op jit(solution)/shard_map/ppermute | solution.py:580
  4.8 1.5 %collective-permute-start.16 = (bf16[256,384]{1,0:T(8,128)(2,1)S(1)}, bf16[256,384]{1,0:T(8,128)(2,1)S(1)}, u32[]{:S(2)}, u32[]{:S(2)}) collective-permute-start(bf16[256,384]{1,0:T(8,128)(2,1)S(1)} %get-tuple-element.76.refs_1_), channel_id=1, source_target_pairs={{0,2},{1,3},{2,0},{3,1},{4,6},{5,7},{6,4},{7,5},{8,10},{9,11},{10,... | collective-permute-start | bytes 589832 | tf_op jit(solution)/shard_map/ppermute | solution.py:580
  6.3 1.6 %collective-permute-start = (bf16[272,384]{1,0:T(8,128)(2,1)S(1)}, bf16[272,384]{1,0:T(8,128)(2,1)S(1)}, u32[]{:S(2)}, u32[]{:S(2)}) collective-permute-start(bf16[272,384]{1,0:T(8,128)(2,1)S(1)} %get-tuple-element.66.refs_0_), channel_id=1, source_target_pairs={{0,4},{1,5},{2,6},{3,7},{4,8},{5,9},{6,10},{7,11},{8,12},{9,13},{1... | collective-permute-start | bytes 626696 | tf_op jit(solution)/shard_map/ppermute | solution.py:580
  8.4 3.8 %collective-permute-done.15.refs_3_ = bf16[256,384]{1,0:T(8,128)(2,1)S(1)} collective-permute-done((bf16[256,384]{1,0:T(8,128)(2,1)S(1)}, bf16[256,384]{1,0:T(8,128)(2,1)S(1)}, u32[]{:S(2)}, u32[]{:S(2)}) %collective-permute-start.15) | collective-permute-done | bytes 196640 | tf_op jit(solution)/shard_map/ppermute | solution.py:580
  12.2 1.0 collective-permute-start.19
  13.2 2.5 %collective-permute-start.20 = (bf16[256,384]{1,0:T(8,128)(2,1)S(1)}, bf16[256,384]{1,0:T(8,128)(2,1)S(1)}, u32[]{:S(2)}, u32[]{:S(2)}) collective-permute-start(bf16[256,384]{1,0:T(8,128)(2,1)S(1)} %collective-permute-done.15.refs_3_), channel_id=1, source_target_pairs={{0,2},{1,3},{2,0},{3,1},{4,6},{5,7},{6,4},{7,5},{8,10},{9,11},{10,... | collective-permute-start | bytes 589832 | tf_op jit(solution)/shard_map/ppermute | solution.py:580
  16.2 1.3 %collective-permute-start.3 = (bf16[272,384]{1,0:T(8,128)(2,1)S(1)}, bf16[272,384]{1,0:T(8,128)(2,1)S(1)}, u32[]{:S(2)}, u32[]{:S(2)}) collective-permute-start(bf16[272,384]{1,0:T(8,128)(2,1)S(1)} %collective-permute-done.refs_2_), channel_id=1, source_target_pairs={{0,4},{1,5},{2,6},{3,7},{4,8},{5,9},{6,10},{7,11},{8,12},{9,13},{1... | collective-permute-start | bytes 626696 | tf_op jit(solution)/shard_map/ppermute | solution.py:580
  17.6 1.3 collective-permute-start.4
  18.9 2.6 %collective-permute-done.19.refs_9_ = bf16[256,384]{1,0:T(8,128)(2,1)S(1)} collective-permute-done((bf16[256,384]{1,0:T(8,128)(2,1)S(1)}, bf16[256,384]{1,0:T(8,128)(2,1)S(1)}, u32[]{:S(2)}, u32[]{:S(2)}) %collective-permute-start.19) | collective-permute-done | bytes 196640 | tf_op jit(solution)/shard_map/ppermute | solution.py:580
  21.5 0.6 collective-permute-start.5
  22.1 0.8 collective-permute-done.22.refs_15_
  22.9 2.9 %collective-permute-done.3.refs_8_ = bf16[272,384]{1,0:T(8,128)(2,1)S(1)} collective-permute-done((bf16[272,384]{1,0:T(8,128)(2,1)S(1)}, bf16[272,384]{1,0:T(8,128)(2,1)S(1)}, u32[]{:S(2)}, u32[]{:S(2)}) %collective-permute-start.3) | collective-permute-done | bytes 208928 | tf_op jit(solution)/shard_map/ppermute | solution.py:580
  25.8 2.2 %collective-permute-start.24 = (bf16[256,384]{1,0:T(8,128)(2,1)S(1)}, bf16[256,384]{1,0:T(8,128)(2,1)}, u32[]{:S(2)}, u32[]{:S(2)}) collective-permute-start(bf16[256,384]{1,0:T(8,128)(2,1)S(1)} %collective-permute-done.19.refs_9_), channel_id=1, source_target_pairs={{0,2},{1,3},{2,0},{3,1},{4,6},{5,7},{6,4},{7,5},{8,10},{9,11},{10,... | collective-permute-start | bytes 589832 | tf_op jit(solution)/shard_map/ppermute | solution.py:580
  28.1 0.5 collective-permute-start.26
  28.6 3.0 %collective-permute-done.23.refs_17_ = bf16[256,384]{1,0:T(8,128)(2,1)S(1)} collective-permute-done((bf16[256,384]{1,0:T(8,128)(2,1)S(1)}, bf16[256,384]{1,0:T(8,128)(2,1)S(1)}, u32[]{:S(2)}, u32[]{:S(2)}) %collective-permute-start.23) | collective-permute-done | bytes 196640 | tf_op jit(solution)/shard_map/ppermute | solution.py:580
  31.6 3.3 %collective-permute-start.8 = (bf16[272,384]{1,0:T(8,128)(2,1)S(1)}, bf16[272,384]{1,0:T(8,128)(2,1)}, u32[]{:S(2)}, u32[]{:S(2)}) collective-permute-start(bf16[272,384]{1,0:T(8,128)(2,1)S(1)} %collective-permute-done.3.refs_8_), channel_id=1, source_target_pairs={{0,2},{1,3},{2,0},{3,1},{4,6},{5,7},{6,4},{7,5},{8,10},{9,11},{10,... | collective-permute-start | bytes 626696 | tf_op jit(solution)/shard_map/ppermute | solution.py:580
  35.4 3.1 %collective-permute-done.7.refs_16_ = bf16[272,384]{1,0:T(8,128)(2,1)} collective-permute-done((bf16[272,384]{1,0:T(8,128)(2,1)S(1)}, bf16[272,384]{1,0:T(8,128)(2,1)}, u32[]{:S(2)}, u32[]{:S(2)}) %collective-permute-start.7) | collective-permute-done | bytes 208928 | tf_op jit(solution)/shard_map/ppermute | solution.py:580
  38.9 2.0 %collective-permute-start.11 = (bf16[272,384]{1,0:T(8,128)(2,1)}, bf16[272,384]{1,0:T(8,128)(2,1)S(1)}, u32[]{:S(2)}, u32[]{:S(2)}) collective-permute-start(bf16[272,384]{1,0:T(8,128)(2,1)} %collective-permute-done.7.refs_16_), channel_id=1, source_target_pairs={{0,2},{1,3},{2,0},{3,1},{4,6},{5,7},{6,4},{7,5},{8,10},{9,11},{10,... | collective-permute-start | bytes 626696 | tf_op jit(solution)/shard_map/ppermute | solution.py:580
  40.9 0.5 collective-permute-start.13
  41.4 1.1 collective-permute-done.18.refs_1_
  42.7 8.6 %project_early.1 = (f32[1024,768]{1,0:T(8,128)S(1)}, bf16[1024,1024]{1,0:T(8,128)(2,1)S(1)}, f32[16,128]{1,0:T(8,128)S(1)}, f32[1024,128]{1,0:T(8,128)S(1)}) custom-call(s32[1]{0:T(128)} %bitcast.me_ref, bf16[1024,4096]{1,0:T(8,128)(2,1)} %x_ref.1, bf16[272,384]{1,0:T(8,128)(2,1)} %copy-done, bf16[256,384]{1,0:T(8,128)(2,1)} %copy-done.1, ...), custom_call_target="tpu_custom_call" | custom-call | flops 1 | bytes 1 | tf_op jit(solution)/shard_map/project_early/pallas_call | solution.py:176
  51.8 2.0 %collective-permute-start.31 = (bf16[2,256,256]{2,1,0:T(8,128)(2,1)S(1)}, bf16[2,256,256]{2,1,0:T(8,128)(2,1)S(1)}, u32[]{:S(2)}, u32[]{:S(2)}) collective-permute-start(bf16[2,256,256]{2,1,0:T(8,128)(2,1)S(1)} %pad_maximum_fusion), channel_id=1, source_target_pairs={{0,4},{1,5},{2,6},{3,7},{4,0},{5,1},{6,2},{7,3},{8,12},{9,13},{10,... | collective-permute-start | bytes 786440 | tf_op jit(solution)/shard_map/ppermute | solution.py:559
  53.8 0.5 collective-permute-start.30
  54.3 1.2 collective-permute-done.30.refs_7_
  55.5 4.3 %project_late.1 = (bf16[1024,768]{1,0:T(8,128)(2,1)}, bf16[16,128,256]{2,1,0:T(8,128)(2,1)}, s32[8,128]{1,0:T(8,128)S(1)}) custom-call(s32[1]{0:T(128)} %bitcast.me_ref, s32[2,8]{1,0:T(2,128)} %cluster_ref.3, f32[1024,768]{1,0:T(8,128)S(1)} %get-tuple-element.100.acc_ref, bf16[1024,1024]{1,0:T(8,128)(2,1)S(1)} %get-tuple-element.101.rest_ref, ...), custom_call_target="tpu_custom_call" | custom-call | flops 1 | bytes 1 | tf_op jit(solution)/shard_map/project_late/pallas_call | solution.py:314
  59.8 0.7 collective-permute-done.31
  60.5 3.8 %all-to-all-start = ((bf16[16,128,256]{2,1,0:T(8,128)(2,1)}), bf16[16,128,256]{2,1,0:T(8,128)(2,1)S(1)}, u32[]{:S(2)}, u32[]{:S(2)}) async-start(bf16[16,128,256]{2,1,0:T(8,128)(2,1)} %get-tuple-element.115), calls=%async_computation | async-start | bytes 2097152 | tf_op jit(solution)/shard_map/all_to_all | solution.py:664
  64.5 1.6 %collective-permute-start.32 = (bf16[2,256,256]{2,1,0:T(8,128)(2,1)S(1)}, bf16[2,256,256]{2,1,0:T(8,128)(2,1)S(1)}, u32[]{:S(2)}, u32[]{:S(2)}) collective-permute-start(bf16[2,256,256]{2,1,0:T(8,128)(2,1)S(1)} %pad_maximum_fusion.2), channel_id=1, source_target_pairs={{0,16},{16,0},{1,17},{17,1},{2,18},{18,2},{3,19},{19,3},{4,20},{20... | collective-permute-start | bytes 786440 | tf_op jit(solution)/shard_map/ppermute | solution.py:624
  66.1 6.8 %collective-permute-done.32.got_ref = bf16[2,256,256]{2,1,0:T(8,128)(2,1)S(1)} collective-permute-done((bf16[2,256,256]{2,1,0:T(8,128)(2,1)S(1)}, bf16[2,256,256]{2,1,0:T(8,128)(2,1)S(1)}, u32[]{:S(2)}, u32[]{:S(2)}) %collective-permute-start.32) | collective-permute-done | bytes 262176 | tf_op jit(solution)/shard_map/ppermute | solution.py:624
  73.1 1.7 %collective-permute-start.33 = (bf16[2,256,512]{2,1,0:T(8,128)(2,1)S(1)}, bf16[2,256,512]{2,1,0:T(8,128)(2,1)S(1)}, u32[]{:S(2)}, u32[]{:S(2)}) collective-permute-start(bf16[2,256,512]{2,1,0:T(8,128)(2,1)S(1)} %join_rows.1.refs_0_), channel_id=1, source_target_pairs={{0,2},{1,3},{2,0},{3,1},{4,6},{5,7},{6,4},{7,5},{8,10},{9,11},{10,... | collective-permute-start | bytes 1572872 | tf_op jit(solution)/shard_map/ppermute | solution.py:559
  74.9 5.4 %inner_attention.1 = (f32[256,1024]{1,0:T(8,128)}, f32[16,1024]{1,0:T(8,128)}) custom-call(bf16[1024,768]{1,0:T(8,128)(2,1)} %get-tuple-element.116.qkv_ref), custom_call_target="tpu_custom_call" | custom-call | flops 1 | bytes 1 | tf_op jit(solution)/shard_map/inner_attention/pallas_call | solution.py:361
  80.2 6.9 %all-to-all-done.in_ref = bf16[16,128,256]{2,1,0:T(8,128)(2,1)S(1)} async-done(((bf16[16,128,256]{2,1,0:T(8,128)(2,1)}), bf16[16,128,256]{2,1,0:T(8,128)(2,1)S(1)}, u32[]{:S(2)}, u32[]{:S(2)}) %all-to-all-start) | async-done | bytes 1048608 | tf_op jit(solution)/shard_map/all_to_all | solution.py:664
  87.1 3.5 %owner_attention.1 = (bf16[16,144,128]{2,1,0:T(8,128)(2,1)}, f32[8,128]{1,0:T(8,128)}) custom-call(s32[8,128]{1,0:T(8,128)S(1)} %get-tuple-element.114.table_ref, bf16[16,128,256]{2,1,0:T(8,128)(2,1)S(1)} %all-to-all-done.in_ref, f32[8,128]{1,0:T(8,128)} %bitcast.9), custom_call_target="tpu_custom_call" | custom-call | flops 1 | bytes 1 | tf_op jit(solution)/shard_map/owner_attention/pallas_call | solution.py:433
  91.1 6.5 %all-to-all-start.1 = ((bf16[16,144,128]{2,1,0:T(8,128)(2,1)}), bf16[16,144,128]{2,1,0:T(8,128)(2,1)S(1)}, u32[]{:S(2)}, u32[]{:S(2)}) async-start(bf16[16,144,128]{2,1,0:T(8,128)(2,1)} %get-tuple-element.124), calls=%async_computation.1 | async-start | bytes 1179648 | tf_op jit(solution)/shard_map/all_to_all | solution.py:676
  98.1 15.0 %all-to-all-done.1.back_ref = bf16[16,144,128]{2,1,0:T(8,128)(2,1)S(1)} async-done(((bf16[16,144,128]{2,1,0:T(8,128)(2,1)}), bf16[16,144,128]{2,1,0:T(8,128)(2,1)S(1)}, u32[]{:S(2)}, u32[]{:S(2)}) %all-to-all-start.1) | async-done | bytes 589856 | tf_op jit(solution)/shard_map/all_to_all | solution.py:676
  113.1 1.5 %merge_attention.1 = (bf16[256,256]{1,0:T(8,128)(2,1)S(1)}, bf16[256,256]{1,0:T(8,128)(2,1)S(1)}, bf16[256,256]{1,0:T(8,128)(2,1)S(1)}, bf16[256,256]{1,0:T(8,128)(2,1)S(1)}) custom-call(s32[2,8]{1,0:T(2,128)} %cluster_ref.3, s32[8,128]{1,0:T(8,128)S(1)} %get-tuple-element.114.table_ref, f32[256,1024]{1,0:T(8,128)} %get-tuple-element.122.sums_ref, ...), custom_call_target="tpu_custom_call" | custom-call | flops 1 | bytes 1 | tf_op jit(solution)/shard_map/merge_attention/pallas_call | solution.py:471
  114.6 1.6 %collective-permute-start.39 = (bf16[256,256]{1,0:T(8,128)(2,1)S(1)}, bf16[256,256]{1,0:T(8,128)(2,1)S(1)}, u32[]{:S(2)}, u32[]{:S(2)}) collective-permute-start(bf16[256,256]{1,0:T(8,128)(2,1)S(1)} %get-tuple-element.128.refs_4_), channel_id=1, source_target_pairs={{0,16},{16,0},{1,17},{17,1},{2,18},{18,2},{3,19},{19,3},{4,20},{20... | collective-permute-start | bytes 393224 | tf_op jit(solution)/shard_map/ppermute | solution.py:680
  116.1 0.5 collective-permute-start.38
  116.7 1.5 %collective-permute-start.37 = (bf16[256,256]{1,0:T(8,128)(2,1)S(1)}, bf16[256,256]{1,0:T(8,128)(2,1)S(1)}, u32[]{:S(2)}, u32[]{:S(2)}) collective-permute-start(bf16[256,256]{1,0:T(8,128)(2,1)S(1)} %get-tuple-element.126.refs_4_), channel_id=1, source_target_pairs={{0,16},{16,0},{1,17},{17,1},{2,18},{18,2},{3,19},{19,3},{4,20},{20... | collective-permute-start | bytes 393224 | tf_op jit(solution)/shard_map/ppermute | solution.py:680
  118.1 0.5 collective-permute-start.36
  118.7 2.3 %collective-permute-done.39.refs_5_ = bf16[256,256]{1,0:T(8,128)(2,1)S(1)} collective-permute-done((bf16[256,256]{1,0:T(8,128)(2,1)S(1)}, bf16[256,256]{1,0:T(8,128)(2,1)S(1)}, u32[]{:S(2)}, u32[]{:S(2)}) %collective-permute-start.39) | collective-permute-done | bytes 131104 | tf_op jit(solution)/shard_map/ppermute | solution.py:680
  121.0 1.6 %output_projection.4.refs_6_ = bf16[2048,1024]{1,0:T(8,128)(2,1)} custom-call(s32[1]{0:T(128)} %bitcast.me_ref, bf16[2,256,512]{2,1,0:T(8,128)(2,1)S(1)} %join_rows.1.refs_0_, bf16[2,256,512]{2,1,0:T(8,128)(2,1)S(1)} %collective-permute-done.33.refs_1_, bf16[2,256,512]{2,1,0:T(8,128)(2,1)S(1)} %collective-permute-done.34.refs_2_, ...), custom_call_target="tpu_custom_call" | custom-call | flops 1 | bytes 1 | tf_op jit(solution)/shard_map/output_projection/pallas_call | solution.py:520
  122.5 1.2 collective-permute-done.38.refs_5_
  123.8 1.6 %output_projection.5.refs_6_ = bf16[2048,1024]{1,0:T(8,128)(2,1)} custom-call(s32[1]{0:T(128)} %bitcast.me_ref, bf16[2,256,512]{2,1,0:T(8,128)(2,1)S(1)} %join_rows.1.refs_0_, bf16[2,256,512]{2,1,0:T(8,128)(2,1)S(1)} %collective-permute-done.33.refs_1_, bf16[2,256,512]{2,1,0:T(8,128)(2,1)S(1)} %collective-permute-done.34.refs_2_, ...), custom_call_target="tpu_custom_call", output_to_operand_aliasing={{}: (7, {})} | custom-call | flops 1 | bytes 1 | tf_op jit(solution)/shard_map/output_projection/pallas_call | solution.py:520
  125.4 1.2 collective-permute-done.37.refs_5_
  126.6 1.6 %output_projection.6.refs_6_ = bf16[2048,1024]{1,0:T(8,128)(2,1)} custom-call(s32[1]{0:T(128)} %bitcast.me_ref, bf16[2,256,512]{2,1,0:T(8,128)(2,1)S(1)} %join_rows.1.refs_0_, bf16[2,256,512]{2,1,0:T(8,128)(2,1)S(1)} %collective-permute-done.33.refs_1_, bf16[2,256,512]{2,1,0:T(8,128)(2,1)S(1)} %collective-permute-done.34.refs_2_, ...), custom_call_target="tpu_custom_call", output_to_operand_aliasing={{}: (7, {})} | custom-call | flops 1 | bytes 1 | tf_op jit(solution)/shard_map/output_projection/pallas_call | solution.py:520
  128.5 1.6 %output_projection.7 = bf16[2048,1024]{1,0:T(8,128)(2,1)} custom-call(s32[1]{0:T(128)} %bitcast.me_ref, bf16[2,256,512]{2,1,0:T(8,128)(2,1)S(1)} %join_rows.1.refs_0_, bf16[2,256,512]{2,1,0:T(8,128)(2,1)S(1)} %collective-permute-done.33.refs_1_, bf16[2,256,512]{2,1,0:T(8,128)(2,1)S(1)} %collective-permute-done.34.refs_2_, ...), custom_call_target="tpu_custom_call", output_to_operand_aliasing={{}: (7, {})} | custom-call | flops 1 | bytes 1 | tf_op jit(solution)/shard_map/output_projection/pallas_call | solution.py:520
  (86 shorter events, 4.3 us)
Async XLA Ops:
  1.7 40.9 %copy-start = (bf16[272,384]{1,0:T(8,128)(2,1)}, bf16[272,384]{1,0:T(8,128)(2,1)S(1)}, u32[]{:S(2)}) copy-start(bf16[272,384]{1,0:T(8,128)(2,1)S(1)} %get-tuple-element.66.refs_0_) | copy-start | bytes 626692
  1.7 40.9 %copy-start.1 = (bf16[256,384]{1,0:T(8,128)(2,1)}, bf16[256,384]{1,0:T(8,128)(2,1)S(1)}, u32[]{:S(2)}) copy-start(bf16[256,384]{1,0:T(8,128)(2,1)S(1)} %get-tuple-element.76.refs_1_) | copy-start | bytes 589828
  1.7 10.4 %collective-permute-start.15 = (bf16[256,384]{1,0:T(8,128)(2,1)S(1)}, bf16[256,384]{1,0:T(8,128)(2,1)S(1)}, u32[]{:S(2)}, u32[]{:S(2)}) collective-permute-start(bf16[256,384]{1,0:T(8,128)(2,1)S(1)} %get-tuple-element.76.refs_1_), channel_id=1, source_target_pairs={{0,4},{1,5},{2,6},{3,7},{4,8},{5,9},{6,10},{7,11},{8,12},{9,13},{1... | collective-permute-start | bytes 589832 | tf_op jit(solution)/shard_map/ppermute | solution.py:580
  4.8 7.4 %collective-permute-start.16 = (bf16[256,384]{1,0:T(8,128)(2,1)S(1)}, bf16[256,384]{1,0:T(8,128)(2,1)S(1)}, u32[]{:S(2)}, u32[]{:S(2)}) collective-permute-start(bf16[256,384]{1,0:T(8,128)(2,1)S(1)} %get-tuple-element.76.refs_1_), channel_id=1, source_target_pairs={{0,2},{1,3},{2,0},{3,1},{4,6},{5,7},{6,4},{7,5},{8,10},{9,11},{10,... | collective-permute-start | bytes 589832 | tf_op jit(solution)/shard_map/ppermute | solution.py:580
  6.3 5.9 %collective-permute-start.17 = (bf16[256,384]{1,0:T(8,128)(2,1)S(1)}, bf16[256,384]{1,0:T(8,128)(2,1)S(1)}, u32[]{:S(2)}, u32[]{:S(2)}) collective-permute-start(bf16[256,384]{1,0:T(8,128)(2,1)S(1)} %get-tuple-element.76.refs_1_), channel_id=1, source_target_pairs={{0,1},{1,0},{2,3},{3,2},{4,5},{5,4},{6,7},{7,6},{8,9},{9,8},{10,11... | collective-permute-start | bytes 589832 | tf_op jit(solution)/shard_map/ppermute | solution.py:580
  6.3 9.9 %collective-permute-start = (bf16[272,384]{1,0:T(8,128)(2,1)S(1)}, bf16[272,384]{1,0:T(8,128)(2,1)S(1)}, u32[]{:S(2)}, u32[]{:S(2)}) collective-permute-start(bf16[272,384]{1,0:T(8,128)(2,1)S(1)} %get-tuple-element.66.refs_0_), channel_id=1, source_target_pairs={{0,4},{1,5},{2,6},{3,7},{4,8},{5,9},{6,10},{7,11},{8,12},{9,13},{1... | collective-permute-start | bytes 626696 | tf_op jit(solution)/shard_map/ppermute | solution.py:580
  7.9 8.3 %collective-permute-start.1 = (bf16[272,384]{1,0:T(8,128)(2,1)S(1)}, bf16[272,384]{1,0:T(8,128)(2,1)S(1)}, u32[]{:S(2)}, u32[]{:S(2)}) collective-permute-start(bf16[272,384]{1,0:T(8,128)(2,1)S(1)} %get-tuple-element.66.refs_0_), channel_id=1, source_target_pairs={{0,2},{1,3},{2,0},{3,1},{4,6},{5,7},{6,4},{7,5},{8,10},{9,11},{10,... | collective-permute-start | bytes 626696 | tf_op jit(solution)/shard_map/ppermute | solution.py:580
  12.1 4.1 %collective-permute-start.2 = (bf16[272,384]{1,0:T(8,128)(2,1)S(1)}, bf16[272,384]{1,0:T(8,128)(2,1)S(1)}, u32[]{:S(2)}, u32[]{:S(2)}) collective-permute-start(bf16[272,384]{1,0:T(8,128)(2,1)S(1)} %get-tuple-element.66.refs_0_), channel_id=1, source_target_pairs={{0,1},{1,0},{2,3},{3,2},{4,5},{5,4},{6,7},{7,6},{8,9},{9,8},{10,11... | collective-permute-start | bytes 626696 | tf_op jit(solution)/shard_map/ppermute | solution.py:580
  12.2 29.2 %copy-start.11 = (bf16[256,384]{1,0:T(8,128)(2,1)}, bf16[256,384]{1,0:T(8,128)(2,1)S(1)}, u32[]{:S(2)}) copy-start(bf16[256,384]{1,0:T(8,128)(2,1)S(1)} %collective-permute-done.16.refs_5_) | copy-start | bytes 589828
  12.2 9.3 %collective-permute-start.19 = (bf16[256,384]{1,0:T(8,128)(2,1)S(1)}, bf16[256,384]{1,0:T(8,128)(2,1)S(1)}, u32[]{:S(2)}, u32[]{:S(2)}) collective-permute-start(bf16[256,384]{1,0:T(8,128)(2,1)S(1)} %collective-permute-done.15.refs_3_), channel_id=1, source_target_pairs={{0,4},{1,5},{2,6},{3,7},{4,8},{5,9},{6,10},{7,11},{8,12},{9,13},{1... | collective-permute-start | bytes 589832 | tf_op jit(solution)/shard_map/ppermute | solution.py:580
  13.2 8.3 %collective-permute-start.20 = (bf16[256,384]{1,0:T(8,128)(2,1)S(1)}, bf16[256,384]{1,0:T(8,128)(2,1)S(1)}, u32[]{:S(2)}, u32[]{:S(2)}) collective-permute-start(bf16[256,384]{1,0:T(8,128)(2,1)S(1)} %collective-permute-done.15.refs_3_), channel_id=1, source_target_pairs={{0,2},{1,3},{2,0},{3,1},{4,6},{5,7},{6,4},{7,5},{8,10},{9,11},{10,... | collective-permute-start | bytes 589832 | tf_op jit(solution)/shard_map/ppermute | solution.py:580
  16.2 26.4 %copy-start.3 = (bf16[272,384]{1,0:T(8,128)(2,1)}, bf16[272,384]{1,0:T(8,128)(2,1)S(1)}, u32[]{:S(2)}) copy-start(bf16[272,384]{1,0:T(8,128)(2,1)S(1)} %collective-permute-done.refs_2_) | copy-start | bytes 626692
  16.2 5.8 %collective-permute-start.21 = (bf16[256,384]{1,0:T(8,128)(2,1)S(1)}, bf16[256,384]{1,0:T(8,128)(2,1)}, u32[]{:S(2)}, u32[]{:S(2)}) collective-permute-start(bf16[256,384]{1,0:T(8,128)(2,1)S(1)} %collective-permute-done.15.refs_3_), channel_id=1, source_target_pairs={{0,1},{1,0},{2,3},{3,2},{4,5},{5,4},{6,7},{7,6},{8,9},{9,8},{10,11... | collective-permute-start | bytes 589832 | tf_op jit(solution)/shard_map/ppermute | solution.py:580
  16.2 26.4 %copy-start.4 = (bf16[272,384]{1,0:T(8,128)(2,1)}, bf16[272,384]{1,0:T(8,128)(2,1)S(1)}, u32[]{:S(2)}) copy-start(bf16[272,384]{1,0:T(8,128)(2,1)S(1)} %collective-permute-done.1.refs_4_) | copy-start | bytes 626692
  16.2 26.4 %copy-start.5 = (bf16[272,384]{1,0:T(8,128)(2,1)}, bf16[272,384]{1,0:T(8,128)(2,1)S(1)}, u32[]{:S(2)}) copy-start(bf16[272,384]{1,0:T(8,128)(2,1)S(1)} %collective-permute-done.2.refs_6_) | copy-start | bytes 626692
  16.2 9.6 %collective-permute-start.3 = (bf16[272,384]{1,0:T(8,128)(2,1)S(1)}, bf16[272,384]{1,0:T(8,128)(2,1)S(1)}, u32[]{:S(2)}, u32[]{:S(2)}) collective-permute-start(bf16[272,384]{1,0:T(8,128)(2,1)S(1)} %collective-permute-done.refs_2_), channel_id=1, source_target_pairs={{0,4},{1,5},{2,6},{3,7},{4,8},{5,9},{6,10},{7,11},{8,12},{9,13},{1... | collective-permute-start | bytes 626696 | tf_op jit(solution)/shard_map/ppermute | solution.py:580
  17.6 10.4 %collective-permute-start.4 = (bf16[272,384]{1,0:T(8,128)(2,1)S(1)}, bf16[272,384]{1,0:T(8,128)(2,1)S(1)}, u32[]{:S(2)}, u32[]{:S(2)}) collective-permute-start(bf16[272,384]{1,0:T(8,128)(2,1)S(1)} %collective-permute-done.refs_2_), channel_id=1, source_target_pairs={{0,2},{1,3},{2,0},{3,1},{4,6},{5,7},{6,4},{7,5},{8,10},{9,11},{10,... | collective-permute-start | bytes 626696 | tf_op jit(solution)/shard_map/ppermute | solution.py:580
  21.4 1.4 %collective-permute-start.22 = (bf16[256,384]{1,0:T(8,128)(2,1)S(1)}, bf16[256,384]{1,0:T(8,128)(2,1)S(1)}, u32[]{:S(2)}, u32[]{:S(2)}) collective-permute-start(bf16[256,384]{1,0:T(8,128)(2,1)S(1)} %collective-permute-done.16.refs_5_), channel_id=1, source_target_pairs={{0,1},{1,0},{2,3},{3,2},{4,5},{5,4},{6,7},{7,6},{8,9},{9,8},{10,11... | collective-permute-start | bytes 589832 | tf_op jit(solution)/shard_map/ppermute | solution.py:580
  21.5 6.6 %collective-permute-start.5 = (bf16[272,384]{1,0:T(8,128)(2,1)S(1)}, bf16[272,384]{1,0:T(8,128)(2,1)S(1)}, u32[]{:S(2)}, u32[]{:S(2)}) collective-permute-start(bf16[272,384]{1,0:T(8,128)(2,1)S(1)} %collective-permute-done.refs_2_), channel_id=1, source_target_pairs={{0,1},{1,0},{2,3},{3,2},{4,5},{5,4},{6,7},{7,6},{8,9},{9,8},{10,11... | collective-permute-start | bytes 626696 | tf_op jit(solution)/shard_map/ppermute | solution.py:580
  22.0 6.6 %collective-permute-start.6 = (bf16[272,384]{1,0:T(8,128)(2,1)S(1)}, bf16[272,384]{1,0:T(8,128)(2,1)S(1)}, u32[]{:S(2)}, u32[]{:S(2)}) collective-permute-start(bf16[272,384]{1,0:T(8,128)(2,1)S(1)} %collective-permute-done.1.refs_4_), channel_id=1, source_target_pairs={{0,1},{1,0},{2,3},{3,2},{4,5},{5,4},{6,7},{7,6},{8,9},{9,8},{10,11... | collective-permute-start | bytes 626696 | tf_op jit(solution)/shard_map/ppermute | solution.py:580
  22.9 8.7 %collective-permute-start.23 = (bf16[256,384]{1,0:T(8,128)(2,1)S(1)}, bf16[256,384]{1,0:T(8,128)(2,1)S(1)}, u32[]{:S(2)}, u32[]{:S(2)}) collective-permute-start(bf16[256,384]{1,0:T(8,128)(2,1)S(1)} %collective-permute-done.19.refs_9_), channel_id=1, source_target_pairs={{0,4},{1,5},{2,6},{3,7},{4,8},{5,9},{6,10},{7,11},{8,12},{9,13},{1... | collective-permute-start | bytes 589832 | tf_op jit(solution)/shard_map/ppermute | solution.py:580
  25.8 9.1 %collective-permute-start.24 = (bf16[256,384]{1,0:T(8,128)(2,1)S(1)}, bf16[256,384]{1,0:T(8,128)(2,1)}, u32[]{:S(2)}, u32[]{:S(2)}) collective-permute-start(bf16[256,384]{1,0:T(8,128)(2,1)S(1)} %collective-permute-done.19.refs_9_), channel_id=1, source_target_pairs={{0,2},{1,3},{2,0},{3,1},{4,6},{5,7},{6,4},{7,5},{8,10},{9,11},{10,... | collective-permute-start | bytes 589832 | tf_op jit(solution)/shard_map/ppermute | solution.py:580
  28.0 6.9 %collective-permute-start.25 = (bf16[256,384]{1,0:T(8,128)(2,1)S(1)}, bf16[256,384]{1,0:T(8,128)(2,1)S(1)}, u32[]{:S(2)}, u32[]{:S(2)}) collective-permute-start(bf16[256,384]{1,0:T(8,128)(2,1)S(1)} %collective-permute-done.19.refs_9_), channel_id=1, source_target_pairs={{0,1},{1,0},{2,3},{3,2},{4,5},{5,4},{6,7},{7,6},{8,9},{9,8},{10,11... | collective-permute-start | bytes 589832 | tf_op jit(solution)/shard_map/ppermute | solution.py:580
  28.1 7.3 %collective-permute-start.26 = (bf16[256,384]{1,0:T(8,128)(2,1)S(1)}, bf16[256,384]{1,0:T(8,128)(2,1)S(1)}, u32[]{:S(2)}, u32[]{:S(2)}) collective-permute-start(bf16[256,384]{1,0:T(8,128)(2,1)S(1)} %collective-permute-done.20.refs_11_), channel_id=1, source_target_pairs={{0,1},{1,0},{2,3},{3,2},{4,5},{5,4},{6,7},{7,6},{8,9},{9,8},{10,11... | collective-permute-start | bytes 589832 | tf_op jit(solution)/shard_map/ppermute | solution.py:580
  28.6 9.9 %collective-permute-start.7 = (bf16[272,384]{1,0:T(8,128)(2,1)S(1)}, bf16[272,384]{1,0:T(8,128)(2,1)}, u32[]{:S(2)}, u32[]{:S(2)}) collective-permute-start(bf16[272,384]{1,0:T(8,128)(2,1)S(1)} %collective-permute-done.3.refs_8_), channel_id=1, source_target_pairs={{0,4},{1,5},{2,6},{3,7},{4,8},{5,9},{6,10},{7,11},{8,12},{9,13},{1... | collective-permute-start | bytes 626696 | tf_op jit(solution)/shard_map/ppermute | solution.py:580
  31.6 7.2 %collective-permute-start.8 = (bf16[272,384]{1,0:T(8,128)(2,1)S(1)}, bf16[272,384]{1,0:T(8,128)(2,1)}, u32[]{:S(2)}, u32[]{:S(2)}) collective-permute-start(bf16[272,384]{1,0:T(8,128)(2,1)S(1)} %collective-permute-done.3.refs_8_), channel_id=1, source_target_pairs={{0,2},{1,3},{2,0},{3,1},{4,6},{5,7},{6,4},{7,5},{8,10},{9,11},{10,... | collective-permute-start | bytes 626696 | tf_op jit(solution)/shard_map/ppermute | solution.py:580
  34.9 3.9 %collective-permute-start.9 = (bf16[272,384]{1,0:T(8,128)(2,1)S(1)}, bf16[272,384]{1,0:T(8,128)(2,1)S(1)}, u32[]{:S(2)}, u32[]{:S(2)}) collective-permute-start(bf16[272,384]{1,0:T(8,128)(2,1)S(1)} %collective-permute-done.3.refs_8_), channel_id=1, source_target_pairs={{0,1},{1,0},{2,3},{3,2},{4,5},{5,4},{6,7},{7,6},{8,9},{9,8},{10,11... | collective-permute-start | bytes 626696 | tf_op jit(solution)/shard_map/ppermute | solution.py:580
  34.9 3.9 %collective-permute-start.10 = (bf16[272,384]{1,0:T(8,128)(2,1)S(1)}, bf16[272,384]{1,0:T(8,128)(2,1)S(1)}, u32[]{:S(2)}, u32[]{:S(2)}) collective-permute-start(bf16[272,384]{1,0:T(8,128)(2,1)S(1)} %collective-permute-done.4.refs_10_), channel_id=1, source_target_pairs={{0,1},{1,0},{2,3},{3,2},{4,5},{5,4},{6,7},{7,6},{8,9},{9,8},{10,11... | collective-permute-start | bytes 626696 | tf_op jit(solution)/shard_map/ppermute | solution.py:580
  35.4 7.1 %collective-permute-start.18 = (bf16[256,384]{1,0:T(8,128)(2,1)S(1)}, bf16[256,384]{1,0:T(8,128)(2,1)S(1)}, u32[]{:S(2)}, u32[]{:S(2)}) collective-permute-start(bf16[256,384]{1,0:T(8,128)(2,1)S(1)} %collective-permute-done.16.refs_5_), channel_id=1, source_target_pairs={{0,12},{1,13},{2,14},{3,15},{4,0},{5,1},{6,2},{7,3},{8,4},{9,5},{1... | collective-permute-start | bytes 589832 | tf_op jit(solution)/shard_map/ppermute | solution.py:580
  38.6 3.9 %collective-permute-start.27 = (bf16[256,384]{1,0:T(8,128)(2,1)S(1)}, bf16[256,384]{1,0:T(8,128)(2,1)S(1)}, u32[]{:S(2)}, u32[]{:S(2)}) collective-permute-start(bf16[256,384]{1,0:T(8,128)(2,1)S(1)} %collective-permute-done.23.refs_17_), channel_id=1, source_target_pairs={{0,1},{1,0},{2,3},{3,2},{4,5},{5,4},{6,7},{7,6},{8,9},{9,8},{10,11... | collective-permute-start | bytes 589832 | tf_op jit(solution)/shard_map/ppermute | solution.py:580
  38.9 12.8 %collective-permute-start.11 = (bf16[272,384]{1,0:T(8,128)(2,1)}, bf16[272,384]{1,0:T(8,128)(2,1)S(1)}, u32[]{:S(2)}, u32[]{:S(2)}) collective-permute-start(bf16[272,384]{1,0:T(8,128)(2,1)} %collective-permute-done.7.refs_16_), channel_id=1, source_target_pairs={{0,2},{1,3},{2,0},{3,1},{4,6},{5,7},{6,4},{7,5},{8,10},{9,11},{10,... | collective-permute-start | bytes 626696 | tf_op jit(solution)/shard_map/ppermute | solution.py:580
  40.9 10.8 %collective-permute-start.12 = (bf16[272,384]{1,0:T(8,128)(2,1)}, bf16[272,384]{1,0:T(8,128)(2,1)S(1)}, u32[]{:S(2)}, u32[]{:S(2)}) collective-permute-start(bf16[272,384]{1,0:T(8,128)(2,1)} %collective-permute-done.7.refs_16_), channel_id=1, source_target_pairs={{0,1},{1,0},{2,3},{3,2},{4,5},{5,4},{6,7},{7,6},{8,9},{9,8},{10,11... | collective-permute-start | bytes 626696 | tf_op jit(solution)/shard_map/ppermute | solution.py:580
  40.9 10.8 %collective-permute-start.13 = (bf16[272,384]{1,0:T(8,128)(2,1)}, bf16[272,384]{1,0:T(8,128)(2,1)S(1)}, u32[]{:S(2)}, u32[]{:S(2)}) collective-permute-start(bf16[272,384]{1,0:T(8,128)(2,1)} %collective-permute-done.8.refs_18_), channel_id=1, source_target_pairs={{0,1},{1,0},{2,3},{3,2},{4,5},{5,4},{6,7},{7,6},{8,9},{9,8},{10,11... | collective-permute-start | bytes 626696 | tf_op jit(solution)/shard_map/ppermute | solution.py:580
  42.5 8.7 %collective-permute-start.28 = (bf16[256,384]{1,0:T(8,128)(2,1)}, bf16[256,384]{1,0:T(8,128)(2,1)S(1)}, u32[]{:S(2)}, u32[]{:S(2)}) collective-permute-start(bf16[256,384]{1,0:T(8,128)(2,1)} %collective-permute-done.24.refs_19_), channel_id=1, source_target_pairs={{0,1},{1,0},{2,3},{3,2},{4,5},{5,4},{6,7},{7,6},{8,9},{9,8},{10,11... | collective-permute-start | bytes 589832 | tf_op jit(solution)/shard_map/ppermute | solution.py:580
  42.5 9.2 %collective-permute-start.14 = (bf16[256,256]{1,0:T(8,128)(2,1)}, bf16[256,256]{1,0:T(8,128)(2,1)S(1)}, u32[]{:S(2)}, u32[]{:S(2)}) collective-permute-start(bf16[256,256]{1,0:T(8,128)(2,1)} %param.8), channel_id=1, source_target_pairs={{0,8},{1,9},{2,10},{3,11},{4,12},{5,13},{6,14},{7,15},{8,0},{9,1},... | collective-permute-start | bytes 393224 | tf_op jit(solution)/shard_map/ppermute | solution.py:580
  51.8 8.7 %collective-permute-start.31 = (bf16[2,256,256]{2,1,0:T(8,128)(2,1)S(1)}, bf16[2,256,256]{2,1,0:T(8,128)(2,1)S(1)}, u32[]{:S(2)}, u32[]{:S(2)}) collective-permute-start(bf16[2,256,256]{2,1,0:T(8,128)(2,1)S(1)} %pad_maximum_fusion), channel_id=1, source_target_pairs={{0,4},{1,5},{2,6},{3,7},{4,0},{5,1},{6,2},{7,3},{8,12},{9,13},{10,... | collective-permute-start | bytes 786440 | tf_op jit(solution)/shard_map/ppermute | solution.py:559
  53.8 1.7 %collective-permute-start.29 = (bf16[272,384]{1,0:T(8,128)(2,1)S(1)}, bf16[272,384]{1,0:T(8,128)(2,1)S(1)}, u32[]{:S(2)}, u32[]{:S(2)}) collective-permute-start(bf16[272,384]{1,0:T(8,128)(2,1)S(1)} %collective-permute-done.11.refs_0_), channel_id=1, source_target_pairs={{0,1},{1,0},{2,3},{3,2},{4,5},{5,4},{6,7},{7,6},{8,9},{9,8},{10,11... | collective-permute-start | bytes 626696 | tf_op jit(solution)/shard_map/ppermute | solution.py:580
  53.8 1.7 %collective-permute-start.30 = (bf16[256,384]{1,0:T(8,128)(2,1)S(1)}, bf16[256,384]{1,0:T(8,128)(2,1)S(1)}, u32[]{:S(2)}, u32[]{:S(2)}) collective-permute-start(bf16[256,384]{1,0:T(8,128)(2,1)S(1)} %collective-permute-done.18.refs_1_), channel_id=1, source_target_pairs={{0,1},{1,0},{2,3},{3,2},{4,5},{5,4},{6,7},{7,6},{8,9},{9,8},{10,11... | collective-permute-start | bytes 589832 | tf_op jit(solution)/shard_map/ppermute | solution.py:580
  60.5 26.6 %all-to-all-start = ((bf16[16,128,256]{2,1,0:T(8,128)(2,1)}), bf16[16,128,256]{2,1,0:T(8,128)(2,1)S(1)}, u32[]{:S(2)}, u32[]{:S(2)}) async-start(bf16[16,128,256]{2,1,0:T(8,128)(2,1)} %get-tuple-element.115), calls=%async_computation | async-start | bytes 2097152 | tf_op jit(solution)/shard_map/all_to_all | solution.py:664
  64.5 8.4 %collective-permute-start.32 = (bf16[2,256,256]{2,1,0:T(8,128)(2,1)S(1)}, bf16[2,256,256]{2,1,0:T(8,128)(2,1)S(1)}, u32[]{:S(2)}, u32[]{:S(2)}) collective-permute-start(bf16[2,256,256]{2,1,0:T(8,128)(2,1)S(1)} %pad_maximum_fusion.2), channel_id=1, source_target_pairs={{0,16},{16,0},{1,17},{17,1},{2,18},{18,2},{3,19},{19,3},{4,20},{20... | collective-permute-start | bytes 786440 | tf_op jit(solution)/shard_map/ppermute | solution.py:624
  73.1 17.9 %collective-permute-start.33 = (bf16[2,256,512]{2,1,0:T(8,128)(2,1)S(1)}, bf16[2,256,512]{2,1,0:T(8,128)(2,1)S(1)}, u32[]{:S(2)}, u32[]{:S(2)}) collective-permute-start(bf16[2,256,512]{2,1,0:T(8,128)(2,1)S(1)} %join_rows.1.refs_0_), channel_id=1, source_target_pairs={{0,2},{1,3},{2,0},{3,1},{4,6},{5,7},{6,4},{7,5},{8,10},{9,11},{10,... | collective-permute-start | bytes 1572872 | tf_op jit(solution)/shard_map/ppermute | solution.py:559
  91.1 22.0 %all-to-all-start.1 = ((bf16[16,144,128]{2,1,0:T(8,128)(2,1)}), bf16[16,144,128]{2,1,0:T(8,128)(2,1)S(1)}, u32[]{:S(2)}, u32[]{:S(2)}) async-start(bf16[16,144,128]{2,1,0:T(8,128)(2,1)} %get-tuple-element.124), calls=%async_computation.1 | async-start | bytes 1179648 | tf_op jit(solution)/shard_map/all_to_all | solution.py:676
  97.6 20.6 %collective-permute-start.34 = (bf16[2,256,512]{2,1,0:T(8,128)(2,1)S(1)}, bf16[2,256,512]{2,1,0:T(8,128)(2,1)S(1)}, u32[]{:S(2)}, u32[]{:S(2)}) collective-permute-start(bf16[2,256,512]{2,1,0:T(8,128)(2,1)S(1)} %join_rows.1.refs_0_), channel_id=1, source_target_pairs={{0,1},{1,0},{2,3},{3,2},{4,5},{5,4},{6,7},{7,6},{8,9},{9,8},{10,11... | collective-permute-start | bytes 1572872 | tf_op jit(solution)/shard_map/ppermute | solution.py:559
  98.0 20.7 %collective-permute-start.35 = (bf16[2,256,512]{2,1,0:T(8,128)(2,1)S(1)}, bf16[2,256,512]{2,1,0:T(8,128)(2,1)S(1)}, u32[]{:S(2)}, u32[]{:S(2)}) collective-permute-start(bf16[2,256,512]{2,1,0:T(8,128)(2,1)S(1)} %collective-permute-done.33.refs_1_), channel_id=1, source_target_pairs={{0,1},{1,0},{2,3},{3,2},{4,5},{5,4},{6,7},{7,6},{8,9},{9,8},{10,11... | collective-permute-start | bytes 1572872 | tf_op jit(solution)/shard_map/ppermute | solution.py:559
  114.6 6.4 %collective-permute-start.39 = (bf16[256,256]{1,0:T(8,128)(2,1)S(1)}, bf16[256,256]{1,0:T(8,128)(2,1)S(1)}, u32[]{:S(2)}, u32[]{:S(2)}) collective-permute-start(bf16[256,256]{1,0:T(8,128)(2,1)S(1)} %get-tuple-element.128.refs_4_), channel_id=1, source_target_pairs={{0,16},{16,0},{1,17},{17,1},{2,18},{18,2},{3,19},{19,3},{4,20},{20... | collective-permute-start | bytes 393224 | tf_op jit(solution)/shard_map/ppermute | solution.py:680
  116.1 7.7 %collective-permute-start.38 = (bf16[256,256]{1,0:T(8,128)(2,1)S(1)}, bf16[256,256]{1,0:T(8,128)(2,1)S(1)}, u32[]{:S(2)}, u32[]{:S(2)}) collective-permute-start(bf16[256,256]{1,0:T(8,128)(2,1)S(1)} %get-tuple-element.127.refs_4_), channel_id=1, source_target_pairs={{0,16},{16,0},{1,17},{17,1},{2,18},{18,2},{3,19},{19,3},{4,20},{20... | collective-permute-start | bytes 393224 | tf_op jit(solution)/shard_map/ppermute | solution.py:680
  116.7 10.0 %collective-permute-start.37 = (bf16[256,256]{1,0:T(8,128)(2,1)S(1)}, bf16[256,256]{1,0:T(8,128)(2,1)S(1)}, u32[]{:S(2)}, u32[]{:S(2)}) collective-permute-start(bf16[256,256]{1,0:T(8,128)(2,1)S(1)} %get-tuple-element.126.refs_4_), channel_id=1, source_target_pairs={{0,16},{16,0},{1,17},{17,1},{2,18},{18,2},{3,19},{19,3},{4,20},{20... | collective-permute-start | bytes 393224 | tf_op jit(solution)/shard_map/ppermute | solution.py:680
  118.1 10.3 %collective-permute-start.36 = (bf16[256,256]{1,0:T(8,128)(2,1)S(1)}, bf16[256,256]{1,0:T(8,128)(2,1)S(1)}, u32[]{:S(2)}, u32[]{:S(2)}) collective-permute-start(bf16[256,256]{1,0:T(8,128)(2,1)S(1)} %get-tuple-element.125.refs_4_), channel_id=1, source_target_pairs={{0,16},{16,0},{1,17},{17,1},{2,18},{18,2},{3,19},{19,3},{4,20},{20... | collective-permute-start | bytes 393224 | tf_op jit(solution)/shard_map/ppermute | solution.py:680
  (11 other events, 135.9 us)
